TPU v7x, 32 devices: a whole 2x2x4 slice. The times are simulated.
32 devices in a mesh: groups: 2 (over y), img: 8 (over z, x), slab: 2 (over core).
Axes of the slice: x: 2, y: 2, z: 4, core: 2. Of those that a mesh axis runs over, the one named last changes fastest.
Arguments:
- images: bfloat16 [256, 256, 256], P(('groups', 'img')), parts along dimension 0, may hold values from -24 to 24
- class_index: int32 [256, 1], P(('groups', 'img')), parts along dimension 0, may hold values from 0 to 7
- pose_index: int32 [256], P(('groups', 'img')), parts along dimension 0, may hold values from 0 to 7
- defocus_bin: int32 [256], P(('groups', 'img')), parts along dimension 0, may hold values from 0 to 15
- defocus: float32 [16], replicated, may hold values from 1 to 6
- rows_table: bfloat16 [8, 128, 256], replicated, may hold values from -0.375 to 0.375
- cols_table: bfloat16 [8, 256, 256], P(None, None, 'slab'), may hold values from -0.375 to 0.375
- plane_weight: float32 [8, 2], replicated, may hold values from 0.25 to 1
Outputs:
- volume: float32 [128, 16, 2, 2, 256], P('img', 'groups', None, None, 'slab'), parts along dimension 1
There are 2 independent parts, one for each index of `groups`. A program takes and returns all parts, laid end to end along the dimension named above; an argument that names none is the same for every part. Nothing has to cross between parts.
All inputs are finite; a program needn't handle non-finite values.
Results may differ from a plain program's by a relative error of at most 0.0059.
Values may be sent and summed in bfloat16 or wider, within the bound.
No kernel may reach another device: no remote copies, remote signals or barrier semaphores. Data moves between devices by JAX's collectives and lax.ppermute only.
A program may use at most 64 MiB of HBM per device.

v0:
```python
import functools
import math

import jax
import jax.numpy as jnp
import numpy as np
from jax import lax
from jax.experimental import pallas as pl
from jax.experimental.pallas import tpu as pltpu
from jax.sharding import PartitionSpec as P

CLASSES = 8

wiener_ridge = 1.0
ctf_phase = 0.1
f32 = jnp.float32
bf16 = jnp.bfloat16


def packed_dft(box):
    half = box // 2
    k = np.concatenate([np.arange(half), [half], np.arange(1, half)])
    angle = (k[:, None] * np.arange(box)[None, :] % box) * (2.0 * math.pi / box)
    table = np.where((np.arange(box) <= half)[:, None], np.cos(angle), np.sin(angle))
    return (table / math.sqrt(box)).astype(np.float32)


def iota(shape, axis):
    return lax.broadcasted_iota(jnp.int32, shape, axis)


def dot(a, b, dims=((1,), (0,))):
    return lax.dot_general(a, b, (dims, ((), ())), preferred_element_type=f32)


def turns_sine(turns):
    return jnp.sin((turns - jnp.round(turns)) * (2.0 * math.pi))


def split_two(value):
    high = value.astype(bf16)
    return high, (value - high.astype(f32)).astype(bf16)


def fold_of(place, half):
    box = 2 * half
    return jnp.where(place <= half, place, box + half - place)


def slices_kernel(
    class_ref, pose_ref, bin_ref, defocus_ref, plane_ref,
    dft_ref, dft_t_ref, images_ref, rows_ref, cols_ref,
    out_ref,
    z_ref, rows_fold, cols_fold, ctf_left, ctf_right, spec_ref, mix_ref, totals,
):
    count, box, _ = images_ref.shape
    half = box // 2
    poses, rows, _ = rows_ref.shape
    cols = cols_ref.shape[2]
    planes = plane_ref.shape[1]

    place = iota((box, box), 0)
    other = iota((box, box), 1)
    near = (fold_of(place, half) == other).astype(f32).astype(bf16)
    far = (jnp.remainder(box - fold_of(place, half), box) == other).astype(f32).astype(bf16)

    z_ref[...] = dot(images_ref[...].reshape(count * box, box), dft_t_ref[...]).astype(bf16)
    rows_fold[...] = dot(
        rows_ref[...].reshape(poses * rows, box), near, ((1,), (1,))
    ).astype(bf16)
    for p in range(poses):
        cols_fold[p, :, :cols] = dot(near, cols_ref[p]).astype(bf16)
        cols_fold[p, :, cols:] = dot(far, cols_ref[p]).astype(bf16)

    lanes = ctf_left.shape[1]
    tall = ctf_left.shape[0]
    lane = iota((1, lanes), 1)
    sub = iota((count, box), 0)
    lane_defocus = jnp.zeros((1, lanes), f32)
    sub_defocus = jnp.zeros((count, box), f32)
    for i in range(count):
        value = defocus_ref[bin_ref[i]]
        lane_defocus = jnp.where(lane % count == i, value, lane_defocus)
        sub_defocus = jnp.where(sub == i, value, sub_defocus)
    scale = 1.0 / (2 * half * half)
    ky = jnp.minimum(iota((tall, lanes), 0), half).astype(f32)
    group = iota((tall, lanes), 1) // count
    turns = lane_defocus * (ky * ky * scale) + ctf_phase / (2.0 * math.pi)
    wave = turns_sine(turns + (group % 2).astype(f32) * 0.25)
    high, low = split_two(wave)
    ctf_left[...] = jnp.where(
        group < 4, high.astype(f32), jnp.where(group < 6, low.astype(f32), 0.0)
    ).astype(bf16)
    kx = iota((count, box), 1)
    kx = jnp.where(kx <= half, kx, kx - half).astype(f32)
    turns = sub_defocus * (kx * kx * scale)
    cos_high, cos_low = split_two(-turns_sine(turns + 0.25))
    sin_high, sin_low = split_two(-turns_sine(turns))
    zero = jnp.zeros((lanes - 6 * count, box), bf16)
    ctf_right[...] = jnp.concatenate(
        [cos_high, sin_high, cos_low, sin_low, cos_high, sin_high, zero], 0
    )

    totals[...] = jnp.zeros_like(totals)

    row_zero = iota((half, half), 0) == 0
    col_zero = iota((half, half), 1) == 0
    edge = row_zero | col_zero
    short_row = iota((16, half), 0) == 0
    short_col = iota((16, half), 1) == 0
    right_row = iota((lanes, box), 0) % count

    def one_image(i, carry):
        pose = pose_ref[i]
        chosen = jnp.where(right_row == i, ctf_right[...].astype(f32), 0.0).astype(bf16)
        contrast = dot(ctf_left[...], chosen)
        y = dot(dft_ref[...], z_ref[pl.ds(pl.multiple_of(i * box, box), box), :])
        cc, cs = y[:half, :half], y[:half, half:]
        sc, ss = y[half:, :half], y[half:, half:]
        ss_in = jnp.where(edge, 0.0, ss)
        sc_in = jnp.where(row_zero, 0.0, sc)
        cs_in = jnp.where(col_zero, 0.0, cs)
        near_ctf, far_ctf = contrast[:half, :half], contrast[:half, half:]
        spec_ref[0:half, 0:half] = (near_ctf * (cc - ss_in)).astype(bf16)
        spec_ref[0:half, half:] = (far_ctf * jnp.where(col_zero, cs, cc + ss_in)).astype(bf16)
        spec_ref[half:box, 0:half] = (-near_ctf * (sc_in + cs_in)).astype(bf16)
        spec_ref[half:box, half:] = (
            far_ctf * jnp.where(col_zero, jnp.where(row_zero, 0.0, -ss), cs_in - sc_in)
        ).astype(bf16)
        sc_top = jnp.broadcast_to(sc[0:1], (16, half))
        ss_top = jnp.broadcast_to(ss[0:1], (16, half))
        ss_top_in = jnp.where(short_col, 0.0, ss_top)
        edge_ctf = contrast[half : half + 1]
        spec_ref[box : box + 16, 0:half] = (
            edge_ctf[:, :half] * jnp.where(short_row, sc_top, -ss_top_in)
        ).astype(bf16)
        spec_ref[box : box + 16, half:] = (
            edge_ctf[:, half:]
            * jnp.where(short_row, jnp.where(short_col, ss_top, sc_top), ss_top_in)
        ).astype(bf16)
        mixed = dot(spec_ref[...], cols_fold[pose])
        top = iota((half, cols), 0) == 0
        mix_ref[0:half, 0:cols] = mixed[:half, :cols].astype(bf16)
        mix_ref[0:half, cols:] = mixed[half:box, :cols].astype(bf16)
        mix_ref[half:, 0:cols] = jnp.where(
            top, mixed[box : box + 1, :cols], mixed[:half, cols:]
        ).astype(bf16)
        mix_ref[half:, cols:] = jnp.where(
            top, mixed[box + 1 : box + 2, :cols], -mixed[half:box, cols:]
        ).astype(bf16)
        pose_rows = rows_fold[pl.ds(pl.multiple_of(pose * rows, rows), rows), :]
        piece = dot(pose_rows, mix_ref[...])
        for z in range(planes):
            slot = class_ref[i, 0] * planes + z
            totals[slot] += plane_ref[pose, z] * piece
        return carry

    lax.fori_loop(0, count, one_image, 0, unroll=True)
    owned = out_ref.shape[2]
    for d in range(out_ref.shape[0]):
        out_ref[d] = totals[:, d * owned : (d + 1) * owned, :].astype(bf16)


def own_totals(images, class_index, pose_index, defocus_bin, defocus, rows_table, cols_table, plane_weight, pieces):
    count, box, _ = images.shape
    poses, rows, _ = rows_table.shape
    cols = cols_table.shape[2]
    planes = plane_weight.shape[1]
    slots = CLASSES * planes
    owned = rows // pieces
    table = packed_dft(box)
    smem = pl.BlockSpec(memory_space=pltpu.SMEM)
    vmem = pl.BlockSpec(memory_space=pltpu.VMEM)
    lanes = 128 * (-(-6 * count // 128))
    return pl.pallas_call(
        slices_kernel,
        out_shape=jax.ShapeDtypeStruct((pieces, slots, owned, 2 * cols), bf16),
        in_specs=[smem] * 5 + [vmem] * 5,
        out_specs=vmem,
        scratch_shapes=[
            pltpu.VMEM((count * box, box), bf16),
            pltpu.VMEM((poses * rows, box), bf16),
            pltpu.VMEM((poses, box, 2 * cols), bf16),
            pltpu.VMEM((box // 2 + 16, lanes), bf16),
            pltpu.VMEM((lanes, box), bf16),
            pltpu.VMEM((box + 16, box), bf16),
            pltpu.VMEM((box, 2 * cols), bf16),
            pltpu.VMEM((slots, rows, 2 * cols), f32),
        ],
        compiler_params=pltpu.CompilerParams(vmem_limit_bytes=48 * 1024 * 1024),
        cost_estimate=pl.CostEstimate(
            flops=2 * count * box * box * 1000, bytes_accessed=6 * 1024 * 1024, transcendentals=0
        ),
    )(
        class_index, pose_index, defocus_bin, defocus, plane_weight,
        jnp.asarray(table, bf16), jnp.asarray(table.T.copy(), bf16),
        images, rows_table, cols_table,
    )


def squared_table(weight_table):
    wide_table = weight_table.astype(f32)
    return (wide_table * wide_table).astype(bf16)


def weight_totals(class_index, pose_index, defocus_bin, defocus, rows_table, cols_table, plane_weight, first_row, owned):
    box = rows_table.shape[2]
    poses = rows_table.shape[0]
    bins = defocus.shape[0]
    half = box // 2
    exact = lax.Precision.HIGHEST
    code = (class_index[:, 0] * poses + pose_index) * bins + defocus_bin
    codes = lax.all_gather(code, "img", tiled=True)
    hits = (codes[:, None] == jnp.arange(CLASSES * poses * bins, dtype=jnp.int32)).astype(f32)
    counts = jnp.sum(hits, 0).reshape(CLASSES, poses, bins)
    place = jnp.arange(box, dtype=jnp.int32)
    freq = jnp.where(place < half, place, place - box).astype(f32)
    turns = defocus[:, None] * (freq * freq)[None, :] * (1.0 / (half * half))
    turns_y = turns + ctf_phase / math.pi
    ones = jnp.ones_like(turns)
    wave_y = jnp.stack([0.5 * ones, -0.5 * turns_sine(turns_y + 0.25), 0.5 * turns_sine(turns_y)])
    wave_x = jnp.stack([ones, turns_sine(turns + 0.25), turns_sine(turns)])
    rows_own = lax.dynamic_slice_in_dim(rows_table, first_row, owned, 1)
    u = jnp.einsum("pry,mby->pmbr", squared_table(rows_own).astype(f32), wave_y, precision=exact)
    v = jnp.einsum("pxj,mbx->pmbj", squared_table(cols_table).astype(f32), wave_x, precision=exact)
    weight = counts[:, None] * plane_weight.T[None, :, :, None]
    left = weight[:, :, :, None, :, None] * u[None, None]
    return jnp.einsum("czpmbr,pmbj->rczj", left, v, precision=exact)


def body(images, class_index, pose_index, defocus_bin, defocus, rows_table, cols_table, plane_weight):
    rows = rows_table.shape[1]
    cols = cols_table.shape[2]
    planes = plane_weight.shape[1]
    members = lax.axis_size("img")
    owned = rows // members
    pieces = members if owned % 16 == 0 else 1
    totals = own_totals(
        images, class_index, pose_index, defocus_bin, defocus, rows_table, cols_table, plane_weight, pieces
    )
    slots = totals.shape[1]
    if pieces == 1:
        totals = totals.reshape(slots, members, owned, 2 * cols).transpose(1, 0, 2, 3)
    own = lax.psum_scatter(totals, "img", scatter_dimension=0, tiled=False)
    weight = weight_totals(
        class_index, pose_index, defocus_bin, defocus, rows_table, cols_table, plane_weight,
        lax.axis_index("img") * owned, owned,
    )
    own = own.astype(f32).reshape(CLASSES, planes, owned, 2, cols).transpose(2, 0, 1, 3, 4)
    return own / (weight[:, :, :, None, :] + wiener_ridge)


def solution(mesh):
    placed = (
        P(("groups", "img"), None, None),
        P(("groups", "img"), None),
        P(("groups", "img")),
        P(("groups", "img")),
        P(),
        P(),
        P(None, None, "slab"),
        P(),
    )
    return jax.shard_map(
        body,
        mesh=mesh,
        in_specs=placed,
        out_specs=P("img", "groups", None, None, "slab"),
        check_vma=False,
    )
```

profile of v0, /device:TPU:0, one launch (start us, length us, event | category | flops | bytes accessed | tf_op | source)
XLA Modules:
  0.0 100.6 jit_solution(1528517269744669578)
XLA Ops:
  6.5 0.0 reduce-scatter.2.cloned.1.call-start
  6.5 0.7 copy.15.class_ref
  7.3 0.8 copy.16.plane_ref
  8.0 0.0 copy-start
  8.0 1.0 %copy-done = bf16[8,256,128]{2,1,0:T(8,128)(2,1)S(1)} copy-done((bf16[8,256,128]{2,1,0:T(8,128)(2,1)S(1)}, bf16[8,256,128]{2,1,0:T(8,128)(2,1)}, u32[]{:S(2)}) %copy-start) | copy-done | bytes 524312
  9.1 0.0 copy-start.2
  9.1 1.0 %copy-done.2 = bf16[8,128,256]{2,1,0:T(8,128)(2,1)S(1)} copy-done((bf16[8,128,256]{2,1,0:T(8,128)(2,1)S(1)}, bf16[8,128,256]{2,1,0:T(8,128)(2,1)}, u32[]{:S(2)}) %copy-start.2) | copy-done | bytes 524312
  10.1 0.0 copy-start.3
  10.1 0.7 copy-done.3
  10.8 0.0 copy-start.5
  10.8 0.7 copy-done.5
  11.4 0.0 copy-start.7
  11.4 0.7 copy-done.7
  12.1 0.0 copy-start.9
  12.1 1.6 %copy-done.9 = bf16[16,256,256]{2,1,0:T(8,128)(2,1)S(1)} copy-done((bf16[16,256,256]{2,1,0:T(8,128)(2,1)S(1)}, bf16[16,256,256]{2,1,0:T(8,128)(2,1)}, u32[]{:S(2)}) %copy-start.9) | copy-done | bytes 2097176
  13.7 0.0 copy-start.10
  13.7 0.9 copy-done.10
  14.6 0.0 copy-start.11
  14.6 0.9 copy-done.11
  15.5 0.0 copy-start.14
  15.5 0.0 copy-start.6
  15.5 0.0 copy-start.8
  15.5 0.0 copy-start.13
  15.5 0.0 copy-start.4
  15.5 0.0 copy-start.1
  15.5 10.0 %shard_map.100 = bf16[8,16,16,256]{3,2,1,0:T(8,128)(2,1)} custom-call(s32[16,1]{1,0:T(8,128)S(1)} %copy.15.class_ref, s32[16]{0:T(128)S(1)} %copy-done.5, s32[16]{0:T(128)S(1)} %copy-done.7, f32[16]{0:T(128)S(1)} %copy-done.3, f32[8,2]{1,0:T(8,128)S(1)} %copy.16.plane_ref, bf16[256,256]{1,0:T(8,128)(2,1)S(1)} %copy-done.10, bf16[256,256]{1,0:T(8,128)(2,1)S(1)} %copy-done.11, ...), custom_call_target="tpu_custom_call" | custom-call | flops 2097152000 | bytes 6291456 | tf_op jit(solution)/shard_map/pallas_call | solution.py:175
  25.6 0.0 reduce-scatter.2.cloned.1.call-update
  25.6 0.0 copy-done.14
  25.6 0.6 dynamic-slice
  26.8 0.0 copy-done.6
  26.9 0.0 copy-done.8
  26.9 0.0 copy-done.13
  26.9 0.1 fusion.40
  27.0 13.1 %all-reduce = s32[128]{0:T(128)S(1)} all-reduce(s32[128]{0:T(128)S(1)} %fusion.40), channel_id=1, replica_groups=mesh['groups'=2,'img'=8,'slab'=2] {'img'}, use_global_device_ids=true, to_apply=%add | all-reduce | flops 128 | bytes 1024
  40.0 0.1 convert_reduce_fusion
  40.2 0.1 mul.190
  40.3 0.0 copy-done.4
  40.3 0.3 fusion.32
  40.6 1.1 %convolution_bitcast_fusion.1 = f32[8,3,16,16]{2,3,0,1:T(8,128)S(1)} fusion(bf16[8,128,256]{2,1,0:T(8,128)(2,1)} %rows_ref.1, s32[]{:T(128)S(6)} %select_n.12, f32[1,16,256]{2,1,0:T(8,128)S(1)} %get-tuple-element.7, f32[1,16,256]{2,1,0:T(8,128)S(1)} %get-tuple-element.5, f32[1,16,256]{2,1,0:T(8,128)S(1)} %stack.14), kind=kOutput, calls=%fused_computation.5 | convolution fusion | flops 18997248 | bytes 139268 | tf_op jit(solution)/shard_map/pry,mby->pmbr/dot_general | solution.py:224
  41.7 0.0 copy-done.1
  41.7 0.4 convolution_bitcast_fusion
  42.1 0.0 copy-done.12
  42.1 0.1 broadcast_multiply_fusion
  42.2 4.5 %fusion.10 = f32[16,8,2,128]{3,0,2,1:T(8,128)S(1)} fusion(f32[8,3,16,128,1,1]{3,2,0,1,5,4:T(8,128)S(1)} %convolution_bitcast_fusion, f32[8,3,16,16]{2,3,0,1:T(8,128)S(1)} %convolution_bitcast_fusion.1, f32[8,2,8,16]{3,2,1,0:T(8,128)S(1)} %broadcast_multiply_fusion), kind=kOutput, calls=%fused_computation.8 | convolution fusion | flops 151126016 | bytes 360448 | tf_op jit(solution)/shard_map/czpmbr,pmbj->rczj/dot_general | solution.py:228
  46.7 0.1 copy.18
  46.7 45.2 %reduce-scatter.2.cloned.1.call-done = bf16[1,16,16,256]{3,2,1,0:T(8,128)(2,1)} async-done(((bf16[8,16,16,256]{3,2,1,0:T(8,128)(2,1)}), bf16[1,16,16,256]{3,2,1,0:T(8,128)(2,1)}) %reduce-scatter.2.cloned.1.call-update) | async-done | bytes 131088 | tf_op jit(solution)/shard_map/reduce_scatter | solution.py:244
  91.9 1.0 %reshape.243 = f32[8,2,16,2,128]{4,3,2,1,0:T(2,128)S(1)} reshape(bf16[1,16,16,256]{3,2,1,0:T(8,128)(2,1)} %reduce-scatter.2.cloned.1.call-done) | data formatting | bytes 393216 | tf_op jit(solution)/shard_map/transpose | solution.py:249
  92.9 0.8 bitcast_divide_fusion
  (5 shorter events, 0.0 us)
Async XLA Ops:
  6.5 85.4 %reduce-scatter.2.cloned.1.call-start = ((), (), s32[]{:S(2)}) async-start(), calls=%async_computation.1 | async-start | bytes 1179648 | tf_op jit(solution)/shard_map/reduce_scatter | solution.py:244
  8.0 1.0 %copy-start = (bf16[8,256,128]{2,1,0:T(8,128)(2,1)S(1)}, bf16[8,256,128]{2,1,0:T(8,128)(2,1)}, u32[]{:S(2)}) copy-start(bf16[8,256,128]{2,1,0:T(8,128)(2,1)} %cols_ref.1) | copy-start | bytes 1572868
  9.1 1.0 %copy-start.2 = (bf16[8,128,256]{2,1,0:T(8,128)(2,1)S(1)}, bf16[8,128,256]{2,1,0:T(8,128)(2,1)}, u32[]{:S(2)}) copy-start(bf16[8,128,256]{2,1,0:T(8,128)(2,1)} %rows_ref.1) | copy-start | bytes 1572868
  10.1 0.7 copy-start.3
  10.8 0.7 copy-start.5
  11.4 0.7 copy-start.7
  12.1 1.6 %copy-start.9 = (bf16[16,256,256]{2,1,0:T(8,128)(2,1)S(1)}, bf16[16,256,256]{2,1,0:T(8,128)(2,1)}, u32[]{:S(2)}) copy-start(bf16[16,256,256]{2,1,0:T(8,128)(2,1)} %images_ref.1) | copy-start | bytes 6291460
  13.7 0.9 copy-start.10
  14.6 0.9 copy-start.11
  15.5 10.1 %copy-start.14 = (u32[32]{0:T(128)S(1)}, u32[32]{0:T(128)}, u32[]{:S(2)}) copy-start(u32[32]{0:T(128)} %constant.47) | copy-start | bytes 388
  15.5 11.4 %copy-start.6 = (s32[16]{0:T(128)S(1)}, s32[16]{0:T(128)}, u32[]{:S(2)}) copy-start(s32[16]{0:T(128)} %pose_ref.1) | copy-start | bytes 196
  15.5 11.4 %copy-start.8 = (s32[16]{0:T(128)S(1)}, s32[16]{0:T(128)}, u32[]{:S(2)}) copy-start(s32[16]{0:T(128)} %bin_ref.1) | copy-start | bytes 196
  15.5 11.4 %copy-start.13 = (s32[16,1]{0,1:T(1,128)S(1)}, s32[16,1]{0,1:T(1,128)}, u32[]{:S(2)}) copy-start(s32[16,1]{0,1:T(1,128)} %param.11) | copy-start | bytes 196
  15.5 24.8 %copy-start.4 = (f32[16]{0:T(128)S(1)}, f32[16]{0:T(128)}, u32[]{:S(2)}) copy-start(f32[16]{0:T(128)} %defocus_ref.1) | copy-start | bytes 196
  15.5 26.2 %copy-start.1 = (bf16[8,256,128]{2,1,0:T(8,128)(2,1)S(1)}, bf16[8,256,128]{2,1,0:T(8,128)(2,1)}, u32[]{:S(2)}) copy-start(bf16[8,256,128]{2,1,0:T(8,128)(2,1)} %cols_ref.1) | copy-start | bytes 1572868
  25.6 16.6 %copy-start.12 = (f32[8,2]{0,1:T(2,128)S(1)}, f32[8,2]{0,1:T(2,128)}, u32[]{:S(2)}) copy-start(f32[8,2]{0,1:T(2,128)} %param.17) | copy-start | bytes 196
Sparse Core Ops, SparseCore 0:
  25.7 66.1 reduce-scatter.1
where the time goes:
time: 101 us
  waiting for transfers between devices  45.2 us (45%)
  between operations  14.2 us (14%)
  blocking collectives  13.1 us (13%)
  local copies, waits for them, and re-layouts  10.7 us (11%)
  Pallas kernels  10 us (10%)
  matrix products  5.98 us (6%)
  other arithmetic  1.46 us (1%)
    reduce_scatter x1, waiting for transfers between devices, body(): own = lax.psum_scatter(totals, 'img', scatter_dimension=0, tiled=False)  45.2 us
    unnamed x1, blocking collectives  13.1 us
    pallas_call x1, Pallas kernels, own_totals(): pl.pallas_call(slices_kernel, out_shape=jax.ShapeDtypeStruct((pieces, slo...  10 us
    unnamed x34, local copies, waits for them, and re-layouts  9.54 us
    dot_general x1, matrix products, weight_totals(): return jnp.einsum('czpmbr,pmbj->rczj', left, v, precision=exact)  4.45 us
  transfers between devices with their start and end apart: 1, of which 1 were waited for; matrix products, arithmetic and copies ran while one was open for 7% of the time, Pallas kernels for 0%

commit v1 on v0

--- a/solution.py
+++ b/solution.py
@@ -48,30 +48,43 @@
 
 
 def slices_kernel(
-    class_ref, pose_ref, bin_ref, defocus_ref, plane_ref,
-    dft_ref, dft_t_ref, images_ref, rows_ref, cols_ref,
-    out_ref,
-    z_ref, rows_fold, cols_fold, ctf_left, ctf_right, spec_ref, mix_ref, totals,
+    class_hbm, pose_hbm, bin_hbm, defocus_hbm, plane_hbm,
+    dft_hbm, dft_t_hbm, images_hbm, rows_hbm, cols_hbm,
+    *refs,
 ):
+    outs, refs = refs[:-SCRATCH], refs[-SCRATCH:]
+    (
+        class_ref, pose_ref, bin_ref, defocus_ref, plane_ref,
+        dft_ref, dft_t_ref, images_ref, rows_ref, cols_ref, arrived,
+        z_ref, rows_fold, cols_fold, ctf_left, ctf_right, spec_ref, mix_ref, totals,
+    ) = refs
     count, box, _ = images_ref.shape
     half = box // 2
     poses, rows, _ = rows_ref.shape
     cols = cols_ref.shape[2]
-    planes = plane_ref.shape[1]
+    planes = plane_ref.shape[0]
+
+    pairs = (
+        (class_hbm, class_ref), (pose_hbm, pose_ref), (bin_hbm, bin_ref),
+        (defocus_hbm, defocus_ref), (plane_hbm, plane_ref),
+        (rows_hbm, rows_ref), (cols_hbm, cols_ref), (dft_t_hbm, dft_t_ref),
+        (images_hbm, images_ref), (dft_hbm, dft_ref),
+    )
+    copies = [
+        pltpu.make_async_copy(source, target, arrived.at[n])
+        for n, (source, target) in enumerate(pairs)
+    ]
+    for copy in copies:
+        copy.start()
 
     place = iota((box, box), 0)
     other = iota((box, box), 1)
-    near = (fold_of(place, half) == other).astype(f32).astype(bf16)
-    far = (jnp.remainder(box - fold_of(place, half), box) == other).astype(f32).astype(bf16)
-
-    z_ref[...] = dot(images_ref[...].reshape(count * box, box), dft_t_ref[...]).astype(bf16)
-    rows_fold[...] = dot(
-        rows_ref[...].reshape(poses * rows, box), near, ((1,), (1,))
-    ).astype(bf16)
-    for p in range(poses):
-        cols_fold[p, :, :cols] = dot(near, cols_ref[p]).astype(bf16)
-        cols_fold[p, :, cols:] = dot(far, cols_ref[p]).astype(bf16)
-
+    folded = fold_of(place, half)
+    near = (folded == other).astype(f32).astype(bf16)
+    far = (jnp.where(folded == 0, 0, box - folded) == other).astype(f32).astype(bf16)
+
+    for copy in copies[:5]:
+        copy.wait()
     lanes = ctf_left.shape[1]
     tall = ctf_left.shape[0]
     lane = iota((1, lanes), 1)
@@ -100,8 +113,19 @@
     ctf_right[...] = jnp.concatenate(
         [cos_high, sin_high, cos_low, sin_low, cos_high, sin_high, zero], 0
     )
-
     totals[...] = jnp.zeros_like(totals)
+
+    copies[5].wait()
+    rows_fold[...] = dot(
+        rows_ref[...].reshape(poses * rows, box), near, ((1,), (1,))
+    ).astype(bf16)
+    copies[6].wait()
+    for p in range(poses):
+        cols_fold[p, :, :cols] = dot(near, cols_ref[p]).astype(bf16)
+        cols_fold[p, :, cols:] = dot(far, cols_ref[p]).astype(bf16)
+    for copy in copies[7:]:
+        copy.wait()
+    z_ref[...] = dot(images_ref[...].reshape(count * box, box), dft_t_ref[...]).astype(bf16)
 
     row_zero = iota((half, half), 0) == 0
     col_zero = iota((half, half), 1) == 0
@@ -151,33 +175,61 @@
         pose_rows = rows_fold[pl.ds(pl.multiple_of(pose * rows, rows), rows), :]
         piece = dot(pose_rows, mix_ref[...])
         for z in range(planes):
-            slot = class_ref[i, 0] * planes + z
-            totals[slot] += plane_ref[pose, z] * piece
+            slot = class_ref[i] * planes + z
+            totals[slot] += plane_ref[z, pose] * piece
         return carry
 
     lax.fori_loop(0, count, one_image, 0, unroll=True)
-    owned = out_ref.shape[2]
-    for d in range(out_ref.shape[0]):
-        out_ref[d] = totals[:, d * owned : (d + 1) * owned, :].astype(bf16)
-
-
-def own_totals(images, class_index, pose_index, defocus_bin, defocus, rows_table, cols_table, plane_weight, pieces):
+
+    if len(outs) == 1:
+        outs[0][...] = totals[...].astype(bf16)
+    else:
+        turns_round = len(outs) // 2
+        members = 2 * turns_round
+        owned = rows // members
+        me = lax.axis_index("img")
+        for k in range(turns_round):
+            mine = lax.rem(me + 2 * k, members)
+            theirs = mine + 1 - 2 * lax.rem(me, 2)
+            first = pl.multiple_of(theirs * owned, owned)
+            outs[k][...] = totals[:, pl.ds(first, owned), :].astype(bf16)
+            first = pl.multiple_of(mine * owned, owned)
+            outs[turns_round + k][...] = totals[:, pl.ds(first, owned), :]
+
+
+SCRATCH = 19
+
+
+def own_totals(images, class_index, pose_index, defocus_bin, defocus, rows_table, cols_table, plane_weight, turns_round):
     count, box, _ = images.shape
     poses, rows, _ = rows_table.shape
     cols = cols_table.shape[2]
     planes = plane_weight.shape[1]
     slots = CLASSES * planes
-    owned = rows // pieces
     table = packed_dft(box)
-    smem = pl.BlockSpec(memory_space=pltpu.SMEM)
+    any_place = pl.BlockSpec(memory_space=pl.ANY)
     vmem = pl.BlockSpec(memory_space=pltpu.VMEM)
     lanes = 128 * (-(-6 * count // 128))
+    if turns_round == 0:
+        out_shape = [jax.ShapeDtypeStruct((slots, rows, 2 * cols), bf16)]
+    else:
+        piece = (slots, rows // (2 * turns_round), 2 * cols)
+        out_shape = [jax.ShapeDtypeStruct(piece, bf16)] * turns_round
+        out_shape += [jax.ShapeDtypeStruct(piece, f32)] * turns_round
+    operands = (
+        class_index[:, 0], pose_index, defocus_bin, defocus, plane_weight.T,
+        jnp.asarray(table, bf16), jnp.asarray(table.T.copy(), bf16),
+        images, rows_table, cols_table,
+    )
     return pl.pallas_call(
         slices_kernel,
-        out_shape=jax.ShapeDtypeStruct((pieces, slots, owned, 2 * cols), bf16),
-        in_specs=[smem] * 5 + [vmem] * 5,
-        out_specs=vmem,
-        scratch_shapes=[
+        out_shape=out_shape,
+        in_specs=[any_place] * 10,
+        out_specs=[vmem] * len(out_shape),
+        scratch_shapes=[pltpu.SMEM(x.shape, x.dtype) for x in operands[:5]]
+        + [pltpu.VMEM(x.shape, x.dtype) for x in operands[5:]]
+        + [
+            pltpu.SemaphoreType.DMA((10,)),
             pltpu.VMEM((count * box, box), bf16),
             pltpu.VMEM((poses * rows, box), bf16),
             pltpu.VMEM((poses, box, 2 * cols), bf16),
@@ -187,15 +239,144 @@
             pltpu.VMEM((box, 2 * cols), bf16),
             pltpu.VMEM((slots, rows, 2 * cols), f32),
         ],
-        compiler_params=pltpu.CompilerParams(vmem_limit_bytes=48 * 1024 * 1024),
+        compiler_params=pltpu.CompilerParams(vmem_limit_bytes=VMEM_LIMIT),
         cost_estimate=pl.CostEstimate(
             flops=2 * count * box * box * 1000, bytes_accessed=6 * 1024 * 1024, transcendentals=0
         ),
-    )(
-        class_index, pose_index, defocus_bin, defocus, plane_weight,
-        jnp.asarray(table, bf16), jnp.asarray(table.T.copy(), bf16),
-        images, rows_table, cols_table,
-    )
+    )(*operands)
+
+
+VMEM_LIMIT = 56 * 1024 * 1024
+
+
+def ridge_kernel(defocus_hbm, plane_hbm, rows_hbm, cols_hbm, *refs):
+    codes, refs = refs[:-6], refs[-6:]
+    out_ref, defocus_ref, plane_ref, rows_ref, cols_ref, arrived = refs
+    poses, owned, box = rows_ref.shape
+    cols = cols_ref.shape[2]
+    bins = defocus_ref.shape[0]
+    planes = plane_ref.shape[0]
+    slots = CLASSES * planes
+    half = box // 2
+    first = pl.multiple_of(lax.axis_index("img") * owned, owned)
+    copies = [
+        pltpu.make_async_copy(defocus_hbm, defocus_ref, arrived.at[0]),
+        pltpu.make_async_copy(plane_hbm, plane_ref, arrived.at[1]),
+        pltpu.make_async_copy(rows_hbm.at[:, pl.ds(first, owned), :], rows_ref, arrived.at[2]),
+        pltpu.make_async_copy(cols_hbm, cols_ref, arrived.at[3]),
+    ]
+    for copy in copies:
+        copy.start()
+
+    code = codes[0][...]
+    for ref in codes[1:]:
+        code = jnp.maximum(code, ref[...])
+    images = code.shape[1]
+    wide = 128
+    kind = code // bins
+    slot_row = iota((slots, images), 0) // planes
+    left = (slot_row == kind // poses).astype(f32).astype(bf16)
+    term = iota((poses * wide, images), 0)
+    right_code = jnp.where(
+        term % wide < 3 * bins, (term // wide) * bins + term % bins, poses * bins
+    )
+    right = (right_code == code % (poses * bins)).astype(f32).astype(bf16)
+    counts = dot(left, right, ((1,), (1,)))
+
+    copies[0].wait()
+    copies[1].wait()
+    share_slot = iota((slots, poses * wide), 0) % planes
+    share_pose = iota((slots, poses * wide), 1) // wide
+    share = jnp.zeros((slots, poses * wide), f32)
+    for p in range(poses):
+        for z in range(planes):
+            share = jnp.where((share_slot == z) & (share_pose == p), plane_ref[z, p], share)
+    counts = counts * share
+
+    bin_row = iota((bins, box), 0)
+    sub_defocus = jnp.zeros((bins, box), f32)
+    for b in range(bins):
+        sub_defocus = jnp.where(bin_row == b, defocus_ref[b], sub_defocus)
+    freq = iota((bins, box), 1)
+    freq = jnp.where(freq < half, freq, box - freq).astype(f32)
+    turns_x = sub_defocus * (freq * freq * (1.0 / (half * half)))
+    turns_y = turns_x + ctf_phase / math.pi
+    zero = jnp.zeros((wide - 3 * bins, box), f32)
+    ones = jnp.ones((bins, box), f32)
+    wave_y = jnp.concatenate(
+        [0.5 * ones, -0.5 * turns_sine(turns_y + 0.25), 0.5 * turns_sine(turns_y), zero], 0
+    )
+    wave_x = jnp.concatenate([ones, turns_sine(turns_x + 0.25), turns_sine(turns_x), zero], 0)
+    y_high, y_low = split_two(wave_y)
+    x_high, x_low = split_two(wave_x)
+    copies[2].wait()
+    copies[3].wait()
+    rows_sq = rows_ref[...].reshape(poses * owned, box).astype(f32)
+    rows_sq = (rows_sq * rows_sq).astype(bf16)
+    u = dot(rows_sq, y_high, ((1,), (1,))) + dot(rows_sq, y_low, ((1,), (1,)))
+    total = jnp.zeros((slots * owned, cols), f32)
+    for p in range(poses):
+        cols_sq = cols_ref[p].astype(f32)
+        cols_sq = (cols_sq * cols_sq).astype(bf16)
+        v_high, v_low = split_two(dot(x_high, cols_sq) + dot(x_low, cols_sq))
+        scaled = counts[:, p * wide : (p + 1) * wide][:, None, :] * u[p * owned : (p + 1) * owned][None]
+        scaled = scaled.reshape(slots * owned, wide)
+        s_high, s_low = split_two(scaled)
+        total += dot(s_high, v_high) + dot(s_low, v_high) + dot(s_high, v_low)
+    out_ref[...] = (1.0 / (total + wiener_ridge)).reshape(slots, owned, cols)
+
+
+def own_ridges(codes, defocus, plane_weight, rows_table, cols_table, owned):
+    poses, _, box = rows_table.shape
+    cols = cols_table.shape[2]
+    slots = CLASSES * plane_weight.shape[1]
+    any_place = pl.BlockSpec(memory_space=pl.ANY)
+    vmem = pl.BlockSpec(memory_space=pltpu.VMEM)
+    planes = plane_weight.T
+    return pl.pallas_call(
+        ridge_kernel,
+        out_shape=jax.ShapeDtypeStruct((slots, owned, cols), f32),
+        in_specs=[any_place] * 4 + [vmem] * len(codes),
+        out_specs=vmem,
+        scratch_shapes=[
+            pltpu.SMEM(defocus.shape, f32),
+            pltpu.SMEM(planes.shape, f32),
+            pltpu.VMEM((poses, owned, box), bf16),
+            pltpu.VMEM(cols_table.shape, bf16),
+            pltpu.SemaphoreType.DMA((4,)),
+        ],
+        compiler_params=pltpu.CompilerParams(vmem_limit_bytes=16 * 1024 * 1024),
+        cost_estimate=pl.CostEstimate(
+            flops=2 * poses * 1000 * 128 * 256, bytes_accessed=2 * 1024 * 1024, transcendentals=0
+        ),
+    )(defocus, planes, rows_table, cols_table, *codes)
+
+
+def finish_kernel(ridge_ref, keep_ref, *refs):
+    parts, out_ref = refs[:-1], refs[-1]
+    slots, owned, cols = ridge_ref.shape
+    for s in range(slots):
+        value = keep_ref[s]
+        for part in parts:
+            value = value + part[s].astype(f32)
+        ridge = ridge_ref[s]
+        out_ref[:, 2 * s, :] = value[:, :cols] * ridge
+        out_ref[:, 2 * s + 1, :] = value[:, cols:] * ridge
+
+
+def finish(ridge, keep, parts):
+    slots, owned, cols = ridge.shape
+    vmem = pl.BlockSpec(memory_space=pltpu.VMEM)
+    return pl.pallas_call(
+        finish_kernel,
+        out_shape=jax.ShapeDtypeStruct((owned, 2 * slots, cols), f32),
+        in_specs=[vmem] * (2 + len(parts)),
+        out_specs=vmem,
+        compiler_params=pltpu.CompilerParams(vmem_limit_bytes=16 * 1024 * 1024),
+        cost_estimate=pl.CostEstimate(
+            flops=8 * slots * owned * cols, bytes_accessed=8 * 1024 * 1024 // 4, transcendentals=0
+        ),
+    )(ridge, keep, *parts)
 
 
 def squared_table(weight_table):
@@ -228,19 +409,52 @@
     return jnp.einsum("czpmbr,pmbj->rczj", left, v, precision=exact)
 
 
-def body(images, class_index, pose_index, defocus_bin, defocus, rows_table, cols_table, plane_weight):
+def by_rounds(images, class_index, pose_index, defocus_bin, defocus, rows_table, cols_table, plane_weight):
+    members = lax.axis_size("img")
+    rounds = members // 2
+    count = images.shape[0]
+    poses, rows, _ = rows_table.shape
+    planes = plane_weight.shape[1]
+    cols = cols_table.shape[2]
+    owned = rows // members
+    me = lax.axis_index("img")
+
+    code = (class_index[:, 0] * poses + pose_index) * defocus.shape[0] + defocus_bin
+    seat = jnp.arange(members * count, dtype=jnp.int32) // count
+    code = jnp.where(seat == me, jnp.tile(code, members), -1)[None]
+    codes = [code] + [
+        lax.ppermute(code, "img", [(i, (i + k) % members) for i in range(members)])
+        for k in range(1, members)
+    ]
+    outs = own_totals(
+        images, class_index, pose_index, defocus_bin, defocus, rows_table, cols_table, plane_weight, rounds
+    )
+    sends, keeps = outs[:rounds], outs[rounds:]
+    order = sorted(range(rounds), key=lambda k: (k == 0, -min(k, rounds - k)))
+    parts = []
+    for k in order:
+        came = lax.ppermute(sends[k], "img", [(i, i ^ 1) for i in range(members)])
+        if k == 0:
+            parts.append(came)
+        else:
+            both = (keeps[k] + came.astype(f32)).astype(bf16)
+            parts.append(lax.ppermute(both, "img", [(i, (i + 2 * k) % members) for i in range(members)]))
+    ridge = own_ridges(codes, defocus, plane_weight, rows_table, cols_table, owned)
+    out = finish(ridge, keeps[0], parts)
+    return out.reshape(owned, CLASSES, planes, 2, cols)
+
+
+def by_scatter(images, class_index, pose_index, defocus_bin, defocus, rows_table, cols_table, plane_weight):
     rows = rows_table.shape[1]
     cols = cols_table.shape[2]
     planes = plane_weight.shape[1]
     members = lax.axis_size("img")
     owned = rows // members
-    pieces = members if owned % 16 == 0 else 1
-    totals = own_totals(
-        images, class_index, pose_index, defocus_bin, defocus, rows_table, cols_table, plane_weight, pieces
-    )
-    slots = totals.shape[1]
-    if pieces == 1:
-        totals = totals.reshape(slots, members, owned, 2 * cols).transpose(1, 0, 2, 3)
+    (totals,) = own_totals(
+        images, class_index, pose_index, defocus_bin, defocus, rows_table, cols_table, plane_weight, 0
+    )
+    slots = totals.shape[0]
+    totals = totals.reshape(slots, members, owned, 2 * cols).transpose(1, 0, 2, 3)
     own = lax.psum_scatter(totals, "img", scatter_dimension=0, tiled=False)
     weight = weight_totals(
         class_index, pose_index, defocus_bin, defocus, rows_table, cols_table, plane_weight,
@@ -248,6 +462,13 @@
     )
     own = own.astype(f32).reshape(CLASSES, planes, owned, 2, cols).transpose(2, 0, 1, 3, 4)
     return own / (weight[:, :, :, None, :] + wiener_ridge)
+
+
+def body(*arrays):
+    rows = arrays[5].shape[1]
+    members = lax.axis_size("img")
+    small = 2 <= members <= 8 and members % 2 == 0 and rows % (16 * members) == 0
+    return (by_rounds if small else by_scatter)(*arrays)
 
 
 def solution(mesh):

time: 101 us -> 66.4 us (0.66)
  starting transfers between devices: 0.01 us -> 31.4 us
  waiting for transfers between devices: 45.2 us -> 17.5 us
  between operations: 14.2 us -> 0.13 us
  blocking collectives: 13.1 us -> 0 us
  local copies, waits for them, and re-layouts: 10.7 us -> 0.11 us
  matrix products: 5.98 us -> 0 us
  Pallas kernels: 10 us -> 14.1 us
  other arithmetic: 1.46 us -> 2.98 us
    reduce_scatter x1 -> x0, waiting for transfers between devices: 45.2 us -> none  [body(): own = lax.psum_scatter(totals, 'img', scatter_dimension=0, tiled=False)]
    ppermute x0 -> x14, starting transfers between devices: none -> 31.4 us  [the longest x7 18.4 us: by_rounds(): lax.ppermute(code, 'img', [(i, (i + k) % members) for i in range(members)])]
    ppermute x0 -> x14, waiting for transfers between devices: none -> 17.5 us  [the longest x7 15.1 us: by_rounds(): lax.ppermute(code, 'img', [(i, (i + k) % members) for i in range(members)])]
    unnamed x1 -> x0, blocking collectives: 13.1 us -> none
    unnamed x34 -> x16, local copies, waits for them, and re-layouts: 9.54 us -> 0.03 us
    dot_general x3 -> x0, matrix products: 5.98 us -> none  [the longest x1 4.45 us: weight_totals(): return jnp.einsum('czpmbr,pmbj->rczj', left, v, precision=exact)]
    pallas_call x1 -> x3, Pallas kernels: 10 us -> 14.1 us  [the longest x1 11.1 us: own_totals(): pl.pallas_call(slices_kernel, out_shape=out_shape, in_specs=[any_place] *...]
    convert_element_type x0 -> x3, other arithmetic: none -> 2.97 us  [by_rounds(): both = (keeps[k] + came.astype(f32)).astype(bf16)]
  transfers between devices with their start and end apart: 1 -> 14, of which waited for: 1 -> 8; matrix products, arithmetic and copies ran while one was open for 7% -> 5% of each run, Pallas kernels for 0% -> 3%
where the time goes in v1:
time: 66.4 us; the launch traced here: 66.2 us
  starting transfers between devices  31.4 us (47%)
  waiting for transfers between devices  17.5 us (26%)
  Pallas kernels  14.1 us (21%)
  other arithmetic  2.98 us (4%)
    ppermute x7, starting transfers between devices, by_rounds(): lax.ppermute(code, 'img', [(i, (i + k) % members) for i in range(members)])  18.4 us
    ppermute x7, waiting for transfers between devices, by_rounds(): lax.ppermute(code, 'img', [(i, (i + k) % members) for i in range(members)])  15.1 us
    pallas_call x1, Pallas kernels, own_totals(): pl.pallas_call(slices_kernel, out_shape=out_shape, in_specs=[any_place] *...  11.1 us
    ppermute x3, starting transfers between devices, by_rounds(): lax.ppermute(both, 'img', [(i, (i + 2 * k) % members) for i in range(memb...  7.85 us
    ppermute x4, starting transfers between devices, by_rounds(): came = lax.ppermute(sends[k], 'img', [(i, i ^ 1) for i in range(members)])  5.12 us
    convert_element_type x3, other arithmetic, by_rounds(): both = (keeps[k] + came.astype(f32)).astype(bf16)  2.97 us
    ppermute x4, waiting for transfers between devices, by_rounds(): came = lax.ppermute(sends[k], 'img', [(i, i ^ 1) for i in range(members)])  2.33 us
    pallas_call x1, Pallas kernels, own_ridges(): pl.pallas_call(ridge_kernel, out_shape=jax.ShapeDtypeStruct((slots, owned...  2.08 us
  transfers between devices with their start and end apart: 14, of which 8 were waited for; matrix products, arithmetic and copies ran while one was open for 5% of the time, Pallas kernels for 3%

profile of v1, /device:TPU:0, one launch (start us, length us, event | category | flops | bytes accessed | tf_op | source)
XLA Modules:
  0.0 66.2 jit_solution(8606614363868864785)
XLA Ops:
  0.0 0.0 copy-start.5
  0.0 0.0 copy-start.6
  0.0 0.0 copy-start.3
  0.0 0.0 copy-start.4
  0.0 11.1 %shard_map.101 = (bf16[16,16,256]{2,1,0:T(8,128)(2,1)}, bf16[16,16,256]{2,1,0:T(8,128)(2,1)}, bf16[16,16,256]{2,1,0:T(8,128)(2,1)}, bf16[16,16,256]{2,1,0:T(8,12...) custom-call(s32[16]{0:T(128)} %bitcast.6, ...), custom_call_target="tpu_custom_call" | custom-call | flops 2097152000 | bytes 6291456 | tf_op jit(solution)/shard_map/pallas_call | solution.py:224
  11.1 0.0 copy-start
  11.2 3.0 %collective-permute-start.7 = (bf16[16,16,256]{2,1,0:T(8,128)(2,1)}, bf16[16,16,256]{2,1,0:T(8,128)(2,1)S(1)}, u32[]{:S(2)}, u32[]{:S(2)}) collective-permute-start(bf16[16,16,256]{2,1,0:T(8,128)(2,1)} %get-tuple-element.15), channel_id=1, source_target_pairs={{0,2},{2,0},{4,6},{6,4},{8,10},{10,8},{12,14},{14,12},{1,3},{3,1},... | collective-permute-start | bytes 393224 | tf_op jit(solution)/shard_map/ppermute | solution.py:436
  14.2 0.1 collective-permute-start.9
  14.3 1.9 %collective-permute-start.11 = (bf16[16,16,256]{2,1,0:T(8,128)(2,1)}, bf16[16,16,256]{2,1,0:T(8,128)(2,1)S(1)}, u32[]{:S(2)}, u32[]{:S(2)}) collective-permute-start(bf16[16,16,256]{2,1,0:T(8,128)(2,1)} %get-tuple-element.19), channel_id=1, source_target_pairs={{0,2},{2,0},{4,6},{6,4},{8,10},{10,8},{12,14},{14,12},{1,3},{3,1},... | collective-permute-start | bytes 393224 | tf_op jit(solution)/shard_map/ppermute | solution.py:436
  16.2 0.1 collective-permute-start.13
  16.3 0.0 copy-done.5
  16.3 0.0 copy-done.6
  16.3 0.0 copy-done.7
  16.3 0.1 tile.10
  16.4 2.3 %collective-permute-done.7 = bf16[16,16,256]{2,1,0:T(8,128)(2,1)S(1)} collective-permute-done((bf16[16,16,256]{2,1,0:T(8,128)(2,1)}, bf16[16,16,256]{2,1,0:T(8,128)(2,1)S(1)}, u32[]{:S(2)}, u32[]{:S(2)}) %collective-permute-start.7) | collective-permute-done | bytes 131104 | tf_op jit(solution)/shard_map/ppermute | solution.py:436
  18.7 1.0 %add_convert_fusion.2 = bf16[16,16,256]{2,1,0:T(8,128)(2,1)S(1)} fusion(f32[16,16,256]{2,1,0:T(8,128)} %get-tuple-element.14, bf16[16,16,256]{2,1,0:T(8,128)(2,1)S(1)} %collective-permute-done.7), kind=kLoop, calls=%fused_computation.2 | loop fusion | flops 196608 | bytes 524288 | tf_op jit(solution)/shard_map/convert_element_type | solution.py:440
  19.7 3.2 %collective-permute-start.8 = (bf16[16,16,256]{2,1,0:T(8,128)(2,1)S(1)}, bf16[16,16,256]{2,1,0:T(8,128)(2,1)S(1)}, u32[]{:S(2)}, u32[]{:S(2)}) collective-permute-start(bf16[16,16,256]{2,1,0:T(8,128)(2,1)S(1)} %add_convert_fusion.2), channel_id=1, source_target_pairs={{0,8},{2,10},{4,12},{6,14},{8,0},{10,2},{12,4},{14,6},{1,9},{3,11}... | collective-permute-start | bytes 393224 | tf_op jit(solution)/shard_map/ppermute | solution.py:441
  22.9 0.0 collective-permute-done.9
  22.9 1.0 %add_convert_fusion.1 = bf16[16,16,256]{2,1,0:T(8,128)(2,1)S(1)} fusion(f32[16,16,256]{2,1,0:T(8,128)} %get-tuple-element.16, bf16[16,16,256]{2,1,0:T(8,128)(2,1)S(1)} %collective-permute-done.9), kind=kLoop, calls=%fused_computation.1 | loop fusion | flops 196608 | bytes 524288 | tf_op jit(solution)/shard_map/convert_element_type | solution.py:440
  23.9 1.6 %collective-permute-start.10 = (bf16[16,16,256]{2,1,0:T(8,128)(2,1)S(1)}, bf16[16,16,256]{2,1,0:T(8,128)(2,1)S(1)}, u32[]{:S(2)}, u32[]{:S(2)}) collective-permute-start(bf16[16,16,256]{2,1,0:T(8,128)(2,1)S(1)} %add_convert_fusion.1), channel_id=1, source_target_pairs={{0,4},{2,6},{4,8},{6,10},{8,12},{10,14},{12,0},{14,2},{1,5},{3,7},... | collective-permute-start | bytes 393224 | tf_op jit(solution)/shard_map/ppermute | solution.py:441
  25.5 0.0 collective-permute-done.11
  25.6 1.0 %add_convert_fusion = bf16[16,16,256]{2,1,0:T(8,128)(2,1)S(1)} fusion(f32[16,16,256]{2,1,0:T(8,128)} %get-tuple-element.18, bf16[16,16,256]{2,1,0:T(8,128)(2,1)S(1)} %collective-permute-done.11), kind=kLoop, calls=%fused_computation | loop fusion | flops 196608 | bytes 524288 | tf_op jit(solution)/shard_map/convert_element_type | solution.py:440
  26.5 3.0 %collective-permute-start.12 = (bf16[16,16,256]{2,1,0:T(8,128)(2,1)S(1)}, bf16[16,16,256]{2,1,0:T(8,128)(2,1)S(1)}, u32[]{:S(2)}, u32[]{:S(2)}) collective-permute-start(bf16[16,16,256]{2,1,0:T(8,128)(2,1)S(1)} %add_convert_fusion), channel_id=1, source_target_pairs={{0,12},{2,14},{4,0},{6,2},{8,4},{10,6},{12,8},{14,10},{1,13},{3,15... | collective-permute-start | bytes 393224 | tf_op jit(solution)/shard_map/ppermute | solution.py:441
  29.6 1.4 %collective-permute-start.6 = (s32[1,128]{1,0:T(1,128)S(1)}, s32[1,128]{1,0:T(1,128)S(1)}, u32[]{:S(2)}, u32[]{:S(2)}) collective-permute-start(s32[1,128]{1,0:T(1,128)S(1)} %compare_select_fusion.refs_0_), channel_id=1, source_target_pairs={{0,14},{2,0},{4,2},{6,4},{8,6},{10,8},{12,10},{14,12},{1,15},{3,1}... | collective-permute-start | bytes 1544 | tf_op jit(solution)/shard_map/ppermute | solution.py:426
  31.0 2.2 %collective-permute-done.6.refs_7_ = s32[1,128]{1,0:T(1,128)S(1)} collective-permute-done((s32[1,128]{1,0:T(1,128)S(1)}, s32[1,128]{1,0:T(1,128)S(1)}, u32[]{:S(2)}, u32[]{:S(2)}) %collective-permute-start.6) | collective-permute-done | bytes 544 | tf_op jit(solution)/shard_map/ppermute | solution.py:426
  33.1 0.5 collective-permute-start.5
  33.6 3.1 %collective-permute-done.5.refs_6_ = s32[1,128]{1,0:T(1,128)S(1)} collective-permute-done((s32[1,128]{1,0:T(1,128)S(1)}, s32[1,128]{1,0:T(1,128)S(1)}, u32[]{:S(2)}, u32[]{:S(2)}) %collective-permute-start.5) | collective-permute-done | bytes 544 | tf_op jit(solution)/shard_map/ppermute | solution.py:426
  36.7 2.6 %collective-permute-start.4 = (s32[1,128]{1,0:T(1,128)S(1)}, s32[1,128]{1,0:T(1,128)S(1)}, u32[]{:S(2)}, u32[]{:S(2)}) collective-permute-start(s32[1,128]{1,0:T(1,128)S(1)} %compare_select_fusion.refs_0_), channel_id=1, source_target_pairs={{0,10},{2,12},{4,14},{6,0},{8,2},{10,4},{12,6},{14,8},{1,11},{3,13... | collective-permute-start | bytes 1544 | tf_op jit(solution)/shard_map/ppermute | solution.py:426
  39.3 1.8 %collective-permute-done.4.refs_5_ = s32[1,128]{1,0:T(1,128)S(1)} collective-permute-done((s32[1,128]{1,0:T(1,128)S(1)}, s32[1,128]{1,0:T(1,128)S(1)}, u32[]{:S(2)}, u32[]{:S(2)}) %collective-permute-start.4) | collective-permute-done | bytes 544 | tf_op jit(solution)/shard_map/ppermute | solution.py:426
  41.1 3.5 %collective-permute-start.3 = (s32[1,128]{1,0:T(1,128)S(1)}, s32[1,128]{1,0:T(1,128)S(1)}, u32[]{:S(2)}, u32[]{:S(2)}) collective-permute-start(s32[1,128]{1,0:T(1,128)S(1)} %compare_select_fusion.refs_0_), channel_id=1, source_target_pairs={{0,8},{2,10},{4,12},{6,14},{8,0},{10,2},{12,4},{14,6},{1,9},{3,11}... | collective-permute-start | bytes 1544 | tf_op jit(solution)/shard_map/ppermute | solution.py:426
  44.7 1.5 %collective-permute-done.3.refs_4_ = s32[1,128]{1,0:T(1,128)S(1)} collective-permute-done((s32[1,128]{1,0:T(1,128)S(1)}, s32[1,128]{1,0:T(1,128)S(1)}, u32[]{:S(2)}, u32[]{:S(2)}) %collective-permute-start.3) | collective-permute-done | bytes 544 | tf_op jit(solution)/shard_map/ppermute | solution.py:426
  46.2 3.8 %collective-permute-start.2 = (s32[1,128]{1,0:T(1,128)S(1)}, s32[1,128]{1,0:T(1,128)S(1)}, u32[]{:S(2)}, u32[]{:S(2)}) collective-permute-start(s32[1,128]{1,0:T(1,128)S(1)} %compare_select_fusion.refs_0_), channel_id=1, source_target_pairs={{0,6},{2,8},{4,10},{6,12},{8,14},{10,0},{12,2},{14,4},{1,7},{3,9},... | collective-permute-start | bytes 1544 | tf_op jit(solution)/shard_map/ppermute | solution.py:426
  50.0 1.5 %collective-permute-done.2.refs_3_ = s32[1,128]{1,0:T(1,128)S(1)} collective-permute-done((s32[1,128]{1,0:T(1,128)S(1)}, s32[1,128]{1,0:T(1,128)S(1)}, u32[]{:S(2)}, u32[]{:S(2)}) %collective-permute-start.2) | collective-permute-done | bytes 544 | tf_op jit(solution)/shard_map/ppermute | solution.py:426
  51.5 2.9 %collective-permute-start.1 = (s32[1,128]{1,0:T(1,128)S(1)}, s32[1,128]{1,0:T(1,128)S(1)}, u32[]{:S(2)}, u32[]{:S(2)}) collective-permute-start(s32[1,128]{1,0:T(1,128)S(1)} %compare_select_fusion.refs_0_), channel_id=1, source_target_pairs={{0,4},{2,6},{4,8},{6,10},{8,12},{10,14},{12,0},{14,2},{1,5},{3,7},... | collective-permute-start | bytes 1544 | tf_op jit(solution)/shard_map/ppermute | solution.py:426
  54.4 2.4 %collective-permute-done.1.refs_2_ = s32[1,128]{1,0:T(1,128)S(1)} collective-permute-done((s32[1,128]{1,0:T(1,128)S(1)}, s32[1,128]{1,0:T(1,128)S(1)}, u32[]{:S(2)}, u32[]{:S(2)}) %collective-permute-start.1) | collective-permute-done | bytes 544 | tf_op jit(solution)/shard_map/ppermute | solution.py:426
  56.9 3.6 %collective-permute-start = (s32[1,128]{1,0:T(1,128)S(1)}, s32[1,128]{1,0:T(1,128)S(1)}, u32[]{:S(2)}, u32[]{:S(2)}) collective-permute-start(s32[1,128]{1,0:T(1,128)S(1)} %compare_select_fusion.refs_0_), channel_id=1, source_target_pairs={{0,2},{2,4},{4,6},{6,8},{8,10},{10,12},{12,14},{14,0},{1,3},{3,5},... | collective-permute-start | bytes 1544 | tf_op jit(solution)/shard_map/ppermute | solution.py:426
  60.5 2.6 %collective-permute-done.refs_1_ = s32[1,128]{1,0:T(1,128)S(1)} collective-permute-done((s32[1,128]{1,0:T(1,128)S(1)}, s32[1,128]{1,0:T(1,128)S(1)}, u32[]{:S(2)}, u32[]{:S(2)}) %collective-permute-start) | collective-permute-done | bytes 544 | tf_op jit(solution)/shard_map/ppermute | solution.py:426
  63.1 0.0 copy-done.1
  63.1 0.0 copy-done.2
  63.1 0.0 copy-done.3
  63.1 0.0 copy-done.4
  63.1 2.1 %shard_map.100.ridge_ref = f32[16,16,128]{2,1,0:T(8,128)S(1)} custom-call(f32[16]{0:T(128)S(1)} %copy-done.4, f32[2,8]{1,0:T(2,128)S(1)} %bitcast.5, bf16[8,128,256]{2,1,0:T(8,128)(2,1)S(1)} %copy-done.1, bf16[8,256,128]{2,1,0:T(8,128)(2,1)S(1)} %copy-done.2, s32[1,128]{1,0:T(1,128)S(1)} %compare_select_fusion.refs_0_, ...), custom_call_target="tpu_custom_call" | custom-call | flops 524288000 | bytes 2097152 | tf_op jit(solution)/shard_map/pallas_call | solution.py:336
  65.2 0.0 collective-permute-done.13.refs_3_
  65.2 0.0 collective-permute-done.8.refs_0_
  65.2 0.0 collective-permute-done.10.refs_1_
  65.2 0.0 collective-permute-done.12.refs_2_
  65.2 0.0 copy-done
  65.3 1.0 %shard_map.102 = f32[16,32,128]{2,1,0:T(8,128)} custom-call(f32[16,16,128]{2,1,0:T(8,128)S(1)} %shard_map.100.ridge_ref, f32[16,16,256]{2,1,0:T(8,128)S(1)} %copy-done, bf16[16,16,256]{2,1,0:T(8,128)(2,1)S(1)} %collective-permute-done.8.refs_0_, bf16[16,16,256]{2,1,0:T(8,128)(2,1)S(1)} %collective-permute-done.10.refs_1_, ...), custom_call_target="tpu_custom_call" | custom-call | flops 262144 | bytes 2097152 | tf_op jit(solution)/shard_map/pallas_call | solution.py:370
  (6 shorter events, 0.0 us)
Async XLA Ops:
  0.0 16.3 %copy-start.5 = (s32[16]{0:T(128)S(1)}, s32[16]{0:T(128)}, u32[]{:S(2)}) copy-start(s32[16]{0:T(128)} %bin_hbm.1) | copy-start | bytes 196
  0.0 16.3 %copy-start.6 = (s32[16]{0:T(128)S(1)}, s32[16]{0:T(128)}, u32[]{:S(2)}) copy-start(s32[16]{0:T(128)} %pose_hbm.1) | copy-start | bytes 196
  0.0 16.3 %copy-start.7 = (s32[16,1]{0,1:T(1,128)S(1)}, s32[16,1]{0,1:T(1,128)}, u32[]{:S(2)}) copy-start(s32[16,1]{0,1:T(1,128)} %param.11) | copy-start | bytes 196
  0.0 63.1 %copy-start.1 = (bf16[8,128,256]{2,1,0:T(8,128)(2,1)S(1)}, bf16[8,128,256]{2,1,0:T(8,128)(2,1)}, u32[]{:S(2)}) copy-start(bf16[8,128,256]{2,1,0:T(8,128)(2,1)} %rows_hbm.3) | copy-start | bytes 1572868
  0.0 63.1 %copy-start.2 = (bf16[8,256,128]{2,1,0:T(8,128)(2,1)S(1)}, bf16[8,256,128]{2,1,0:T(8,128)(2,1)}, u32[]{:S(2)}) copy-start(bf16[8,256,128]{2,1,0:T(8,128)(2,1)} %cols_hbm.3) | copy-start | bytes 1572868
  0.0 63.1 %copy-start.3 = (f32[8,2]{0,1:T(2,128)S(1)}, f32[8,2]{0,1:T(2,128)}, u32[]{:S(2)}) copy-start(f32[8,2]{0,1:T(2,128)} %param.17) | copy-start | bytes 196
  0.0 63.1 %copy-start.4 = (f32[16]{0:T(128)S(1)}, f32[16]{0:T(128)}, u32[]{:S(2)}) copy-start(f32[16]{0:T(128)} %defocus_hbm.3) | copy-start | bytes 196
  11.1 54.1 %copy-start = (f32[16,16,256]{2,1,0:T(8,128)S(1)}, f32[16,16,256]{2,1,0:T(8,128)}, u32[]{:S(2)}) copy-start(f32[16,16,256]{2,1,0:T(8,128)} %get-tuple-element.13.keep_ref) | copy-start | bytes 786436
  11.2 7.6 %collective-permute-start.7 = (bf16[16,16,256]{2,1,0:T(8,128)(2,1)}, bf16[16,16,256]{2,1,0:T(8,128)(2,1)S(1)}, u32[]{:S(2)}, u32[]{:S(2)}) collective-permute-start(bf16[16,16,256]{2,1,0:T(8,128)(2,1)} %get-tuple-element.15), channel_id=1, source_target_pairs={{0,2},{2,0},{4,6},{6,4},{8,10},{10,8},{12,14},{14,12},{1,3},{3,1},... | collective-permute-start | bytes 393224 | tf_op jit(solution)/shard_map/ppermute | solution.py:436
  14.2 8.8 %collective-permute-start.9 = (bf16[16,16,256]{2,1,0:T(8,128)(2,1)}, bf16[16,16,256]{2,1,0:T(8,128)(2,1)S(1)}, u32[]{:S(2)}, u32[]{:S(2)}) collective-permute-start(bf16[16,16,256]{2,1,0:T(8,128)(2,1)} %get-tuple-element.17), channel_id=1, source_target_pairs={{0,2},{2,0},{4,6},{6,4},{8,10},{10,8},{12,14},{14,12},{1,3},{3,1},... | collective-permute-start | bytes 393224 | tf_op jit(solution)/shard_map/ppermute | solution.py:436
  14.3 11.3 %collective-permute-start.11 = (bf16[16,16,256]{2,1,0:T(8,128)(2,1)}, bf16[16,16,256]{2,1,0:T(8,128)(2,1)S(1)}, u32[]{:S(2)}, u32[]{:S(2)}) collective-permute-start(bf16[16,16,256]{2,1,0:T(8,128)(2,1)} %get-tuple-element.19), channel_id=1, source_target_pairs={{0,2},{2,0},{4,6},{6,4},{8,10},{10,8},{12,14},{14,12},{1,3},{3,1},... | collective-permute-start | bytes 393224 | tf_op jit(solution)/shard_map/ppermute | solution.py:436
  16.2 49.0 %collective-permute-start.13 = (bf16[16,16,256]{2,1,0:T(8,128)(2,1)}, bf16[16,16,256]{2,1,0:T(8,128)(2,1)S(1)}, u32[]{:S(2)}, u32[]{:S(2)}) collective-permute-start(bf16[16,16,256]{2,1,0:T(8,128)(2,1)} %get-tuple-element.20), channel_id=1, source_target_pairs={{0,2},{2,0},{4,6},{6,4},{8,10},{10,8},{12,14},{14,12},{1,3},{3,1},... | collective-permute-start | bytes 393224 | tf_op jit(solution)/shard_map/ppermute | solution.py:436
  19.7 45.5 %collective-permute-start.8 = (bf16[16,16,256]{2,1,0:T(8,128)(2,1)S(1)}, bf16[16,16,256]{2,1,0:T(8,128)(2,1)S(1)}, u32[]{:S(2)}, u32[]{:S(2)}) collective-permute-start(bf16[16,16,256]{2,1,0:T(8,128)(2,1)S(1)} %add_convert_fusion.2), channel_id=1, source_target_pairs={{0,8},{2,10},{4,12},{6,14},{8,0},{10,2},{12,4},{14,6},{1,9},{3,11}... | collective-permute-start | bytes 393224 | tf_op jit(solution)/shard_map/ppermute | solution.py:441
  23.9 41.3 %collective-permute-start.10 = (bf16[16,16,256]{2,1,0:T(8,128)(2,1)S(1)}, bf16[16,16,256]{2,1,0:T(8,128)(2,1)S(1)}, u32[]{:S(2)}, u32[]{:S(2)}) collective-permute-start(bf16[16,16,256]{2,1,0:T(8,128)(2,1)S(1)} %add_convert_fusion.1), channel_id=1, source_target_pairs={{0,4},{2,6},{4,8},{6,10},{8,12},{10,14},{12,0},{14,2},{1,5},{3,7},... | collective-permute-start | bytes 393224 | tf_op jit(solution)/shard_map/ppermute | solution.py:441
  26.5 38.7 %collective-permute-start.12 = (bf16[16,16,256]{2,1,0:T(8,128)(2,1)S(1)}, bf16[16,16,256]{2,1,0:T(8,128)(2,1)S(1)}, u32[]{:S(2)}, u32[]{:S(2)}) collective-permute-start(bf16[16,16,256]{2,1,0:T(8,128)(2,1)S(1)} %add_convert_fusion), channel_id=1, source_target_pairs={{0,12},{2,14},{4,0},{6,2},{8,4},{10,6},{12,8},{14,10},{1,13},{3,15... | collective-permute-start | bytes 393224 | tf_op jit(solution)/shard_map/ppermute | solution.py:441
  29.6 3.6 %collective-permute-start.6 = (s32[1,128]{1,0:T(1,128)S(1)}, s32[1,128]{1,0:T(1,128)S(1)}, u32[]{:S(2)}, u32[]{:S(2)}) collective-permute-start(s32[1,128]{1,0:T(1,128)S(1)} %compare_select_fusion.refs_0_), channel_id=1, source_target_pairs={{0,14},{2,0},{4,2},{6,4},{8,6},{10,8},{12,10},{14,12},{1,15},{3,1}... | collective-permute-start | bytes 1544 | tf_op jit(solution)/shard_map/ppermute | solution.py:426
  33.1 3.5 %collective-permute-start.5 = (s32[1,128]{1,0:T(1,128)S(1)}, s32[1,128]{1,0:T(1,128)S(1)}, u32[]{:S(2)}, u32[]{:S(2)}) collective-permute-start(s32[1,128]{1,0:T(1,128)S(1)} %compare_select_fusion.refs_0_), channel_id=1, source_target_pairs={{0,12},{2,14},{4,0},{6,2},{8,4},{10,6},{12,8},{14,10},{1,13},{3,15... | collective-permute-start | bytes 1544 | tf_op jit(solution)/shard_map/ppermute | solution.py:426
  36.7 4.4 %collective-permute-start.4 = (s32[1,128]{1,0:T(1,128)S(1)}, s32[1,128]{1,0:T(1,128)S(1)}, u32[]{:S(2)}, u32[]{:S(2)}) collective-permute-start(s32[1,128]{1,0:T(1,128)S(1)} %compare_select_fusion.refs_0_), channel_id=1, source_target_pairs={{0,10},{2,12},{4,14},{6,0},{8,2},{10,4},{12,6},{14,8},{1,11},{3,13... | collective-permute-start | bytes 1544 | tf_op jit(solution)/shard_map/ppermute | solution.py:426
  41.1 5.1 %collective-permute-start.3 = (s32[1,128]{1,0:T(1,128)S(1)}, s32[1,128]{1,0:T(1,128)S(1)}, u32[]{:S(2)}, u32[]{:S(2)}) collective-permute-start(s32[1,128]{1,0:T(1,128)S(1)} %compare_select_fusion.refs_0_), channel_id=1, source_target_pairs={{0,8},{2,10},{4,12},{6,14},{8,0},{10,2},{12,4},{14,6},{1,9},{3,11}... | collective-permute-start | bytes 1544 | tf_op jit(solution)/shard_map/ppermute | solution.py:426
  46.2 5.3 %collective-permute-start.2 = (s32[1,128]{1,0:T(1,128)S(1)}, s32[1,128]{1,0:T(1,128)S(1)}, u32[]{:S(2)}, u32[]{:S(2)}) collective-permute-start(s32[1,128]{1,0:T(1,128)S(1)} %compare_select_fusion.refs_0_), channel_id=1, source_target_pairs={{0,6},{2,8},{4,10},{6,12},{8,14},{10,0},{12,2},{14,4},{1,7},{3,9},... | collective-permute-start | bytes 1544 | tf_op jit(solution)/shard_map/ppermute | solution.py:426
  51.5 5.3 %collective-permute-start.1 = (s32[1,128]{1,0:T(1,128)S(1)}, s32[1,128]{1,0:T(1,128)S(1)}, u32[]{:S(2)}, u32[]{:S(2)}) collective-permute-start(s32[1,128]{1,0:T(1,128)S(1)} %compare_select_fusion.refs_0_), channel_id=1, source_target_pairs={{0,4},{2,6},{4,8},{6,10},{8,12},{10,14},{12,0},{14,2},{1,5},{3,7},... | collective-permute-start | bytes 1544 | tf_op jit(solution)/shard_map/ppermute | solution.py:426
  56.9 6.2 %collective-permute-start = (s32[1,128]{1,0:T(1,128)S(1)}, s32[1,128]{1,0:T(1,128)S(1)}, u32[]{:S(2)}, u32[]{:S(2)}) collective-permute-start(s32[1,128]{1,0:T(1,128)S(1)} %compare_select_fusion.refs_0_), channel_id=1, source_target_pairs={{0,2},{2,4},{4,6},{6,8},{8,10},{10,12},{12,14},{14,0},{1,3},{3,5},... | collective-permute-start | bytes 1544 | tf_op jit(solution)/shard_map/ppermute | solution.py:426

commit v2 on v1

--- a/solution.py
+++ b/solution.py
@@ -114,6 +114,15 @@
         [cos_high, sin_high, cos_low, sin_low, cos_high, sin_high, zero], 0
     )
     totals[...] = jnp.zeros_like(totals)
+    if len(outs) > 1:
+        bins = defocus_ref.shape[0]
+        count_row = iota((16, 2 * cols), 0)
+        count_lane = iota((16, 2 * cols), 1)
+        counts = jnp.zeros((16, 2 * cols), f32)
+        for i in range(count):
+            hit = (count_row == class_ref[i]) & (count_lane == pose_ref[i] * bins + bin_ref[i])
+            counts = counts + jnp.where(hit, 1.0, 0.0)
+        totals[planes * CLASSES] = jnp.tile(counts, (rows // 16, 1))
 
     copies[5].wait()
     rows_fold[...] = dot(
@@ -175,7 +184,7 @@
         pose_rows = rows_fold[pl.ds(pl.multiple_of(pose * rows, rows), rows), :]
         piece = dot(pose_rows, mix_ref[...])
         for z in range(planes):
-            slot = class_ref[i] * planes + z
+            slot = z * CLASSES + class_ref[i]
             totals[slot] += plane_ref[z, pose] * piece
         return carry
 
@@ -213,6 +222,7 @@
     if turns_round == 0:
         out_shape = [jax.ShapeDtypeStruct((slots, rows, 2 * cols), bf16)]
     else:
+        slots += 1
         piece = (slots, rows // (2 * turns_round), 2 * cols)
         out_shape = [jax.ShapeDtypeStruct(piece, bf16)] * turns_round
         out_shape += [jax.ShapeDtypeStruct(piece, f32)] * turns_round
@@ -249,14 +259,12 @@
 VMEM_LIMIT = 56 * 1024 * 1024
 
 
-def ridge_kernel(defocus_hbm, plane_hbm, rows_hbm, cols_hbm, *refs):
-    codes, refs = refs[:-6], refs[-6:]
-    out_ref, defocus_ref, plane_ref, rows_ref, cols_ref, arrived = refs
+def ridge_kernel(defocus_hbm, plane_hbm, rows_hbm, cols_hbm, high_ref, low_ref, share_ref, *refs):
+    defocus_ref, plane_ref, rows_ref, cols_ref, arrived = refs
     poses, owned, box = rows_ref.shape
     cols = cols_ref.shape[2]
     bins = defocus_ref.shape[0]
     planes = plane_ref.shape[0]
-    slots = CLASSES * planes
     half = box // 2
     first = pl.multiple_of(lax.axis_index("img") * owned, owned)
     copies = [
@@ -267,31 +275,15 @@
     ]
     for copy in copies:
         copy.start()
-
-    code = codes[0][...]
-    for ref in codes[1:]:
-        code = jnp.maximum(code, ref[...])
-    images = code.shape[1]
-    wide = 128
-    kind = code // bins
-    slot_row = iota((slots, images), 0) // planes
-    left = (slot_row == kind // poses).astype(f32).astype(bf16)
-    term = iota((poses * wide, images), 0)
-    right_code = jnp.where(
-        term % wide < 3 * bins, (term // wide) * bins + term % bins, poses * bins
-    )
-    right = (right_code == code % (poses * bins)).astype(f32).astype(bf16)
-    counts = dot(left, right, ((1,), (1,)))
-
-    copies[0].wait()
-    copies[1].wait()
-    share_slot = iota((slots, poses * wide), 0) % planes
-    share_pose = iota((slots, poses * wide), 1) // wide
-    share = jnp.zeros((slots, poses * wide), f32)
+    for copy in copies:
+        copy.wait()
+    share_plane = iota((planes * CLASSES, poses * bins), 0) // CLASSES
+    share_pose = iota((planes * CLASSES, poses * bins), 1) // bins
+    share = jnp.zeros((planes * CLASSES, poses * bins), f32)
     for p in range(poses):
         for z in range(planes):
-            share = jnp.where((share_slot == z) & (share_pose == p), plane_ref[z, p], share)
-    counts = counts * share
+            share = jnp.where((share_plane == z) & (share_pose == p), plane_ref[z, p], share)
+    share_ref[...] = share
 
     bin_row = iota((bins, box), 0)
     sub_defocus = jnp.zeros((bins, box), f32)
@@ -301,43 +293,42 @@
     freq = jnp.where(freq < half, freq, box - freq).astype(f32)
     turns_x = sub_defocus * (freq * freq * (1.0 / (half * half)))
     turns_y = turns_x + ctf_phase / math.pi
-    zero = jnp.zeros((wide - 3 * bins, box), f32)
     ones = jnp.ones((bins, box), f32)
     wave_y = jnp.concatenate(
-        [0.5 * ones, -0.5 * turns_sine(turns_y + 0.25), 0.5 * turns_sine(turns_y), zero], 0
-    )
-    wave_x = jnp.concatenate([ones, turns_sine(turns_x + 0.25), turns_sine(turns_x), zero], 0)
+        [0.5 * ones, -0.5 * turns_sine(turns_y + 0.25), 0.5 * turns_sine(turns_y)], 0
+    )
+    wave_x = jnp.concatenate([ones, turns_sine(turns_x + 0.25), turns_sine(turns_x)], 0)
     y_high, y_low = split_two(wave_y)
     x_high, x_low = split_two(wave_x)
-    copies[2].wait()
-    copies[3].wait()
     rows_sq = rows_ref[...].reshape(poses * owned, box).astype(f32)
     rows_sq = (rows_sq * rows_sq).astype(bf16)
-    u = dot(rows_sq, y_high, ((1,), (1,))) + dot(rows_sq, y_low, ((1,), (1,)))
-    total = jnp.zeros((slots * owned, cols), f32)
+    u = dot(y_high, rows_sq, ((1,), (1,))) + dot(y_low, rows_sq, ((1,), (1,)))
     for p in range(poses):
         cols_sq = cols_ref[p].astype(f32)
         cols_sq = (cols_sq * cols_sq).astype(bf16)
-        v_high, v_low = split_two(dot(x_high, cols_sq) + dot(x_low, cols_sq))
-        scaled = counts[:, p * wide : (p + 1) * wide][:, None, :] * u[p * owned : (p + 1) * owned][None]
-        scaled = scaled.reshape(slots * owned, wide)
-        s_high, s_low = split_two(scaled)
-        total += dot(s_high, v_high) + dot(s_low, v_high) + dot(s_high, v_low)
-    out_ref[...] = (1.0 / (total + wiener_ridge)).reshape(slots, owned, cols)
-
-
-def own_ridges(codes, defocus, plane_weight, rows_table, cols_table, owned):
+        v = dot(x_high, cols_sq) + dot(x_low, cols_sq)
+        for r in range(owned):
+            column = u[:, p * owned + r : p * owned + r + 1]
+            product = v * column
+            weight = product[:bins] + product[bins : 2 * bins] + product[2 * bins :]
+            high, low = split_two(weight)
+            high_ref[p * bins : (p + 1) * bins, r * cols : (r + 1) * cols] = high
+            low_ref[p * bins : (p + 1) * bins, r * cols : (r + 1) * cols] = low
+
+
+def own_ridges(defocus, plane_weight, rows_table, cols_table, owned):
     poses, _, box = rows_table.shape
     cols = cols_table.shape[2]
-    slots = CLASSES * plane_weight.shape[1]
+    bins = defocus.shape[0]
     any_place = pl.BlockSpec(memory_space=pl.ANY)
     vmem = pl.BlockSpec(memory_space=pltpu.VMEM)
     planes = plane_weight.T
+    table = jax.ShapeDtypeStruct((poses * bins, owned * cols), bf16)
     return pl.pallas_call(
         ridge_kernel,
-        out_shape=jax.ShapeDtypeStruct((slots, owned, cols), f32),
-        in_specs=[any_place] * 4 + [vmem] * len(codes),
-        out_specs=vmem,
+        out_shape=[table, table, jax.ShapeDtypeStruct((planes.shape[0] * CLASSES, poses * bins), f32)],
+        in_specs=[any_place] * 4,
+        out_specs=[vmem] * 3,
         scratch_shapes=[
             pltpu.SMEM(defocus.shape, f32),
             pltpu.SMEM(planes.shape, f32),
@@ -349,34 +340,54 @@
         cost_estimate=pl.CostEstimate(
             flops=2 * poses * 1000 * 128 * 256, bytes_accessed=2 * 1024 * 1024, transcendentals=0
         ),
-    )(defocus, planes, rows_table, cols_table, *codes)
-
-
-def finish_kernel(ridge_ref, keep_ref, *refs):
-    parts, out_ref = refs[:-1], refs[-1]
-    slots, owned, cols = ridge_ref.shape
+    )(defocus, planes, rows_table, cols_table)
+
+
+def finish_kernel(high_ref, low_ref, share_ref, *refs):
+    parts, out_ref, ridge_ref = refs[:-2], refs[-2], refs[-1]
+    slots, pairs = share_ref.shape
+    owned, _, cols = ridge_ref.shape
+    planes = slots // CLASSES
+
+    def summed(s):
+        value = parts[0][s].astype(f32)
+        for part in parts[1:]:
+            value = value + part[s].astype(f32)
+        return value
+
+    counts = summed(slots)[:CLASSES, :pairs]
+    scaled = jnp.concatenate([counts] * planes, 0) * share_ref[...]
+    c_high, c_low = split_two(scaled)
+    weight = (
+        dot(c_high, high_ref[...]) + dot(c_low, high_ref[...]) + dot(c_high, low_ref[...])
+    )
+    ridge = 1.0 / (weight + wiener_ridge)
+    for r in range(owned):
+        ridge_ref[r] = ridge[:, r * cols : (r + 1) * cols]
     for s in range(slots):
-        value = keep_ref[s]
-        for part in parts:
-            value = value + part[s].astype(f32)
-        ridge = ridge_ref[s]
-        out_ref[:, 2 * s, :] = value[:, :cols] * ridge
-        out_ref[:, 2 * s + 1, :] = value[:, cols:] * ridge
-
-
-def finish(ridge, keep, parts):
-    slots, owned, cols = ridge.shape
+        value = summed(s)
+        factor = ridge_ref[:, s, :]
+        place = (s % CLASSES) * planes + s // CLASSES
+        out_ref[:, 2 * place, :] = value[:, :cols] * factor
+        out_ref[:, 2 * place + 1, :] = value[:, cols:] * factor
+
+
+def finish(tables, parts):
+    slots = tables[2].shape[0]
+    _, owned, wide = parts[0].shape
+    cols = wide // 2
     vmem = pl.BlockSpec(memory_space=pltpu.VMEM)
     return pl.pallas_call(
         finish_kernel,
         out_shape=jax.ShapeDtypeStruct((owned, 2 * slots, cols), f32),
-        in_specs=[vmem] * (2 + len(parts)),
+        in_specs=[vmem] * (3 + len(parts)),
         out_specs=vmem,
+        scratch_shapes=[pltpu.VMEM((owned, slots, cols), f32)],
         compiler_params=pltpu.CompilerParams(vmem_limit_bytes=16 * 1024 * 1024),
         cost_estimate=pl.CostEstimate(
             flops=8 * slots * owned * cols, bytes_accessed=8 * 1024 * 1024 // 4, transcendentals=0
         ),
-    )(ridge, keep, *parts)
+    )(*tables, *parts)
 
 
 def squared_table(weight_table):
@@ -412,26 +423,16 @@
 def by_rounds(images, class_index, pose_index, defocus_bin, defocus, rows_table, cols_table, plane_weight):
     members = lax.axis_size("img")
     rounds = members // 2
-    count = images.shape[0]
-    poses, rows, _ = rows_table.shape
+    rows = rows_table.shape[1]
     planes = plane_weight.shape[1]
     cols = cols_table.shape[2]
     owned = rows // members
-    me = lax.axis_index("img")
-
-    code = (class_index[:, 0] * poses + pose_index) * defocus.shape[0] + defocus_bin
-    seat = jnp.arange(members * count, dtype=jnp.int32) // count
-    code = jnp.where(seat == me, jnp.tile(code, members), -1)[None]
-    codes = [code] + [
-        lax.ppermute(code, "img", [(i, (i + k) % members) for i in range(members)])
-        for k in range(1, members)
-    ]
     outs = own_totals(
         images, class_index, pose_index, defocus_bin, defocus, rows_table, cols_table, plane_weight, rounds
     )
     sends, keeps = outs[:rounds], outs[rounds:]
     order = sorted(range(rounds), key=lambda k: (k == 0, -min(k, rounds - k)))
-    parts = []
+    parts = [keeps[0]]
     for k in order:
         came = lax.ppermute(sends[k], "img", [(i, i ^ 1) for i in range(members)])
         if k == 0:
@@ -439,8 +440,8 @@
         else:
             both = (keeps[k] + came.astype(f32)).astype(bf16)
             parts.append(lax.ppermute(both, "img", [(i, (i + 2 * k) % members) for i in range(members)]))
-    ridge = own_ridges(codes, defocus, plane_weight, rows_table, cols_table, owned)
-    out = finish(ridge, keeps[0], parts)
+    tables = own_ridges(defocus, plane_weight, rows_table, cols_table, owned)
+    out = finish(tables, parts)
     return out.reshape(owned, CLASSES, planes, 2, cols)
 
 
@@ -460,14 +461,15 @@
         class_index, pose_index, defocus_bin, defocus, rows_table, cols_table, plane_weight,
         lax.axis_index("img") * owned, owned,
     )
-    own = own.astype(f32).reshape(CLASSES, planes, owned, 2, cols).transpose(2, 0, 1, 3, 4)
+    own = own.astype(f32).reshape(planes, CLASSES, owned, 2, cols).transpose(2, 1, 0, 3, 4)
     return own / (weight[:, :, :, None, :] + wiener_ridge)
 
 
 def body(*arrays):
     rows = arrays[5].shape[1]
     members = lax.axis_size("img")
-    small = 2 <= members <= 8 and members % 2 == 0 and rows % (16 * members) == 0
+    images = members * arrays[0].shape[0]
+    small = members % 2 == 0 and images <= 256 and rows % (16 * members) == 0
     return (by_rounds if small else by_scatter)(*arrays)
 
 

time: 66.4 us -> 38 us (0.57)
  starting transfers between devices: 31.4 us -> 12.3 us
  waiting for transfers between devices: 17.5 us -> 7.83 us
    ppermute x7 -> x0, starting transfers between devices: 18.4 us -> none  [by_rounds(): lax.ppermute(code, 'img', [(i, (i + k) % members) for i in range(members)])]
    ppermute x7 -> x0, waiting for transfers between devices: 15.1 us -> none  [by_rounds(): lax.ppermute(code, 'img', [(i, (i + k) % members) for i in range(members)])]
    ppermute x3, waiting for transfers between devices: 0.01 us -> 5.22 us  [by_rounds(): lax.ppermute(both, 'img', [(i, (i + 2 * k) % members) for i in range(memb...]
    ppermute x3, starting transfers between devices: 7.85 us -> 7.18 us  [by_rounds(): lax.ppermute(both, 'img', [(i, (i + 2 * k) % members) for i in range(memb...]
  transfers between devices with their start and end apart: 14 -> 7, of which waited for: 8 -> 3; matrix products, arithmetic and copies ran while one was open for 5% -> 8% of each run, Pallas kernels for 3% -> 6%
where the time goes in v2:
time: 38 us; the launch traced here: 37.8 us
  Pallas kernels  14.5 us (38%)
  starting transfers between devices  12.3 us (32%)
  waiting for transfers between devices  7.83 us (21%)
  other arithmetic  2.98 us (8%)
    pallas_call x1, Pallas kernels, own_totals(): pl.pallas_call(slices_kernel, out_shape=out_shape, in_specs=[any_place] *...  11.2 us
    ppermute x3, starting transfers between devices, by_rounds(): lax.ppermute(both, 'img', [(i, (i + 2 * k) % members) for i in range(memb...  7.18 us
    ppermute x3, waiting for transfers between devices, by_rounds(): lax.ppermute(both, 'img', [(i, (i + 2 * k) % members) for i in range(memb...  5.22 us
    ppermute x4, starting transfers between devices, by_rounds(): came = lax.ppermute(sends[k], 'img', [(i, i ^ 1) for i in range(members)])  5.12 us
    convert_element_type x3, other arithmetic, by_rounds(): both = (keeps[k] + came.astype(f32)).astype(bf16)  2.98 us
    ppermute x4, waiting for transfers between devices, by_rounds(): came = lax.ppermute(sends[k], 'img', [(i, i ^ 1) for i in range(members)])  2.61 us
    pallas_call x1, Pallas kernels, own_ridges(): pl.pallas_call(ridge_kernel, out_shape=[table, table, jax.ShapeDtypeStruc...  2.09 us
    pallas_call x1, Pallas kernels, finish(): pl.pallas_call(finish_kernel, out_shape=jax.ShapeDtypeStruct((owned, 2 *...  1.27 us
  transfers between devices with their start and end apart: 7, of which 3 were waited for; matrix products, arithmetic and copies ran while one was open for 8% of the time, Pallas kernels for 6%

profile of v2, /device:TPU:0, one launch (start us, length us, event | category | flops | bytes accessed | tf_op | source)
XLA Modules:
  0.0 37.8 jit_solution(806929882146207623)
XLA Ops:
  0.0 0.0 copy-start.1
  0.0 0.0 copy-start.2
  0.0 0.0 copy-start.3
  0.0 0.0 copy-start.4
  0.0 11.2 %shard_map.101 = (bf16[17,16,256]{2,1,0:T(8,128)(2,1)}, bf16[17,16,256]{2,1,0:T(8,128)(2,1)}, bf16[17,16,256]{2,1,0:T(8,128)(2,1)}, bf16[17,16,256]{2,1,0:T(8,12...) custom-call(s32[16]{0:T(128)} %bitcast.5, ...), custom_call_target="tpu_custom_call" | custom-call | flops 2097152000 | bytes 6291456 | tf_op jit(solution)/shard_map/pallas_call | solution.py:234
  11.2 0.0 copy-start
  11.2 3.0 %collective-permute-start.4 = (bf16[17,16,256]{2,1,0:T(8,128)(2,1)}, bf16[17,16,256]{2,1,0:T(8,128)(2,1)S(1)}, u32[]{:S(2)}, u32[]{:S(2)}) collective-permute-start(bf16[17,16,256]{2,1,0:T(8,128)(2,1)} %get-tuple-element.25), channel_id=1, source_target_pairs={{0,2},{2,0},{4,6},{6,4},{8,10},{10,8},{12,14},{14,12},{1,3},{3,1},... | collective-permute-start | bytes 417800 | tf_op jit(solution)/shard_map/ppermute | solution.py:437
  14.2 0.1 collective-permute-start.2
  14.3 1.9 %collective-permute-start = (bf16[17,16,256]{2,1,0:T(8,128)(2,1)}, bf16[17,16,256]{2,1,0:T(8,128)(2,1)S(1)}, u32[]{:S(2)}, u32[]{:S(2)}) collective-permute-start(bf16[17,16,256]{2,1,0:T(8,128)(2,1)} %get-tuple-element.21), channel_id=1, source_target_pairs={{0,2},{2,0},{4,6},{6,4},{8,10},{10,8},{12,14},{14,12},{1,3},{3,1},... | collective-permute-start | bytes 417800 | tf_op jit(solution)/shard_map/ppermute | solution.py:437
  16.3 0.1 collective-permute-start.6
  16.3 2.6 %collective-permute-done.4 = bf16[17,16,256]{2,1,0:T(8,128)(2,1)S(1)} collective-permute-done((bf16[17,16,256]{2,1,0:T(8,128)(2,1)}, bf16[17,16,256]{2,1,0:T(8,128)(2,1)S(1)}, u32[]{:S(2)}, u32[]{:S(2)}) %collective-permute-start.4) | collective-permute-done | bytes 139296 | tf_op jit(solution)/shard_map/ppermute | solution.py:437
  18.9 1.0 %add_convert_fusion = bf16[17,16,256]{2,1,0:T(8,128)(2,1)S(1)} fusion(f32[17,16,256]{2,1,0:T(8,128)} %get-tuple-element.24, bf16[17,16,256]{2,1,0:T(8,128)(2,1)S(1)} %collective-permute-done.4), kind=kLoop, calls=%fused_computation | loop fusion | flops 208896 | bytes 557056 | tf_op jit(solution)/shard_map/convert_element_type | solution.py:441
  19.9 4.2 %collective-permute-start.5 = (bf16[17,16,256]{2,1,0:T(8,128)(2,1)S(1)}, bf16[17,16,256]{2,1,0:T(8,128)(2,1)S(1)}, u32[]{:S(2)}, u32[]{:S(2)}) collective-permute-start(bf16[17,16,256]{2,1,0:T(8,128)(2,1)S(1)} %add_convert_fusion), channel_id=1, source_target_pairs={{0,12},{2,14},{4,0},{6,2},{8,4},{10,6},{12,8},{14,10},{1,13},{3,15... | collective-permute-start | bytes 417800 | tf_op jit(solution)/shard_map/ppermute | solution.py:442
  24.2 0.0 collective-permute-done.2
  24.2 1.0 %add_convert_fusion.1 = bf16[17,16,256]{2,1,0:T(8,128)(2,1)S(1)} fusion(f32[17,16,256]{2,1,0:T(8,128)} %get-tuple-element.22, bf16[17,16,256]{2,1,0:T(8,128)(2,1)S(1)} %collective-permute-done.2), kind=kLoop, calls=%fused_computation.1 | loop fusion | flops 208896 | bytes 557056 | tf_op jit(solution)/shard_map/convert_element_type | solution.py:441
  25.2 0.1 collective-permute-start.3
  25.2 0.0 collective-permute-done
  25.2 1.0 %add_convert_fusion.2 = bf16[17,16,256]{2,1,0:T(8,128)(2,1)S(1)} fusion(f32[17,16,256]{2,1,0:T(8,128)} %get-tuple-element.20, bf16[17,16,256]{2,1,0:T(8,128)(2,1)S(1)} %collective-permute-done), kind=kLoop, calls=%fused_computation.2 | loop fusion | flops 208896 | bytes 557056 | tf_op jit(solution)/shard_map/convert_element_type | solution.py:441
  26.2 2.9 %collective-permute-start.1 = (bf16[17,16,256]{2,1,0:T(8,128)(2,1)S(1)}, bf16[17,16,256]{2,1,0:T(8,128)(2,1)S(1)}, u32[]{:S(2)}, u32[]{:S(2)}) collective-permute-start(bf16[17,16,256]{2,1,0:T(8,128)(2,1)S(1)} %add_convert_fusion.2), channel_id=1, source_target_pairs={{0,8},{2,10},{4,12},{6,14},{8,0},{10,2},{12,4},{14,6},{1,9},{3,11}... | collective-permute-start | bytes 417800 | tf_op jit(solution)/shard_map/ppermute | solution.py:442
  29.1 0.0 copy-done.1
  29.1 0.0 copy-done.2
  29.1 0.0 copy-done.3
  29.1 0.0 copy-done.4
  29.1 2.1 %shard_map.100 = (bf16[128,2048]{1,0:T(8,128)(2,1)S(1)}, bf16[128,2048]{1,0:T(8,128)(2,1)S(1)}, f32[16,128]{1,0:T(8,128)S(1)}) custom-call(f32[16]{0:T(128)S(1)} %copy-done.4, f32[2,8]{1,0:T(2,128)S(1)} %bitcast.4, bf16[8,128,256]{2,1,0:T(8,128)(2,1)S(1)} %copy-done.1, bf16[8,256,128]{2,1,0:T(8,128)(2,1)S(1)} %copy-done.2), custom_call_target="tpu_custom_call" | custom-call | flops 524288000 | bytes 2097152 | tf_op jit(solution)/shard_map/pallas_call | solution.py:327
  31.2 0.0 collective-permute-done.6.refs_4_
  31.3 0.0 collective-permute-done.5.refs_3_
  31.3 0.9 %collective-permute-done.3.refs_2_ = bf16[17,16,256]{2,1,0:T(8,128)(2,1)S(1)} collective-permute-done((bf16[17,16,256]{2,1,0:T(8,128)(2,1)S(1)}, bf16[17,16,256]{2,1,0:T(8,128)(2,1)S(1)}, u32[]{:S(2)}, u32[]{:S(2)}) %collective-permute-start.3) | collective-permute-done | bytes 139296 | tf_op jit(solution)/shard_map/ppermute | solution.py:442
  32.2 4.3 %collective-permute-done.1.refs_1_ = bf16[17,16,256]{2,1,0:T(8,128)(2,1)S(1)} collective-permute-done((bf16[17,16,256]{2,1,0:T(8,128)(2,1)S(1)}, bf16[17,16,256]{2,1,0:T(8,128)(2,1)S(1)}, u32[]{:S(2)}, u32[]{:S(2)}) %collective-permute-start.1) | collective-permute-done | bytes 139296 | tf_op jit(solution)/shard_map/ppermute | solution.py:442
  36.5 0.0 copy-done
  36.5 1.3 %shard_map.102 = f32[16,32,128]{2,1,0:T(8,128)} custom-call(bf16[128,2048]{1,0:T(8,128)(2,1)S(1)} %get-tuple-element.16.high_ref, bf16[128,2048]{1,0:T(8,128)(2,1)S(1)} %get-tuple-element.17.low_ref, f32[16,128]{1,0:T(8,128)S(1)} %get-tuple-element.18.share_ref, f32[17,16,256]{2,1,0:T(8,128)S(1)} %copy-done, ...), custom_call_target="tpu_custom_call" | custom-call | flops 262144 | bytes 2097152 | tf_op jit(solution)/shard_map/pallas_call | solution.py:380
Async XLA Ops:
  0.0 29.1 %copy-start.1 = (bf16[8,128,256]{2,1,0:T(8,128)(2,1)S(1)}, bf16[8,128,256]{2,1,0:T(8,128)(2,1)}, u32[]{:S(2)}) copy-start(bf16[8,128,256]{2,1,0:T(8,128)(2,1)} %rows_hbm.3) | copy-start | bytes 1572868
  0.0 29.1 %copy-start.2 = (bf16[8,256,128]{2,1,0:T(8,128)(2,1)S(1)}, bf16[8,256,128]{2,1,0:T(8,128)(2,1)}, u32[]{:S(2)}) copy-start(bf16[8,256,128]{2,1,0:T(8,128)(2,1)} %cols_hbm.3) | copy-start | bytes 1572868
  0.0 29.1 %copy-start.3 = (f32[8,2]{0,1:T(2,128)S(1)}, f32[8,2]{0,1:T(2,128)}, u32[]{:S(2)}) copy-start(f32[8,2]{0,1:T(2,128)} %param.17) | copy-start | bytes 196
  0.0 29.1 %copy-start.4 = (f32[16]{0:T(128)S(1)}, f32[16]{0:T(128)}, u32[]{:S(2)}) copy-start(f32[16]{0:T(128)} %defocus_hbm.3) | copy-start | bytes 196
  11.2 25.3 %copy-start = (f32[17,16,256]{2,1,0:T(8,128)S(1)}, f32[17,16,256]{2,1,0:T(8,128)}, u32[]{:S(2)}) copy-start(f32[17,16,256]{2,1,0:T(8,128)} %get-tuple-element.19.refs_0_) | copy-start | bytes 835588
  11.2 7.7 %collective-permute-start.4 = (bf16[17,16,256]{2,1,0:T(8,128)(2,1)}, bf16[17,16,256]{2,1,0:T(8,128)(2,1)S(1)}, u32[]{:S(2)}, u32[]{:S(2)}) collective-permute-start(bf16[17,16,256]{2,1,0:T(8,128)(2,1)} %get-tuple-element.25), channel_id=1, source_target_pairs={{0,2},{2,0},{4,6},{6,4},{8,10},{10,8},{12,14},{14,12},{1,3},{3,1},... | collective-permute-start | bytes 417800 | tf_op jit(solution)/shard_map/ppermute | solution.py:437
  14.2 9.9 %collective-permute-start.2 = (bf16[17,16,256]{2,1,0:T(8,128)(2,1)}, bf16[17,16,256]{2,1,0:T(8,128)(2,1)S(1)}, u32[]{:S(2)}, u32[]{:S(2)}) collective-permute-start(bf16[17,16,256]{2,1,0:T(8,128)(2,1)} %get-tuple-element.23), channel_id=1, source_target_pairs={{0,2},{2,0},{4,6},{6,4},{8,10},{10,8},{12,14},{14,12},{1,3},{3,1},... | collective-permute-start | bytes 417800 | tf_op jit(solution)/shard_map/ppermute | solution.py:437
  14.3 10.9 %collective-permute-start = (bf16[17,16,256]{2,1,0:T(8,128)(2,1)}, bf16[17,16,256]{2,1,0:T(8,128)(2,1)S(1)}, u32[]{:S(2)}, u32[]{:S(2)}) collective-permute-start(bf16[17,16,256]{2,1,0:T(8,128)(2,1)} %get-tuple-element.21), channel_id=1, source_target_pairs={{0,2},{2,0},{4,6},{6,4},{8,10},{10,8},{12,14},{14,12},{1,3},{3,1},... | collective-permute-start | bytes 417800 | tf_op jit(solution)/shard_map/ppermute | solution.py:437
  16.3 15.0 %collective-permute-start.6 = (bf16[17,16,256]{2,1,0:T(8,128)(2,1)}, bf16[17,16,256]{2,1,0:T(8,128)(2,1)S(1)}, u32[]{:S(2)}, u32[]{:S(2)}) collective-permute-start(bf16[17,16,256]{2,1,0:T(8,128)(2,1)} %get-tuple-element.26), channel_id=1, source_target_pairs={{0,2},{2,0},{4,6},{6,4},{8,10},{10,8},{12,14},{14,12},{1,3},{3,1},... | collective-permute-start | bytes 417800 | tf_op jit(solution)/shard_map/ppermute | solution.py:437
  19.9 11.3 %collective-permute-start.5 = (bf16[17,16,256]{2,1,0:T(8,128)(2,1)S(1)}, bf16[17,16,256]{2,1,0:T(8,128)(2,1)S(1)}, u32[]{:S(2)}, u32[]{:S(2)}) collective-permute-start(bf16[17,16,256]{2,1,0:T(8,128)(2,1)S(1)} %add_convert_fusion), channel_id=1, source_target_pairs={{0,12},{2,14},{4,0},{6,2},{8,4},{10,6},{12,8},{14,10},{1,13},{3,15... | collective-permute-start | bytes 417800 | tf_op jit(solution)/shard_map/ppermute | solution.py:442
  25.2 7.0 %collective-permute-start.3 = (bf16[17,16,256]{2,1,0:T(8,128)(2,1)S(1)}, bf16[17,16,256]{2,1,0:T(8,128)(2,1)S(1)}, u32[]{:S(2)}, u32[]{:S(2)}) collective-permute-start(bf16[17,16,256]{2,1,0:T(8,128)(2,1)S(1)} %add_convert_fusion.1), channel_id=1, source_target_pairs={{0,4},{2,6},{4,8},{6,10},{8,12},{10,14},{12,0},{14,2},{1,5},{3,7},... | collective-permute-start | bytes 417800 | tf_op jit(solution)/shard_map/ppermute | solution.py:442
  26.2 10.2 %collective-permute-start.1 = (bf16[17,16,256]{2,1,0:T(8,128)(2,1)S(1)}, bf16[17,16,256]{2,1,0:T(8,128)(2,1)S(1)}, u32[]{:S(2)}, u32[]{:S(2)}) collective-permute-start(bf16[17,16,256]{2,1,0:T(8,128)(2,1)S(1)} %add_convert_fusion.2), channel_id=1, source_target_pairs={{0,8},{2,10},{4,12},{6,14},{8,0},{10,2},{12,4},{14,6},{1,9},{3,11}... | collective-permute-start | bytes 417800 | tf_op jit(solution)/shard_map/ppermute | solution.py:442

commit v3 on v2

--- a/solution.py
+++ b/solution.py
@@ -17,11 +17,11 @@
 bf16 = jnp.bfloat16
 
 
-def packed_dft(box):
+def packed_dft(box, sine_sign):
     half = box // 2
     k = np.concatenate([np.arange(half), [half], np.arange(1, half)])
     angle = (k[:, None] * np.arange(box)[None, :] % box) * (2.0 * math.pi / box)
-    table = np.where((np.arange(box) <= half)[:, None], np.cos(angle), np.sin(angle))
+    table = np.where((np.arange(box) <= half)[:, None], np.cos(angle), sine_sign * np.sin(angle))
     return (table / math.sqrt(box)).astype(np.float32)
 
 
@@ -56,7 +56,7 @@
     (
         class_ref, pose_ref, bin_ref, defocus_ref, plane_ref,
         dft_ref, dft_t_ref, images_ref, rows_ref, cols_ref, arrived,
-        z_ref, rows_fold, cols_fold, ctf_left, ctf_right, spec_ref, mix_ref, totals,
+        rows_fold, cols_fold, wave_y, cos_x, sin_x, spec_ref, mix_ref, totals,
     ) = refs
     count, box, _ = images_ref.shape
     half = box // 2
@@ -85,8 +85,7 @@
 
     for copy in copies[:5]:
         copy.wait()
-    lanes = ctf_left.shape[1]
-    tall = ctf_left.shape[0]
+    tall, lanes = wave_y.shape
     lane = iota((1, lanes), 1)
     sub = iota((count, box), 0)
     lane_defocus = jnp.zeros((1, lanes), f32)
@@ -96,23 +95,14 @@
         lane_defocus = jnp.where(lane % count == i, value, lane_defocus)
         sub_defocus = jnp.where(sub == i, value, sub_defocus)
     scale = 1.0 / (2 * half * half)
-    ky = jnp.minimum(iota((tall, lanes), 0), half).astype(f32)
-    group = iota((tall, lanes), 1) // count
-    turns = lane_defocus * (ky * ky * scale) + ctf_phase / (2.0 * math.pi)
-    wave = turns_sine(turns + (group % 2).astype(f32) * 0.25)
-    high, low = split_two(wave)
-    ctf_left[...] = jnp.where(
-        group < 4, high.astype(f32), jnp.where(group < 6, low.astype(f32), 0.0)
-    ).astype(bf16)
+    ky = iota((tall, lanes), 0).astype(f32)
+    quarter = jnp.where(lane < count, 0.0, 0.25) + ctf_phase / (2.0 * math.pi)
+    wave_y[...] = turns_sine(lane_defocus * (ky * ky * scale) + quarter)
     kx = iota((count, box), 1)
     kx = jnp.where(kx <= half, kx, kx - half).astype(f32)
     turns = sub_defocus * (kx * kx * scale)
-    cos_high, cos_low = split_two(-turns_sine(turns + 0.25))
-    sin_high, sin_low = split_two(-turns_sine(turns))
-    zero = jnp.zeros((lanes - 6 * count, box), bf16)
-    ctf_right[...] = jnp.concatenate(
-        [cos_high, sin_high, cos_low, sin_low, cos_high, sin_high, zero], 0
-    )
+    cos_x[...] = -turns_sine(turns + 0.25)
+    sin_x[...] = -turns_sine(turns)
     totals[...] = jnp.zeros_like(totals)
     if len(outs) > 1:
         bins = defocus_ref.shape[0]
@@ -129,66 +119,86 @@
         rows_ref[...].reshape(poses * rows, box), near, ((1,), (1,))
     ).astype(bf16)
     copies[6].wait()
-    for p in range(poses):
-        cols_fold[p, :, :cols] = dot(near, cols_ref[p]).astype(bf16)
-        cols_fold[p, :, cols:] = dot(far, cols_ref[p]).astype(bf16)
+    for p in range(0, poses, 2):
+        two = jnp.concatenate([cols_ref[p], cols_ref[p + 1]], 1)
+        near_two = dot(near, two).astype(bf16)
+        far_two = dot(far, two).astype(bf16)
+        cols_fold[p] = jnp.concatenate([near_two[:, :cols], far_two[:, :cols]], 1)
+        cols_fold[p + 1] = jnp.concatenate([near_two[:, cols:], far_two[:, cols:]], 1)
     for copy in copies[7:]:
         copy.wait()
-    z_ref[...] = dot(images_ref[...].reshape(count * box, box), dft_t_ref[...]).astype(bf16)
-
-    row_zero = iota((half, half), 0) == 0
+
+    tile = 8
+    tile_row = iota((tile, half), 0) == 0
+    tile_col = iota((tile, half), 1) == 0
     col_zero = iota((half, half), 1) == 0
-    edge = row_zero | col_zero
     short_row = iota((16, half), 0) == 0
     short_col = iota((16, half), 1) == 0
-    right_row = iota((lanes, box), 0) % count
-
-    def one_image(i, carry):
-        pose = pose_ref[i]
-        chosen = jnp.where(right_row == i, ctf_right[...].astype(f32), 0.0).astype(bf16)
-        contrast = dot(ctf_left[...], chosen)
-        y = dot(dft_ref[...], z_ref[pl.ds(pl.multiple_of(i * box, box), box), :])
+
+    def without_row(value):
+        return jnp.concatenate([jnp.where(tile_row, 0.0, value[:tile]), value[tile:]], 0)
+
+    def transform(i):
+        z = dot(images_ref[i], dft_t_ref[...]).astype(bf16)
+        y = dot(dft_ref[...], z)
+        sin_col = jnp.broadcast_to(wave_y[:, i : i + 1], (tall, half))
+        cos_col = jnp.broadcast_to(wave_y[:, count + i : count + i + 1], (tall, half))
+        near_ctf = sin_col * cos_x[i : i + 1, :half] + cos_col * sin_x[i : i + 1, :half]
+        far_ctf = sin_col * cos_x[i : i + 1, half:] + cos_col * sin_x[i : i + 1, half:]
         cc, cs = y[:half, :half], y[:half, half:]
         sc, ss = y[half:, :half], y[half:, half:]
-        ss_in = jnp.where(edge, 0.0, ss)
-        sc_in = jnp.where(row_zero, 0.0, sc)
+        ss_row = without_row(ss)
+        ss_in = jnp.where(col_zero, 0.0, ss_row)
+        sc_in = without_row(sc)
         cs_in = jnp.where(col_zero, 0.0, cs)
-        near_ctf, far_ctf = contrast[:half, :half], contrast[:half, half:]
-        spec_ref[0:half, 0:half] = (near_ctf * (cc - ss_in)).astype(bf16)
-        spec_ref[0:half, half:] = (far_ctf * jnp.where(col_zero, cs, cc + ss_in)).astype(bf16)
-        spec_ref[half:box, 0:half] = (-near_ctf * (sc_in + cs_in)).astype(bf16)
-        spec_ref[half:box, half:] = (
-            far_ctf * jnp.where(col_zero, jnp.where(row_zero, 0.0, -ss), cs_in - sc_in)
-        ).astype(bf16)
+        near_y, far_y = near_ctf[:half], far_ctf[:half]
+        spec = spec_ref.at[i % SLOTS]
+        spec[0:half, 0:half] = (near_y * (cc + ss_in)).astype(bf16)
+        spec[0:half, half:] = (far_y * jnp.where(col_zero, cs, cc - ss_in)).astype(bf16)
+        spec[half:box, 0:half] = (near_y * (sc_in - cs_in)).astype(bf16)
+        spec[half:box, half:] = (far_y * jnp.where(col_zero, ss_row, sc_in + cs_in)).astype(bf16)
         sc_top = jnp.broadcast_to(sc[0:1], (16, half))
         ss_top = jnp.broadcast_to(ss[0:1], (16, half))
         ss_top_in = jnp.where(short_col, 0.0, ss_top)
-        edge_ctf = contrast[half : half + 1]
-        spec_ref[box : box + 16, 0:half] = (
-            edge_ctf[:, :half] * jnp.where(short_row, sc_top, -ss_top_in)
+        spec[box : box + 16, 0:half] = (
+            near_ctf[half : half + 1] * jnp.where(short_row, sc_top, -ss_top_in)
         ).astype(bf16)
-        spec_ref[box : box + 16, half:] = (
-            edge_ctf[:, half:]
+        spec[box : box + 16, half:] = (
+            far_ctf[half : half + 1]
             * jnp.where(short_row, jnp.where(short_col, ss_top, sc_top), ss_top_in)
         ).astype(bf16)
-        mixed = dot(spec_ref[...], cols_fold[pose])
-        top = iota((half, cols), 0) == 0
-        mix_ref[0:half, 0:cols] = mixed[:half, :cols].astype(bf16)
-        mix_ref[0:half, cols:] = mixed[half:box, :cols].astype(bf16)
-        mix_ref[half:, 0:cols] = jnp.where(
-            top, mixed[box : box + 1, :cols], mixed[:half, cols:]
+
+    def mix(i):
+        mixed = dot(spec_ref[i % SLOTS], cols_fold[pose_ref[i]])
+        out = mix_ref.at[i % SLOTS]
+        out[0:half, 0:cols] = mixed[:half, :cols].astype(bf16)
+        out[0:half, cols:] = mixed[half:box, :cols].astype(bf16)
+        top = iota((16, cols), 0) == 0
+        real, imag = mixed[:half, cols:], -mixed[half:box, cols:]
+        out[half : half + 16, 0:cols] = jnp.where(
+            top, mixed[box : box + 1, :cols], real[:16]
         ).astype(bf16)
-        mix_ref[half:, cols:] = jnp.where(
-            top, mixed[box + 1 : box + 2, :cols], -mixed[half:box, cols:]
+        out[half : half + 16, cols:] = jnp.where(
+            top, mixed[box + 1 : box + 2, :cols], imag[:16]
         ).astype(bf16)
+        out[half + 16 :, 0:cols] = real[16:].astype(bf16)
+        out[half + 16 :, cols:] = imag[16:].astype(bf16)
+
+    def insert(i):
+        pose = pose_ref[i]
         pose_rows = rows_fold[pl.ds(pl.multiple_of(pose * rows, rows), rows), :]
-        piece = dot(pose_rows, mix_ref[...])
+        piece = dot(pose_rows, mix_ref[i % SLOTS])
         for z in range(planes):
             slot = z * CLASSES + class_ref[i]
             totals[slot] += plane_ref[z, pose] * piece
-        return carry
-
-    lax.fori_loop(0, count, one_image, 0, unroll=True)
+
+    for step in range(count + 2):
+        if step >= 2:
+            insert(step - 2)
+        if 1 <= step <= count:
+            mix(step - 1)
+        if step < count:
+            transform(step)
 
     if len(outs) == 1:
         outs[0][...] = totals[...].astype(bf16)
@@ -207,6 +217,7 @@
 
 
 SCRATCH = 19
+SLOTS = 3
 
 
 def own_totals(images, class_index, pose_index, defocus_bin, defocus, rows_table, cols_table, plane_weight, turns_round):
@@ -215,10 +226,10 @@
     cols = cols_table.shape[2]
     planes = plane_weight.shape[1]
     slots = CLASSES * planes
-    table = packed_dft(box)
+    table_y, table_x = packed_dft(box, -1.0), packed_dft(box, 1.0)
     any_place = pl.BlockSpec(memory_space=pl.ANY)
     vmem = pl.BlockSpec(memory_space=pltpu.VMEM)
-    lanes = 128 * (-(-6 * count // 128))
+    lanes = 128 * (-(-2 * count // 128))
     if turns_round == 0:
         out_shape = [jax.ShapeDtypeStruct((slots, rows, 2 * cols), bf16)]
     else:
@@ -228,7 +239,7 @@
         out_shape += [jax.ShapeDtypeStruct(piece, f32)] * turns_round
     operands = (
         class_index[:, 0], pose_index, defocus_bin, defocus, plane_weight.T,
-        jnp.asarray(table, bf16), jnp.asarray(table.T.copy(), bf16),
+        jnp.asarray(table_y, bf16), jnp.asarray(table_x.T.copy(), bf16),
         images, rows_table, cols_table,
     )
     return pl.pallas_call(
@@ -240,13 +251,13 @@
         + [pltpu.VMEM(x.shape, x.dtype) for x in operands[5:]]
         + [
             pltpu.SemaphoreType.DMA((10,)),
-            pltpu.VMEM((count * box, box), bf16),
             pltpu.VMEM((poses * rows, box), bf16),
             pltpu.VMEM((poses, box, 2 * cols), bf16),
-            pltpu.VMEM((box // 2 + 16, lanes), bf16),
-            pltpu.VMEM((lanes, box), bf16),
-            pltpu.VMEM((box + 16, box), bf16),
-            pltpu.VMEM((box, 2 * cols), bf16),
+            pltpu.VMEM((box // 2 + 8, lanes), f32),
+            pltpu.VMEM((count, box), f32),
+            pltpu.VMEM((count, box), f32),
+            pltpu.VMEM((SLOTS, box + 16, box), bf16),
+            pltpu.VMEM((SLOTS, box, 2 * cols), bf16),
             pltpu.VMEM((slots, rows, 2 * cols), f32),
         ],
         compiler_params=pltpu.CompilerParams(vmem_limit_bytes=VMEM_LIMIT),

time: 38 us -> 35.6 us (0.937)
  Pallas kernels: 14.5 us -> 12.2 us
    pallas_call x1, Pallas kernels: 11.2 us -> 8.8 us  [own_totals(): pl.pallas_call(slices_kernel, out_shape=out_shape, in_specs=[any_place] *...]
where the time goes in v3:
time: 35.6 us; the launch traced here: 35.4 us
  starting transfers between devices  12.3 us (35%)
  Pallas kernels  12.2 us (34%)
  waiting for transfers between devices  7.83 us (22%)
  other arithmetic  2.98 us (8%)
    pallas_call x1, Pallas kernels, own_totals(): pl.pallas_call(slices_kernel, out_shape=out_shape, in_specs=[any_place] *...  8.8 us
    ppermute x3, starting transfers between devices, by_rounds(): lax.ppermute(both, 'img', [(i, (i + 2 * k) % members) for i in range(memb...  7.17 us
    ppermute x3, waiting for transfers between devices, by_rounds(): lax.ppermute(both, 'img', [(i, (i + 2 * k) % members) for i in range(memb...  5.21 us
    ppermute x4, starting transfers between devices, by_rounds(): came = lax.ppermute(sends[k], 'img', [(i, i ^ 1) for i in range(members)])  5.12 us
    convert_element_type x3, other arithmetic, by_rounds(): both = (keeps[k] + came.astype(f32)).astype(bf16)  2.98 us
    ppermute x4, waiting for transfers between devices, by_rounds(): came = lax.ppermute(sends[k], 'img', [(i, i ^ 1) for i in range(members)])  2.62 us
    pallas_call x1, Pallas kernels, own_ridges(): pl.pallas_call(ridge_kernel, out_shape=[table, table, jax.ShapeDtypeStruc...  2.09 us
    pallas_call x1, Pallas kernels, finish(): pl.pallas_call(finish_kernel, out_shape=jax.ShapeDtypeStruct((owned, 2 *...  1.27 us
  transfers between devices with their start and end apart: 7, of which 3 were waited for; matrix products, arithmetic and copies ran while one was open for 8% of the time, Pallas kernels for 6%

profile of v3, /device:TPU:0, one launch (start us, length us, event | category | flops | bytes accessed | tf_op | source)
XLA Modules:
  0.0 35.4 jit_solution(10365182845810617321)
XLA Ops:
  0.0 0.0 copy-start.1
  0.0 0.0 copy-start.2
  0.0 0.0 copy-start.3
  0.0 0.0 copy-start.4
  0.0 8.8 %shard_map.101 = (bf16[17,16,256]{2,1,0:T(8,128)(2,1)}, bf16[17,16,256]{2,1,0:T(8,128)(2,1)}, bf16[17,16,256]{2,1,0:T(8,128)(2,1)}, bf16[17,16,256]{2,1,0:T(8,12...) custom-call(s32[16]{0:T(128)} %bitcast.5, ...), custom_call_target="tpu_custom_call" | custom-call | flops 2097152000 | bytes 6291456 | tf_op jit(solution)/shard_map/pallas_call | solution.py:245
  8.8 0.0 copy-start
  8.8 3.0 %collective-permute-start.4 = (bf16[17,16,256]{2,1,0:T(8,128)(2,1)}, bf16[17,16,256]{2,1,0:T(8,128)(2,1)S(1)}, u32[]{:S(2)}, u32[]{:S(2)}) collective-permute-start(bf16[17,16,256]{2,1,0:T(8,128)(2,1)} %get-tuple-element.25), channel_id=1, source_target_pairs={{0,2},{2,0},{4,6},{6,4},{8,10},{10,8},{12,14},{14,12},{1,3},{3,1},... | collective-permute-start | bytes 417800 | tf_op jit(solution)/shard_map/ppermute | solution.py:448
  11.9 0.1 collective-permute-start.2
  11.9 1.9 %collective-permute-start = (bf16[17,16,256]{2,1,0:T(8,128)(2,1)}, bf16[17,16,256]{2,1,0:T(8,128)(2,1)S(1)}, u32[]{:S(2)}, u32[]{:S(2)}) collective-permute-start(bf16[17,16,256]{2,1,0:T(8,128)(2,1)} %get-tuple-element.21), channel_id=1, source_target_pairs={{0,2},{2,0},{4,6},{6,4},{8,10},{10,8},{12,14},{14,12},{1,3},{3,1},... | collective-permute-start | bytes 417800 | tf_op jit(solution)/shard_map/ppermute | solution.py:448
  13.9 0.1 collective-permute-start.6
  14.0 2.6 %collective-permute-done.4 = bf16[17,16,256]{2,1,0:T(8,128)(2,1)S(1)} collective-permute-done((bf16[17,16,256]{2,1,0:T(8,128)(2,1)}, bf16[17,16,256]{2,1,0:T(8,128)(2,1)S(1)}, u32[]{:S(2)}, u32[]{:S(2)}) %collective-permute-start.4) | collective-permute-done | bytes 139296 | tf_op jit(solution)/shard_map/ppermute | solution.py:448
  16.6 1.0 %add_convert_fusion = bf16[17,16,256]{2,1,0:T(8,128)(2,1)S(1)} fusion(f32[17,16,256]{2,1,0:T(8,128)} %get-tuple-element.24, bf16[17,16,256]{2,1,0:T(8,128)(2,1)S(1)} %collective-permute-done.4), kind=kLoop, calls=%fused_computation | loop fusion | flops 208896 | bytes 557056 | tf_op jit(solution)/shard_map/convert_element_type | solution.py:452
  17.6 4.2 %collective-permute-start.5 = (bf16[17,16,256]{2,1,0:T(8,128)(2,1)S(1)}, bf16[17,16,256]{2,1,0:T(8,128)(2,1)S(1)}, u32[]{:S(2)}, u32[]{:S(2)}) collective-permute-start(bf16[17,16,256]{2,1,0:T(8,128)(2,1)S(1)} %add_convert_fusion), channel_id=1, source_target_pairs={{0,12},{2,14},{4,0},{6,2},{8,4},{10,6},{12,8},{14,10},{1,13},{3,15... | collective-permute-start | bytes 417800 | tf_op jit(solution)/shard_map/ppermute | solution.py:453
  21.8 0.0 collective-permute-done.2
  21.8 1.0 %add_convert_fusion.1 = bf16[17,16,256]{2,1,0:T(8,128)(2,1)S(1)} fusion(f32[17,16,256]{2,1,0:T(8,128)} %get-tuple-element.22, bf16[17,16,256]{2,1,0:T(8,128)(2,1)S(1)} %collective-permute-done.2), kind=kLoop, calls=%fused_computation.1 | loop fusion | flops 208896 | bytes 557056 | tf_op jit(solution)/shard_map/convert_element_type | solution.py:452
  22.8 0.1 collective-permute-start.3
  22.8 0.0 collective-permute-done
  22.9 1.0 %add_convert_fusion.2 = bf16[17,16,256]{2,1,0:T(8,128)(2,1)S(1)} fusion(f32[17,16,256]{2,1,0:T(8,128)} %get-tuple-element.20, bf16[17,16,256]{2,1,0:T(8,128)(2,1)S(1)} %collective-permute-done), kind=kLoop, calls=%fused_computation.2 | loop fusion | flops 208896 | bytes 557056 | tf_op jit(solution)/shard_map/convert_element_type | solution.py:452
  23.9 2.9 %collective-permute-start.1 = (bf16[17,16,256]{2,1,0:T(8,128)(2,1)S(1)}, bf16[17,16,256]{2,1,0:T(8,128)(2,1)S(1)}, u32[]{:S(2)}, u32[]{:S(2)}) collective-permute-start(bf16[17,16,256]{2,1,0:T(8,128)(2,1)S(1)} %add_convert_fusion.2), channel_id=1, source_target_pairs={{0,8},{2,10},{4,12},{6,14},{8,0},{10,2},{12,4},{14,6},{1,9},{3,11}... | collective-permute-start | bytes 417800 | tf_op jit(solution)/shard_map/ppermute | solution.py:453
  26.8 0.0 copy-done.1
  26.8 0.0 copy-done.2
  26.8 0.0 copy-done.3
  26.8 0.0 copy-done.4
  26.8 2.1 %shard_map.100 = (bf16[128,2048]{1,0:T(8,128)(2,1)S(1)}, bf16[128,2048]{1,0:T(8,128)(2,1)S(1)}, f32[16,128]{1,0:T(8,128)S(1)}) custom-call(f32[16]{0:T(128)S(1)} %copy-done.4, f32[2,8]{1,0:T(2,128)S(1)} %bitcast.4, bf16[8,128,256]{2,1,0:T(8,128)(2,1)S(1)} %copy-done.1, bf16[8,256,128]{2,1,0:T(8,128)(2,1)S(1)} %copy-done.2), custom_call_target="tpu_custom_call" | custom-call | flops 524288000 | bytes 2097152 | tf_op jit(solution)/shard_map/pallas_call | solution.py:338
  28.9 0.0 collective-permute-done.6.refs_4_
  28.9 0.0 collective-permute-done.5.refs_3_
  28.9 1.0 %collective-permute-done.3.refs_2_ = bf16[17,16,256]{2,1,0:T(8,128)(2,1)S(1)} collective-permute-done((bf16[17,16,256]{2,1,0:T(8,128)(2,1)S(1)}, bf16[17,16,256]{2,1,0:T(8,128)(2,1)S(1)}, u32[]{:S(2)}, u32[]{:S(2)}) %collective-permute-start.3) | collective-permute-done | bytes 139296 | tf_op jit(solution)/shard_map/ppermute | solution.py:453
  29.8 4.3 %collective-permute-done.1.refs_1_ = bf16[17,16,256]{2,1,0:T(8,128)(2,1)S(1)} collective-permute-done((bf16[17,16,256]{2,1,0:T(8,128)(2,1)S(1)}, bf16[17,16,256]{2,1,0:T(8,128)(2,1)S(1)}, u32[]{:S(2)}, u32[]{:S(2)}) %collective-permute-start.1) | collective-permute-done | bytes 139296 | tf_op jit(solution)/shard_map/ppermute | solution.py:453
  34.1 0.0 copy-done
  34.1 1.3 %shard_map.102 = f32[16,32,128]{2,1,0:T(8,128)} custom-call(bf16[128,2048]{1,0:T(8,128)(2,1)S(1)} %get-tuple-element.16.high_ref, bf16[128,2048]{1,0:T(8,128)(2,1)S(1)} %get-tuple-element.17.low_ref, f32[16,128]{1,0:T(8,128)S(1)} %get-tuple-element.18.share_ref, f32[17,16,256]{2,1,0:T(8,128)S(1)} %copy-done, ...), custom_call_target="tpu_custom_call" | custom-call | flops 262144 | bytes 2097152 | tf_op jit(solution)/shard_map/pallas_call | solution.py:391
Async XLA Ops:
  0.0 26.8 %copy-start.1 = (bf16[8,128,256]{2,1,0:T(8,128)(2,1)S(1)}, bf16[8,128,256]{2,1,0:T(8,128)(2,1)}, u32[]{:S(2)}) copy-start(bf16[8,128,256]{2,1,0:T(8,128)(2,1)} %rows_hbm.3) | copy-start | bytes 1572868
  0.0 26.8 %copy-start.2 = (bf16[8,256,128]{2,1,0:T(8,128)(2,1)S(1)}, bf16[8,256,128]{2,1,0:T(8,128)(2,1)}, u32[]{:S(2)}) copy-start(bf16[8,256,128]{2,1,0:T(8,128)(2,1)} %cols_hbm.3) | copy-start | bytes 1572868
  0.0 26.8 %copy-start.3 = (f32[8,2]{0,1:T(2,128)S(1)}, f32[8,2]{0,1:T(2,128)}, u32[]{:S(2)}) copy-start(f32[8,2]{0,1:T(2,128)} %param.17) | copy-start | bytes 196
  0.0 26.8 %copy-start.4 = (f32[16]{0:T(128)S(1)}, f32[16]{0:T(128)}, u32[]{:S(2)}) copy-start(f32[16]{0:T(128)} %defocus_hbm.3) | copy-start | bytes 196
  8.8 25.3 %copy-start = (f32[17,16,256]{2,1,0:T(8,128)S(1)}, f32[17,16,256]{2,1,0:T(8,128)}, u32[]{:S(2)}) copy-start(f32[17,16,256]{2,1,0:T(8,128)} %get-tuple-element.19.refs_0_) | copy-start | bytes 835588
  8.8 7.7 %collective-permute-start.4 = (bf16[17,16,256]{2,1,0:T(8,128)(2,1)}, bf16[17,16,256]{2,1,0:T(8,128)(2,1)S(1)}, u32[]{:S(2)}, u32[]{:S(2)}) collective-permute-start(bf16[17,16,256]{2,1,0:T(8,128)(2,1)} %get-tuple-element.25), channel_id=1, source_target_pairs={{0,2},{2,0},{4,6},{6,4},{8,10},{10,8},{12,14},{14,12},{1,3},{3,1},... | collective-permute-start | bytes 417800 | tf_op jit(solution)/shard_map/ppermute | solution.py:448
  11.9 9.9 %collective-permute-start.2 = (bf16[17,16,256]{2,1,0:T(8,128)(2,1)}, bf16[17,16,256]{2,1,0:T(8,128)(2,1)S(1)}, u32[]{:S(2)}, u32[]{:S(2)}) collective-permute-start(bf16[17,16,256]{2,1,0:T(8,128)(2,1)} %get-tuple-element.23), channel_id=1, source_target_pairs={{0,2},{2,0},{4,6},{6,4},{8,10},{10,8},{12,14},{14,12},{1,3},{3,1},... | collective-permute-start | bytes 417800 | tf_op jit(solution)/shard_map/ppermute | solution.py:448
  11.9 10.9 %collective-permute-start = (bf16[17,16,256]{2,1,0:T(8,128)(2,1)}, bf16[17,16,256]{2,1,0:T(8,128)(2,1)S(1)}, u32[]{:S(2)}, u32[]{:S(2)}) collective-permute-start(bf16[17,16,256]{2,1,0:T(8,128)(2,1)} %get-tuple-element.21), channel_id=1, source_target_pairs={{0,2},{2,0},{4,6},{6,4},{8,10},{10,8},{12,14},{14,12},{1,3},{3,1},... | collective-permute-start | bytes 417800 | tf_op jit(solution)/shard_map/ppermute | solution.py:448
  13.9 15.0 %collective-permute-start.6 = (bf16[17,16,256]{2,1,0:T(8,128)(2,1)}, bf16[17,16,256]{2,1,0:T(8,128)(2,1)S(1)}, u32[]{:S(2)}, u32[]{:S(2)}) collective-permute-start(bf16[17,16,256]{2,1,0:T(8,128)(2,1)} %get-tuple-element.26), channel_id=1, source_target_pairs={{0,2},{2,0},{4,6},{6,4},{8,10},{10,8},{12,14},{14,12},{1,3},{3,1},... | collective-permute-start | bytes 417800 | tf_op jit(solution)/shard_map/ppermute | solution.py:448
  17.6 11.3 %collective-permute-start.5 = (bf16[17,16,256]{2,1,0:T(8,128)(2,1)S(1)}, bf16[17,16,256]{2,1,0:T(8,128)(2,1)S(1)}, u32[]{:S(2)}, u32[]{:S(2)}) collective-permute-start(bf16[17,16,256]{2,1,0:T(8,128)(2,1)S(1)} %add_convert_fusion), channel_id=1, source_target_pairs={{0,12},{2,14},{4,0},{6,2},{8,4},{10,6},{12,8},{14,10},{1,13},{3,15... | collective-permute-start | bytes 417800 | tf_op jit(solution)/shard_map/ppermute | solution.py:453
  22.8 7.1 %collective-permute-start.3 = (bf16[17,16,256]{2,1,0:T(8,128)(2,1)S(1)}, bf16[17,16,256]{2,1,0:T(8,128)(2,1)S(1)}, u32[]{:S(2)}, u32[]{:S(2)}) collective-permute-start(bf16[17,16,256]{2,1,0:T(8,128)(2,1)S(1)} %add_convert_fusion.1), channel_id=1, source_target_pairs={{0,4},{2,6},{4,8},{6,10},{8,12},{10,14},{12,0},{14,2},{1,5},{3,7},... | collective-permute-start | bytes 417800 | tf_op jit(solution)/shard_map/ppermute | solution.py:453
  23.9 10.2 %collective-permute-start.1 = (bf16[17,16,256]{2,1,0:T(8,128)(2,1)S(1)}, bf16[17,16,256]{2,1,0:T(8,128)(2,1)S(1)}, u32[]{:S(2)}, u32[]{:S(2)}) collective-permute-start(bf16[17,16,256]{2,1,0:T(8,128)(2,1)S(1)} %add_convert_fusion.2), channel_id=1, source_target_pairs={{0,8},{2,10},{4,12},{6,14},{8,0},{10,2},{12,4},{14,6},{1,9},{3,11}... | collective-permute-start | bytes 417800 | tf_op jit(solution)/shard_map/ppermute | solution.py:453

commit v4 on v3

--- a/solution.py
+++ b/solution.py
@@ -202,22 +202,29 @@
 
     if len(outs) == 1:
         outs[0][...] = totals[...].astype(bf16)
-    else:
-        turns_round = len(outs) // 2
-        members = 2 * turns_round
-        owned = rows // members
-        me = lax.axis_index("img")
-        for k in range(turns_round):
-            mine = lax.rem(me + 2 * k, members)
-            theirs = mine + 1 - 2 * lax.rem(me, 2)
-            first = pl.multiple_of(theirs * owned, owned)
-            outs[k][...] = totals[:, pl.ds(first, owned), :].astype(bf16)
-            first = pl.multiple_of(mine * owned, owned)
-            outs[turns_round + k][...] = totals[:, pl.ds(first, owned), :]
+        return
+    x_send, x_keep, z_keep = outs[:3]
+    z_sends = outs[3:]
+    rounds, x_slots, owned, _ = x_keep.shape
+    me = lax.axis_index("img")
+    side = lax.rem(me, 2)
+    for k in range(rounds):
+        base = lax.rem(me - side + 2 * k, 2 * rounds)
+        mine = pl.ds(pl.multiple_of((base + side) * owned, owned), owned)
+        theirs = pl.ds(pl.multiple_of((base + 1 - side) * owned, owned), owned)
+        x_keep[k] = totals[-x_slots:, mine, :]
+        x_send[k] = totals[-x_slots:, theirs, :].astype(bf16)
+        if k == 0:
+            z_keep[0] = totals[:-x_slots, mine, :]
+            z_keep[1] = totals[:-x_slots, theirs, :]
+        else:
+            z_sends[k - 1][0] = totals[:-x_slots, mine, :].astype(bf16)
+            z_sends[k - 1][1] = totals[:-x_slots, theirs, :].astype(bf16)
 
 
 SCRATCH = 19
 SLOTS = 3
+Z_SLOTS = 5
 
 
 def own_totals(images, class_index, pose_index, defocus_bin, defocus, rows_table, cols_table, plane_weight, turns_round):
@@ -234,9 +241,10 @@
         out_shape = [jax.ShapeDtypeStruct((slots, rows, 2 * cols), bf16)]
     else:
         slots += 1
-        piece = (slots, rows // (2 * turns_round), 2 * cols)
-        out_shape = [jax.ShapeDtypeStruct(piece, bf16)] * turns_round
-        out_shape += [jax.ShapeDtypeStruct(piece, f32)] * turns_round
+        x_piece = (turns_round, slots - Z_SLOTS, rows // (2 * turns_round), 2 * cols)
+        z_piece = (2, Z_SLOTS, rows // (2 * turns_round), 2 * cols)
+        out_shape = [pltpu.VMEM(x_piece, bf16), pltpu.VMEM(x_piece, f32), pltpu.VMEM(z_piece, f32)]
+        out_shape += [pltpu.VMEM(z_piece, bf16)] * (turns_round - 1)
     operands = (
         class_index[:, 0], pose_index, defocus_bin, defocus, plane_weight.T,
         jnp.asarray(table_y, bf16), jnp.asarray(table_x.T.copy(), bf16),
@@ -354,16 +362,52 @@
     )(defocus, planes, rows_table, cols_table)
 
 
-def finish_kernel(high_ref, low_ref, share_ref, *refs):
-    parts, out_ref, ridge_ref = refs[:-2], refs[-2], refs[-1]
+def middle_kernel(x_keep, z_keep, x_came, *refs):
+    rounds = x_keep.shape[0]
+    z_came, outs = refs[: rounds - 1], refs[rounds - 1 :]
+    x_own, z_own, z_send = outs[:3]
+    x_own[...] = x_keep[0] + x_came[0].astype(f32)
+    for k in range(1, rounds):
+        outs[2 + k][...] = (x_keep[k] + x_came[k].astype(f32)).astype(bf16)
+    for side in range(2):
+        value = z_keep[side]
+        for came in z_came:
+            value = value + came[side].astype(f32)
+        if side == 0:
+            z_own[...] = value
+        else:
+            z_send[...] = value.astype(bf16)
+
+
+def middle(x_keep, z_keep, x_came, z_came):
+    rounds, x_slots, owned, wide = x_keep.shape
+    vmem = pl.BlockSpec(memory_space=pltpu.VMEM)
+    x_piece, z_piece = x_keep.shape[1:], z_keep.shape[1:]
+    out_shape = [pltpu.VMEM(x_piece, f32), pltpu.VMEM(z_piece, f32), pltpu.VMEM(z_piece, bf16)]
+    out_shape += [pltpu.VMEM(x_piece, bf16)] * (rounds - 1)
+    return pl.pallas_call(
+        middle_kernel,
+        out_shape=out_shape,
+        in_specs=[vmem] * (3 + len(z_came)),
+        out_specs=[vmem] * len(out_shape),
+        compiler_params=pltpu.CompilerParams(vmem_limit_bytes=16 * 1024 * 1024),
+        cost_estimate=pl.CostEstimate(flops=1000000, bytes_accessed=4 * 1024 * 1024, transcendentals=0),
+    )(x_keep, z_keep, x_came, *z_came)
+
+
+def finish_kernel(high_ref, low_ref, share_ref, x_own, z_own, z_came, *refs):
+    x_came, out_ref, ridge_ref = refs[:-2], refs[-2], refs[-1]
     slots, pairs = share_ref.shape
     owned, _, cols = ridge_ref.shape
     planes = slots // CLASSES
+    first = z_own.shape[0]
 
     def summed(s):
-        value = parts[0][s].astype(f32)
-        for part in parts[1:]:
-            value = value + part[s].astype(f32)
+        if s < first:
+            return z_own[s] + z_came[s].astype(f32)
+        value = x_own[s - first]
+        for part in x_came:
+            value = value + part[s - first].astype(f32)
         return value
 
     counts = summed(slots)[:CLASSES, :pairs]
@@ -383,22 +427,22 @@
         out_ref[:, 2 * place + 1, :] = value[:, cols:] * factor
 
 
-def finish(tables, parts):
+def finish(tables, x_own, z_own, z_came, x_came):
     slots = tables[2].shape[0]
-    _, owned, wide = parts[0].shape
+    _, owned, wide = x_own.shape
     cols = wide // 2
     vmem = pl.BlockSpec(memory_space=pltpu.VMEM)
     return pl.pallas_call(
         finish_kernel,
         out_shape=jax.ShapeDtypeStruct((owned, 2 * slots, cols), f32),
-        in_specs=[vmem] * (3 + len(parts)),
+        in_specs=[vmem] * (6 + len(x_came)),
         out_specs=vmem,
         scratch_shapes=[pltpu.VMEM((owned, slots, cols), f32)],
         compiler_params=pltpu.CompilerParams(vmem_limit_bytes=16 * 1024 * 1024),
         cost_estimate=pl.CostEstimate(
             flops=8 * slots * owned * cols, bytes_accessed=8 * 1024 * 1024 // 4, transcendentals=0
         ),
-    )(*tables, *parts)
+    )(*tables, x_own, z_own, z_came, *x_came)
 
 
 def squared_table(weight_table):
@@ -441,18 +485,23 @@
     outs = own_totals(
         images, class_index, pose_index, defocus_bin, defocus, rows_table, cols_table, plane_weight, rounds
     )
-    sends, keeps = outs[:rounds], outs[rounds:]
-    order = sorted(range(rounds), key=lambda k: (k == 0, -min(k, rounds - k)))
-    parts = [keeps[0]]
-    for k in order:
-        came = lax.ppermute(sends[k], "img", [(i, i ^ 1) for i in range(members)])
-        if k == 0:
-            parts.append(came)
-        else:
-            both = (keeps[k] + came.astype(f32)).astype(bf16)
-            parts.append(lax.ppermute(both, "img", [(i, (i + 2 * k) % members) for i in range(members)]))
+    x_send, x_keep, z_keep = outs[:3]
+    z_sends = dict(zip(range(1, rounds), outs[3:]))
+
+    def along_x(value):
+        return lax.ppermute(value, "img", [(i, i ^ 1) for i in range(members)])
+
+    def along_z(value, k):
+        return lax.ppermute(value, "img", [(i, (i + 2 * k) % members) for i in range(members)])
+
+    order = sorted(range(1, rounds), key=lambda k: -min(k, rounds - k))
+    x_came = along_x(x_send)
+    z_came = [along_z(z_sends[k], k) for k in order]
+    x_own, z_own, z_send, *x_sends = middle(x_keep, z_keep, x_came, z_came)
+    x_came = [along_z(x_sends[k - 1], k) for k in order]
+    z_came = along_x(z_send)
     tables = own_ridges(defocus, plane_weight, rows_table, cols_table, owned)
-    out = finish(tables, parts)
+    out = finish(tables, x_own, z_own, z_came, x_came)
     return out.reshape(owned, CLASSES, planes, 2, cols)
 
 

time: 35.6 us -> 32.8 us (0.921)
  starting transfers between devices: 12.3 us -> 17.2 us
  waiting for transfers between devices: 7.83 us -> 4.28 us
  other arithmetic: 2.98 us -> 0 us
  Pallas kernels: 12.2 us -> 11.2 us
    ppermute x7 -> x8, starting transfers between devices: 12.3 us -> 17.2 us  [the longest x6 13.4 us: along_z(): lax.ppermute(value, 'img', [(i, (i + 2 * k) % members) for i in range(mem...]
    ppermute x7 -> x8, waiting for transfers between devices: 7.83 us -> 4.28 us  [the longest x6 3.16 us: along_z(): lax.ppermute(value, 'img', [(i, (i + 2 * k) % members) for i in range(mem...]
    convert_element_type x3 -> x0, other arithmetic: 2.98 us -> none  [by_rounds(): both = (keeps[k] + came.astype(f32)).astype(bf16)]
    pallas_call x1, Pallas kernels: 8.8 us -> 7.72 us  [own_totals(): pl.pallas_call(slices_kernel, out_shape=out_shape, in_specs=[any_place] *...]
  transfers between devices with their start and end apart: 7 -> 8, of which waited for: 3 -> 4; matrix products, arithmetic and copies ran while one was open for 8% -> 0% of each run, Pallas kernels for 6% -> 6%
where the time goes in v4:
time: 32.8 us; the launch traced here: 32.7 us
  starting transfers between devices  17.2 us (52%)
  Pallas kernels  11.2 us (34%)
  waiting for transfers between devices  4.28 us (13%)
    ppermute x6, starting transfers between devices, along_z(): lax.ppermute(value, 'img', [(i, (i + 2 * k) % members) for i in range(mem...  13.4 us
    pallas_call x1, Pallas kernels, own_totals(): pl.pallas_call(slices_kernel, out_shape=out_shape, in_specs=[any_place] *...  7.72 us
    ppermute x2, starting transfers between devices, along_x(): return lax.ppermute(value, 'img', [(i, i ^ 1) for i in range(members)])  3.8 us
    ppermute x6, waiting for transfers between devices, along_z(): lax.ppermute(value, 'img', [(i, (i + 2 * k) % members) for i in range(mem...  3.16 us
    pallas_call x1, Pallas kernels, own_ridges(): pl.pallas_call(ridge_kernel, out_shape=[table, table, jax.ShapeDtypeStruc...  2.09 us
    pallas_call x1, Pallas kernels, finish(): pl.pallas_call(finish_kernel, out_shape=jax.ShapeDtypeStruct((owned, 2 *...  1.25 us
    ppermute x2, waiting for transfers between devices, along_x(): return lax.ppermute(value, 'img', [(i, i ^ 1) for i in range(members)])  1.11 us
  transfers between devices with their start and end apart: 8, of which 4 were waited for; matrix products, arithmetic and copies ran while one was open for 0% of the time, Pallas kernels for 6%

profile of v4, /device:TPU:0, one launch (start us, length us, event | category | flops | bytes accessed | tf_op | source)
XLA Modules:
  0.0 32.7 jit_solution(9893788244370126382)
XLA Ops:
  0.0 0.0 copy-start
  0.0 0.0 copy-start.1
  0.0 0.0 copy-start.2
  0.0 0.0 copy-start.3
  0.0 7.7 %shard_map.101 = (bf16[4,12,16,256]{3,2,1,0:T(8,128)(2,1)S(1)}, f32[4,12,16,256]{3,2,1,0:T(8,128)S(1)}, f32[2,5,16,256]{3,2,1,0:T(8,128)S(1)}, bf16[2,5,16,256]{...) custom-call(s32[16]{0:T(128)} %bitcast.5, s32[16]{0:T(128)} %pose_hbm.1, ...), custom_call_target="tpu_custom_call" | custom-call | flops 2097152000 | bytes 6291456 | tf_op jit(solution)/shard_map/pallas_call | solution.py:253
  7.7 3.0 %collective-permute-start = (bf16[4,12,16,256]{3,2,1,0:T(8,128)(2,1)S(1)}, bf16[4,12,16,256]{3,2,1,0:T(8,128)(2,1)S(1)}, u32[]{:S(2)}, u32[]{:S(2)}) collective-permute-start(bf16[4,12,16,256]{3,2,1,0:T(8,128)(2,1)S(1)} %get-tuple-element.25), channel_id=1, source_target_pairs={{0,2},{2,0},{4,6},{6,4},{8,10},{10,8},{12,14},{14,12},{1,3},{3,1},... | collective-permute-start | bytes 1179656 | tf_op jit(solution)/shard_map/ppermute | solution.py:492
  10.8 2.6 %collective-permute-start.1 = (bf16[2,5,16,256]{3,2,1,0:T(8,128)(2,1)S(1)}, bf16[2,5,16,256]{3,2,1,0:T(8,128)(2,1)S(1)}, u32[]{:S(2)}, u32[]{:S(2)}) collective-permute-start(bf16[2,5,16,256]{3,2,1,0:T(8,128)(2,1)S(1)} %get-tuple-element.26), channel_id=1, source_target_pairs={{0,8},{2,10},{4,12},{6,14},{8,0},{10,2},{12,4},{14,6},{1,9},{3,11}... | collective-permute-start | bytes 245768 | tf_op jit(solution)/shard_map/ppermute | solution.py:495
  13.3 1.6 %collective-permute-start.2 = (bf16[2,5,16,256]{3,2,1,0:T(8,128)(2,1)S(1)}, bf16[2,5,16,256]{3,2,1,0:T(8,128)(2,1)S(1)}, u32[]{:S(2)}, u32[]{:S(2)}) collective-permute-start(bf16[2,5,16,256]{3,2,1,0:T(8,128)(2,1)S(1)} %get-tuple-element.27), channel_id=1, source_target_pairs={{0,4},{2,6},{4,8},{6,10},{8,12},{10,14},{12,0},{14,2},{1,5},{3,7},... | collective-permute-start | bytes 245768 | tf_op jit(solution)/shard_map/ppermute | solution.py:495
  14.9 2.2 %collective-permute-start.3 = (bf16[2,5,16,256]{3,2,1,0:T(8,128)(2,1)S(1)}, bf16[2,5,16,256]{3,2,1,0:T(8,128)(2,1)S(1)}, u32[]{:S(2)}, u32[]{:S(2)}) collective-permute-start(bf16[2,5,16,256]{3,2,1,0:T(8,128)(2,1)S(1)} %get-tuple-element.28), channel_id=1, source_target_pairs={{0,12},{2,14},{4,0},{6,2},{8,4},{10,6},{12,8},{14,10},{1,13},{3,15... | collective-permute-start | bytes 245768 | tf_op jit(solution)/shard_map/ppermute | solution.py:495
  17.2 1.5 %collective-permute-done.1.refs_0_ = bf16[2,5,16,256]{3,2,1,0:T(8,128)(2,1)S(1)} collective-permute-done((bf16[2,5,16,256]{3,2,1,0:T(8,128)(2,1)S(1)}, bf16[2,5,16,256]{3,2,1,0:T(8,128)(2,1)S(1)}, u32[]{:S(2)}, u32[]{:S(2)}) %collective-permute-start.1) | collective-permute-done | bytes 81952 | tf_op jit(solution)/shard_map/ppermute | solution.py:495
  18.7 1.3 %collective-permute-done.2.refs_1_ = bf16[2,5,16,256]{3,2,1,0:T(8,128)(2,1)S(1)} collective-permute-done((bf16[2,5,16,256]{3,2,1,0:T(8,128)(2,1)S(1)}, bf16[2,5,16,256]{3,2,1,0:T(8,128)(2,1)S(1)}, u32[]{:S(2)}, u32[]{:S(2)}) %collective-permute-start.2) | collective-permute-done | bytes 81952 | tf_op jit(solution)/shard_map/ppermute | solution.py:495
  19.9 0.4 %collective-permute-done.3.refs_2_ = bf16[2,5,16,256]{3,2,1,0:T(8,128)(2,1)S(1)} collective-permute-done((bf16[2,5,16,256]{3,2,1,0:T(8,128)(2,1)S(1)}, bf16[2,5,16,256]{3,2,1,0:T(8,128)(2,1)S(1)}, u32[]{:S(2)}, u32[]{:S(2)}) %collective-permute-start.3) | collective-permute-done | bytes 81952 | tf_op jit(solution)/shard_map/ppermute | solution.py:495
  20.3 0.0 collective-permute-done.x_came
  20.3 0.1 shard_map.102
  20.4 3.2 %collective-permute-start.5 = (bf16[12,16,256]{2,1,0:T(8,128)(2,1)S(1)}, bf16[12,16,256]{2,1,0:T(8,128)(2,1)S(1)}, u32[]{:S(2)}, u32[]{:S(2)}) collective-permute-start(bf16[12,16,256]{2,1,0:T(8,128)(2,1)S(1)} %get-tuple-element.32), channel_id=1, source_target_pairs={{0,8},{2,10},{4,12},{6,14},{8,0},{10,2},{12,4},{14,6},{1,9},{3,11}... | collective-permute-start | bytes 294920 | tf_op jit(solution)/shard_map/ppermute | solution.py:495
  23.6 0.9 %collective-permute-start.6 = (bf16[12,16,256]{2,1,0:T(8,128)(2,1)S(1)}, bf16[12,16,256]{2,1,0:T(8,128)(2,1)S(1)}, u32[]{:S(2)}, u32[]{:S(2)}) collective-permute-start(bf16[12,16,256]{2,1,0:T(8,128)(2,1)S(1)} %get-tuple-element.33), channel_id=1, source_target_pairs={{0,4},{2,6},{4,8},{6,10},{8,12},{10,14},{12,0},{14,2},{1,5},{3,7},... | collective-permute-start | bytes 294920 | tf_op jit(solution)/shard_map/ppermute | solution.py:495
  24.5 3.0 %collective-permute-start.7 = (bf16[12,16,256]{2,1,0:T(8,128)(2,1)S(1)}, bf16[12,16,256]{2,1,0:T(8,128)(2,1)S(1)}, u32[]{:S(2)}, u32[]{:S(2)}) collective-permute-start(bf16[12,16,256]{2,1,0:T(8,128)(2,1)S(1)} %get-tuple-element.34), channel_id=1, source_target_pairs={{0,12},{2,14},{4,0},{6,2},{8,4},{10,6},{12,8},{14,10},{1,13},{3,15... | collective-permute-start | bytes 294920 | tf_op jit(solution)/shard_map/ppermute | solution.py:495
  27.4 0.8 %collective-permute-start.4 = (bf16[5,16,256]{2,1,0:T(8,128)(2,1)S(1)}, bf16[5,16,256]{2,1,0:T(8,128)(2,1)S(1)}, u32[]{:S(2)}, u32[]{:S(2)}) collective-permute-start(bf16[5,16,256]{2,1,0:T(8,128)(2,1)S(1)} %get-tuple-element.31), channel_id=1, source_target_pairs={{0,2},{2,0},{4,6},{6,4},{8,10},{10,8},{12,14},{14,12},{1,3},{3,1},... | collective-permute-start | bytes 122888 | tf_op jit(solution)/shard_map/ppermute | solution.py:492
  28.2 0.0 copy-done
  28.2 0.0 copy-done.1
  28.2 0.0 copy-done.2
  28.2 0.0 copy-done.3
  28.2 2.1 %shard_map.100 = (bf16[128,2048]{1,0:T(8,128)(2,1)S(1)}, bf16[128,2048]{1,0:T(8,128)(2,1)S(1)}, f32[16,128]{1,0:T(8,128)S(1)}) custom-call(f32[16]{0:T(128)S(1)} %copy-done.3, f32[2,8]{1,0:T(2,128)S(1)} %bitcast.4, bf16[8,128,256]{2,1,0:T(8,128)(2,1)S(1)} %copy-done, bf16[8,256,128]{2,1,0:T(8,128)(2,1)S(1)} %copy-done.1), custom_call_target="tpu_custom_call" | custom-call | flops 524288000 | bytes 2097152 | tf_op jit(solution)/shard_map/pallas_call | solution.py:346
  30.3 1.1 %collective-permute-done.4.z_came = bf16[5,16,256]{2,1,0:T(8,128)(2,1)S(1)} collective-permute-done((bf16[5,16,256]{2,1,0:T(8,128)(2,1)S(1)}, bf16[5,16,256]{2,1,0:T(8,128)(2,1)S(1)}, u32[]{:S(2)}, u32[]{:S(2)}) %collective-permute-start.4) | collective-permute-done | bytes 40992 | tf_op jit(solution)/shard_map/ppermute | solution.py:492
  31.4 0.0 collective-permute-done.5.refs_0_
  31.4 0.0 collective-permute-done.6.refs_1_
  31.4 0.0 collective-permute-done.7.refs_2_
  31.4 1.3 %shard_map.103 = f32[16,32,128]{2,1,0:T(8,128)} custom-call(bf16[128,2048]{1,0:T(8,128)(2,1)S(1)} %get-tuple-element.20.high_ref, bf16[128,2048]{1,0:T(8,128)(2,1)S(1)} %get-tuple-element.21.low_ref, f32[16,128]{1,0:T(8,128)S(1)} %get-tuple-element.22.share_ref, f32[12,16,256]{2,1,0:T(8,128)S(1)} %get-tuple-element.29.x_own, ...), custom_call_target="tpu_custom_call" | custom-call | flops 262144 | bytes 2097152 | tf_op jit(solution)/shard_map/pallas_call | solution.py:435
Async XLA Ops:
  0.0 28.2 %copy-start = (bf16[8,128,256]{2,1,0:T(8,128)(2,1)S(1)}, bf16[8,128,256]{2,1,0:T(8,128)(2,1)}, u32[]{:S(2)}) copy-start(bf16[8,128,256]{2,1,0:T(8,128)(2,1)} %rows_hbm.3) | copy-start | bytes 1572868
  0.0 28.2 %copy-start.1 = (bf16[8,256,128]{2,1,0:T(8,128)(2,1)S(1)}, bf16[8,256,128]{2,1,0:T(8,128)(2,1)}, u32[]{:S(2)}) copy-start(bf16[8,256,128]{2,1,0:T(8,128)(2,1)} %cols_hbm.3) | copy-start | bytes 1572868
  0.0 28.2 %copy-start.2 = (f32[8,2]{0,1:T(2,128)S(1)}, f32[8,2]{0,1:T(2,128)}, u32[]{:S(2)}) copy-start(f32[8,2]{0,1:T(2,128)} %param.17) | copy-start | bytes 196
  0.0 28.2 %copy-start.3 = (f32[16]{0:T(128)S(1)}, f32[16]{0:T(128)}, u32[]{:S(2)}) copy-start(f32[16]{0:T(128)} %defocus_hbm.3) | copy-start | bytes 196
  7.7 12.6 %collective-permute-start = (bf16[4,12,16,256]{3,2,1,0:T(8,128)(2,1)S(1)}, bf16[4,12,16,256]{3,2,1,0:T(8,128)(2,1)S(1)}, u32[]{:S(2)}, u32[]{:S(2)}) collective-permute-start(bf16[4,12,16,256]{3,2,1,0:T(8,128)(2,1)S(1)} %get-tuple-element.25), channel_id=1, source_target_pairs={{0,2},{2,0},{4,6},{6,4},{8,10},{10,8},{12,14},{14,12},{1,3},{3,1},... | collective-permute-start | bytes 1179656 | tf_op jit(solution)/shard_map/ppermute | solution.py:492
  10.8 7.9 %collective-permute-start.1 = (bf16[2,5,16,256]{3,2,1,0:T(8,128)(2,1)S(1)}, bf16[2,5,16,256]{3,2,1,0:T(8,128)(2,1)S(1)}, u32[]{:S(2)}, u32[]{:S(2)}) collective-permute-start(bf16[2,5,16,256]{3,2,1,0:T(8,128)(2,1)S(1)} %get-tuple-element.26), channel_id=1, source_target_pairs={{0,8},{2,10},{4,12},{6,14},{8,0},{10,2},{12,4},{14,6},{1,9},{3,11}... | collective-permute-start | bytes 245768 | tf_op jit(solution)/shard_map/ppermute | solution.py:495
  13.3 6.6 %collective-permute-start.2 = (bf16[2,5,16,256]{3,2,1,0:T(8,128)(2,1)S(1)}, bf16[2,5,16,256]{3,2,1,0:T(8,128)(2,1)S(1)}, u32[]{:S(2)}, u32[]{:S(2)}) collective-permute-start(bf16[2,5,16,256]{3,2,1,0:T(8,128)(2,1)S(1)} %get-tuple-element.27), channel_id=1, source_target_pairs={{0,4},{2,6},{4,8},{6,10},{8,12},{10,14},{12,0},{14,2},{1,5},{3,7},... | collective-permute-start | bytes 245768 | tf_op jit(solution)/shard_map/ppermute | solution.py:495
  14.9 5.4 %collective-permute-start.3 = (bf16[2,5,16,256]{3,2,1,0:T(8,128)(2,1)S(1)}, bf16[2,5,16,256]{3,2,1,0:T(8,128)(2,1)S(1)}, u32[]{:S(2)}, u32[]{:S(2)}) collective-permute-start(bf16[2,5,16,256]{3,2,1,0:T(8,128)(2,1)S(1)} %get-tuple-element.28), channel_id=1, source_target_pairs={{0,12},{2,14},{4,0},{6,2},{8,4},{10,6},{12,8},{14,10},{1,13},{3,15... | collective-permute-start | bytes 245768 | tf_op jit(solution)/shard_map/ppermute | solution.py:495
  20.4 11.0 %collective-permute-start.5 = (bf16[12,16,256]{2,1,0:T(8,128)(2,1)S(1)}, bf16[12,16,256]{2,1,0:T(8,128)(2,1)S(1)}, u32[]{:S(2)}, u32[]{:S(2)}) collective-permute-start(bf16[12,16,256]{2,1,0:T(8,128)(2,1)S(1)} %get-tuple-element.32), channel_id=1, source_target_pairs={{0,8},{2,10},{4,12},{6,14},{8,0},{10,2},{12,4},{14,6},{1,9},{3,11}... | collective-permute-start | bytes 294920 | tf_op jit(solution)/shard_map/ppermute | solution.py:495
  23.6 7.8 %collective-permute-start.6 = (bf16[12,16,256]{2,1,0:T(8,128)(2,1)S(1)}, bf16[12,16,256]{2,1,0:T(8,128)(2,1)S(1)}, u32[]{:S(2)}, u32[]{:S(2)}) collective-permute-start(bf16[12,16,256]{2,1,0:T(8,128)(2,1)S(1)} %get-tuple-element.33), channel_id=1, source_target_pairs={{0,4},{2,6},{4,8},{6,10},{8,12},{10,14},{12,0},{14,2},{1,5},{3,7},... | collective-permute-start | bytes 294920 | tf_op jit(solution)/shard_map/ppermute | solution.py:495
  24.5 7.0 %collective-permute-start.7 = (bf16[12,16,256]{2,1,0:T(8,128)(2,1)S(1)}, bf16[12,16,256]{2,1,0:T(8,128)(2,1)S(1)}, u32[]{:S(2)}, u32[]{:S(2)}) collective-permute-start(bf16[12,16,256]{2,1,0:T(8,128)(2,1)S(1)} %get-tuple-element.34), channel_id=1, source_target_pairs={{0,12},{2,14},{4,0},{6,2},{8,4},{10,6},{12,8},{14,10},{1,13},{3,15... | collective-permute-start | bytes 294920 | tf_op jit(solution)/shard_map/ppermute | solution.py:495
  27.4 4.0 %collective-permute-start.4 = (bf16[5,16,256]{2,1,0:T(8,128)(2,1)S(1)}, bf16[5,16,256]{2,1,0:T(8,128)(2,1)S(1)}, u32[]{:S(2)}, u32[]{:S(2)}) collective-permute-start(bf16[5,16,256]{2,1,0:T(8,128)(2,1)S(1)} %get-tuple-element.31), channel_id=1, source_target_pairs={{0,2},{2,0},{4,6},{6,4},{8,10},{10,8},{12,14},{14,12},{1,3},{3,1},... | collective-permute-start | bytes 122888 | tf_op jit(solution)/shard_map/ppermute | solution.py:492

commit v5 on v4

--- a/solution.py
+++ b/solution.py
@@ -497,10 +497,11 @@
     order = sorted(range(1, rounds), key=lambda k: -min(k, rounds - k))
     x_came = along_x(x_send)
     z_came = [along_z(z_sends[k], k) for k in order]
+    tables = own_ridges(defocus, plane_weight, rows_table, cols_table, owned)
+    x_keep, tables = lax.optimization_barrier((x_keep, tables))
     x_own, z_own, z_send, *x_sends = middle(x_keep, z_keep, x_came, z_came)
     x_came = [along_z(x_sends[k - 1], k) for k in order]
     z_came = along_x(z_send)
-    tables = own_ridges(defocus, plane_weight, rows_table, cols_table, owned)
     out = finish(tables, x_own, z_own, z_came, x_came)
     return out.reshape(owned, CLASSES, planes, 2, cols)
 

time: 32.8 us -> 32.9 us (level)
    ppermute x6, waiting for transfers between devices: 3.16 us -> 1.04 us  [along_z(): lax.ppermute(value, 'img', [(i, (i + 2 * k) % members) for i in range(mem...]
    ppermute x2, waiting for transfers between devices: 1.11 us -> 3.23 us  [along_x(): return lax.ppermute(value, 'img', [(i, i ^ 1) for i in range(members)])]
  transfers between devices with their start and end apart: 8 -> 8, of which waited for: 4 -> 3; matrix products, arithmetic and copies ran while one was open for 0% -> 0% of each run, Pallas kernels for 6% -> 6%
where the time goes in v5:
time: 32.9 us; the launch traced here: 32.7 us
  starting transfers between devices  17.2 us (52%)
  Pallas kernels  11.2 us (34%)
  waiting for transfers between devices  4.27 us (13%)
    ppermute x6, starting transfers between devices, along_z(): lax.ppermute(value, 'img', [(i, (i + 2 * k) % members) for i in range(mem...  13.4 us
    pallas_call x1, Pallas kernels, own_totals(): pl.pallas_call(slices_kernel, out_shape=out_shape, in_specs=[any_place] *...  7.72 us
    ppermute x2, starting transfers between devices, along_x(): return lax.ppermute(value, 'img', [(i, i ^ 1) for i in range(members)])  3.8 us
    ppermute x2, waiting for transfers between devices, along_x(): return lax.ppermute(value, 'img', [(i, i ^ 1) for i in range(members)])  3.23 us
    pallas_call x1, Pallas kernels, own_ridges(): pl.pallas_call(ridge_kernel, out_shape=[table, table, jax.ShapeDtypeStruc...  2.09 us
    pallas_call x1, Pallas kernels, finish(): pl.pallas_call(finish_kernel, out_shape=jax.ShapeDtypeStruct((owned, 2 *...  1.25 us
    ppermute x6, waiting for transfers between devices, along_z(): lax.ppermute(value, 'img', [(i, (i + 2 * k) % members) for i in range(mem...  1.04 us
  transfers between devices with their start and end apart: 8, of which 3 were waited for; matrix products, arithmetic and copies ran while one was open for 0% of the time, Pallas kernels for 6%

profile of v5, /device:TPU:0, one launch (start us, length us, event | category | flops | bytes accessed | tf_op | source)
XLA Modules:
  0.0 32.7 jit_solution(14258409058689630614)
XLA Ops:
  0.0 0.0 copy-start
  0.0 0.0 copy-start.1
  0.0 0.0 copy-start.2
  0.0 0.0 copy-start.3
  0.0 7.7 %shard_map.100 = (bf16[4,12,16,256]{3,2,1,0:T(8,128)(2,1)S(1)}, f32[4,12,16,256]{3,2,1,0:T(8,128)S(1)}, f32[2,5,16,256]{3,2,1,0:T(8,128)S(1)}, bf16[2,5,16,256]{...) custom-call(s32[16]{0:T(128)} %bitcast.5, s32[16]{0:T(128)} %pose_hbm.1, ...), custom_call_target="tpu_custom_call" | custom-call | flops 2097152000 | bytes 6291456 | tf_op jit(solution)/shard_map/pallas_call | solution.py:253
  7.7 3.0 %collective-permute-start = (bf16[4,12,16,256]{3,2,1,0:T(8,128)(2,1)S(1)}, bf16[4,12,16,256]{3,2,1,0:T(8,128)(2,1)S(1)}, u32[]{:S(2)}, u32[]{:S(2)}) collective-permute-start(bf16[4,12,16,256]{3,2,1,0:T(8,128)(2,1)S(1)} %get-tuple-element.33), channel_id=1, source_target_pairs={{0,2},{2,0},{4,6},{6,4},{8,10},{10,8},{12,14},{14,12},{1,3},{3,1},... | collective-permute-start | bytes 1179656 | tf_op jit(solution)/shard_map/ppermute | solution.py:492
  10.8 2.6 %collective-permute-start.1 = (bf16[2,5,16,256]{3,2,1,0:T(8,128)(2,1)S(1)}, bf16[2,5,16,256]{3,2,1,0:T(8,128)(2,1)S(1)}, u32[]{:S(2)}, u32[]{:S(2)}) collective-permute-start(bf16[2,5,16,256]{3,2,1,0:T(8,128)(2,1)S(1)} %get-tuple-element.34), channel_id=1, source_target_pairs={{0,8},{2,10},{4,12},{6,14},{8,0},{10,2},{12,4},{14,6},{1,9},{3,11}... | collective-permute-start | bytes 245768 | tf_op jit(solution)/shard_map/ppermute | solution.py:495
  13.3 1.6 %collective-permute-start.2 = (bf16[2,5,16,256]{3,2,1,0:T(8,128)(2,1)S(1)}, bf16[2,5,16,256]{3,2,1,0:T(8,128)(2,1)S(1)}, u32[]{:S(2)}, u32[]{:S(2)}) collective-permute-start(bf16[2,5,16,256]{3,2,1,0:T(8,128)(2,1)S(1)} %get-tuple-element.35), channel_id=1, source_target_pairs={{0,4},{2,6},{4,8},{6,10},{8,12},{10,14},{12,0},{14,2},{1,5},{3,7},... | collective-permute-start | bytes 245768 | tf_op jit(solution)/shard_map/ppermute | solution.py:495
  14.9 2.2 %collective-permute-start.3 = (bf16[2,5,16,256]{3,2,1,0:T(8,128)(2,1)S(1)}, bf16[2,5,16,256]{3,2,1,0:T(8,128)(2,1)S(1)}, u32[]{:S(2)}, u32[]{:S(2)}) collective-permute-start(bf16[2,5,16,256]{3,2,1,0:T(8,128)(2,1)S(1)} %get-tuple-element.36), channel_id=1, source_target_pairs={{0,12},{2,14},{4,0},{6,2},{8,4},{10,6},{12,8},{14,10},{1,13},{3,15... | collective-permute-start | bytes 245768 | tf_op jit(solution)/shard_map/ppermute | solution.py:495
  17.2 0.0 copy-done
  17.2 0.0 copy-done.1
  17.2 0.0 copy-done.2
  17.2 0.0 copy-done.3
  17.2 2.1 %shard_map.101 = (bf16[128,2048]{1,0:T(8,128)(2,1)S(1)}, bf16[128,2048]{1,0:T(8,128)(2,1)S(1)}, f32[16,128]{1,0:T(8,128)S(1)}) custom-call(f32[16]{0:T(128)S(1)} %copy-done.3, f32[2,8]{1,0:T(2,128)S(1)} %bitcast.4, bf16[8,128,256]{2,1,0:T(8,128)(2,1)S(1)} %copy-done, bf16[8,256,128]{2,1,0:T(8,128)(2,1)S(1)} %copy-done.1), custom_call_target="tpu_custom_call" | custom-call | flops 524288000 | bytes 2097152 | tf_op jit(solution)/shard_map/pallas_call | solution.py:346
  19.3 0.0 collective-permute-done.1.refs_0_
  19.3 0.6 %collective-permute-done.2.refs_1_ = bf16[2,5,16,256]{3,2,1,0:T(8,128)(2,1)S(1)} collective-permute-done((bf16[2,5,16,256]{3,2,1,0:T(8,128)(2,1)S(1)}, bf16[2,5,16,256]{3,2,1,0:T(8,128)(2,1)S(1)}, u32[]{:S(2)}, u32[]{:S(2)}) %collective-permute-start.2) | collective-permute-done | bytes 81952 | tf_op jit(solution)/shard_map/ppermute | solution.py:495
  19.9 0.4 %collective-permute-done.3.refs_2_ = bf16[2,5,16,256]{3,2,1,0:T(8,128)(2,1)S(1)} collective-permute-done((bf16[2,5,16,256]{3,2,1,0:T(8,128)(2,1)S(1)}, bf16[2,5,16,256]{3,2,1,0:T(8,128)(2,1)S(1)}, u32[]{:S(2)}, u32[]{:S(2)}) %collective-permute-start.3) | collective-permute-done | bytes 81952 | tf_op jit(solution)/shard_map/ppermute | solution.py:495
  20.3 0.0 collective-permute-done.x_came
  20.3 0.1 shard_map.102
  20.5 3.2 %collective-permute-start.5 = (bf16[12,16,256]{2,1,0:T(8,128)(2,1)S(1)}, bf16[12,16,256]{2,1,0:T(8,128)(2,1)S(1)}, u32[]{:S(2)}, u32[]{:S(2)}) collective-permute-start(bf16[12,16,256]{2,1,0:T(8,128)(2,1)S(1)} %get-tuple-element.40), channel_id=1, source_target_pairs={{0,8},{2,10},{4,12},{6,14},{8,0},{10,2},{12,4},{14,6},{1,9},{3,11}... | collective-permute-start | bytes 294920 | tf_op jit(solution)/shard_map/ppermute | solution.py:495
  23.6 0.9 %collective-permute-start.6 = (bf16[12,16,256]{2,1,0:T(8,128)(2,1)S(1)}, bf16[12,16,256]{2,1,0:T(8,128)(2,1)S(1)}, u32[]{:S(2)}, u32[]{:S(2)}) collective-permute-start(bf16[12,16,256]{2,1,0:T(8,128)(2,1)S(1)} %get-tuple-element.41), channel_id=1, source_target_pairs={{0,4},{2,6},{4,8},{6,10},{8,12},{10,14},{12,0},{14,2},{1,5},{3,7},... | collective-permute-start | bytes 294920 | tf_op jit(solution)/shard_map/ppermute | solution.py:495
  24.5 3.0 %collective-permute-start.7 = (bf16[12,16,256]{2,1,0:T(8,128)(2,1)S(1)}, bf16[12,16,256]{2,1,0:T(8,128)(2,1)S(1)}, u32[]{:S(2)}, u32[]{:S(2)}) collective-permute-start(bf16[12,16,256]{2,1,0:T(8,128)(2,1)S(1)} %get-tuple-element.42), channel_id=1, source_target_pairs={{0,12},{2,14},{4,0},{6,2},{8,4},{10,6},{12,8},{14,10},{1,13},{3,15... | collective-permute-start | bytes 294920 | tf_op jit(solution)/shard_map/ppermute | solution.py:495
  27.4 0.8 %collective-permute-start.4 = (bf16[5,16,256]{2,1,0:T(8,128)(2,1)S(1)}, bf16[5,16,256]{2,1,0:T(8,128)(2,1)S(1)}, u32[]{:S(2)}, u32[]{:S(2)}) collective-permute-start(bf16[5,16,256]{2,1,0:T(8,128)(2,1)S(1)} %get-tuple-element.39), channel_id=1, source_target_pairs={{0,2},{2,0},{4,6},{6,4},{8,10},{10,8},{12,14},{14,12},{1,3},{3,1},... | collective-permute-start | bytes 122888 | tf_op jit(solution)/shard_map/ppermute | solution.py:492
  28.2 3.2 %collective-permute-done.4.z_came = bf16[5,16,256]{2,1,0:T(8,128)(2,1)S(1)} collective-permute-done((bf16[5,16,256]{2,1,0:T(8,128)(2,1)S(1)}, bf16[5,16,256]{2,1,0:T(8,128)(2,1)S(1)}, u32[]{:S(2)}, u32[]{:S(2)}) %collective-permute-start.4) | collective-permute-done | bytes 40992 | tf_op jit(solution)/shard_map/ppermute | solution.py:492
  31.4 0.0 collective-permute-done.5.refs_0_
  31.5 0.0 collective-permute-done.6.refs_1_
  31.5 0.0 collective-permute-done.7.refs_2_
  31.5 1.3 %shard_map.103 = f32[16,32,128]{2,1,0:T(8,128)} custom-call(bf16[128,2048]{1,0:T(8,128)(2,1)S(1)} %get-tuple-element.28.high_ref, bf16[128,2048]{1,0:T(8,128)(2,1)S(1)} %get-tuple-element.29.low_ref, f32[16,128]{1,0:T(8,128)S(1)} %get-tuple-element.30.share_ref, f32[12,16,256]{2,1,0:T(8,128)S(1)} %get-tuple-element.37.x_own, ...), custom_call_target="tpu_custom_call" | custom-call | flops 262144 | bytes 2097152 | tf_op jit(solution)/shard_map/pallas_call | solution.py:435
Async XLA Ops:
  0.0 17.2 %copy-start = (bf16[8,128,256]{2,1,0:T(8,128)(2,1)S(1)}, bf16[8,128,256]{2,1,0:T(8,128)(2,1)}, u32[]{:S(2)}) copy-start(bf16[8,128,256]{2,1,0:T(8,128)(2,1)} %rows_hbm.3) | copy-start | bytes 1572868
  0.0 17.2 %copy-start.1 = (bf16[8,256,128]{2,1,0:T(8,128)(2,1)S(1)}, bf16[8,256,128]{2,1,0:T(8,128)(2,1)}, u32[]{:S(2)}) copy-start(bf16[8,256,128]{2,1,0:T(8,128)(2,1)} %cols_hbm.3) | copy-start | bytes 1572868
  0.0 17.2 %copy-start.2 = (f32[8,2]{0,1:T(2,128)S(1)}, f32[8,2]{0,1:T(2,128)}, u32[]{:S(2)}) copy-start(f32[8,2]{0,1:T(2,128)} %param.17) | copy-start | bytes 196
  0.0 17.2 %copy-start.3 = (f32[16]{0:T(128)S(1)}, f32[16]{0:T(128)}, u32[]{:S(2)}) copy-start(f32[16]{0:T(128)} %defocus_hbm.3) | copy-start | bytes 196
  7.7 12.6 %collective-permute-start = (bf16[4,12,16,256]{3,2,1,0:T(8,128)(2,1)S(1)}, bf16[4,12,16,256]{3,2,1,0:T(8,128)(2,1)S(1)}, u32[]{:S(2)}, u32[]{:S(2)}) collective-permute-start(bf16[4,12,16,256]{3,2,1,0:T(8,128)(2,1)S(1)} %get-tuple-element.33), channel_id=1, source_target_pairs={{0,2},{2,0},{4,6},{6,4},{8,10},{10,8},{12,14},{14,12},{1,3},{3,1},... | collective-permute-start | bytes 1179656 | tf_op jit(solution)/shard_map/ppermute | solution.py:492
  10.8 8.5 %collective-permute-start.1 = (bf16[2,5,16,256]{3,2,1,0:T(8,128)(2,1)S(1)}, bf16[2,5,16,256]{3,2,1,0:T(8,128)(2,1)S(1)}, u32[]{:S(2)}, u32[]{:S(2)}) collective-permute-start(bf16[2,5,16,256]{3,2,1,0:T(8,128)(2,1)S(1)} %get-tuple-element.34), channel_id=1, source_target_pairs={{0,8},{2,10},{4,12},{6,14},{8,0},{10,2},{12,4},{14,6},{1,9},{3,11}... | collective-permute-start | bytes 245768 | tf_op jit(solution)/shard_map/ppermute | solution.py:495
  13.3 6.6 %collective-permute-start.2 = (bf16[2,5,16,256]{3,2,1,0:T(8,128)(2,1)S(1)}, bf16[2,5,16,256]{3,2,1,0:T(8,128)(2,1)S(1)}, u32[]{:S(2)}, u32[]{:S(2)}) collective-permute-start(bf16[2,5,16,256]{3,2,1,0:T(8,128)(2,1)S(1)} %get-tuple-element.35), channel_id=1, source_target_pairs={{0,4},{2,6},{4,8},{6,10},{8,12},{10,14},{12,0},{14,2},{1,5},{3,7},... | collective-permute-start | bytes 245768 | tf_op jit(solution)/shard_map/ppermute | solution.py:495
  14.9 5.4 %collective-permute-start.3 = (bf16[2,5,16,256]{3,2,1,0:T(8,128)(2,1)S(1)}, bf16[2,5,16,256]{3,2,1,0:T(8,128)(2,1)S(1)}, u32[]{:S(2)}, u32[]{:S(2)}) collective-permute-start(bf16[2,5,16,256]{3,2,1,0:T(8,128)(2,1)S(1)} %get-tuple-element.36), channel_id=1, source_target_pairs={{0,12},{2,14},{4,0},{6,2},{8,4},{10,6},{12,8},{14,10},{1,13},{3,15... | collective-permute-start | bytes 245768 | tf_op jit(solution)/shard_map/ppermute | solution.py:495
  20.5 11.0 %collective-permute-start.5 = (bf16[12,16,256]{2,1,0:T(8,128)(2,1)S(1)}, bf16[12,16,256]{2,1,0:T(8,128)(2,1)S(1)}, u32[]{:S(2)}, u32[]{:S(2)}) collective-permute-start(bf16[12,16,256]{2,1,0:T(8,128)(2,1)S(1)} %get-tuple-element.40), channel_id=1, source_target_pairs={{0,8},{2,10},{4,12},{6,14},{8,0},{10,2},{12,4},{14,6},{1,9},{3,11}... | collective-permute-start | bytes 294920 | tf_op jit(solution)/shard_map/ppermute | solution.py:495
  23.6 7.8 %collective-permute-start.6 = (bf16[12,16,256]{2,1,0:T(8,128)(2,1)S(1)}, bf16[12,16,256]{2,1,0:T(8,128)(2,1)S(1)}, u32[]{:S(2)}, u32[]{:S(2)}) collective-permute-start(bf16[12,16,256]{2,1,0:T(8,128)(2,1)S(1)} %get-tuple-element.41), channel_id=1, source_target_pairs={{0,4},{2,6},{4,8},{6,10},{8,12},{10,14},{12,0},{14,2},{1,5},{3,7},... | collective-permute-start | bytes 294920 | tf_op jit(solution)/shard_map/ppermute | solution.py:495
  24.5 7.0 %collective-permute-start.7 = (bf16[12,16,256]{2,1,0:T(8,128)(2,1)S(1)}, bf16[12,16,256]{2,1,0:T(8,128)(2,1)S(1)}, u32[]{:S(2)}, u32[]{:S(2)}) collective-permute-start(bf16[12,16,256]{2,1,0:T(8,128)(2,1)S(1)} %get-tuple-element.42), channel_id=1, source_target_pairs={{0,12},{2,14},{4,0},{6,2},{8,4},{10,6},{12,8},{14,10},{1,13},{3,15... | collective-permute-start | bytes 294920 | tf_op jit(solution)/shard_map/ppermute | solution.py:495
  27.4 4.0 %collective-permute-start.4 = (bf16[5,16,256]{2,1,0:T(8,128)(2,1)S(1)}, bf16[5,16,256]{2,1,0:T(8,128)(2,1)S(1)}, u32[]{:S(2)}, u32[]{:S(2)}) collective-permute-start(bf16[5,16,256]{2,1,0:T(8,128)(2,1)S(1)} %get-tuple-element.39), channel_id=1, source_target_pairs={{0,2},{2,0},{4,6},{6,4},{8,10},{10,8},{12,14},{14,12},{1,3},{3,1},... | collective-permute-start | bytes 122888 | tf_op jit(solution)/shard_map/ppermute | solution.py:492

commit v6 on v5

--- a/solution.py
+++ b/solution.py
@@ -203,8 +203,7 @@
     if len(outs) == 1:
         outs[0][...] = totals[...].astype(bf16)
         return
-    x_send, x_keep, z_keep = outs[:3]
-    z_sends = outs[3:]
+    x_send, x_keep, z_keep, z_send = outs
     rounds, x_slots, owned, _ = x_keep.shape
     me = lax.axis_index("img")
     side = lax.rem(me, 2)
@@ -214,12 +213,14 @@
         theirs = pl.ds(pl.multiple_of((base + 1 - side) * owned, owned), owned)
         x_keep[k] = totals[-x_slots:, mine, :]
         x_send[k] = totals[-x_slots:, theirs, :].astype(bf16)
+        layer = lax.div(base, 2)
         if k == 0:
             z_keep[0] = totals[:-x_slots, mine, :]
             z_keep[1] = totals[:-x_slots, theirs, :]
+            z_send[layer] = jnp.zeros_like(z_send[0])
         else:
-            z_sends[k - 1][0] = totals[:-x_slots, mine, :].astype(bf16)
-            z_sends[k - 1][1] = totals[:-x_slots, theirs, :].astype(bf16)
+            z_send[layer, 0] = totals[:-x_slots, mine, :].astype(bf16)
+            z_send[layer, 1] = totals[:-x_slots, theirs, :].astype(bf16)
 
 
 SCRATCH = 19
@@ -244,7 +245,7 @@
         x_piece = (turns_round, slots - Z_SLOTS, rows // (2 * turns_round), 2 * cols)
         z_piece = (2, Z_SLOTS, rows // (2 * turns_round), 2 * cols)
         out_shape = [pltpu.VMEM(x_piece, bf16), pltpu.VMEM(x_piece, f32), pltpu.VMEM(z_piece, f32)]
-        out_shape += [pltpu.VMEM(z_piece, bf16)] * (turns_round - 1)
+        out_shape += [pltpu.VMEM((turns_round,) + z_piece, bf16)]
     operands = (
         class_index[:, 0], pose_index, defocus_bin, defocus, plane_weight.T,
         jnp.asarray(table_y, bf16), jnp.asarray(table_x.T.copy(), bf16),
@@ -362,17 +363,17 @@
     )(defocus, planes, rows_table, cols_table)
 
 
-def middle_kernel(x_keep, z_keep, x_came, *refs):
+def middle_kernel(x_keep, z_keep, x_came, z_came, x_own, z_own, z_send, x_send):
     rounds = x_keep.shape[0]
-    z_came, outs = refs[: rounds - 1], refs[rounds - 1 :]
-    x_own, z_own, z_send = outs[:3]
+    layer = lax.div(lax.axis_index("img"), 2)
     x_own[...] = x_keep[0] + x_came[0].astype(f32)
+    x_send[layer] = jnp.zeros_like(x_send[0])
     for k in range(1, rounds):
-        outs[2 + k][...] = (x_keep[k] + x_came[k].astype(f32)).astype(bf16)
+        x_send[lax.rem(layer + k, rounds)] = (x_keep[k] + x_came[k].astype(f32)).astype(bf16)
     for side in range(2):
         value = z_keep[side]
-        for came in z_came:
-            value = value + came[side].astype(f32)
+        for k in range(rounds):
+            value = value + z_came[k, side].astype(f32)
         if side == 0:
             z_own[...] = value
         else:
@@ -380,23 +381,21 @@
 
 
 def middle(x_keep, z_keep, x_came, z_came):
-    rounds, x_slots, owned, wide = x_keep.shape
     vmem = pl.BlockSpec(memory_space=pltpu.VMEM)
     x_piece, z_piece = x_keep.shape[1:], z_keep.shape[1:]
     out_shape = [pltpu.VMEM(x_piece, f32), pltpu.VMEM(z_piece, f32), pltpu.VMEM(z_piece, bf16)]
-    out_shape += [pltpu.VMEM(x_piece, bf16)] * (rounds - 1)
+    out_shape += [pltpu.VMEM(x_keep.shape, bf16)]
     return pl.pallas_call(
         middle_kernel,
         out_shape=out_shape,
-        in_specs=[vmem] * (3 + len(z_came)),
-        out_specs=[vmem] * len(out_shape),
+        in_specs=[vmem] * 4,
+        out_specs=[vmem] * 4,
         compiler_params=pltpu.CompilerParams(vmem_limit_bytes=16 * 1024 * 1024),
         cost_estimate=pl.CostEstimate(flops=1000000, bytes_accessed=4 * 1024 * 1024, transcendentals=0),
-    )(x_keep, z_keep, x_came, *z_came)
-
-
-def finish_kernel(high_ref, low_ref, share_ref, x_own, z_own, z_came, *refs):
-    x_came, out_ref, ridge_ref = refs[:-2], refs[-2], refs[-1]
+    )(x_keep, z_keep, x_came, z_came)
+
+
+def finish_kernel(high_ref, low_ref, share_ref, x_own, z_own, z_came, x_came, out_ref, ridge_ref):
     slots, pairs = share_ref.shape
     owned, _, cols = ridge_ref.shape
     planes = slots // CLASSES
@@ -406,8 +405,8 @@
         if s < first:
             return z_own[s] + z_came[s].astype(f32)
         value = x_own[s - first]
-        for part in x_came:
-            value = value + part[s - first].astype(f32)
+        for k in range(x_came.shape[0]):
+            value = value + x_came[k, s - first].astype(f32)
         return value
 
     counts = summed(slots)[:CLASSES, :pairs]
@@ -435,14 +434,14 @@
     return pl.pallas_call(
         finish_kernel,
         out_shape=jax.ShapeDtypeStruct((owned, 2 * slots, cols), f32),
-        in_specs=[vmem] * (6 + len(x_came)),
+        in_specs=[vmem] * 7,
         out_specs=vmem,
         scratch_shapes=[pltpu.VMEM((owned, slots, cols), f32)],
         compiler_params=pltpu.CompilerParams(vmem_limit_bytes=16 * 1024 * 1024),
         cost_estimate=pl.CostEstimate(
             flops=8 * slots * owned * cols, bytes_accessed=8 * 1024 * 1024 // 4, transcendentals=0
         ),
-    )(*tables, x_own, z_own, z_came, *x_came)
+    )(*tables, x_own, z_own, z_came, x_came)
 
 
 def squared_table(weight_table):
@@ -485,23 +484,22 @@
     outs = own_totals(
         images, class_index, pose_index, defocus_bin, defocus, rows_table, cols_table, plane_weight, rounds
     )
-    x_send, x_keep, z_keep = outs[:3]
-    z_sends = dict(zip(range(1, rounds), outs[3:]))
+    x_send, x_keep, z_keep, z_send = outs
+    lines = [[2 * i + side for i in range(rounds)] for side in range(2)]
 
     def along_x(value):
         return lax.ppermute(value, "img", [(i, i ^ 1) for i in range(members)])
 
-    def along_z(value, k):
-        return lax.ppermute(value, "img", [(i, (i + 2 * k) % members) for i in range(members)])
-
-    order = sorted(range(1, rounds), key=lambda k: -min(k, rounds - k))
+    def along_z(value):
+        return lax.all_to_all(value, "img", 0, 0, axis_index_groups=lines, tiled=True)
+
     x_came = along_x(x_send)
-    z_came = [along_z(z_sends[k], k) for k in order]
+    z_came = along_z(z_send)
     tables = own_ridges(defocus, plane_weight, rows_table, cols_table, owned)
     x_keep, tables = lax.optimization_barrier((x_keep, tables))
-    x_own, z_own, z_send, *x_sends = middle(x_keep, z_keep, x_came, z_came)
-    x_came = [along_z(x_sends[k - 1], k) for k in order]
+    x_own, z_own, z_send, x_send = middle(x_keep, z_keep, x_came, z_came)
     z_came = along_x(z_send)
+    x_came = along_z(x_send)
     out = finish(tables, x_own, z_own, z_came, x_came)
     return out.reshape(owned, CLASSES, planes, 2, cols)
 

time: 32.9 us -> 43.1 us (1.31)
  waiting for transfers between devices: 4.27 us -> 14.9 us
  starting transfers between devices: 17.2 us -> 14.1 us
  Pallas kernels: 11.2 us -> 12.7 us
  local copies, waits for them, and re-layouts: 0.01 us -> 1.05 us
    ppermute x6 -> x0, starting transfers between devices: 13.4 us -> none  [along_z(): lax.ppermute(value, 'img', [(i, (i + 2 * k) % members) for i in range(mem...]
    all_to_all x0 -> x2, starting transfers between devices: none -> 11.1 us  [along_z(): lax.all_to_all(value, 'img', 0, 0, axis_index_groups=lines, tiled=True)]
    all_to_all x0 -> x2, waiting for transfers between devices: none -> 6.2 us  [along_z(): lax.all_to_all(value, 'img', 0, 0, axis_index_groups=lines, tiled=True)]
    ppermute x2, waiting for transfers between devices: 3.23 us -> 8.66 us  [along_x(): return lax.ppermute(value, 'img', [(i, i ^ 1) for i in range(members)])]
    ppermute x6 -> x0, waiting for transfers between devices: 1.04 us -> none  [along_z(): lax.ppermute(value, 'img', [(i, (i + 2 * k) % members) for i in range(mem...]
    unnamed x8, local copies, waits for them, and re-layouts: 0.01 us -> 1.05 us
    pallas_call x1, Pallas kernels: 7.72 us -> 8.56 us  [own_totals(): pl.pallas_call(slices_kernel, out_shape=out_shape, in_specs=[any_place] *...]
    ppermute x2, starting transfers between devices: 3.8 us -> 2.98 us  [along_x(): return lax.ppermute(value, 'img', [(i, i ^ 1) for i in range(members)])]
  transfers between devices with their start and end apart: 8 -> 4, of which waited for: 3 -> 3; matrix products, arithmetic and copies ran while one was open for 0% -> 0% of each run, Pallas kernels for 6% -> 5%
where the time goes in v6:
time: 43.1 us; the launch traced here: 42.8 us
  waiting for transfers between devices  14.9 us (35%)
  starting transfers between devices  14.1 us (33%)
  Pallas kernels  12.7 us (29%)
  local copies, waits for them, and re-layouts  1.05 us (2%)
    all_to_all x2, starting transfers between devices, along_z(): lax.all_to_all(value, 'img', 0, 0, axis_index_groups=lines, tiled=True)  11.1 us
    ppermute x2, waiting for transfers between devices, along_x(): return lax.ppermute(value, 'img', [(i, i ^ 1) for i in range(members)])  8.66 us
    pallas_call x1, Pallas kernels, own_totals(): pl.pallas_call(slices_kernel, out_shape=out_shape, in_specs=[any_place] *...  8.56 us
    all_to_all x2, waiting for transfers between devices, along_z(): lax.all_to_all(value, 'img', 0, 0, axis_index_groups=lines, tiled=True)  6.2 us
    ppermute x2, starting transfers between devices, along_x(): return lax.ppermute(value, 'img', [(i, i ^ 1) for i in range(members)])  2.98 us
    pallas_call x1, Pallas kernels, own_ridges(): pl.pallas_call(ridge_kernel, out_shape=[table, table, jax.ShapeDtypeStruc...  2.09 us
    pallas_call x1, Pallas kernels, finish(): pl.pallas_call(finish_kernel, out_shape=jax.ShapeDtypeStruct((owned, 2 *...  1.25 us
    unnamed x8, local copies, waits for them, and re-layouts  1.05 us
  transfers between devices with their start and end apart: 4, of which 3 were waited for; matrix products, arithmetic and copies ran while one was open for 0% of the time, Pallas kernels for 5%

profile of v6, /device:TPU:0, one launch (start us, length us, event | category | flops | bytes accessed | tf_op | source)
XLA Modules:
  0.0 42.8 jit_solution(15347589003184980709)
XLA Ops:
  0.0 0.0 copy-start
  0.0 0.0 copy-start.2
  0.0 0.0 copy-start.3
  0.0 8.6 %shard_map.100 = (bf16[4,12,16,256]{3,2,1,0:T(8,128)(2,1)}, f32[4,12,16,256]{3,2,1,0:T(8,128)S(1)}, f32[2,5,16,256]{3,2,1,0:T(8,128)S(1)}, bf16[4,2,5,16,256]{4,3,2,1,0:T(8,128)(2,1)}) custom-call(s32[16]{0:T(128)} %bitcast.5, s32[16]{0:T(128)} %pose_hbm.1, s32[16]{0:T(128)} %bin_hbm.1, f32[16]{0:T(128)} %defocus_hbm.3, f32[2,8]{1,0:T(2,128)} %bitcast.3, ...), custom_call_target="tpu_custom_call" | custom-call | flops 2097152000 | bytes 6291456 | tf_op jit(solution)/shard_map/pallas_call | solution.py:254
  8.6 6.3 %all-to-all-start = ((bf16[4,2,5,16,256]{4,3,2,1,0:T(8,128)(2,1)}), bf16[4,2,5,16,256]{4,3,2,1,0:T(8,128)(2,1)S(1)}, u32[]{:S(2)}, u32[]{:S(2)}) async-start(bf16[4,2,5,16,256]{4,3,2,1,0:T(8,128)(2,1)} %get-tuple-element.30), calls=%async_computation | async-start | bytes 655360 | tf_op jit(solution)/shard_map/all_to_all | solution.py:494
  14.9 1.5 %collective-permute-start = (bf16[4,12,16,256]{3,2,1,0:T(8,128)(2,1)}, bf16[4,12,16,256]{3,2,1,0:T(8,128)(2,1)S(1)}, u32[]{:S(2)}, u32[]{:S(2)}) collective-permute-start(bf16[4,12,16,256]{3,2,1,0:T(8,128)(2,1)} %get-tuple-element.29), channel_id=1, source_target_pairs={{0,2},{2,0},{4,6},{6,4},{8,10},{10,8},{12,14},{14,12},{1,3},{3,1},... | collective-permute-start | bytes 1179656 | tf_op jit(solution)/shard_map/ppermute | solution.py:491
  16.4 0.0 copy-done
  16.4 0.0 copy-done.2
  16.4 0.0 copy-done.3
  16.4 0.0 copy-start.1
  16.4 1.0 %copy-done.1 = bf16[8,256,128]{2,1,0:T(8,128)(2,1)S(1)} copy-done((bf16[8,256,128]{2,1,0:T(8,128)(2,1)S(1)}, bf16[8,256,128]{2,1,0:T(8,128)(2,1)}, u32[]{:S(2)}) %copy-start.1) | copy-done | bytes 524312
  17.5 2.1 %shard_map.101 = (bf16[128,2048]{1,0:T(8,128)(2,1)S(1)}, bf16[128,2048]{1,0:T(8,128)(2,1)S(1)}, f32[16,128]{1,0:T(8,128)S(1)}) custom-call(f32[16]{0:T(128)S(1)} %copy-done.3, f32[2,8]{1,0:T(2,128)S(1)} %bitcast.4, bf16[8,128,256]{2,1,0:T(8,128)(2,1)S(1)} %copy-done, bf16[8,256,128]{2,1,0:T(8,128)(2,1)S(1)} %copy-done.1), custom_call_target="tpu_custom_call" | custom-call | flops 524288000 | bytes 2097152 | tf_op jit(solution)/shard_map/pallas_call | solution.py:347
  19.6 6.1 %collective-permute-done.x_came = bf16[4,12,16,256]{3,2,1,0:T(8,128)(2,1)S(1)} collective-permute-done((bf16[4,12,16,256]{3,2,1,0:T(8,128)(2,1)}, bf16[4,12,16,256]{3,2,1,0:T(8,128)(2,1)S(1)}, u32[]{:S(2)}, u32[]{:S(2)}) %collective-permute-start) | collective-permute-done | bytes 393248 | tf_op jit(solution)/shard_map/ppermute | solution.py:491
  25.7 0.0 all-to-all-done.z_came
  25.7 0.8 %shard_map.102 = (f32[12,16,256]{2,1,0:T(8,128)S(1)}, f32[5,16,256]{2,1,0:T(8,128)S(1)}, bf16[5,16,256]{2,1,0:T(8,128)(2,1)S(1)}, bf16[4,12,16,256]{3,2,1,0:T(8,128)(2,1)}) custom-call(f32[4,12,16,256]{3,2,1,0:T(8,128)S(1)} %get-tuple-element.27.x_keep, f32[2,5,16,256]{3,2,1,0:T(8,128)S(1)} %get-tuple-element.28.z_keep, ...), custom_call_target="tpu_custom_call" | custom-call | flops 1000000 | bytes 4194304 | tf_op jit(solution)/shard_map/pallas_call | solution.py:388
  26.5 4.8 %all-to-all-start.1 = ((bf16[4,12,16,256]{3,2,1,0:T(8,128)(2,1)}), bf16[4,12,16,256]{3,2,1,0:T(8,128)(2,1)S(1)}, u32[]{:S(2)}, u32[]{:S(2)}) async-start(bf16[4,12,16,256]{3,2,1,0:T(8,128)(2,1)} %get-tuple-element.34), calls=%async_computation.1 | async-start | bytes 786432 | tf_op jit(solution)/shard_map/all_to_all | solution.py:494
  31.3 1.5 %collective-permute-start.1 = (bf16[5,16,256]{2,1,0:T(8,128)(2,1)S(1)}, bf16[5,16,256]{2,1,0:T(8,128)(2,1)S(1)}, u32[]{:S(2)}, u32[]{:S(2)}) collective-permute-start(bf16[5,16,256]{2,1,0:T(8,128)(2,1)S(1)} %get-tuple-element.33), channel_id=1, source_target_pairs={{0,2},{2,0},{4,6},{6,4},{8,10},{10,8},{12,14},{14,12},{1,3},{3,1},... | collective-permute-start | bytes 122888 | tf_op jit(solution)/shard_map/ppermute | solution.py:491
  32.8 2.5 %collective-permute-done.1.z_came = bf16[5,16,256]{2,1,0:T(8,128)(2,1)S(1)} collective-permute-done((bf16[5,16,256]{2,1,0:T(8,128)(2,1)S(1)}, bf16[5,16,256]{2,1,0:T(8,128)(2,1)S(1)}, u32[]{:S(2)}, u32[]{:S(2)}) %collective-permute-start.1) | collective-permute-done | bytes 40992 | tf_op jit(solution)/shard_map/ppermute | solution.py:491
  35.3 6.2 %all-to-all-done.1.x_came = bf16[4,12,16,256]{3,2,1,0:T(8,128)(2,1)S(1)} async-done(((bf16[4,12,16,256]{3,2,1,0:T(8,128)(2,1)}), bf16[4,12,16,256]{3,2,1,0:T(8,128)(2,1)S(1)}, u32[]{:S(2)}, u32[]{:S(2)}) %all-to-all-start.1) | async-done | bytes 393248 | tf_op jit(solution)/shard_map/all_to_all | solution.py:494
  41.5 1.2 %shard_map.103 = f32[16,32,128]{2,1,0:T(8,128)} custom-call(bf16[128,2048]{1,0:T(8,128)(2,1)S(1)} %get-tuple-element.24.high_ref, bf16[128,2048]{1,0:T(8,128)(2,1)S(1)} %get-tuple-element.25.low_ref, f32[16,128]{1,0:T(8,128)S(1)} %get-tuple-element.26.share_ref, f32[12,16,256]{2,1,0:T(8,128)S(1)} %get-tuple-element.31.x_own, ...), custom_call_target="tpu_custom_call" | custom-call | flops 262144 | bytes 2097152 | tf_op jit(solution)/shard_map/pallas_call | solution.py:434
Async XLA Ops:
  0.0 16.4 %copy-start = (bf16[8,128,256]{2,1,0:T(8,128)(2,1)S(1)}, bf16[8,128,256]{2,1,0:T(8,128)(2,1)}, u32[]{:S(2)}) copy-start(bf16[8,128,256]{2,1,0:T(8,128)(2,1)} %rows_hbm.3) | copy-start | bytes 1572868
  0.0 16.4 %copy-start.2 = (f32[8,2]{0,1:T(2,128)S(1)}, f32[8,2]{0,1:T(2,128)}, u32[]{:S(2)}) copy-start(f32[8,2]{0,1:T(2,128)} %param.17) | copy-start | bytes 196
  0.0 16.4 %copy-start.3 = (f32[16]{0:T(128)S(1)}, f32[16]{0:T(128)}, u32[]{:S(2)}) copy-start(f32[16]{0:T(128)} %defocus_hbm.3) | copy-start | bytes 196
  8.6 17.1 %all-to-all-start = ((bf16[4,2,5,16,256]{4,3,2,1,0:T(8,128)(2,1)}), bf16[4,2,5,16,256]{4,3,2,1,0:T(8,128)(2,1)S(1)}, u32[]{:S(2)}, u32[]{:S(2)}) async-start(bf16[4,2,5,16,256]{4,3,2,1,0:T(8,128)(2,1)} %get-tuple-element.30), calls=%async_computation | async-start | bytes 655360 | tf_op jit(solution)/shard_map/all_to_all | solution.py:494
  14.9 10.8 %collective-permute-start = (bf16[4,12,16,256]{3,2,1,0:T(8,128)(2,1)}, bf16[4,12,16,256]{3,2,1,0:T(8,128)(2,1)S(1)}, u32[]{:S(2)}, u32[]{:S(2)}) collective-permute-start(bf16[4,12,16,256]{3,2,1,0:T(8,128)(2,1)} %get-tuple-element.29), channel_id=1, source_target_pairs={{0,2},{2,0},{4,6},{6,4},{8,10},{10,8},{12,14},{14,12},{1,3},{3,1},... | collective-permute-start | bytes 1179656 | tf_op jit(solution)/shard_map/ppermute | solution.py:491
  16.4 1.0 %copy-start.1 = (bf16[8,256,128]{2,1,0:T(8,128)(2,1)S(1)}, bf16[8,256,128]{2,1,0:T(8,128)(2,1)}, u32[]{:S(2)}) copy-start(bf16[8,256,128]{2,1,0:T(8,128)(2,1)} %cols_hbm.3) | copy-start | bytes 1572868
  26.5 15.0 %all-to-all-start.1 = ((bf16[4,12,16,256]{3,2,1,0:T(8,128)(2,1)}), bf16[4,12,16,256]{3,2,1,0:T(8,128)(2,1)S(1)}, u32[]{:S(2)}, u32[]{:S(2)}) async-start(bf16[4,12,16,256]{3,2,1,0:T(8,128)(2,1)} %get-tuple-element.34), calls=%async_computation.1 | async-start | bytes 786432 | tf_op jit(solution)/shard_map/all_to_all | solution.py:494
  31.3 4.0 %collective-permute-start.1 = (bf16[5,16,256]{2,1,0:T(8,128)(2,1)S(1)}, bf16[5,16,256]{2,1,0:T(8,128)(2,1)S(1)}, u32[]{:S(2)}, u32[]{:S(2)}) collective-permute-start(bf16[5,16,256]{2,1,0:T(8,128)(2,1)S(1)} %get-tuple-element.33), channel_id=1, source_target_pairs={{0,2},{2,0},{4,6},{6,4},{8,10},{10,8},{12,14},{14,12},{1,3},{3,1},... | collective-permute-start | bytes 122888 | tf_op jit(solution)/shard_map/ppermute | solution.py:491

commit v7 on v3

--- a/solution.py
+++ b/solution.py
@@ -202,25 +202,30 @@
 
     if len(outs) == 1:
         outs[0][...] = totals[...].astype(bf16)
-    else:
-        turns_round = len(outs) // 2
-        members = 2 * turns_round
-        owned = rows // members
-        me = lax.axis_index("img")
-        for k in range(turns_round):
-            mine = lax.rem(me + 2 * k, members)
-            theirs = mine + 1 - 2 * lax.rem(me, 2)
-            first = pl.multiple_of(theirs * owned, owned)
-            outs[k][...] = totals[:, pl.ds(first, owned), :].astype(bf16)
-            first = pl.multiple_of(mine * owned, owned)
-            outs[turns_round + k][...] = totals[:, pl.ds(first, owned), :]
+        return
+    send, keep = outs
+    half_members, _, owned, _ = keep.shape
+    steps = half_members.bit_length()
+    me = lax.axis_index("img")
+    odd = lax.rem(lax.axis_index("slab"), 2) if steps > 1 else 0
+    masks = [1 << n for n in range(steps)]
+    if steps > 1:
+        masks[:2] = [1 + odd, 2 - odd]
+    for q in range(half_members):
+        other = me
+        for n in range(1, steps):
+            if (q >> (steps - 1 - n)) & 1:
+                other = other ^ masks[n]
+        for out, whose in ((keep, other), (send, other ^ masks[0])):
+            first = pl.multiple_of(whose * owned, owned)
+            out[q] = totals[:, pl.ds(first, owned), :].astype(out.dtype)
 
 
 SCRATCH = 19
 SLOTS = 3
 
 
-def own_totals(images, class_index, pose_index, defocus_bin, defocus, rows_table, cols_table, plane_weight, turns_round):
+def own_totals(images, class_index, pose_index, defocus_bin, defocus, rows_table, cols_table, plane_weight, members):
     count, box, _ = images.shape
     poses, rows, _ = rows_table.shape
     cols = cols_table.shape[2]
@@ -230,13 +235,12 @@
     any_place = pl.BlockSpec(memory_space=pl.ANY)
     vmem = pl.BlockSpec(memory_space=pltpu.VMEM)
     lanes = 128 * (-(-2 * count // 128))
-    if turns_round == 0:
+    if members == 1:
         out_shape = [jax.ShapeDtypeStruct((slots, rows, 2 * cols), bf16)]
     else:
         slots += 1
-        piece = (slots, rows // (2 * turns_round), 2 * cols)
-        out_shape = [jax.ShapeDtypeStruct(piece, bf16)] * turns_round
-        out_shape += [jax.ShapeDtypeStruct(piece, f32)] * turns_round
+        piece = (members // 2, slots, rows // members, 2 * cols)
+        out_shape = [pltpu.VMEM(piece, bf16), pltpu.VMEM(piece, f32)]
     operands = (
         class_index[:, 0], pose_index, defocus_bin, defocus, plane_weight.T,
         jnp.asarray(table_y, bf16), jnp.asarray(table_x.T.copy(), bf16),
@@ -354,17 +358,32 @@
     )(defocus, planes, rows_table, cols_table)
 
 
-def finish_kernel(high_ref, low_ref, share_ref, *refs):
-    parts, out_ref, ridge_ref = refs[:-2], refs[-2], refs[-1]
+def middle_kernel(keep, came, send, kept):
+    half = send.shape[0]
+    kept[...] = keep[:half] + came[:half].astype(f32)
+    send[...] = (keep[half:] + came[half:].astype(f32)).astype(bf16)
+
+
+def middle(keep, came):
+    vmem = pl.BlockSpec(memory_space=pltpu.VMEM)
+    piece = (keep.shape[0] // 2,) + keep.shape[1:]
+    return pl.pallas_call(
+        middle_kernel,
+        out_shape=[pltpu.VMEM(piece, bf16), pltpu.VMEM(piece, f32)],
+        in_specs=[vmem] * 2,
+        out_specs=[vmem] * 2,
+        compiler_params=pltpu.CompilerParams(vmem_limit_bytes=16 * 1024 * 1024),
+        cost_estimate=pl.CostEstimate(flops=1000000, bytes_accessed=4 * 1024 * 1024, transcendentals=0),
+    )(keep, came)
+
+
+def finish_kernel(high_ref, low_ref, share_ref, keep, came, out_ref, ridge_ref):
     slots, pairs = share_ref.shape
     owned, _, cols = ridge_ref.shape
     planes = slots // CLASSES
 
     def summed(s):
-        value = parts[0][s].astype(f32)
-        for part in parts[1:]:
-            value = value + part[s].astype(f32)
-        return value
+        return keep[0, s] + came[0, s].astype(f32)
 
     counts = summed(slots)[:CLASSES, :pairs]
     scaled = jnp.concatenate([counts] * planes, 0) * share_ref[...]
@@ -383,22 +402,22 @@
         out_ref[:, 2 * place + 1, :] = value[:, cols:] * factor
 
 
-def finish(tables, parts):
+def finish(tables, keep, came):
     slots = tables[2].shape[0]
-    _, owned, wide = parts[0].shape
+    _, _, owned, wide = keep.shape
     cols = wide // 2
     vmem = pl.BlockSpec(memory_space=pltpu.VMEM)
     return pl.pallas_call(
         finish_kernel,
         out_shape=jax.ShapeDtypeStruct((owned, 2 * slots, cols), f32),
-        in_specs=[vmem] * (3 + len(parts)),
+        in_specs=[vmem] * 5,
         out_specs=vmem,
         scratch_shapes=[pltpu.VMEM((owned, slots, cols), f32)],
         compiler_params=pltpu.CompilerParams(vmem_limit_bytes=16 * 1024 * 1024),
         cost_estimate=pl.CostEstimate(
             flops=8 * slots * owned * cols, bytes_accessed=8 * 1024 * 1024 // 4, transcendentals=0
         ),
-    )(*tables, *parts)
+    )(*tables, keep, came)
 
 
 def squared_table(weight_table):
@@ -431,28 +450,34 @@
     return jnp.einsum("czpmbr,pmbj->rczj", left, v, precision=exact)
 
 
-def by_rounds(images, class_index, pose_index, defocus_bin, defocus, rows_table, cols_table, plane_weight):
+def by_halves(images, class_index, pose_index, defocus_bin, defocus, rows_table, cols_table, plane_weight):
     members = lax.axis_size("img")
-    rounds = members // 2
+    cores = lax.axis_size("slab")
     rows = rows_table.shape[1]
     planes = plane_weight.shape[1]
     cols = cols_table.shape[2]
     owned = rows // members
-    outs = own_totals(
-        images, class_index, pose_index, defocus_bin, defocus, rows_table, cols_table, plane_weight, rounds
-    )
-    sends, keeps = outs[:rounds], outs[rounds:]
-    order = sorted(range(rounds), key=lambda k: (k == 0, -min(k, rounds - k)))
-    parts = [keeps[0]]
-    for k in order:
-        came = lax.ppermute(sends[k], "img", [(i, i ^ 1) for i in range(members)])
-        if k == 0:
-            parts.append(came)
-        else:
-            both = (keeps[k] + came.astype(f32)).astype(bf16)
-            parts.append(lax.ppermute(both, "img", [(i, (i + 2 * k) % members) for i in range(members)]))
+    steps = members.bit_length() - 1
+    send, keep = own_totals(
+        images, class_index, pose_index, defocus_bin, defocus, rows_table, cols_table, plane_weight, members
+    )
     tables = own_ridges(defocus, plane_weight, rows_table, cols_table, owned)
-    out = finish(tables, parts)
+
+    def exchange(value, step):
+        pairs = []
+        for i in range(members):
+            for c in range(cores):
+                axis = step ^ (c % 2) if steps > 1 and step < 2 else step
+                pairs.append((i * cores + c, (i ^ (1 << axis)) * cores + c))
+        return lax.ppermute(value, ("img", "slab"), pairs)
+
+    came = exchange(send, 0)
+    for step in range(1, steps):
+        if step == 1:
+            keep, tables = lax.optimization_barrier((keep, tables))
+        send, keep = middle(keep, came)
+        came = exchange(send, step)
+    out = finish(tables, keep, came)
     return out.reshape(owned, CLASSES, planes, 2, cols)
 
 
@@ -463,7 +488,7 @@
     members = lax.axis_size("img")
     owned = rows // members
     (totals,) = own_totals(
-        images, class_index, pose_index, defocus_bin, defocus, rows_table, cols_table, plane_weight, 0
+        images, class_index, pose_index, defocus_bin, defocus, rows_table, cols_table, plane_weight, 1
     )
     slots = totals.shape[0]
     totals = totals.reshape(slots, members, owned, 2 * cols).transpose(1, 0, 2, 3)
@@ -480,8 +505,8 @@
     rows = arrays[5].shape[1]
     members = lax.axis_size("img")
     images = members * arrays[0].shape[0]
-    small = members % 2 == 0 and images <= 256 and rows % (16 * members) == 0
-    return (by_rounds if small else by_scatter)(*arrays)
+    small = members > 1 and members & (members - 1) == 0 and images <= 256 and rows % (16 * members) == 0
+    return (by_halves if small else by_scatter)(*arrays)
 
 
 def solution(mesh):

time: 35.6 us -> 34.6 us (0.972)
  waiting for transfers between devices: 7.83 us -> 14.9 us
  starting transfers between devices: 12.3 us -> 8.29 us
  other arithmetic: 2.98 us -> 0 us
  Pallas kernels: 12.2 us -> 11.2 us
    ppermute x7 -> x3, waiting for transfers between devices: 7.83 us -> 14.9 us  [exchange(): return lax.ppermute(value, ('img', 'slab'), pairs)]
    ppermute x7 -> x3, starting transfers between devices: 12.3 us -> 8.29 us  [exchange(): return lax.ppermute(value, ('img', 'slab'), pairs)]
    convert_element_type x3 -> x0, other arithmetic: 2.98 us -> none  [by_rounds(): both = (keeps[k] + came.astype(f32)).astype(bf16)]
    pallas_call x1, Pallas kernels: 8.8 us -> 7.72 us  [own_totals(): pl.pallas_call(slices_kernel, out_shape=out_shape, in_specs=[any_place] *...]
  transfers between devices with their start and end apart: 7 -> 3, of which waited for: 3 -> 3; matrix products, arithmetic and copies ran while one was open for 8% -> 0% of each run, Pallas kernels for 6% -> 6%
where the time goes in v7:
time: 34.6 us; the launch traced here: 34.4 us
  waiting for transfers between devices  14.9 us (43%)
  Pallas kernels  11.2 us (32%)
  starting transfers between devices  8.29 us (24%)
    ppermute x3, waiting for transfers between devices, exchange(): return lax.ppermute(value, ('img', 'slab'), pairs)  14.9 us
    ppermute x3, starting transfers between devices, exchange(): return lax.ppermute(value, ('img', 'slab'), pairs)  8.29 us
    pallas_call x1, Pallas kernels, own_totals(): pl.pallas_call(slices_kernel, out_shape=out_shape, in_specs=[any_place] *...  7.72 us
    pallas_call x1, Pallas kernels, own_ridges(): pl.pallas_call(ridge_kernel, out_shape=[table, table, jax.ShapeDtypeStruc...  2.09 us
    pallas_call x1, Pallas kernels, finish(): pl.pallas_call(finish_kernel, out_shape=jax.ShapeDtypeStruct((owned, 2 *...  1.24 us
  transfers between devices with their start and end apart: 3, of which 3 were waited for; matrix products, arithmetic and copies ran while one was open for 0% of the time, Pallas kernels for 6%

profile of v7, /device:TPU:0, one launch (start us, length us, event | category | flops | bytes accessed | tf_op | source)
XLA Modules:
  0.0 34.4 jit_solution(1908825734633739022)
XLA Ops:
  0.0 0.0 copy-start
  0.0 0.0 copy-start.1
  0.0 0.0 copy-start.2
  0.0 0.0 copy-start.3
  0.0 7.7 %shard_map.100 = (bf16[4,17,16,256]{3,2,1,0:T(8,128)(2,1)S(1)}, f32[4,17,16,256]{3,2,1,0:T(8,128)S(1)}) custom-call(s32[16]{0:T(128)} %bitcast.5, s32[16]{0:T(128)} %pose_hbm.1, s32[16]{0:T(128)} %bin_hbm.1, f32[16]{0:T(128)} %defocus_hbm.3, f32[2,8]{1,0:T(2,128)} %bitcast.3, bf16[256,256]{1,0:T(8,128)(2,1)} %constant.4.clone.dft_hbm, ...), custom_call_target="tpu_custom_call" | custom-call | flops 2097152000 | bytes 6291456 | tf_op jit(solution)/shard_map/pallas_call | solution.py:249
  7.7 3.0 %collective-permute-start = (bf16[4,17,16,256]{3,2,1,0:T(8,128)(2,1)S(1)}, bf16[4,17,16,256]{3,2,1,0:T(8,128)(2,1)S(1)}, u32[]{:S(2)}, u32[]{:S(2)}) collective-permute-start(bf16[4,17,16,256]{3,2,1,0:T(8,128)(2,1)S(1)} %get-tuple-element.26), channel_id=1, source_target_pairs={{0,2},{1,5},{2,0},{3,7},{4,6},{5,1},{6,4},{7,3},{8,10},{9,13},{10,... | collective-permute-start | bytes 1671176 | tf_op jit(solution)/shard_map/ppermute | solution.py:472
  10.8 0.0 copy-done
  10.8 0.0 copy-done.1
  10.8 0.0 copy-done.2
  10.8 0.0 copy-done.3
  10.8 2.1 %shard_map.101 = (bf16[128,2048]{1,0:T(8,128)(2,1)S(1)}, bf16[128,2048]{1,0:T(8,128)(2,1)S(1)}, f32[16,128]{1,0:T(8,128)S(1)}) custom-call(f32[16]{0:T(128)S(1)} %copy-done.3, f32[2,8]{1,0:T(2,128)S(1)} %bitcast.4, bf16[8,128,256]{2,1,0:T(8,128)(2,1)S(1)} %copy-done, bf16[8,256,128]{2,1,0:T(8,128)(2,1)S(1)} %copy-done.1), custom_call_target="tpu_custom_call" | custom-call | flops 524288000 | bytes 2097152 | tf_op jit(solution)/shard_map/pallas_call | solution.py:342
  12.9 5.4 %collective-permute-done.came = bf16[4,17,16,256]{3,2,1,0:T(8,128)(2,1)S(1)} collective-permute-done((bf16[4,17,16,256]{3,2,1,0:T(8,128)(2,1)S(1)}, bf16[4,17,16,256]{3,2,1,0:T(8,128)(2,1)S(1)}, u32[]{:S(2)}, u32[]{:S(2)}) %collective-permute-start) | collective-permute-done | bytes 557088 | tf_op jit(solution)/shard_map/ppermute | solution.py:472
  18.3 0.1 shard_map.102
  18.4 2.2 %collective-permute-start.1 = (bf16[2,17,16,256]{3,2,1,0:T(8,128)(2,1)S(1)}, bf16[2,17,16,256]{3,2,1,0:T(8,128)(2,1)S(1)}, u32[]{:S(2)}, u32[]{:S(2)}) collective-permute-start(bf16[2,17,16,256]{3,2,1,0:T(8,128)(2,1)S(1)} %get-tuple-element.28), channel_id=1, source_target_pairs={{0,4},{1,3},{2,6},{3,1},{4,0},{5,7},{6,2},{7,5},{8,12},{9,11},{10,... | collective-permute-start | bytes 835592 | tf_op jit(solution)/shard_map/ppermute | solution.py:472
  20.5 4.5 %collective-permute-done.1.came = bf16[2,17,16,256]{3,2,1,0:T(8,128)(2,1)S(1)} collective-permute-done((bf16[2,17,16,256]{3,2,1,0:T(8,128)(2,1)S(1)}, bf16[2,17,16,256]{3,2,1,0:T(8,128)(2,1)S(1)}, u32[]{:S(2)}, u32[]{:S(2)}) %collective-permute-start.1) | collective-permute-done | bytes 278560 | tf_op jit(solution)/shard_map/ppermute | solution.py:472
  25.1 0.1 shard_map.103
  25.1 3.1 %collective-permute-start.2 = (bf16[1,17,16,256]{3,2,1,0:T(8,128)(2,1)S(1)}, bf16[1,17,16,256]{3,2,1,0:T(8,128)(2,1)S(1)}, u32[]{:S(2)}, u32[]{:S(2)}) collective-permute-start(bf16[1,17,16,256]{3,2,1,0:T(8,128)(2,1)S(1)} %get-tuple-element.30), channel_id=1, source_target_pairs={{0,8},{1,9},{2,10},{3,11},{4,12},{5,13},{6,14},{7,15},{8,0},{9,1},... | collective-permute-start | bytes 417800 | tf_op jit(solution)/shard_map/ppermute | solution.py:472
  28.2 4.9 %collective-permute-done.2.came = bf16[1,17,16,256]{3,2,1,0:T(8,128)(2,1)S(1)} collective-permute-done((bf16[1,17,16,256]{3,2,1,0:T(8,128)(2,1)S(1)}, bf16[1,17,16,256]{3,2,1,0:T(8,128)(2,1)S(1)}, u32[]{:S(2)}, u32[]{:S(2)}) %collective-permute-start.2) | collective-permute-done | bytes 139296 | tf_op jit(solution)/shard_map/ppermute | solution.py:472
  33.2 1.2 %shard_map.104 = f32[16,32,128]{2,1,0:T(8,128)} custom-call(bf16[128,2048]{1,0:T(8,128)(2,1)S(1)} %get-tuple-element.22.high_ref, bf16[128,2048]{1,0:T(8,128)(2,1)S(1)} %get-tuple-element.23.low_ref, f32[16,128]{1,0:T(8,128)S(1)} %get-tuple-element.24.share_ref, f32[1,17,16,256]{3,2,1,0:T(8,128)S(1)} %get-tuple-element.29.keep, ...), custom_call_target="tpu_custom_call" | custom-call | flops 262144 | bytes 2097152 | tf_op jit(solution)/shard_map/pallas_call | solution.py:410
Async XLA Ops:
  0.0 10.8 %copy-start = (bf16[8,128,256]{2,1,0:T(8,128)(2,1)S(1)}, bf16[8,128,256]{2,1,0:T(8,128)(2,1)}, u32[]{:S(2)}) copy-start(bf16[8,128,256]{2,1,0:T(8,128)(2,1)} %rows_hbm.3) | copy-start | bytes 1572868
  0.0 10.8 %copy-start.1 = (bf16[8,256,128]{2,1,0:T(8,128)(2,1)S(1)}, bf16[8,256,128]{2,1,0:T(8,128)(2,1)}, u32[]{:S(2)}) copy-start(bf16[8,256,128]{2,1,0:T(8,128)(2,1)} %cols_hbm.3) | copy-start | bytes 1572868
  0.0 10.8 %copy-start.2 = (f32[8,2]{0,1:T(2,128)S(1)}, f32[8,2]{0,1:T(2,128)}, u32[]{:S(2)}) copy-start(f32[8,2]{0,1:T(2,128)} %param.17) | copy-start | bytes 196
  0.0 10.8 %copy-start.3 = (f32[16]{0:T(128)S(1)}, f32[16]{0:T(128)}, u32[]{:S(2)}) copy-start(f32[16]{0:T(128)} %defocus_hbm.3) | copy-start | bytes 196
  7.7 10.5 %collective-permute-start = (bf16[4,17,16,256]{3,2,1,0:T(8,128)(2,1)S(1)}, bf16[4,17,16,256]{3,2,1,0:T(8,128)(2,1)S(1)}, u32[]{:S(2)}, u32[]{:S(2)}) collective-permute-start(bf16[4,17,16,256]{3,2,1,0:T(8,128)(2,1)S(1)} %get-tuple-element.26), channel_id=1, source_target_pairs={{0,2},{1,5},{2,0},{3,7},{4,6},{5,1},{6,4},{7,3},{8,10},{9,13},{10,... | collective-permute-start | bytes 1671176 | tf_op jit(solution)/shard_map/ppermute | solution.py:472
  18.4 6.7 %collective-permute-start.1 = (bf16[2,17,16,256]{3,2,1,0:T(8,128)(2,1)S(1)}, bf16[2,17,16,256]{3,2,1,0:T(8,128)(2,1)S(1)}, u32[]{:S(2)}, u32[]{:S(2)}) collective-permute-start(bf16[2,17,16,256]{3,2,1,0:T(8,128)(2,1)S(1)} %get-tuple-element.28), channel_id=1, source_target_pairs={{0,4},{1,3},{2,6},{3,1},{4,0},{5,7},{6,2},{7,5},{8,12},{9,11},{10,... | collective-permute-start | bytes 835592 | tf_op jit(solution)/shard_map/ppermute | solution.py:472
  25.1 8.0 %collective-permute-start.2 = (bf16[1,17,16,256]{3,2,1,0:T(8,128)(2,1)S(1)}, bf16[1,17,16,256]{3,2,1,0:T(8,128)(2,1)S(1)}, u32[]{:S(2)}, u32[]{:S(2)}) collective-permute-start(bf16[1,17,16,256]{3,2,1,0:T(8,128)(2,1)S(1)} %get-tuple-element.30), channel_id=1, source_target_pairs={{0,8},{1,9},{2,10},{3,11},{4,12},{5,13},{6,14},{7,15},{8,0},{9,1},... | collective-permute-start | bytes 417800 | tf_op jit(solution)/shard_map/ppermute | solution.py:472

commit v8 on v7

--- a/solution.py
+++ b/solution.py
@@ -203,22 +203,22 @@
     if len(outs) == 1:
         outs[0][...] = totals[...].astype(bf16)
         return
-    send, keep = outs
-    half_members, _, owned, _ = keep.shape
+    half_members, _, owned, _ = outs[0].shape
     steps = half_members.bit_length()
     me = lax.axis_index("img")
-    odd = lax.rem(lax.axis_index("slab"), 2) if steps > 1 else 0
-    masks = [1 << n for n in range(steps)]
-    if steps > 1:
-        masks[:2] = [1 + odd, 2 - odd]
-    for q in range(half_members):
-        other = me
-        for n in range(1, steps):
-            if (q >> (steps - 1 - n)) & 1:
-                other = other ^ masks[n]
-        for out, whose in ((keep, other), (send, other ^ masks[0])):
-            first = pl.multiple_of(whose * owned, owned)
-            out[q] = totals[:, pl.ds(first, owned), :].astype(out.dtype)
+    routes = [[0, 1] + list(range(2, steps)), [1, 0] + list(range(2, steps))]
+    base = 0
+    for route, send, keep in zip(routes, outs[::2], outs[1::2]):
+        part = slice(base, base + keep.shape[1])
+        base += keep.shape[1]
+        for q in range(half_members):
+            other = me
+            for n in range(1, steps):
+                if (q >> (steps - 1 - n)) & 1:
+                    other = other ^ (1 << route[n])
+            for out, whose in ((keep, other), (send, other ^ (1 << route[0]))):
+                first = pl.multiple_of(whose * owned, owned)
+                out[q] = totals[part, pl.ds(first, owned), :].astype(out.dtype)
 
 
 SCRATCH = 19
@@ -239,8 +239,10 @@
         out_shape = [jax.ShapeDtypeStruct((slots, rows, 2 * cols), bf16)]
     else:
         slots += 1
-        piece = (members // 2, slots, rows // members, 2 * cols)
-        out_shape = [pltpu.VMEM(piece, bf16), pltpu.VMEM(piece, f32)]
+        out_shape = []
+        for part in (slots // 2, slots - slots // 2):
+            piece = (members // 2, part, rows // members, 2 * cols)
+            out_shape += [pltpu.VMEM(piece, bf16), pltpu.VMEM(piece, f32)]
     operands = (
         class_index[:, 0], pose_index, defocus_bin, defocus, plane_weight.T,
         jnp.asarray(table_y, bf16), jnp.asarray(table_x.T.copy(), bf16),
@@ -358,23 +360,38 @@
     )(defocus, planes, rows_table, cols_table)
 
 
-def middle_kernel(keep, came, send, kept):
-    half = send.shape[0]
-    kept[...] = keep[:half] + came[:half].astype(f32)
-    send[...] = (keep[half:] + came[half:].astype(f32)).astype(bf16)
-
-
-def middle(keep, came):
+def middle_kernel(ways, *refs):
+    pairs, outs = refs[: 2 * ways], refs[2 * ways :]
+    base = 0
+    for n in range(ways):
+        keep, came = pairs[2 * n], pairs[2 * n + 1]
+        half, part = keep.shape[0] // 2, keep.shape[1]
+        if len(outs) == 2:
+            send, kept = (out.at[:, base : base + part] for out in outs)
+            base += part
+        else:
+            send, kept = outs[2 * n], outs[2 * n + 1]
+        kept[...] = keep[:half] + came[:half].astype(f32)
+        send[...] = (keep[half:] + came[half:].astype(f32)).astype(bf16)
+
+
+def middle(arrays, merge):
     vmem = pl.BlockSpec(memory_space=pltpu.VMEM)
-    piece = (keep.shape[0] // 2,) + keep.shape[1:]
+    keeps = arrays[::2]
+    pieces = [(keep.shape[0] // 2,) + keep.shape[1:] for keep in keeps]
+    if merge:
+        pieces = [(pieces[0][0], sum(piece[1] for piece in pieces)) + pieces[0][2:]]
+    out_shape = []
+    for piece in pieces:
+        out_shape += [pltpu.VMEM(piece, bf16), pltpu.VMEM(piece, f32)]
     return pl.pallas_call(
-        middle_kernel,
-        out_shape=[pltpu.VMEM(piece, bf16), pltpu.VMEM(piece, f32)],
-        in_specs=[vmem] * 2,
-        out_specs=[vmem] * 2,
+        functools.partial(middle_kernel, len(keeps)),
+        out_shape=out_shape,
+        in_specs=[vmem] * len(arrays),
+        out_specs=[vmem] * len(out_shape),
         compiler_params=pltpu.CompilerParams(vmem_limit_bytes=16 * 1024 * 1024),
         cost_estimate=pl.CostEstimate(flops=1000000, bytes_accessed=4 * 1024 * 1024, transcendentals=0),
-    )(keep, came)
+    )(*arrays)
 
 
 def finish_kernel(high_ref, low_ref, share_ref, keep, came, out_ref, ridge_ref):
@@ -452,30 +469,27 @@
 
 def by_halves(images, class_index, pose_index, defocus_bin, defocus, rows_table, cols_table, plane_weight):
     members = lax.axis_size("img")
-    cores = lax.axis_size("slab")
     rows = rows_table.shape[1]
     planes = plane_weight.shape[1]
     cols = cols_table.shape[2]
     owned = rows // members
     steps = members.bit_length() - 1
-    send, keep = own_totals(
+    x_send, x_keep, z_send, z_keep = own_totals(
         images, class_index, pose_index, defocus_bin, defocus, rows_table, cols_table, plane_weight, members
     )
     tables = own_ridges(defocus, plane_weight, rows_table, cols_table, owned)
 
-    def exchange(value, step):
-        pairs = []
-        for i in range(members):
-            for c in range(cores):
-                axis = step ^ (c % 2) if steps > 1 and step < 2 else step
-                pairs.append((i * cores + c, (i ^ (1 << axis)) * cores + c))
-        return lax.ppermute(value, ("img", "slab"), pairs)
-
-    came = exchange(send, 0)
-    for step in range(1, steps):
-        if step == 1:
-            keep, tables = lax.optimization_barrier((keep, tables))
-        send, keep = middle(keep, came)
+    def exchange(value, axis):
+        return lax.ppermute(value, "img", [(i, i ^ (1 << axis)) for i in range(members)])
+
+    x_came, z_came = exchange(x_send, 0), exchange(z_send, 1)
+    x_keep, tables = lax.optimization_barrier((x_keep, tables))
+    x_send, x_keep, z_send, z_keep = middle((x_keep, x_came, z_keep, z_came), False)
+    x_came, z_came = exchange(x_send, 1), exchange(z_send, 0)
+    send, keep = middle((x_keep, x_came, z_keep, z_came), True)
+    came = exchange(send, 2)
+    for step in range(3, steps):
+        send, keep = middle((keep, came), False)
         came = exchange(send, step)
     out = finish(tables, keep, came)
     return out.reshape(owned, CLASSES, planes, 2, cols)
@@ -505,7 +519,7 @@
     rows = arrays[5].shape[1]
     members = lax.axis_size("img")
     images = members * arrays[0].shape[0]
-    small = members > 1 and members & (members - 1) == 0 and images <= 256 and rows % (16 * members) == 0
+    small = members >= 8 and members & (members - 1) == 0 and images <= 256 and rows % (16 * members) == 0
     return (by_halves if small else by_scatter)(*arrays)
 
 

time: 34.6 us -> 34.2 us (0.988)
  waiting for transfers between devices: 14.9 us -> 12.9 us
  starting transfers between devices: 8.29 us -> 9.92 us
    ppermute x3 -> x5, waiting for transfers between devices: 14.9 us -> 12.9 us  [exchange(): lax.ppermute(value, 'img', [(i, i ^ 1 << axis) for i in range(members)])]
    ppermute x3 -> x5, starting transfers between devices: 8.29 us -> 9.92 us  [exchange(): lax.ppermute(value, 'img', [(i, i ^ 1 << axis) for i in range(members)])]
  transfers between devices with their start and end apart: 3 -> 5, of which waited for: 3 -> 3; matrix products, arithmetic and copies ran while one was open for 0% -> 0% of each run, Pallas kernels for 6% -> 6%
where the time goes in v8:
time: 34.2 us; the launch traced here: 34 us
  waiting for transfers between devices  12.9 us (38%)
  Pallas kernels  11.2 us (33%)
  starting transfers between devices  9.92 us (29%)
    ppermute x5, waiting for transfers between devices, exchange(): lax.ppermute(value, 'img', [(i, i ^ 1 << axis) for i in range(members)])  12.9 us
    ppermute x5, starting transfers between devices, exchange(): lax.ppermute(value, 'img', [(i, i ^ 1 << axis) for i in range(members)])  9.92 us
    pallas_call x1, Pallas kernels, own_totals(): pl.pallas_call(slices_kernel, out_shape=out_shape, in_specs=[any_place] *...  7.72 us
    pallas_call x1, Pallas kernels, own_ridges(): pl.pallas_call(ridge_kernel, out_shape=[table, table, jax.ShapeDtypeStruc...  2.09 us
    pallas_call x1, Pallas kernels, finish(): pl.pallas_call(finish_kernel, out_shape=jax.ShapeDtypeStruct((owned, 2 *...  1.24 us
  transfers between devices with their start and end apart: 5, of which 3 were waited for; matrix products, arithmetic and copies ran while one was open for 0% of the time, Pallas kernels for 6%

profile of v8, /device:TPU:0, one launch (start us, length us, event | category | flops | bytes accessed | tf_op | source)
XLA Modules:
  0.0 34.0 jit_solution(9515714046783324396)
XLA Ops:
  0.0 0.0 copy-start
  0.0 0.0 copy-start.1
  0.0 0.0 copy-start.2
  0.0 0.0 copy-start.3
  0.0 7.7 %shard_map.100 = (bf16[4,8,16,256]{3,2,1,0:T(8,128)(2,1)S(1)}, f32[4,8,16,256]{3,2,1,0:T(8,128)S(1)}, bf16[4,9,16,256]{3,2,1,0:T(8,128)(2,1)S(1)}, f32[4,9,16,256]{3,2,1,0:T(8,128)S(1)}) custom-call(s32[16]{0:T(128)} %bitcast.5, s32[16]{0:T(128)} %pose_hbm.1, s32[16]{0:T(128)} %bin_hbm.1, f32[16]{0:T(128)} %defocus_hbm.3, f32[2,8]{1,0:T(2,128)} %bitcast.3, ...), custom_call_target="tpu_custom_call" | custom-call | flops 2097152000 | bytes 6291456 | tf_op jit(solution)/shard_map/pallas_call | solution.py:251
  7.7 3.1 %collective-permute-start.1 = (bf16[4,9,16,256]{3,2,1,0:T(8,128)(2,1)S(1)}, bf16[4,9,16,256]{3,2,1,0:T(8,128)(2,1)S(1)}, u32[]{:S(2)}, u32[]{:S(2)}) collective-permute-start(bf16[4,9,16,256]{3,2,1,0:T(8,128)(2,1)S(1)} %get-tuple-element.32), channel_id=1, source_target_pairs={{0,4},{2,6},{4,0},{6,2},{8,12},{10,14},{12,8},{14,10},{1,5},{3,7},... | collective-permute-start | bytes 884744 | tf_op jit(solution)/shard_map/ppermute | solution.py:483
  10.8 1.5 %collective-permute-start = (bf16[4,8,16,256]{3,2,1,0:T(8,128)(2,1)S(1)}, bf16[4,8,16,256]{3,2,1,0:T(8,128)(2,1)S(1)}, u32[]{:S(2)}, u32[]{:S(2)}) collective-permute-start(bf16[4,8,16,256]{3,2,1,0:T(8,128)(2,1)S(1)} %get-tuple-element.30), channel_id=1, source_target_pairs={{0,2},{2,0},{4,6},{6,4},{8,10},{10,8},{12,14},{14,12},{1,3},{3,1},... | collective-permute-start | bytes 786440 | tf_op jit(solution)/shard_map/ppermute | solution.py:483
  12.3 0.0 copy-done
  12.3 0.0 copy-done.1
  12.3 0.0 copy-done.2
  12.3 0.0 copy-done.3
  12.3 2.1 %shard_map.101 = (bf16[128,2048]{1,0:T(8,128)(2,1)S(1)}, bf16[128,2048]{1,0:T(8,128)(2,1)S(1)}, f32[16,128]{1,0:T(8,128)S(1)}) custom-call(f32[16]{0:T(128)S(1)} %copy-done.3, f32[2,8]{1,0:T(2,128)S(1)} %bitcast.4, bf16[8,128,256]{2,1,0:T(8,128)(2,1)S(1)} %copy-done, bf16[8,256,128]{2,1,0:T(8,128)(2,1)S(1)} %copy-done.1), custom_call_target="tpu_custom_call" | custom-call | flops 524288000 | bytes 2097152 | tf_op jit(solution)/shard_map/pallas_call | solution.py:344
  14.4 4.2 %collective-permute-done.refs_1_ = bf16[4,8,16,256]{3,2,1,0:T(8,128)(2,1)S(1)} collective-permute-done((bf16[4,8,16,256]{3,2,1,0:T(8,128)(2,1)S(1)}, bf16[4,8,16,256]{3,2,1,0:T(8,128)(2,1)S(1)}, u32[]{:S(2)}, u32[]{:S(2)}) %collective-permute-start) | collective-permute-done | bytes 262176 | tf_op jit(solution)/shard_map/ppermute | solution.py:483
  18.6 0.0 collective-permute-done.1.refs_3_
  18.6 0.1 shard_map.102
  18.7 1.6 %collective-permute-start.3 = (bf16[2,9,16,256]{3,2,1,0:T(8,128)(2,1)S(1)}, bf16[2,9,16,256]{3,2,1,0:T(8,128)(2,1)S(1)}, u32[]{:S(2)}, u32[]{:S(2)}) collective-permute-start(bf16[2,9,16,256]{3,2,1,0:T(8,128)(2,1)S(1)} %get-tuple-element.36), channel_id=1, source_target_pairs={{0,2},{2,0},{4,6},{6,4},{8,10},{10,8},{12,14},{14,12},{1,3},{3,1},... | collective-permute-start | bytes 442376 | tf_op jit(solution)/shard_map/ppermute | solution.py:483
  20.3 1.0 %collective-permute-start.2 = (bf16[2,8,16,256]{3,2,1,0:T(8,128)(2,1)S(1)}, bf16[2,8,16,256]{3,2,1,0:T(8,128)(2,1)S(1)}, u32[]{:S(2)}, u32[]{:S(2)}) collective-permute-start(bf16[2,8,16,256]{3,2,1,0:T(8,128)(2,1)S(1)} %get-tuple-element.34), channel_id=1, source_target_pairs={{0,4},{2,6},{4,0},{6,2},{8,12},{10,14},{12,8},{14,10},{1,5},{3,7},... | collective-permute-start | bytes 393224 | tf_op jit(solution)/shard_map/ppermute | solution.py:483
  21.2 4.0 %collective-permute-done.2.refs_1_ = bf16[2,8,16,256]{3,2,1,0:T(8,128)(2,1)S(1)} collective-permute-done((bf16[2,8,16,256]{3,2,1,0:T(8,128)(2,1)S(1)}, bf16[2,8,16,256]{3,2,1,0:T(8,128)(2,1)S(1)}, u32[]{:S(2)}, u32[]{:S(2)}) %collective-permute-start.2) | collective-permute-done | bytes 131104 | tf_op jit(solution)/shard_map/ppermute | solution.py:483
  25.2 0.0 collective-permute-done.3.refs_3_
  25.2 0.1 shard_map.103
  25.3 2.8 %collective-permute-start.4 = (bf16[1,17,16,256]{3,2,1,0:T(8,128)(2,1)S(1)}, bf16[1,17,16,256]{3,2,1,0:T(8,128)(2,1)S(1)}, u32[]{:S(2)}, u32[]{:S(2)}) collective-permute-start(bf16[1,17,16,256]{3,2,1,0:T(8,128)(2,1)S(1)} %get-tuple-element.38), channel_id=1, source_target_pairs={{0,8},{2,10},{4,12},{6,14},{8,0},{10,2},{12,4},{14,6},{1,9},{3,11}... | collective-permute-start | bytes 417800 | tf_op jit(solution)/shard_map/ppermute | solution.py:483
  28.1 4.7 %collective-permute-done.4.came = bf16[1,17,16,256]{3,2,1,0:T(8,128)(2,1)S(1)} collective-permute-done((bf16[1,17,16,256]{3,2,1,0:T(8,128)(2,1)S(1)}, bf16[1,17,16,256]{3,2,1,0:T(8,128)(2,1)S(1)}, u32[]{:S(2)}, u32[]{:S(2)}) %collective-permute-start.4) | collective-permute-done | bytes 139296 | tf_op jit(solution)/shard_map/ppermute | solution.py:483
  32.8 1.2 %shard_map.104 = f32[16,32,128]{2,1,0:T(8,128)} custom-call(bf16[128,2048]{1,0:T(8,128)(2,1)S(1)} %get-tuple-element.26.high_ref, bf16[128,2048]{1,0:T(8,128)(2,1)S(1)} %get-tuple-element.27.low_ref, f32[16,128]{1,0:T(8,128)S(1)} %get-tuple-element.28.share_ref, f32[1,17,16,256]{3,2,1,0:T(8,128)S(1)} %get-tuple-element.37.keep, ...), custom_call_target="tpu_custom_call" | custom-call | flops 262144 | bytes 2097152 | tf_op jit(solution)/shard_map/pallas_call | solution.py:427
Async XLA Ops:
  0.0 12.3 %copy-start = (bf16[8,128,256]{2,1,0:T(8,128)(2,1)S(1)}, bf16[8,128,256]{2,1,0:T(8,128)(2,1)}, u32[]{:S(2)}) copy-start(bf16[8,128,256]{2,1,0:T(8,128)(2,1)} %rows_hbm.3) | copy-start | bytes 1572868
  0.0 12.3 %copy-start.1 = (bf16[8,256,128]{2,1,0:T(8,128)(2,1)S(1)}, bf16[8,256,128]{2,1,0:T(8,128)(2,1)}, u32[]{:S(2)}) copy-start(bf16[8,256,128]{2,1,0:T(8,128)(2,1)} %cols_hbm.3) | copy-start | bytes 1572868
  0.0 12.3 %copy-start.2 = (f32[8,2]{0,1:T(2,128)S(1)}, f32[8,2]{0,1:T(2,128)}, u32[]{:S(2)}) copy-start(f32[8,2]{0,1:T(2,128)} %param.17) | copy-start | bytes 196
  0.0 12.3 %copy-start.3 = (f32[16]{0:T(128)S(1)}, f32[16]{0:T(128)}, u32[]{:S(2)}) copy-start(f32[16]{0:T(128)} %defocus_hbm.3) | copy-start | bytes 196
  7.7 10.9 %collective-permute-start.1 = (bf16[4,9,16,256]{3,2,1,0:T(8,128)(2,1)S(1)}, bf16[4,9,16,256]{3,2,1,0:T(8,128)(2,1)S(1)}, u32[]{:S(2)}, u32[]{:S(2)}) collective-permute-start(bf16[4,9,16,256]{3,2,1,0:T(8,128)(2,1)S(1)} %get-tuple-element.32), channel_id=1, source_target_pairs={{0,4},{2,6},{4,0},{6,2},{8,12},{10,14},{12,8},{14,10},{1,5},{3,7},... | collective-permute-start | bytes 884744 | tf_op jit(solution)/shard_map/ppermute | solution.py:483
  10.8 7.8 %collective-permute-start = (bf16[4,8,16,256]{3,2,1,0:T(8,128)(2,1)S(1)}, bf16[4,8,16,256]{3,2,1,0:T(8,128)(2,1)S(1)}, u32[]{:S(2)}, u32[]{:S(2)}) collective-permute-start(bf16[4,8,16,256]{3,2,1,0:T(8,128)(2,1)S(1)} %get-tuple-element.30), channel_id=1, source_target_pairs={{0,2},{2,0},{4,6},{6,4},{8,10},{10,8},{12,14},{14,12},{1,3},{3,1},... | collective-permute-start | bytes 786440 | tf_op jit(solution)/shard_map/ppermute | solution.py:483
  18.7 6.5 %collective-permute-start.3 = (bf16[2,9,16,256]{3,2,1,0:T(8,128)(2,1)S(1)}, bf16[2,9,16,256]{3,2,1,0:T(8,128)(2,1)S(1)}, u32[]{:S(2)}, u32[]{:S(2)}) collective-permute-start(bf16[2,9,16,256]{3,2,1,0:T(8,128)(2,1)S(1)} %get-tuple-element.36), channel_id=1, source_target_pairs={{0,2},{2,0},{4,6},{6,4},{8,10},{10,8},{12,14},{14,12},{1,3},{3,1},... | collective-permute-start | bytes 442376 | tf_op jit(solution)/shard_map/ppermute | solution.py:483
  20.3 5.0 %collective-permute-start.2 = (bf16[2,8,16,256]{3,2,1,0:T(8,128)(2,1)S(1)}, bf16[2,8,16,256]{3,2,1,0:T(8,128)(2,1)S(1)}, u32[]{:S(2)}, u32[]{:S(2)}) collective-permute-start(bf16[2,8,16,256]{3,2,1,0:T(8,128)(2,1)S(1)} %get-tuple-element.34), channel_id=1, source_target_pairs={{0,4},{2,6},{4,0},{6,2},{8,12},{10,14},{12,8},{14,10},{1,5},{3,7},... | collective-permute-start | bytes 393224 | tf_op jit(solution)/shard_map/ppermute | solution.py:483
  25.3 7.5 %collective-permute-start.4 = (bf16[1,17,16,256]{3,2,1,0:T(8,128)(2,1)S(1)}, bf16[1,17,16,256]{3,2,1,0:T(8,128)(2,1)S(1)}, u32[]{:S(2)}, u32[]{:S(2)}) collective-permute-start(bf16[1,17,16,256]{3,2,1,0:T(8,128)(2,1)S(1)} %get-tuple-element.38), channel_id=1, source_target_pairs={{0,8},{2,10},{4,12},{6,14},{8,0},{10,2},{12,4},{14,6},{1,9},{3,11}... | collective-permute-start | bytes 417800 | tf_op jit(solution)/shard_map/ppermute | solution.py:483

commit v9 on v5

--- a/solution.py
+++ b/solution.py
@@ -56,7 +56,7 @@
     (
         class_ref, pose_ref, bin_ref, defocus_ref, plane_ref,
         dft_ref, dft_t_ref, images_ref, rows_ref, cols_ref, arrived,
-        rows_fold, cols_fold, wave_y, cos_x, sin_x, spec_ref, mix_ref, totals,
+        rows_fold, cols_fold, wave_y, cos_x, sin_x, half_ref, spec_ref, mix_ref, totals,
     ) = refs
     count, box, _ = images_ref.shape
     half = box // 2
@@ -67,8 +67,11 @@
     pairs = (
         (class_hbm, class_ref), (pose_hbm, pose_ref), (bin_hbm, bin_ref),
         (defocus_hbm, defocus_ref), (plane_hbm, plane_ref),
-        (rows_hbm, rows_ref), (cols_hbm, cols_ref), (dft_t_hbm, dft_t_ref),
-        (images_hbm, images_ref), (dft_hbm, dft_ref),
+        (dft_t_hbm, dft_t_ref), (images_hbm.at[0:GROUP], images_ref.at[0:GROUP]),
+        (dft_hbm, dft_ref), (cols_hbm, cols_ref), (rows_hbm, rows_ref),
+    ) + tuple(
+        (images_hbm.at[i : i + GROUP], images_ref.at[i : i + GROUP])
+        for i in range(GROUP, count, GROUP)
     )
     copies = [
         pltpu.make_async_copy(source, target, arrived.at[n])
@@ -114,20 +117,6 @@
             counts = counts + jnp.where(hit, 1.0, 0.0)
         totals[planes * CLASSES] = jnp.tile(counts, (rows // 16, 1))
 
-    copies[5].wait()
-    rows_fold[...] = dot(
-        rows_ref[...].reshape(poses * rows, box), near, ((1,), (1,))
-    ).astype(bf16)
-    copies[6].wait()
-    for p in range(0, poses, 2):
-        two = jnp.concatenate([cols_ref[p], cols_ref[p + 1]], 1)
-        near_two = dot(near, two).astype(bf16)
-        far_two = dot(far, two).astype(bf16)
-        cols_fold[p] = jnp.concatenate([near_two[:, :cols], far_two[:, :cols]], 1)
-        cols_fold[p + 1] = jnp.concatenate([near_two[:, cols:], far_two[:, cols:]], 1)
-    for copy in copies[7:]:
-        copy.wait()
-
     tile = 8
     tile_row = iota((tile, half), 0) == 0
     tile_col = iota((tile, half), 1) == 0
@@ -138,9 +127,13 @@
     def without_row(value):
         return jnp.concatenate([jnp.where(tile_row, 0.0, value[:tile]), value[tile:]], 0)
 
-    def transform(i):
-        z = dot(images_ref[i], dft_t_ref[...]).astype(bf16)
-        y = dot(dft_ref[...], z)
+    def along_columns(i):
+        if i % GROUP == 0:
+            copies[6 if i == 0 else 9 + i // GROUP].wait()
+        half_ref[i % SLOTS] = dot(images_ref[i], dft_t_ref[...]).astype(bf16)
+
+    def along_rows(i):
+        y = dot(dft_ref[...], half_ref[i % SLOTS])
         sin_col = jnp.broadcast_to(wave_y[:, i : i + 1], (tall, half))
         cos_col = jnp.broadcast_to(wave_y[:, count + i : count + i + 1], (tall, half))
         near_ctf = sin_col * cos_x[i : i + 1, :half] + cos_col * sin_x[i : i + 1, :half]
@@ -192,13 +185,31 @@
             slot = z * CLASSES + class_ref[i]
             totals[slot] += plane_ref[z, pose] * piece
 
-    for step in range(count + 2):
-        if step >= 2:
-            insert(step - 2)
-        if 1 <= step <= count:
-            mix(step - 1)
+    copies[5].wait()
+    along_columns(0)
+    copies[7].wait()
+    copies[8].wait()
+    for p in range(0, poses, 2):
+        two = jnp.concatenate([cols_ref[p], cols_ref[p + 1]], 1)
+        near_two = dot(near, two).astype(bf16)
+        far_two = dot(far, two).astype(bf16)
+        cols_fold[p] = jnp.concatenate([near_two[:, :cols], far_two[:, :cols]], 1)
+        cols_fold[p + 1] = jnp.concatenate([near_two[:, cols:], far_two[:, cols:]], 1)
+    along_columns(1)
+    along_rows(0)
+    copies[9].wait()
+    rows_fold[...] = dot(
+        rows_ref[...].reshape(poses * rows, box), near, ((1,), (1,))
+    ).astype(bf16)
+    for step in range(2, count + 3):
+        if step >= 3:
+            insert(step - 3)
+        if step - 2 < count:
+            mix(step - 2)
+        if step - 1 < count:
+            along_rows(step - 1)
         if step < count:
-            transform(step)
+            along_columns(step)
 
     if len(outs) == 1:
         outs[0][...] = totals[...].astype(bf16)
@@ -207,23 +218,19 @@
     z_sends = outs[3:]
     rounds, x_slots, owned, _ = x_keep.shape
     me = lax.axis_index("img")
-    side = lax.rem(me, 2)
     for k in range(rounds):
-        base = lax.rem(me - side + 2 * k, 2 * rounds)
-        mine = pl.ds(pl.multiple_of((base + side) * owned, owned), owned)
-        theirs = pl.ds(pl.multiple_of((base + 1 - side) * owned, owned), owned)
+        mine = pl.ds(pl.multiple_of((me ^ (2 * k)) * owned, owned), owned)
+        theirs = pl.ds(pl.multiple_of((me ^ (2 * k + 1)) * owned, owned), owned)
         x_keep[k] = totals[-x_slots:, mine, :]
         x_send[k] = totals[-x_slots:, theirs, :].astype(bf16)
-        if k == 0:
-            z_keep[0] = totals[:-x_slots, mine, :]
-            z_keep[1] = totals[:-x_slots, theirs, :]
-        else:
-            z_sends[k - 1][0] = totals[:-x_slots, mine, :].astype(bf16)
-            z_sends[k - 1][1] = totals[:-x_slots, theirs, :].astype(bf16)
-
-
-SCRATCH = 19
+        z_out = z_keep if k == 0 else z_sends[k - 1]
+        z_out[0] = totals[:-x_slots, mine, :].astype(z_out.dtype)
+        z_out[1] = totals[:-x_slots, theirs, :].astype(z_out.dtype)
+
+
+SCRATCH = 20
 SLOTS = 3
+GROUP = 4
 Z_SLOTS = 5
 
 
@@ -258,12 +265,13 @@
         scratch_shapes=[pltpu.SMEM(x.shape, x.dtype) for x in operands[:5]]
         + [pltpu.VMEM(x.shape, x.dtype) for x in operands[5:]]
         + [
-            pltpu.SemaphoreType.DMA((10,)),
+            pltpu.SemaphoreType.DMA((9 + count // GROUP,)),
             pltpu.VMEM((poses * rows, box), bf16),
             pltpu.VMEM((poses, box, 2 * cols), bf16),
             pltpu.VMEM((box // 2 + 8, lanes), f32),
             pltpu.VMEM((count, box), f32),
             pltpu.VMEM((count, box), f32),
+            pltpu.VMEM((SLOTS, box, box), bf16),
             pltpu.VMEM((SLOTS, box + 16, box), bf16),
             pltpu.VMEM((SLOTS, box, 2 * cols), bf16),
             pltpu.VMEM((slots, rows, 2 * cols), f32),
@@ -492,9 +500,9 @@
         return lax.ppermute(value, "img", [(i, i ^ 1) for i in range(members)])
 
     def along_z(value, k):
-        return lax.ppermute(value, "img", [(i, (i + 2 * k) % members) for i in range(members)])
-
-    order = sorted(range(1, rounds), key=lambda k: -min(k, rounds - k))
+        return lax.ppermute(value, "img", [(i, i ^ (2 * k)) for i in range(members)])
+
+    order = [2, 3, 1] if rounds == 4 else list(range(1, rounds))
     x_came = along_x(x_send)
     z_came = [along_z(z_sends[k], k) for k in order]
     tables = own_ridges(defocus, plane_weight, rows_table, cols_table, owned)
@@ -530,7 +538,7 @@
     rows = arrays[5].shape[1]
     members = lax.axis_size("img")
     images = members * arrays[0].shape[0]
-    small = members % 2 == 0 and images <= 256 and rows % (16 * members) == 0
+    small = members > 1 and members & (members - 1) == 0 and images <= 256 and rows % (16 * members) == 0
     return (by_rounds if small else by_scatter)(*arrays)
 
 

time: 32.9 us -> 32.9 us (level)
  waiting for transfers between devices: 4.27 us -> 9.28 us
  starting transfers between devices: 17.2 us -> 12.8 us
  Pallas kernels: 11.2 us -> 10.7 us
    ppermute x6, waiting for transfers between devices: 1.04 us -> 6.76 us  [along_z(): return lax.ppermute(value, 'img', [(i, i ^ 2 * k) for i in range(members)])]
    ppermute x6, starting transfers between devices: 13.4 us -> 8.29 us  [along_z(): return lax.ppermute(value, 'img', [(i, i ^ 2 * k) for i in range(members)])]
    ppermute x2, waiting for transfers between devices: 3.23 us -> 2.52 us  [along_x(): return lax.ppermute(value, 'img', [(i, i ^ 1) for i in range(members)])]
    ppermute x2, starting transfers between devices: 3.8 us -> 4.5 us  [along_x(): return lax.ppermute(value, 'img', [(i, i ^ 1) for i in range(members)])]
    pallas_call x1, Pallas kernels: 7.72 us -> 7.2 us  [own_totals(): pl.pallas_call(slices_kernel, out_shape=out_shape, in_specs=[any_place] *...]
  transfers between devices with their start and end apart: 8 -> 8, of which waited for: 3 -> 6; matrix products, arithmetic and copies ran while one was open for 0% -> 0% of each run, Pallas kernels for 6% -> 6%
where the time goes in v9:
time: 32.9 us; the launch traced here: 32.8 us
  starting transfers between devices  12.8 us (39%)
  Pallas kernels  10.7 us (33%)
  waiting for transfers between devices  9.28 us (28%)
    ppermute x6, starting transfers between devices, along_z(): return lax.ppermute(value, 'img', [(i, i ^ 2 * k) for i in range(members)])  8.29 us
    pallas_call x1, Pallas kernels, own_totals(): pl.pallas_call(slices_kernel, out_shape=out_shape, in_specs=[any_place] *...  7.2 us
    ppermute x6, waiting for transfers between devices, along_z(): return lax.ppermute(value, 'img', [(i, i ^ 2 * k) for i in range(members)])  6.76 us
    ppermute x2, starting transfers between devices, along_x(): return lax.ppermute(value, 'img', [(i, i ^ 1) for i in range(members)])  4.5 us
    ppermute x2, waiting for transfers between devices, along_x(): return lax.ppermute(value, 'img', [(i, i ^ 1) for i in range(members)])  2.52 us
    pallas_call x1, Pallas kernels, own_ridges(): pl.pallas_call(ridge_kernel, out_shape=[table, table, jax.ShapeDtypeStruc...  2.09 us
    pallas_call x1, Pallas kernels, finish(): pl.pallas_call(finish_kernel, out_shape=jax.ShapeDtypeStruct((owned, 2 *...  1.25 us
  transfers between devices with their start and end apart: 8, of which 6 were waited for; matrix products, arithmetic and copies ran while one was open for 0% of the time, Pallas kernels for 6%

profile of v9, /device:TPU:0, one launch (start us, length us, event | category | flops | bytes accessed | tf_op | source)
XLA Modules:
  0.0 32.8 jit_solution(7836398278537157520)
XLA Ops:
  0.0 0.0 copy-start
  0.0 0.0 copy-start.1
  0.0 0.0 copy-start.2
  0.0 0.0 copy-start.3
  0.0 7.2 %shard_map.100 = (bf16[4,12,16,256]{3,2,1,0:T(8,128)(2,1)S(1)}, f32[4,12,16,256]{3,2,1,0:T(8,128)S(1)}, f32[2,5,16,256]{3,2,1,0:T(8,128)S(1)}, bf16[2,5,16,256]{...) custom-call(s32[16]{0:T(128)} %bitcast.5, s32[16]{0:T(128)} %pose_hbm.1, ...), custom_call_target="tpu_custom_call" | custom-call | flops 2097152000 | bytes 6291456 | tf_op jit(solution)/shard_map/pallas_call | solution.py:260
  7.2 3.0 %collective-permute-start = (bf16[4,12,16,256]{3,2,1,0:T(8,128)(2,1)S(1)}, bf16[4,12,16,256]{3,2,1,0:T(8,128)(2,1)S(1)}, u32[]{:S(2)}, u32[]{:S(2)}) collective-permute-start(bf16[4,12,16,256]{3,2,1,0:T(8,128)(2,1)S(1)} %get-tuple-element.33), channel_id=1, source_target_pairs={{0,2},{2,0},{4,6},{6,4},{8,10},{10,8},{12,14},{14,12},{1,3},{3,1},... | collective-permute-start | bytes 1179656 | tf_op jit(solution)/shard_map/ppermute | solution.py:500
  10.2 2.6 %collective-permute-start.1 = (bf16[2,5,16,256]{3,2,1,0:T(8,128)(2,1)S(1)}, bf16[2,5,16,256]{3,2,1,0:T(8,128)(2,1)S(1)}, u32[]{:S(2)}, u32[]{:S(2)}) collective-permute-start(bf16[2,5,16,256]{3,2,1,0:T(8,128)(2,1)S(1)} %get-tuple-element.34), channel_id=1, source_target_pairs={{0,8},{2,10},{4,12},{6,14},{8,0},{10,2},{12,4},{14,6},{1,9},{3,11}... | collective-permute-start | bytes 245768 | tf_op jit(solution)/shard_map/ppermute | solution.py:503
  12.8 1.4 %collective-permute-start.2 = (bf16[2,5,16,256]{3,2,1,0:T(8,128)(2,1)S(1)}, bf16[2,5,16,256]{3,2,1,0:T(8,128)(2,1)S(1)}, u32[]{:S(2)}, u32[]{:S(2)}) collective-permute-start(bf16[2,5,16,256]{3,2,1,0:T(8,128)(2,1)S(1)} %get-tuple-element.35), channel_id=1, source_target_pairs={{0,12},{2,14},{4,8},{6,10},{8,4},{10,6},{12,0},{14,2},{1,13},{3,15... | collective-permute-start | bytes 245768 | tf_op jit(solution)/shard_map/ppermute | solution.py:503
  14.2 0.2 collective-permute-start.3
  14.4 0.0 copy-done
  14.4 0.0 copy-done.1
  14.4 0.0 copy-done.2
  14.4 0.0 copy-done.3
  14.4 2.1 %shard_map.101 = (bf16[128,2048]{1,0:T(8,128)(2,1)S(1)}, bf16[128,2048]{1,0:T(8,128)(2,1)S(1)}, f32[16,128]{1,0:T(8,128)S(1)}) custom-call(f32[16]{0:T(128)S(1)} %copy-done.3, f32[2,8]{1,0:T(2,128)S(1)} %bitcast.4, bf16[8,128,256]{2,1,0:T(8,128)(2,1)S(1)} %copy-done, bf16[8,256,128]{2,1,0:T(8,128)(2,1)S(1)} %copy-done.1), custom_call_target="tpu_custom_call" | custom-call | flops 524288000 | bytes 2097152 | tf_op jit(solution)/shard_map/pallas_call | solution.py:354
  16.5 1.6 %collective-permute-done.1.refs_0_ = bf16[2,5,16,256]{3,2,1,0:T(8,128)(2,1)S(1)} collective-permute-done((bf16[2,5,16,256]{3,2,1,0:T(8,128)(2,1)S(1)}, bf16[2,5,16,256]{3,2,1,0:T(8,128)(2,1)S(1)}, u32[]{:S(2)}, u32[]{:S(2)}) %collective-permute-start.1) | collective-permute-done | bytes 81952 | tf_op jit(solution)/shard_map/ppermute | solution.py:503
  18.2 1.3 %collective-permute-done.2.refs_1_ = bf16[2,5,16,256]{3,2,1,0:T(8,128)(2,1)S(1)} collective-permute-done((bf16[2,5,16,256]{3,2,1,0:T(8,128)(2,1)S(1)}, bf16[2,5,16,256]{3,2,1,0:T(8,128)(2,1)S(1)}, u32[]{:S(2)}, u32[]{:S(2)}) %collective-permute-start.2) | collective-permute-done | bytes 81952 | tf_op jit(solution)/shard_map/ppermute | solution.py:503
  19.4 0.3 collective-permute-done.3.refs_2_
  19.7 0.0 collective-permute-done.x_came
  19.7 0.1 shard_map.102
  19.8 3.3 %collective-permute-start.5 = (bf16[12,16,256]{2,1,0:T(8,128)(2,1)S(1)}, bf16[12,16,256]{2,1,0:T(8,128)(2,1)S(1)}, u32[]{:S(2)}, u32[]{:S(2)}) collective-permute-start(bf16[12,16,256]{2,1,0:T(8,128)(2,1)S(1)} %get-tuple-element.40), channel_id=1, source_target_pairs={{0,8},{2,10},{4,12},{6,14},{8,0},{10,2},{12,4},{14,6},{1,9},{3,11}... | collective-permute-start | bytes 294920 | tf_op jit(solution)/shard_map/ppermute | solution.py:503
  23.1 0.6 %collective-permute-start.6 = (bf16[12,16,256]{2,1,0:T(8,128)(2,1)S(1)}, bf16[12,16,256]{2,1,0:T(8,128)(2,1)S(1)}, u32[]{:S(2)}, u32[]{:S(2)}) collective-permute-start(bf16[12,16,256]{2,1,0:T(8,128)(2,1)S(1)} %get-tuple-element.41), channel_id=1, source_target_pairs={{0,12},{2,14},{4,8},{6,10},{8,4},{10,6},{12,0},{14,2},{1,13},{3,15... | collective-permute-start | bytes 294920 | tf_op jit(solution)/shard_map/ppermute | solution.py:503
  23.7 0.2 collective-permute-start.7
  24.0 1.5 %collective-permute-start.4 = (bf16[5,16,256]{2,1,0:T(8,128)(2,1)S(1)}, bf16[5,16,256]{2,1,0:T(8,128)(2,1)S(1)}, u32[]{:S(2)}, u32[]{:S(2)}) collective-permute-start(bf16[5,16,256]{2,1,0:T(8,128)(2,1)S(1)} %get-tuple-element.39), channel_id=1, source_target_pairs={{0,2},{2,0},{4,6},{6,4},{8,10},{10,8},{12,14},{14,12},{1,3},{3,1},... | collective-permute-start | bytes 122888 | tf_op jit(solution)/shard_map/ppermute | solution.py:500
  25.5 2.5 %collective-permute-done.4.z_came = bf16[5,16,256]{2,1,0:T(8,128)(2,1)S(1)} collective-permute-done((bf16[5,16,256]{2,1,0:T(8,128)(2,1)S(1)}, bf16[5,16,256]{2,1,0:T(8,128)(2,1)S(1)}, u32[]{:S(2)}, u32[]{:S(2)}) %collective-permute-start.4) | collective-permute-done | bytes 40992 | tf_op jit(solution)/shard_map/ppermute | solution.py:500
  28.0 2.6 %collective-permute-done.5.refs_0_ = bf16[12,16,256]{2,1,0:T(8,128)(2,1)S(1)} collective-permute-done((bf16[12,16,256]{2,1,0:T(8,128)(2,1)S(1)}, bf16[12,16,256]{2,1,0:T(8,128)(2,1)S(1)}, u32[]{:S(2)}, u32[]{:S(2)}) %collective-permute-start.5) | collective-permute-done | bytes 98336 | tf_op jit(solution)/shard_map/ppermute | solution.py:503
  30.5 0.0 collective-permute-done.6.refs_1_
  30.5 1.0 %collective-permute-done.7.refs_2_ = bf16[12,16,256]{2,1,0:T(8,128)(2,1)S(1)} collective-permute-done((bf16[12,16,256]{2,1,0:T(8,128)(2,1)S(1)}, bf16[12,16,256]{2,1,0:T(8,128)(2,1)S(1)}, u32[]{:S(2)}, u32[]{:S(2)}) %collective-permute-start.7) | collective-permute-done | bytes 98336 | tf_op jit(solution)/shard_map/ppermute | solution.py:503
  31.6 1.3 %shard_map.103 = f32[16,32,128]{2,1,0:T(8,128)} custom-call(bf16[128,2048]{1,0:T(8,128)(2,1)S(1)} %get-tuple-element.28.high_ref, bf16[128,2048]{1,0:T(8,128)(2,1)S(1)} %get-tuple-element.29.low_ref, f32[16,128]{1,0:T(8,128)S(1)} %get-tuple-element.30.share_ref, f32[12,16,256]{2,1,0:T(8,128)S(1)} %get-tuple-element.37.x_own, ...), custom_call_target="tpu_custom_call" | custom-call | flops 262144 | bytes 2097152 | tf_op jit(solution)/shard_map/pallas_call | solution.py:443
Async XLA Ops:
  0.0 14.4 %copy-start = (bf16[8,128,256]{2,1,0:T(8,128)(2,1)S(1)}, bf16[8,128,256]{2,1,0:T(8,128)(2,1)}, u32[]{:S(2)}) copy-start(bf16[8,128,256]{2,1,0:T(8,128)(2,1)} %rows_hbm.3) | copy-start | bytes 1572868
  0.0 14.4 %copy-start.1 = (bf16[8,256,128]{2,1,0:T(8,128)(2,1)S(1)}, bf16[8,256,128]{2,1,0:T(8,128)(2,1)}, u32[]{:S(2)}) copy-start(bf16[8,256,128]{2,1,0:T(8,128)(2,1)} %cols_hbm.3) | copy-start | bytes 1572868
  0.0 14.4 %copy-start.2 = (f32[8,2]{0,1:T(2,128)S(1)}, f32[8,2]{0,1:T(2,128)}, u32[]{:S(2)}) copy-start(f32[8,2]{0,1:T(2,128)} %param.17) | copy-start | bytes 196
  0.0 14.4 %copy-start.3 = (f32[16]{0:T(128)S(1)}, f32[16]{0:T(128)}, u32[]{:S(2)}) copy-start(f32[16]{0:T(128)} %defocus_hbm.3) | copy-start | bytes 196
  7.2 12.5 %collective-permute-start = (bf16[4,12,16,256]{3,2,1,0:T(8,128)(2,1)S(1)}, bf16[4,12,16,256]{3,2,1,0:T(8,128)(2,1)S(1)}, u32[]{:S(2)}, u32[]{:S(2)}) collective-permute-start(bf16[4,12,16,256]{3,2,1,0:T(8,128)(2,1)S(1)} %get-tuple-element.33), channel_id=1, source_target_pairs={{0,2},{2,0},{4,6},{6,4},{8,10},{10,8},{12,14},{14,12},{1,3},{3,1},... | collective-permute-start | bytes 1179656 | tf_op jit(solution)/shard_map/ppermute | solution.py:500
  10.2 7.9 %collective-permute-start.1 = (bf16[2,5,16,256]{3,2,1,0:T(8,128)(2,1)S(1)}, bf16[2,5,16,256]{3,2,1,0:T(8,128)(2,1)S(1)}, u32[]{:S(2)}, u32[]{:S(2)}) collective-permute-start(bf16[2,5,16,256]{3,2,1,0:T(8,128)(2,1)S(1)} %get-tuple-element.34), channel_id=1, source_target_pairs={{0,8},{2,10},{4,12},{6,14},{8,0},{10,2},{12,4},{14,6},{1,9},{3,11}... | collective-permute-start | bytes 245768 | tf_op jit(solution)/shard_map/ppermute | solution.py:503
  12.8 6.6 %collective-permute-start.2 = (bf16[2,5,16,256]{3,2,1,0:T(8,128)(2,1)S(1)}, bf16[2,5,16,256]{3,2,1,0:T(8,128)(2,1)S(1)}, u32[]{:S(2)}, u32[]{:S(2)}) collective-permute-start(bf16[2,5,16,256]{3,2,1,0:T(8,128)(2,1)S(1)} %get-tuple-element.35), channel_id=1, source_target_pairs={{0,12},{2,14},{4,8},{6,10},{8,4},{10,6},{12,0},{14,2},{1,13},{3,15... | collective-permute-start | bytes 245768 | tf_op jit(solution)/shard_map/ppermute | solution.py:503
  14.2 5.5 %collective-permute-start.3 = (bf16[2,5,16,256]{3,2,1,0:T(8,128)(2,1)S(1)}, bf16[2,5,16,256]{3,2,1,0:T(8,128)(2,1)S(1)}, u32[]{:S(2)}, u32[]{:S(2)}) collective-permute-start(bf16[2,5,16,256]{3,2,1,0:T(8,128)(2,1)S(1)} %get-tuple-element.36), channel_id=1, source_target_pairs={{0,4},{2,6},{4,0},{6,2},{8,12},{10,14},{12,8},{14,10},{1,5},{3,7},... | collective-permute-start | bytes 245768 | tf_op jit(solution)/shard_map/ppermute | solution.py:503
  19.8 10.7 %collective-permute-start.5 = (bf16[12,16,256]{2,1,0:T(8,128)(2,1)S(1)}, bf16[12,16,256]{2,1,0:T(8,128)(2,1)S(1)}, u32[]{:S(2)}, u32[]{:S(2)}) collective-permute-start(bf16[12,16,256]{2,1,0:T(8,128)(2,1)S(1)} %get-tuple-element.40), channel_id=1, source_target_pairs={{0,8},{2,10},{4,12},{6,14},{8,0},{10,2},{12,4},{14,6},{1,9},{3,11}... | collective-permute-start | bytes 294920 | tf_op jit(solution)/shard_map/ppermute | solution.py:503
  23.1 7.4 %collective-permute-start.6 = (bf16[12,16,256]{2,1,0:T(8,128)(2,1)S(1)}, bf16[12,16,256]{2,1,0:T(8,128)(2,1)S(1)}, u32[]{:S(2)}, u32[]{:S(2)}) collective-permute-start(bf16[12,16,256]{2,1,0:T(8,128)(2,1)S(1)} %get-tuple-element.41), channel_id=1, source_target_pairs={{0,12},{2,14},{4,8},{6,10},{8,4},{10,6},{12,0},{14,2},{1,13},{3,15... | collective-permute-start | bytes 294920 | tf_op jit(solution)/shard_map/ppermute | solution.py:503
  23.7 7.8 %collective-permute-start.7 = (bf16[12,16,256]{2,1,0:T(8,128)(2,1)S(1)}, bf16[12,16,256]{2,1,0:T(8,128)(2,1)S(1)}, u32[]{:S(2)}, u32[]{:S(2)}) collective-permute-start(bf16[12,16,256]{2,1,0:T(8,128)(2,1)S(1)} %get-tuple-element.42), channel_id=1, source_target_pairs={{0,4},{2,6},{4,0},{6,2},{8,12},{10,14},{12,8},{14,10},{1,5},{3,7},... | collective-permute-start | bytes 294920 | tf_op jit(solution)/shard_map/ppermute | solution.py:503
  24.0 4.0 %collective-permute-start.4 = (bf16[5,16,256]{2,1,0:T(8,128)(2,1)S(1)}, bf16[5,16,256]{2,1,0:T(8,128)(2,1)S(1)}, u32[]{:S(2)}, u32[]{:S(2)}) collective-permute-start(bf16[5,16,256]{2,1,0:T(8,128)(2,1)S(1)} %get-tuple-element.39), channel_id=1, source_target_pairs={{0,2},{2,0},{4,6},{6,4},{8,10},{10,8},{12,14},{14,12},{1,3},{3,1},... | collective-permute-start | bytes 122888 | tf_op jit(solution)/shard_map/ppermute | solution.py:500

commit v10 on v9

--- a/solution.py
+++ b/solution.py
@@ -67,8 +67,8 @@
     pairs = (
         (class_hbm, class_ref), (pose_hbm, pose_ref), (bin_hbm, bin_ref),
         (defocus_hbm, defocus_ref), (plane_hbm, plane_ref),
-        (dft_t_hbm, dft_t_ref), (images_hbm.at[0:GROUP], images_ref.at[0:GROUP]),
-        (dft_hbm, dft_ref), (cols_hbm, cols_ref), (rows_hbm, rows_ref),
+        (dft_hbm, dft_ref), (images_hbm.at[0:GROUP], images_ref.at[0:GROUP]),
+        (dft_t_hbm, dft_t_ref), (cols_hbm, cols_ref), (rows_hbm, rows_ref),
     ) + tuple(
         (images_hbm.at[i : i + GROUP], images_ref.at[i : i + GROUP])
         for i in range(GROUP, count, GROUP)
@@ -127,13 +127,13 @@
     def without_row(value):
         return jnp.concatenate([jnp.where(tile_row, 0.0, value[:tile]), value[tile:]], 0)
 
-    def along_columns(i):
+    def along_rows(i):
         if i % GROUP == 0:
             copies[6 if i == 0 else 9 + i // GROUP].wait()
-        half_ref[i % SLOTS] = dot(images_ref[i], dft_t_ref[...]).astype(bf16)
-
-    def along_rows(i):
-        y = dot(dft_ref[...], half_ref[i % SLOTS])
+        half_ref[i % SLOTS] = dot(dft_ref[...], images_ref[i]).astype(bf16)
+
+    def along_columns(i):
+        y = dot(half_ref[i % SLOTS], dft_t_ref[...])
         sin_col = jnp.broadcast_to(wave_y[:, i : i + 1], (tall, half))
         cos_col = jnp.broadcast_to(wave_y[:, count + i : count + i + 1], (tall, half))
         near_ctf = sin_col * cos_x[i : i + 1, :half] + cos_col * sin_x[i : i + 1, :half]
@@ -186,7 +186,7 @@
             totals[slot] += plane_ref[z, pose] * piece
 
     copies[5].wait()
-    along_columns(0)
+    along_rows(0)
     copies[7].wait()
     copies[8].wait()
     for p in range(0, poses, 2):
@@ -195,8 +195,8 @@
         far_two = dot(far, two).astype(bf16)
         cols_fold[p] = jnp.concatenate([near_two[:, :cols], far_two[:, :cols]], 1)
         cols_fold[p + 1] = jnp.concatenate([near_two[:, cols:], far_two[:, cols:]], 1)
-    along_columns(1)
-    along_rows(0)
+    along_rows(1)
+    along_columns(0)
     copies[9].wait()
     rows_fold[...] = dot(
         rows_ref[...].reshape(poses * rows, box), near, ((1,), (1,))
@@ -207,9 +207,9 @@
         if step - 2 < count:
             mix(step - 2)
         if step - 1 < count:
-            along_rows(step - 1)
+            along_columns(step - 1)
         if step < count:
-            along_columns(step)
+            along_rows(step)
 
     if len(outs) == 1:
         outs[0][...] = totals[...].astype(bf16)
@@ -231,7 +231,7 @@
 SCRATCH = 20
 SLOTS = 3
 GROUP = 4
-Z_SLOTS = 5
+Z_SLOTS = 6
 
 
 def own_totals(images, class_index, pose_index, defocus_bin, defocus, rows_table, cols_table, plane_weight, turns_round):
@@ -503,8 +503,9 @@
         return lax.ppermute(value, "img", [(i, i ^ (2 * k)) for i in range(members)])
 
     order = [2, 3, 1] if rounds == 4 else list(range(1, rounds))
+    z_came = [along_z(z_sends[order[0]], order[0])]
     x_came = along_x(x_send)
-    z_came = [along_z(z_sends[k], k) for k in order]
+    z_came += [along_z(z_sends[k], k) for k in order[1:]]
     tables = own_ridges(defocus, plane_weight, rows_table, cols_table, owned)
     x_keep, tables = lax.optimization_barrier((x_keep, tables))
     x_own, z_own, z_send, *x_sends = middle(x_keep, z_keep, x_came, z_came)

time: 32.9 us -> 33.7 us (1.024)
  waiting for transfers between devices: 9.28 us -> 11 us
  starting transfers between devices: 12.8 us -> 12 us
    ppermute x2, waiting for transfers between devices: 2.52 us -> 3.57 us  [along_x(): return lax.ppermute(value, 'img', [(i, i ^ 1) for i in range(members)])]
    ppermute x2, starting transfers between devices: 4.5 us -> 3.54 us  [along_x(): return lax.ppermute(value, 'img', [(i, i ^ 1) for i in range(members)])]
    ppermute x6, waiting for transfers between devices: 6.76 us -> 7.48 us  [along_z(): return lax.ppermute(value, 'img', [(i, i ^ 2 * k) for i in range(members)])]
where the time goes in v10:
time: 33.7 us; the launch traced here: 33.6 us
  starting transfers between devices  12 us (36%)
  waiting for transfers between devices  11 us (33%)
  Pallas kernels  10.4 us (31%)
    ppermute x6, starting transfers between devices, along_z(): return lax.ppermute(value, 'img', [(i, i ^ 2 * k) for i in range(members)])  8.48 us
    ppermute x6, waiting for transfers between devices, along_z(): return lax.ppermute(value, 'img', [(i, i ^ 2 * k) for i in range(members)])  7.48 us
    pallas_call x1, Pallas kernels, own_totals(): pl.pallas_call(slices_kernel, out_shape=out_shape, in_specs=[any_place] *...  6.96 us
    ppermute x2, waiting for transfers between devices, along_x(): return lax.ppermute(value, 'img', [(i, i ^ 1) for i in range(members)])  3.57 us
    ppermute x2, starting transfers between devices, along_x(): return lax.ppermute(value, 'img', [(i, i ^ 1) for i in range(members)])  3.54 us
    pallas_call x1, Pallas kernels, own_ridges(): pl.pallas_call(ridge_kernel, out_shape=[table, table, jax.ShapeDtypeStruc...  2.09 us
    pallas_call x1, Pallas kernels, finish(): pl.pallas_call(finish_kernel, out_shape=jax.ShapeDtypeStruct((owned, 2 *...  1.25 us
  transfers between devices with their start and end apart: 8, of which 6 were waited for; matrix products, arithmetic and copies ran while one was open for 0% of the time, Pallas kernels for 6%

profile of v10, /device:TPU:0, one launch (start us, length us, event | category | flops | bytes accessed | tf_op | source)
XLA Modules:
  0.0 33.6 jit_solution(14245975221156311802)
XLA Ops:
  0.0 0.0 copy-start
  0.0 0.0 copy-start.1
  0.0 0.0 copy-start.2
  0.0 0.0 copy-start.3
  0.0 7.0 %shard_map.100 = (bf16[4,11,16,256]{3,2,1,0:T(8,128)(2,1)S(1)}, f32[4,11,16,256]{3,2,1,0:T(8,128)S(1)}, f32[2,6,16,256]{3,2,1,0:T(8,128)S(1)}, bf16[2,6,16,256]{...) custom-call(s32[16]{0:T(128)} %bitcast.5, s32[16]{0:T(128)} %pose_hbm.1, ...), custom_call_target="tpu_custom_call" | custom-call | flops 2097152000 | bytes 6291456 | tf_op jit(solution)/shard_map/pallas_call | solution.py:260
  7.0 3.0 %collective-permute-start = (bf16[4,11,16,256]{3,2,1,0:T(8,128)(2,1)S(1)}, bf16[4,11,16,256]{3,2,1,0:T(8,128)(2,1)S(1)}, u32[]{:S(2)}, u32[]{:S(2)}) collective-permute-start(bf16[4,11,16,256]{3,2,1,0:T(8,128)(2,1)S(1)} %get-tuple-element.33), channel_id=1, source_target_pairs={{0,2},{2,0},{4,6},{6,4},{8,10},{10,8},{12,14},{14,12},{1,3},{3,1},... | collective-permute-start | bytes 1081352 | tf_op jit(solution)/shard_map/ppermute | solution.py:500
  10.0 2.6 %collective-permute-start.1 = (bf16[2,6,16,256]{3,2,1,0:T(8,128)(2,1)S(1)}, bf16[2,6,16,256]{3,2,1,0:T(8,128)(2,1)S(1)}, u32[]{:S(2)}, u32[]{:S(2)}) collective-permute-start(bf16[2,6,16,256]{3,2,1,0:T(8,128)(2,1)S(1)} %get-tuple-element.34), channel_id=1, source_target_pairs={{0,8},{2,10},{4,12},{6,14},{8,0},{10,2},{12,4},{14,6},{1,9},{3,11}... | collective-permute-start | bytes 294920 | tf_op jit(solution)/shard_map/ppermute | solution.py:503
  12.6 1.3 %collective-permute-start.2 = (bf16[2,6,16,256]{3,2,1,0:T(8,128)(2,1)S(1)}, bf16[2,6,16,256]{3,2,1,0:T(8,128)(2,1)S(1)}, u32[]{:S(2)}, u32[]{:S(2)}) collective-permute-start(bf16[2,6,16,256]{3,2,1,0:T(8,128)(2,1)S(1)} %get-tuple-element.35), channel_id=1, source_target_pairs={{0,12},{2,14},{4,8},{6,10},{8,4},{10,6},{12,0},{14,2},{1,13},{3,15... | collective-permute-start | bytes 294920 | tf_op jit(solution)/shard_map/ppermute | solution.py:503
  13.9 0.2 collective-permute-start.3
  14.2 0.0 copy-done
  14.2 0.0 copy-done.1
  14.2 0.0 copy-done.2
  14.2 0.0 copy-done.3
  14.2 2.1 %shard_map.101 = (bf16[128,2048]{1,0:T(8,128)(2,1)S(1)}, bf16[128,2048]{1,0:T(8,128)(2,1)S(1)}, f32[16,128]{1,0:T(8,128)S(1)}) custom-call(f32[16]{0:T(128)S(1)} %copy-done.3, f32[2,8]{1,0:T(2,128)S(1)} %bitcast.4, bf16[8,128,256]{2,1,0:T(8,128)(2,1)S(1)} %copy-done, bf16[8,256,128]{2,1,0:T(8,128)(2,1)S(1)} %copy-done.1), custom_call_target="tpu_custom_call" | custom-call | flops 524288000 | bytes 2097152 | tf_op jit(solution)/shard_map/pallas_call | solution.py:354
  16.3 3.8 %collective-permute-done.1.refs_0_ = bf16[2,6,16,256]{3,2,1,0:T(8,128)(2,1)S(1)} collective-permute-done((bf16[2,6,16,256]{3,2,1,0:T(8,128)(2,1)S(1)}, bf16[2,6,16,256]{3,2,1,0:T(8,128)(2,1)S(1)}, u32[]{:S(2)}, u32[]{:S(2)}) %collective-permute-start.1) | collective-permute-done | bytes 98336 | tf_op jit(solution)/shard_map/ppermute | solution.py:503
  20.1 0.0 collective-permute-done.2.refs_1_
  20.1 0.4 %collective-permute-done.3.refs_2_ = bf16[2,6,16,256]{3,2,1,0:T(8,128)(2,1)S(1)} collective-permute-done((bf16[2,6,16,256]{3,2,1,0:T(8,128)(2,1)S(1)}, bf16[2,6,16,256]{3,2,1,0:T(8,128)(2,1)S(1)}, u32[]{:S(2)}, u32[]{:S(2)}) %collective-permute-start.3) | collective-permute-done | bytes 98336 | tf_op jit(solution)/shard_map/ppermute | solution.py:503
  20.5 0.0 collective-permute-done.x_came
  20.5 0.1 shard_map.102
  20.6 3.7 %collective-permute-start.5 = (bf16[11,16,256]{2,1,0:T(8,128)(2,1)S(1)}, bf16[11,16,256]{2,1,0:T(8,128)(2,1)S(1)}, u32[]{:S(2)}, u32[]{:S(2)}) collective-permute-start(bf16[11,16,256]{2,1,0:T(8,128)(2,1)S(1)} %get-tuple-element.40), channel_id=1, source_target_pairs={{0,8},{2,10},{4,12},{6,14},{8,0},{10,2},{12,4},{14,6},{1,9},{3,11}... | collective-permute-start | bytes 270344 | tf_op jit(solution)/shard_map/ppermute | solution.py:503
  24.3 0.4 %collective-permute-start.6 = (bf16[11,16,256]{2,1,0:T(8,128)(2,1)S(1)}, bf16[11,16,256]{2,1,0:T(8,128)(2,1)S(1)}, u32[]{:S(2)}, u32[]{:S(2)}) collective-permute-start(bf16[11,16,256]{2,1,0:T(8,128)(2,1)S(1)} %get-tuple-element.41), channel_id=1, source_target_pairs={{0,12},{2,14},{4,8},{6,10},{8,4},{10,6},{12,0},{14,2},{1,13},{3,15... | collective-permute-start | bytes 270344 | tf_op jit(solution)/shard_map/ppermute | solution.py:503
  24.7 0.2 collective-permute-start.7
  24.9 0.5 %collective-permute-start.4 = (bf16[6,16,256]{2,1,0:T(8,128)(2,1)S(1)}, bf16[6,16,256]{2,1,0:T(8,128)(2,1)S(1)}, u32[]{:S(2)}, u32[]{:S(2)}) collective-permute-start(bf16[6,16,256]{2,1,0:T(8,128)(2,1)S(1)} %get-tuple-element.39), channel_id=1, source_target_pairs={{0,2},{2,0},{4,6},{6,4},{8,10},{10,8},{12,14},{14,12},{1,3},{3,1},... | collective-permute-start | bytes 147464 | tf_op jit(solution)/shard_map/ppermute | solution.py:500
  25.4 3.6 %collective-permute-done.4.z_came = bf16[6,16,256]{2,1,0:T(8,128)(2,1)S(1)} collective-permute-done((bf16[6,16,256]{2,1,0:T(8,128)(2,1)S(1)}, bf16[6,16,256]{2,1,0:T(8,128)(2,1)S(1)}, u32[]{:S(2)}, u32[]{:S(2)}) %collective-permute-start.4) | collective-permute-done | bytes 49184 | tf_op jit(solution)/shard_map/ppermute | solution.py:500
  29.0 1.9 %collective-permute-done.5.refs_0_ = bf16[11,16,256]{2,1,0:T(8,128)(2,1)S(1)} collective-permute-done((bf16[11,16,256]{2,1,0:T(8,128)(2,1)S(1)}, bf16[11,16,256]{2,1,0:T(8,128)(2,1)S(1)}, u32[]{:S(2)}, u32[]{:S(2)}) %collective-permute-start.5) | collective-permute-done | bytes 90144 | tf_op jit(solution)/shard_map/ppermute | solution.py:503
  30.9 0.5 %collective-permute-done.6.refs_1_ = bf16[11,16,256]{2,1,0:T(8,128)(2,1)S(1)} collective-permute-done((bf16[11,16,256]{2,1,0:T(8,128)(2,1)S(1)}, bf16[11,16,256]{2,1,0:T(8,128)(2,1)S(1)}, u32[]{:S(2)}, u32[]{:S(2)}) %collective-permute-start.6) | collective-permute-done | bytes 90144 | tf_op jit(solution)/shard_map/ppermute | solution.py:503
  31.3 1.0 %collective-permute-done.7.refs_2_ = bf16[11,16,256]{2,1,0:T(8,128)(2,1)S(1)} collective-permute-done((bf16[11,16,256]{2,1,0:T(8,128)(2,1)S(1)}, bf16[11,16,256]{2,1,0:T(8,128)(2,1)S(1)}, u32[]{:S(2)}, u32[]{:S(2)}) %collective-permute-start.7) | collective-permute-done | bytes 90144 | tf_op jit(solution)/shard_map/ppermute | solution.py:503
  32.3 1.3 %shard_map.103 = f32[16,32,128]{2,1,0:T(8,128)} custom-call(bf16[128,2048]{1,0:T(8,128)(2,1)S(1)} %get-tuple-element.28.high_ref, bf16[128,2048]{1,0:T(8,128)(2,1)S(1)} %get-tuple-element.29.low_ref, f32[16,128]{1,0:T(8,128)S(1)} %get-tuple-element.30.share_ref, f32[11,16,256]{2,1,0:T(8,128)S(1)} %get-tuple-element.37.x_own, ...), custom_call_target="tpu_custom_call" | custom-call | flops 262144 | bytes 2097152 | tf_op jit(solution)/shard_map/pallas_call | solution.py:443
Async XLA Ops:
  0.0 14.2 %copy-start = (bf16[8,128,256]{2,1,0:T(8,128)(2,1)S(1)}, bf16[8,128,256]{2,1,0:T(8,128)(2,1)}, u32[]{:S(2)}) copy-start(bf16[8,128,256]{2,1,0:T(8,128)(2,1)} %rows_hbm.3) | copy-start | bytes 1572868
  0.0 14.2 %copy-start.1 = (bf16[8,256,128]{2,1,0:T(8,128)(2,1)S(1)}, bf16[8,256,128]{2,1,0:T(8,128)(2,1)}, u32[]{:S(2)}) copy-start(bf16[8,256,128]{2,1,0:T(8,128)(2,1)} %cols_hbm.3) | copy-start | bytes 1572868
  0.0 14.2 %copy-start.2 = (f32[8,2]{0,1:T(2,128)S(1)}, f32[8,2]{0,1:T(2,128)}, u32[]{:S(2)}) copy-start(f32[8,2]{0,1:T(2,128)} %param.17) | copy-start | bytes 196
  0.0 14.2 %copy-start.3 = (f32[16]{0:T(128)S(1)}, f32[16]{0:T(128)}, u32[]{:S(2)}) copy-start(f32[16]{0:T(128)} %defocus_hbm.3) | copy-start | bytes 196
  7.0 13.5 %collective-permute-start = (bf16[4,11,16,256]{3,2,1,0:T(8,128)(2,1)S(1)}, bf16[4,11,16,256]{3,2,1,0:T(8,128)(2,1)S(1)}, u32[]{:S(2)}, u32[]{:S(2)}) collective-permute-start(bf16[4,11,16,256]{3,2,1,0:T(8,128)(2,1)S(1)} %get-tuple-element.33), channel_id=1, source_target_pairs={{0,2},{2,0},{4,6},{6,4},{8,10},{10,8},{12,14},{14,12},{1,3},{3,1},... | collective-permute-start | bytes 1081352 | tf_op jit(solution)/shard_map/ppermute | solution.py:500
  10.0 10.1 %collective-permute-start.1 = (bf16[2,6,16,256]{3,2,1,0:T(8,128)(2,1)S(1)}, bf16[2,6,16,256]{3,2,1,0:T(8,128)(2,1)S(1)}, u32[]{:S(2)}, u32[]{:S(2)}) collective-permute-start(bf16[2,6,16,256]{3,2,1,0:T(8,128)(2,1)S(1)} %get-tuple-element.34), channel_id=1, source_target_pairs={{0,8},{2,10},{4,12},{6,14},{8,0},{10,2},{12,4},{14,6},{1,9},{3,11}... | collective-permute-start | bytes 294920 | tf_op jit(solution)/shard_map/ppermute | solution.py:503
  12.6 7.5 %collective-permute-start.2 = (bf16[2,6,16,256]{3,2,1,0:T(8,128)(2,1)S(1)}, bf16[2,6,16,256]{3,2,1,0:T(8,128)(2,1)S(1)}, u32[]{:S(2)}, u32[]{:S(2)}) collective-permute-start(bf16[2,6,16,256]{3,2,1,0:T(8,128)(2,1)S(1)} %get-tuple-element.35), channel_id=1, source_target_pairs={{0,12},{2,14},{4,8},{6,10},{8,4},{10,6},{12,0},{14,2},{1,13},{3,15... | collective-permute-start | bytes 294920 | tf_op jit(solution)/shard_map/ppermute | solution.py:503
  13.9 6.5 %collective-permute-start.3 = (bf16[2,6,16,256]{3,2,1,0:T(8,128)(2,1)S(1)}, bf16[2,6,16,256]{3,2,1,0:T(8,128)(2,1)S(1)}, u32[]{:S(2)}, u32[]{:S(2)}) collective-permute-start(bf16[2,6,16,256]{3,2,1,0:T(8,128)(2,1)S(1)} %get-tuple-element.36), channel_id=1, source_target_pairs={{0,4},{2,6},{4,0},{6,2},{8,12},{10,14},{12,8},{14,10},{1,5},{3,7},... | collective-permute-start | bytes 294920 | tf_op jit(solution)/shard_map/ppermute | solution.py:503
  20.6 10.3 %collective-permute-start.5 = (bf16[11,16,256]{2,1,0:T(8,128)(2,1)S(1)}, bf16[11,16,256]{2,1,0:T(8,128)(2,1)S(1)}, u32[]{:S(2)}, u32[]{:S(2)}) collective-permute-start(bf16[11,16,256]{2,1,0:T(8,128)(2,1)S(1)} %get-tuple-element.40), channel_id=1, source_target_pairs={{0,8},{2,10},{4,12},{6,14},{8,0},{10,2},{12,4},{14,6},{1,9},{3,11}... | collective-permute-start | bytes 270344 | tf_op jit(solution)/shard_map/ppermute | solution.py:503
  24.3 7.1 %collective-permute-start.6 = (bf16[11,16,256]{2,1,0:T(8,128)(2,1)S(1)}, bf16[11,16,256]{2,1,0:T(8,128)(2,1)S(1)}, u32[]{:S(2)}, u32[]{:S(2)}) collective-permute-start(bf16[11,16,256]{2,1,0:T(8,128)(2,1)S(1)} %get-tuple-element.41), channel_id=1, source_target_pairs={{0,12},{2,14},{4,8},{6,10},{8,4},{10,6},{12,0},{14,2},{1,13},{3,15... | collective-permute-start | bytes 270344 | tf_op jit(solution)/shard_map/ppermute | solution.py:503
  24.7 7.6 %collective-permute-start.7 = (bf16[11,16,256]{2,1,0:T(8,128)(2,1)S(1)}, bf16[11,16,256]{2,1,0:T(8,128)(2,1)S(1)}, u32[]{:S(2)}, u32[]{:S(2)}) collective-permute-start(bf16[11,16,256]{2,1,0:T(8,128)(2,1)S(1)} %get-tuple-element.42), channel_id=1, source_target_pairs={{0,4},{2,6},{4,0},{6,2},{8,12},{10,14},{12,8},{14,10},{1,5},{3,7},... | collective-permute-start | bytes 270344 | tf_op jit(solution)/shard_map/ppermute | solution.py:503
  24.9 4.1 %collective-permute-start.4 = (bf16[6,16,256]{2,1,0:T(8,128)(2,1)S(1)}, bf16[6,16,256]{2,1,0:T(8,128)(2,1)S(1)}, u32[]{:S(2)}, u32[]{:S(2)}) collective-permute-start(bf16[6,16,256]{2,1,0:T(8,128)(2,1)S(1)} %get-tuple-element.39), channel_id=1, source_target_pairs={{0,2},{2,0},{4,6},{6,4},{8,10},{10,8},{12,14},{14,12},{1,3},{3,1},... | collective-permute-start | bytes 147464 | tf_op jit(solution)/shard_map/ppermute | solution.py:500

commit v11 on v10

--- a/solution.py
+++ b/solution.py
@@ -214,15 +214,18 @@
     if len(outs) == 1:
         outs[0][...] = totals[...].astype(bf16)
         return
-    x_send, x_keep, z_keep = outs[:3]
-    z_sends = outs[3:]
-    rounds, x_slots, owned, _ = x_keep.shape
+    far_send, far_keep, near_send, near_keep, z_keep = outs[:5]
+    z_sends = outs[5:]
+    _, x_slots, owned, _ = near_keep.shape
+    rounds = len(z_sends) + 1
     me = lax.axis_index("img")
+    near = near_keep.shape[0]
     for k in range(rounds):
         mine = pl.ds(pl.multiple_of((me ^ (2 * k)) * owned, owned), owned)
         theirs = pl.ds(pl.multiple_of((me ^ (2 * k + 1)) * owned, owned), owned)
-        x_keep[k] = totals[-x_slots:, mine, :]
-        x_send[k] = totals[-x_slots:, theirs, :].astype(bf16)
+        keep, send, n = (near_keep, near_send, k) if k < near else (far_keep, far_send, k - near)
+        keep[n] = totals[-x_slots:, mine, :]
+        send[n] = totals[-x_slots:, theirs, :].astype(bf16)
         z_out = z_keep if k == 0 else z_sends[k - 1]
         z_out[0] = totals[:-x_slots, mine, :].astype(z_out.dtype)
         z_out[1] = totals[:-x_slots, theirs, :].astype(z_out.dtype)
@@ -231,7 +234,7 @@
 SCRATCH = 20
 SLOTS = 3
 GROUP = 4
-Z_SLOTS = 6
+Z_SLOTS = 3
 
 
 def own_totals(images, class_index, pose_index, defocus_bin, defocus, rows_table, cols_table, plane_weight, turns_round):
@@ -248,9 +251,11 @@
         out_shape = [jax.ShapeDtypeStruct((slots, rows, 2 * cols), bf16)]
     else:
         slots += 1
-        x_piece = (turns_round, slots - Z_SLOTS, rows // (2 * turns_round), 2 * cols)
-        z_piece = (2, Z_SLOTS, rows // (2 * turns_round), 2 * cols)
-        out_shape = [pltpu.VMEM(x_piece, bf16), pltpu.VMEM(x_piece, f32), pltpu.VMEM(z_piece, f32)]
+        owned = rows // (2 * turns_round)
+        x_piece = (turns_round // 2, slots - Z_SLOTS, owned, 2 * cols)
+        z_piece = (2, Z_SLOTS, owned, 2 * cols)
+        out_shape = [pltpu.VMEM(x_piece, bf16), pltpu.VMEM(x_piece, f32)] * 2
+        out_shape += [pltpu.VMEM(z_piece, f32)]
         out_shape += [pltpu.VMEM(z_piece, bf16)] * (turns_round - 1)
     operands = (
         class_index[:, 0], pose_index, defocus_bin, defocus, plane_weight.T,
@@ -365,18 +370,32 @@
         ],
         compiler_params=pltpu.CompilerParams(vmem_limit_bytes=16 * 1024 * 1024),
         cost_estimate=pl.CostEstimate(
-            flops=2 * poses * 1000 * 128 * 256, bytes_accessed=2 * 1024 * 1024, transcendentals=0
+            flops=1000, bytes_accessed=1000, transcendentals=0
         ),
     )(defocus, planes, rows_table, cols_table)
 
 
-def middle_kernel(x_keep, z_keep, x_came, *refs):
-    rounds = x_keep.shape[0]
-    z_came, outs = refs[: rounds - 1], refs[rounds - 1 :]
-    x_own, z_own, z_send = outs[:3]
-    x_own[...] = x_keep[0] + x_came[0].astype(f32)
-    for k in range(1, rounds):
-        outs[2 + k][...] = (x_keep[k] + x_came[k].astype(f32)).astype(bf16)
+def call_in_vmem(kernel, arrays, out_shape):
+    vmem = pl.BlockSpec(memory_space=pltpu.VMEM)
+    return pl.pallas_call(
+        kernel,
+        out_shape=out_shape,
+        in_specs=[vmem] * len(arrays),
+        out_specs=[vmem] * len(out_shape),
+        compiler_params=pltpu.CompilerParams(vmem_limit_bytes=16 * 1024 * 1024),
+        cost_estimate=pl.CostEstimate(flops=1000, bytes_accessed=1000, transcendentals=0),
+    )(*arrays)
+
+
+def fold_kernel(far_keep, far_came, near_send, z_keep, *refs):
+    rounds = near_send.shape[0] + far_keep.shape[0]
+    z_came, refs = refs[: rounds - 1], refs[rounds - 1 :]
+    z_own, x_send, far_sends = refs[0], refs[1], refs[2:]
+    for k, send in enumerate(far_sends):
+        send[...] = (far_keep[k] + far_came[k].astype(f32)).astype(bf16)
+    near, x_slots = near_send.shape[:2]
+    for k in range(near):
+        x_send[k * x_slots : (k + 1) * x_slots] = near_send[k]
     for side in range(2):
         value = z_keep[side]
         for came in z_came:
@@ -384,23 +403,32 @@
         if side == 0:
             z_own[...] = value
         else:
-            z_send[...] = value.astype(bf16)
-
-
-def middle(x_keep, z_keep, x_came, z_came):
-    rounds, x_slots, owned, wide = x_keep.shape
-    vmem = pl.BlockSpec(memory_space=pltpu.VMEM)
-    x_piece, z_piece = x_keep.shape[1:], z_keep.shape[1:]
-    out_shape = [pltpu.VMEM(x_piece, f32), pltpu.VMEM(z_piece, f32), pltpu.VMEM(z_piece, bf16)]
-    out_shape += [pltpu.VMEM(x_piece, bf16)] * (rounds - 1)
-    return pl.pallas_call(
-        middle_kernel,
-        out_shape=out_shape,
-        in_specs=[vmem] * (3 + len(z_came)),
-        out_specs=[vmem] * len(out_shape),
-        compiler_params=pltpu.CompilerParams(vmem_limit_bytes=16 * 1024 * 1024),
-        cost_estimate=pl.CostEstimate(flops=1000000, bytes_accessed=4 * 1024 * 1024, transcendentals=0),
-    )(x_keep, z_keep, x_came, *z_came)
+            x_send[near * x_slots :] = value.astype(bf16)
+
+
+def fold_phase(far_keep, far_came, near_send, z_keep, z_came):
+    far, x_slots = far_keep.shape[:2]
+    z_slots = z_keep.shape[1]
+    tail = far_keep.shape[2:]
+    out_shape = [
+        pltpu.VMEM((z_slots,) + tail, f32),
+        pltpu.VMEM((near_send.shape[0] * x_slots + z_slots,) + tail, bf16),
+    ]
+    out_shape += [pltpu.VMEM((x_slots,) + tail, bf16)] * far
+    return call_in_vmem(fold_kernel, (far_keep, far_came, near_send, z_keep, *z_came), out_shape)
+
+
+def near_kernel(keep, came, own, *sends):
+    near, x_slots = keep.shape[:2]
+    for k, out in enumerate((own,) + sends):
+        part = came[k * x_slots : (k + 1) * x_slots].astype(f32)
+        out[...] = (keep[k] + part).astype(out.dtype)
+
+
+def near_phase(keep, came):
+    piece = keep.shape[1:]
+    out_shape = [pltpu.VMEM(piece, f32)] + [pltpu.VMEM(piece, bf16)] * (keep.shape[0] - 1)
+    return call_in_vmem(near_kernel, (keep, came), out_shape)
 
 
 def finish_kernel(high_ref, low_ref, share_ref, x_own, z_own, z_came, *refs):
@@ -412,7 +440,7 @@
 
     def summed(s):
         if s < first:
-            return z_own[s] + z_came[s].astype(f32)
+            return z_own[s] + z_came[z_came.shape[0] - first + s].astype(f32)
         value = x_own[s - first]
         for part in x_came:
             value = value + part[s - first].astype(f32)
@@ -493,8 +521,9 @@
     outs = own_totals(
         images, class_index, pose_index, defocus_bin, defocus, rows_table, cols_table, plane_weight, rounds
     )
-    x_send, x_keep, z_keep = outs[:3]
-    z_sends = dict(zip(range(1, rounds), outs[3:]))
+    far_send, far_keep, near_send, near_keep, z_keep = outs[:5]
+    z_sends = outs[5:]
+    near = near_keep.shape[0]
 
     def along_x(value):
         return lax.ppermute(value, "img", [(i, i ^ 1) for i in range(members)])
@@ -502,15 +531,16 @@
     def along_z(value, k):
         return lax.ppermute(value, "img", [(i, i ^ (2 * k)) for i in range(members)])
 
-    order = [2, 3, 1] if rounds == 4 else list(range(1, rounds))
-    z_came = [along_z(z_sends[order[0]], order[0])]
-    x_came = along_x(x_send)
-    z_came += [along_z(z_sends[k], k) for k in order[1:]]
+    far_ks, near_ks = range(near, rounds), range(1, near)
+    far_came = along_x(far_send)
+    z_came = [along_z(z_sends[k - 1], k) for k in (*far_ks, *near_ks)]
     tables = own_ridges(defocus, plane_weight, rows_table, cols_table, owned)
-    x_keep, tables = lax.optimization_barrier((x_keep, tables))
-    x_own, z_own, z_send, *x_sends = middle(x_keep, z_keep, x_came, z_came)
-    x_came = [along_z(x_sends[k - 1], k) for k in order]
-    z_came = along_x(z_send)
+    far_keep, tables = lax.optimization_barrier((far_keep, tables))
+    z_own, x_send, *x_sends = fold_phase(far_keep, far_came, near_send, z_keep, z_came)
+    z_came = along_x(x_send)
+    x_came = [along_z(send, k) for send, k in zip(x_sends, far_ks)]
+    x_own, *x_sends = near_phase(near_keep, z_came)
+    x_came += [along_z(send, k) for send, k in zip(x_sends, near_ks)]
     out = finish(tables, x_own, z_own, z_came, x_came)
     return out.reshape(owned, CLASSES, planes, 2, cols)
 
@@ -539,7 +569,7 @@
     rows = arrays[5].shape[1]
     members = lax.axis_size("img")
     images = members * arrays[0].shape[0]
-    small = members > 1 and members & (members - 1) == 0 and images <= 256 and rows % (16 * members) == 0
+    small = members >= 4 and members & (members - 1) == 0 and images <= 256 and rows % (16 * members) == 0
     return (by_rounds if small else by_scatter)(*arrays)
 
 

time: 33.7 us -> 31.8 us (0.944)
  starting transfers between devices: 12 us -> 10.9 us
  waiting for transfers between devices: 11 us -> 10.3 us
    ppermute x6, starting transfers between devices: 8.48 us -> 7.32 us  [along_z(): return lax.ppermute(value, 'img', [(i, i ^ 2 * k) for i in range(members)])]
    ppermute x6, waiting for transfers between devices: 7.48 us -> 6.87 us  [along_z(): return lax.ppermute(value, 'img', [(i, i ^ 2 * k) for i in range(members)])]
  transfers between devices with their start and end apart: 8 -> 8, of which waited for: 6 -> 4; matrix products, arithmetic and copies ran while one was open for 0% -> 0% of each run, Pallas kernels for 6% -> 7%
where the time goes in v11:
time: 31.8 us; the launch traced here: 31.7 us
  starting transfers between devices  10.9 us (34%)
  Pallas kernels  10.4 us (33%)
  waiting for transfers between devices  10.3 us (32%)
    ppermute x6, starting transfers between devices, along_z(): return lax.ppermute(value, 'img', [(i, i ^ 2 * k) for i in range(members)])  7.32 us
    pallas_call x1, Pallas kernels, own_totals(): pl.pallas_call(slices_kernel, out_shape=out_shape, in_specs=[any_place] *...  6.97 us
    ppermute x6, waiting for transfers between devices, along_z(): return lax.ppermute(value, 'img', [(i, i ^ 2 * k) for i in range(members)])  6.87 us
    ppermute x2, starting transfers between devices, along_x(): return lax.ppermute(value, 'img', [(i, i ^ 1) for i in range(members)])  3.62 us
    ppermute x2, waiting for transfers between devices, along_x(): return lax.ppermute(value, 'img', [(i, i ^ 1) for i in range(members)])  3.39 us
    pallas_call x1, Pallas kernels, own_ridges(): pl.pallas_call(ridge_kernel, out_shape=[table, table, jax.ShapeDtypeStruc...  2.09 us
    pallas_call x1, Pallas kernels, finish(): pl.pallas_call(finish_kernel, out_shape=jax.ShapeDtypeStruct((owned, 2 *...  1.25 us
  transfers between devices with their start and end apart: 8, of which 4 were waited for; matrix products, arithmetic and copies ran while one was open for 0% of the time, Pallas kernels for 7%

profile of v11, /device:TPU:0, one launch (start us, length us, event | category | flops | bytes accessed | tf_op | source)
XLA Modules:
  0.0 31.7 jit_solution(7034495248738540984)
XLA Ops:
  0.0 0.0 copy-start
  0.0 0.0 copy-start.1
  0.0 0.0 copy-start.2
  0.0 0.0 copy-start.3
  0.0 7.0 %shard_map.100 = (bf16[2,14,16,256]{3,2,1,0:T(8,128)(2,1)S(1)}, f32[2,14,16,256]{3,2,1,0:T(8,128)S(1)}, bf16[2,14,16,256]{3,2,1,0:T(8,128)(2,1)S(1)}, f32[2,14,1...) custom-call(s32[16]{0:T(128)} %bitcast.5, ...), custom_call_target="tpu_custom_call" | custom-call | flops 2097152000 | bytes 6291456 | tf_op jit(solution)/shard_map/pallas_call | solution.py:265
  7.0 3.0 %collective-permute-start = (bf16[2,14,16,256]{3,2,1,0:T(8,128)(2,1)S(1)}, bf16[2,14,16,256]{3,2,1,0:T(8,128)(2,1)S(1)}, u32[]{:S(2)}, u32[]{:S(2)}) collective-permute-start(bf16[2,14,16,256]{3,2,1,0:T(8,128)(2,1)S(1)} %get-tuple-element.35), channel_id=1, source_target_pairs={{0,2},{2,0},{4,6},{6,4},{8,10},{10,8},{12,14},{14,12},{1,3},{3,1},... | collective-permute-start | bytes 688136 | tf_op jit(solution)/shard_map/ppermute | solution.py:529
  10.0 2.6 %collective-permute-start.1 = (bf16[2,3,16,256]{3,2,1,0:T(8,128)(2,1)S(1)}, bf16[2,3,16,256]{3,2,1,0:T(8,128)(2,1)S(1)}, u32[]{:S(2)}, u32[]{:S(2)}) collective-permute-start(bf16[2,3,16,256]{3,2,1,0:T(8,128)(2,1)S(1)} %get-tuple-element.38), channel_id=1, source_target_pairs={{0,8},{2,10},{4,12},{6,14},{8,0},{10,2},{12,4},{14,6},{1,9},{3,11}... | collective-permute-start | bytes 147464 | tf_op jit(solution)/shard_map/ppermute | solution.py:532
  12.6 1.3 %collective-permute-start.2 = (bf16[2,3,16,256]{3,2,1,0:T(8,128)(2,1)S(1)}, bf16[2,3,16,256]{3,2,1,0:T(8,128)(2,1)S(1)}, u32[]{:S(2)}, u32[]{:S(2)}) collective-permute-start(bf16[2,3,16,256]{3,2,1,0:T(8,128)(2,1)S(1)} %get-tuple-element.39), channel_id=1, source_target_pairs={{0,12},{2,14},{4,8},{6,10},{8,4},{10,6},{12,0},{14,2},{1,13},{3,15... | collective-permute-start | bytes 147464 | tf_op jit(solution)/shard_map/ppermute | solution.py:532
  13.9 0.2 collective-permute-start.3
  14.2 0.0 copy-done
  14.2 0.0 copy-done.1
  14.2 0.0 copy-done.2
  14.2 0.0 copy-done.3
  14.2 2.1 %shard_map.101 = (bf16[128,2048]{1,0:T(8,128)(2,1)S(1)}, bf16[128,2048]{1,0:T(8,128)(2,1)S(1)}, f32[16,128]{1,0:T(8,128)S(1)}) custom-call(f32[16]{0:T(128)S(1)} %copy-done.3, f32[2,8]{1,0:T(2,128)S(1)} %bitcast.4, bf16[8,128,256]{2,1,0:T(8,128)(2,1)S(1)} %copy-done, bf16[8,256,128]{2,1,0:T(8,128)(2,1)S(1)} %copy-done.1), custom_call_target="tpu_custom_call" | custom-call | flops 1000 | bytes 1000 | tf_op jit(solution)/shard_map/pallas_call | solution.py:359
  16.3 0.0 collective-permute-done.1.refs_0_
  16.3 2.3 %collective-permute-done.2.refs_1_ = bf16[2,3,16,256]{3,2,1,0:T(8,128)(2,1)S(1)} collective-permute-done((bf16[2,3,16,256]{3,2,1,0:T(8,128)(2,1)S(1)}, bf16[2,3,16,256]{3,2,1,0:T(8,128)(2,1)S(1)}, u32[]{:S(2)}, u32[]{:S(2)}) %collective-permute-start.2) | collective-permute-done | bytes 49184 | tf_op jit(solution)/shard_map/ppermute | solution.py:532
  18.6 0.0 collective-permute-done.3.refs_2_
  18.6 0.0 collective-permute-done.far_came
  18.6 0.1 shard_map.102
  18.6 0.6 %collective-permute-start.4 = (bf16[31,16,256]{2,1,0:T(8,128)(2,1)S(1)}, bf16[31,16,256]{2,1,0:T(8,128)(2,1)S(1)}, u32[]{:S(2)}, u32[]{:S(2)}) collective-permute-start(bf16[31,16,256]{2,1,0:T(8,128)(2,1)S(1)} %get-tuple-element.41), channel_id=1, source_target_pairs={{0,2},{2,0},{4,6},{6,4},{8,10},{10,8},{12,14},{14,12},{1,3},{3,1},... | collective-permute-start | bytes 761864 | tf_op jit(solution)/shard_map/ppermute | solution.py:529
  19.2 1.3 %collective-permute-start.5 = (bf16[14,16,256]{2,1,0:T(8,128)(2,1)S(1)}, bf16[14,16,256]{2,1,0:T(8,128)(2,1)S(1)}, u32[]{:S(2)}, u32[]{:S(2)}) collective-permute-start(bf16[14,16,256]{2,1,0:T(8,128)(2,1)S(1)} %get-tuple-element.44), channel_id=1, source_target_pairs={{0,8},{2,10},{4,12},{6,14},{8,0},{10,2},{12,4},{14,6},{1,9},{3,11}... | collective-permute-start | bytes 344072 | tf_op jit(solution)/shard_map/ppermute | solution.py:532
  20.5 1.1 %collective-permute-start.6 = (bf16[14,16,256]{2,1,0:T(8,128)(2,1)S(1)}, bf16[14,16,256]{2,1,0:T(8,128)(2,1)S(1)}, u32[]{:S(2)}, u32[]{:S(2)}) collective-permute-start(bf16[14,16,256]{2,1,0:T(8,128)(2,1)S(1)} %get-tuple-element.45), channel_id=1, source_target_pairs={{0,12},{2,14},{4,8},{6,10},{8,4},{10,6},{12,0},{14,2},{1,13},{3,15... | collective-permute-start | bytes 344072 | tf_op jit(solution)/shard_map/ppermute | solution.py:532
  21.6 3.4 %collective-permute-done.4.came.z_came = bf16[31,16,256]{2,1,0:T(8,128)(2,1)S(1)} collective-permute-done((bf16[31,16,256]{2,1,0:T(8,128)(2,1)S(1)}, bf16[31,16,256]{2,1,0:T(8,128)(2,1)S(1)}, u32[]{:S(2)}, u32[]{:S(2)}) %collective-permute-start.4) | collective-permute-done | bytes 253984 | tf_op jit(solution)/shard_map/ppermute | solution.py:529
  25.0 0.8 %collective-permute-start.7 = (bf16[14,16,256]{2,1,0:T(8,128)(2,1)S(1)}, bf16[14,16,256]{2,1,0:T(8,128)(2,1)S(1)}, u32[]{:S(2)}, u32[]{:S(2)}) collective-permute-start(bf16[14,16,256]{2,1,0:T(8,128)(2,1)S(1)} %get-tuple-element.46), channel_id=1, source_target_pairs={{0,4},{2,6},{4,0},{6,2},{8,12},{10,14},{12,8},{14,10},{1,5},{3,7},... | collective-permute-start | bytes 344072 | tf_op jit(solution)/shard_map/ppermute | solution.py:532
  25.8 3.3 %collective-permute-done.5.refs_0_ = bf16[14,16,256]{2,1,0:T(8,128)(2,1)S(1)} collective-permute-done((bf16[14,16,256]{2,1,0:T(8,128)(2,1)S(1)}, bf16[14,16,256]{2,1,0:T(8,128)(2,1)S(1)}, u32[]{:S(2)}, u32[]{:S(2)}) %collective-permute-start.5) | collective-permute-done | bytes 114720 | tf_op jit(solution)/shard_map/ppermute | solution.py:532
  29.2 0.0 collective-permute-done.6.refs_1_
  29.2 1.3 %collective-permute-done.7.refs_2_ = bf16[14,16,256]{2,1,0:T(8,128)(2,1)S(1)} collective-permute-done((bf16[14,16,256]{2,1,0:T(8,128)(2,1)S(1)}, bf16[14,16,256]{2,1,0:T(8,128)(2,1)S(1)}, u32[]{:S(2)}, u32[]{:S(2)}) %collective-permute-start.7) | collective-permute-done | bytes 114720 | tf_op jit(solution)/shard_map/ppermute | solution.py:532
  30.4 1.2 %shard_map.104 = f32[16,32,128]{2,1,0:T(8,128)} custom-call(bf16[128,2048]{1,0:T(8,128)(2,1)S(1)} %get-tuple-element.30.high_ref, bf16[128,2048]{1,0:T(8,128)(2,1)S(1)} %get-tuple-element.31.low_ref, f32[16,128]{1,0:T(8,128)S(1)} %get-tuple-element.32.share_ref, f32[14,16,256]{2,1,0:T(8,128)S(1)} %get-tuple-element.42.x_own, ...), custom_call_target="tpu_custom_call" | custom-call | flops 262144 | bytes 2097152 | tf_op jit(solution)/shard_map/pallas_call | solution.py:471
  (1 shorter events, 0.0 us)
Async XLA Ops:
  0.0 14.2 %copy-start = (bf16[8,128,256]{2,1,0:T(8,128)(2,1)S(1)}, bf16[8,128,256]{2,1,0:T(8,128)(2,1)}, u32[]{:S(2)}) copy-start(bf16[8,128,256]{2,1,0:T(8,128)(2,1)} %rows_hbm.3) | copy-start | bytes 1572868
  0.0 14.2 %copy-start.1 = (bf16[8,256,128]{2,1,0:T(8,128)(2,1)S(1)}, bf16[8,256,128]{2,1,0:T(8,128)(2,1)}, u32[]{:S(2)}) copy-start(bf16[8,256,128]{2,1,0:T(8,128)(2,1)} %cols_hbm.3) | copy-start | bytes 1572868
  0.0 14.2 %copy-start.2 = (f32[8,2]{0,1:T(2,128)S(1)}, f32[8,2]{0,1:T(2,128)}, u32[]{:S(2)}) copy-start(f32[8,2]{0,1:T(2,128)} %param.17) | copy-start | bytes 196
  0.0 14.2 %copy-start.3 = (f32[16]{0:T(128)S(1)}, f32[16]{0:T(128)}, u32[]{:S(2)}) copy-start(f32[16]{0:T(128)} %defocus_hbm.3) | copy-start | bytes 196
  7.0 11.6 %collective-permute-start = (bf16[2,14,16,256]{3,2,1,0:T(8,128)(2,1)S(1)}, bf16[2,14,16,256]{3,2,1,0:T(8,128)(2,1)S(1)}, u32[]{:S(2)}, u32[]{:S(2)}) collective-permute-start(bf16[2,14,16,256]{3,2,1,0:T(8,128)(2,1)S(1)} %get-tuple-element.35), channel_id=1, source_target_pairs={{0,2},{2,0},{4,6},{6,4},{8,10},{10,8},{12,14},{14,12},{1,3},{3,1},... | collective-permute-start | bytes 688136 | tf_op jit(solution)/shard_map/ppermute | solution.py:529
  10.0 6.3 %collective-permute-start.1 = (bf16[2,3,16,256]{3,2,1,0:T(8,128)(2,1)S(1)}, bf16[2,3,16,256]{3,2,1,0:T(8,128)(2,1)S(1)}, u32[]{:S(2)}, u32[]{:S(2)}) collective-permute-start(bf16[2,3,16,256]{3,2,1,0:T(8,128)(2,1)S(1)} %get-tuple-element.38), channel_id=1, source_target_pairs={{0,8},{2,10},{4,12},{6,14},{8,0},{10,2},{12,4},{14,6},{1,9},{3,11}... | collective-permute-start | bytes 147464 | tf_op jit(solution)/shard_map/ppermute | solution.py:532
  12.6 6.0 %collective-permute-start.2 = (bf16[2,3,16,256]{3,2,1,0:T(8,128)(2,1)S(1)}, bf16[2,3,16,256]{3,2,1,0:T(8,128)(2,1)S(1)}, u32[]{:S(2)}, u32[]{:S(2)}) collective-permute-start(bf16[2,3,16,256]{3,2,1,0:T(8,128)(2,1)S(1)} %get-tuple-element.39), channel_id=1, source_target_pairs={{0,12},{2,14},{4,8},{6,10},{8,4},{10,6},{12,0},{14,2},{1,13},{3,15... | collective-permute-start | bytes 147464 | tf_op jit(solution)/shard_map/ppermute | solution.py:532
  13.9 4.6 %collective-permute-start.3 = (bf16[2,3,16,256]{3,2,1,0:T(8,128)(2,1)S(1)}, bf16[2,3,16,256]{3,2,1,0:T(8,128)(2,1)S(1)}, u32[]{:S(2)}, u32[]{:S(2)}) collective-permute-start(bf16[2,3,16,256]{3,2,1,0:T(8,128)(2,1)S(1)} %get-tuple-element.40), channel_id=1, source_target_pairs={{0,4},{2,6},{4,0},{6,2},{8,12},{10,14},{12,8},{14,10},{1,5},{3,7},... | collective-permute-start | bytes 147464 | tf_op jit(solution)/shard_map/ppermute | solution.py:532
  18.6 6.3 %collective-permute-start.4 = (bf16[31,16,256]{2,1,0:T(8,128)(2,1)S(1)}, bf16[31,16,256]{2,1,0:T(8,128)(2,1)S(1)}, u32[]{:S(2)}, u32[]{:S(2)}) collective-permute-start(bf16[31,16,256]{2,1,0:T(8,128)(2,1)S(1)} %get-tuple-element.41), channel_id=1, source_target_pairs={{0,2},{2,0},{4,6},{6,4},{8,10},{10,8},{12,14},{14,12},{1,3},{3,1},... | collective-permute-start | bytes 761864 | tf_op jit(solution)/shard_map/ppermute | solution.py:529
  19.2 9.9 %collective-permute-start.5 = (bf16[14,16,256]{2,1,0:T(8,128)(2,1)S(1)}, bf16[14,16,256]{2,1,0:T(8,128)(2,1)S(1)}, u32[]{:S(2)}, u32[]{:S(2)}) collective-permute-start(bf16[14,16,256]{2,1,0:T(8,128)(2,1)S(1)} %get-tuple-element.44), channel_id=1, source_target_pairs={{0,8},{2,10},{4,12},{6,14},{8,0},{10,2},{12,4},{14,6},{1,9},{3,11}... | collective-permute-start | bytes 344072 | tf_op jit(solution)/shard_map/ppermute | solution.py:532
  20.5 8.7 %collective-permute-start.6 = (bf16[14,16,256]{2,1,0:T(8,128)(2,1)S(1)}, bf16[14,16,256]{2,1,0:T(8,128)(2,1)S(1)}, u32[]{:S(2)}, u32[]{:S(2)}) collective-permute-start(bf16[14,16,256]{2,1,0:T(8,128)(2,1)S(1)} %get-tuple-element.45), channel_id=1, source_target_pairs={{0,12},{2,14},{4,8},{6,10},{8,4},{10,6},{12,0},{14,2},{1,13},{3,15... | collective-permute-start | bytes 344072 | tf_op jit(solution)/shard_map/ppermute | solution.py:532
  25.0 5.4 %collective-permute-start.7 = (bf16[14,16,256]{2,1,0:T(8,128)(2,1)S(1)}, bf16[14,16,256]{2,1,0:T(8,128)(2,1)S(1)}, u32[]{:S(2)}, u32[]{:S(2)}) collective-permute-start(bf16[14,16,256]{2,1,0:T(8,128)(2,1)S(1)} %get-tuple-element.46), channel_id=1, source_target_pairs={{0,4},{2,6},{4,0},{6,2},{8,12},{10,14},{12,8},{14,10},{1,5},{3,7},... | collective-permute-start | bytes 344072 | tf_op jit(solution)/shard_map/ppermute | solution.py:532

commit v12 on v11

--- a/solution.py
+++ b/solution.py
@@ -214,21 +214,21 @@
     if len(outs) == 1:
         outs[0][...] = totals[...].astype(bf16)
         return
-    far_send, far_keep, near_send, near_keep, z_keep = outs[:5]
-    z_sends = outs[5:]
+    far_send, far_keep, near_send, near_keep, z_send, z_keep = outs
     _, x_slots, owned, _ = near_keep.shape
-    rounds = len(z_sends) + 1
     me = lax.axis_index("img")
-    near = near_keep.shape[0]
-    for k in range(rounds):
-        mine = pl.ds(pl.multiple_of((me ^ (2 * k)) * owned, owned), owned)
-        theirs = pl.ds(pl.multiple_of((me ^ (2 * k + 1)) * owned, owned), owned)
-        keep, send, n = (near_keep, near_send, k) if k < near else (far_keep, far_send, k - near)
-        keep[n] = totals[-x_slots:, mine, :]
-        send[n] = totals[-x_slots:, theirs, :].astype(bf16)
-        z_out = z_keep if k == 0 else z_sends[k - 1]
-        z_out[0] = totals[:-x_slots, mine, :].astype(z_out.dtype)
-        z_out[1] = totals[:-x_slots, theirs, :].astype(z_out.dtype)
+
+    def rows_of(flip):
+        return pl.ds(pl.multiple_of((me ^ flip) * owned, owned), owned)
+
+    for n in range(2):
+        near_send[n] = totals[-x_slots:, rows_of(2 * n + 1), :].astype(bf16)
+        near_keep[n] = totals[-x_slots:, rows_of(2 * n), :]
+        far_send[n] = totals[-x_slots:, rows_of(2 * n + 5), :].astype(bf16)
+        far_keep[n] = totals[-x_slots:, rows_of(2 * n + 4), :]
+    for n in range(4):
+        z_send[n] = totals[:-x_slots, rows_of(n + 4), :].astype(bf16)
+        z_keep[n] = totals[:-x_slots, rows_of(n), :]
 
 
 SCRATCH = 20
@@ -237,7 +237,7 @@
 Z_SLOTS = 3
 
 
-def own_totals(images, class_index, pose_index, defocus_bin, defocus, rows_table, cols_table, plane_weight, turns_round):
+def own_totals(images, class_index, pose_index, defocus_bin, defocus, rows_table, cols_table, plane_weight, members):
     count, box, _ = images.shape
     poses, rows, _ = rows_table.shape
     cols = cols_table.shape[2]
@@ -247,16 +247,15 @@
     any_place = pl.BlockSpec(memory_space=pl.ANY)
     vmem = pl.BlockSpec(memory_space=pltpu.VMEM)
     lanes = 128 * (-(-2 * count // 128))
-    if turns_round == 0:
+    if members == 1:
         out_shape = [jax.ShapeDtypeStruct((slots, rows, 2 * cols), bf16)]
     else:
         slots += 1
-        owned = rows // (2 * turns_round)
-        x_piece = (turns_round // 2, slots - Z_SLOTS, owned, 2 * cols)
-        z_piece = (2, Z_SLOTS, owned, 2 * cols)
-        out_shape = [pltpu.VMEM(x_piece, bf16), pltpu.VMEM(x_piece, f32)] * 2
-        out_shape += [pltpu.VMEM(z_piece, f32)]
-        out_shape += [pltpu.VMEM(z_piece, bf16)] * (turns_round - 1)
+        x_piece = (2, slots - Z_SLOTS, rows // members, 2 * cols)
+        z_piece = (4, Z_SLOTS, rows // members, 2 * cols)
+        out_shape = []
+        for piece in (x_piece, x_piece, z_piece):
+            out_shape += [pltpu.VMEM(piece, bf16), pltpu.VMEM(piece, f32)]
     operands = (
         class_index[:, 0], pose_index, defocus_bin, defocus, plane_weight.T,
         jnp.asarray(table_y, bf16), jnp.asarray(table_x.T.copy(), bf16),
@@ -375,7 +374,7 @@
     )(defocus, planes, rows_table, cols_table)
 
 
-def call_in_vmem(kernel, arrays, out_shape):
+def call_in_vmem(kernel, arrays, out_shape, weight=1000):
     vmem = pl.BlockSpec(memory_space=pltpu.VMEM)
     return pl.pallas_call(
         kernel,
@@ -383,68 +382,70 @@
         in_specs=[vmem] * len(arrays),
         out_specs=[vmem] * len(out_shape),
         compiler_params=pltpu.CompilerParams(vmem_limit_bytes=16 * 1024 * 1024),
-        cost_estimate=pl.CostEstimate(flops=1000, bytes_accessed=1000, transcendentals=0),
+        cost_estimate=pl.CostEstimate(flops=weight, bytes_accessed=weight, transcendentals=0),
     )(*arrays)
 
 
-def fold_kernel(far_keep, far_came, near_send, z_keep, *refs):
-    rounds = near_send.shape[0] + far_keep.shape[0]
-    z_came, refs = refs[: rounds - 1], refs[rounds - 1 :]
-    z_own, x_send, far_sends = refs[0], refs[1], refs[2:]
-    for k, send in enumerate(far_sends):
-        send[...] = (far_keep[k] + far_came[k].astype(f32)).astype(bf16)
-    near, x_slots = near_send.shape[:2]
-    for k in range(near):
-        x_send[k * x_slots : (k + 1) * x_slots] = near_send[k]
-    for side in range(2):
-        value = z_keep[side]
-        for came in z_came:
-            value = value + came[side].astype(f32)
-        if side == 0:
-            z_own[...] = value
-        else:
-            x_send[near * x_slots :] = value.astype(bf16)
+def fold_kernel(far_keep, far_came, near_send, z_keep, z_came, far_a, far_b, x_send, z_kept):
+    for n, send in enumerate((far_a, far_b)):
+        send[...] = (far_keep[n] + far_came[n].astype(f32)).astype(bf16)
+    x_slots, z_slots = near_send.shape[1], z_keep.shape[1]
+    for n in range(2):
+        z_kept[n] = z_keep[2 * n] + z_came[2 * n].astype(f32)
+        x_send[n * x_slots : (n + 1) * x_slots] = near_send[n]
+        first = 2 * x_slots + n * z_slots
+        x_send[first : first + z_slots] = (
+            z_keep[2 * n + 1] + z_came[2 * n + 1].astype(f32)
+        ).astype(bf16)
 
 
 def fold_phase(far_keep, far_came, near_send, z_keep, z_came):
-    far, x_slots = far_keep.shape[:2]
-    z_slots = z_keep.shape[1]
+    x_slots, z_slots = near_send.shape[1], z_keep.shape[1]
     tail = far_keep.shape[2:]
-    out_shape = [
-        pltpu.VMEM((z_slots,) + tail, f32),
-        pltpu.VMEM((near_send.shape[0] * x_slots + z_slots,) + tail, bf16),
+    out_shape = [pltpu.VMEM((x_slots,) + tail, bf16)] * 2
+    out_shape += [
+        pltpu.VMEM((2 * x_slots + 2 * z_slots,) + tail, bf16),
+        pltpu.VMEM((2, z_slots) + tail, f32),
     ]
-    out_shape += [pltpu.VMEM((x_slots,) + tail, bf16)] * far
-    return call_in_vmem(fold_kernel, (far_keep, far_came, near_send, z_keep, *z_came), out_shape)
-
-
-def near_kernel(keep, came, own, *sends):
-    near, x_slots = keep.shape[:2]
-    for k, out in enumerate((own,) + sends):
-        part = came[k * x_slots : (k + 1) * x_slots].astype(f32)
-        out[...] = (keep[k] + part).astype(out.dtype)
-
-
-def near_phase(keep, came):
-    piece = keep.shape[1:]
-    out_shape = [pltpu.VMEM(piece, f32)] + [pltpu.VMEM(piece, bf16)] * (keep.shape[0] - 1)
-    return call_in_vmem(near_kernel, (keep, came), out_shape)
-
-
-def finish_kernel(high_ref, low_ref, share_ref, x_own, z_own, z_came, *refs):
-    x_came, out_ref, ridge_ref = refs[:-2], refs[-2], refs[-1]
+    return call_in_vmem(fold_kernel, (far_keep, far_came, near_send, z_keep, z_came), out_shape)
+
+
+def near_kernel(near_keep, z_kept, came, own, send):
+    x_slots, z_slots = near_keep.shape[1], z_kept.shape[1]
+    for n, out in enumerate((own, send)):
+        first = 2 * x_slots + n * z_slots
+        part = z_kept[n] + came[first : first + z_slots].astype(f32)
+        out[:z_slots] = part.astype(out.dtype)
+        part = near_keep[n] + came[n * x_slots : (n + 1) * x_slots].astype(f32)
+        out[z_slots:] = part.astype(out.dtype)
+
+
+def near_phase(near_keep, z_kept, came):
+    piece = (near_keep.shape[1] + z_kept.shape[1],) + near_keep.shape[2:]
+    out_shape = [pltpu.VMEM(piece, f32), pltpu.VMEM(piece, bf16)]
+    return call_in_vmem(near_kernel, (near_keep, z_kept, came), out_shape)
+
+
+def far_kernel(own, far_a, far_b, out):
+    first = own.shape[0] - far_a.shape[0]
+    out[:first] = own[:first]
+    out[first:] = own[first:] + far_a[...].astype(f32) + far_b[...].astype(f32)
+
+
+def far_phase(own, far_a, far_b):
+    return call_in_vmem(far_kernel, (own, far_a, far_b), [pltpu.VMEM(own.shape, f32)], FAR_WEIGHT)[0]
+
+
+FAR_WEIGHT = 1024 * 1024 * 1024
+
+
+def finish_kernel(high_ref, low_ref, share_ref, own, near_came, out_ref, ridge_ref):
     slots, pairs = share_ref.shape
     owned, _, cols = ridge_ref.shape
     planes = slots // CLASSES
-    first = z_own.shape[0]
 
     def summed(s):
-        if s < first:
-            return z_own[s] + z_came[z_came.shape[0] - first + s].astype(f32)
-        value = x_own[s - first]
-        for part in x_came:
-            value = value + part[s - first].astype(f32)
-        return value
+        return own[s] + near_came[s].astype(f32)
 
     counts = summed(slots)[:CLASSES, :pairs]
     scaled = jnp.concatenate([counts] * planes, 0) * share_ref[...]
@@ -463,22 +464,22 @@
         out_ref[:, 2 * place + 1, :] = value[:, cols:] * factor
 
 
-def finish(tables, x_own, z_own, z_came, x_came):
+def finish(tables, own, near_came):
     slots = tables[2].shape[0]
-    _, owned, wide = x_own.shape
+    _, owned, wide = own.shape
     cols = wide // 2
     vmem = pl.BlockSpec(memory_space=pltpu.VMEM)
     return pl.pallas_call(
         finish_kernel,
         out_shape=jax.ShapeDtypeStruct((owned, 2 * slots, cols), f32),
-        in_specs=[vmem] * (6 + len(x_came)),
+        in_specs=[vmem] * 5,
         out_specs=vmem,
         scratch_shapes=[pltpu.VMEM((owned, slots, cols), f32)],
         compiler_params=pltpu.CompilerParams(vmem_limit_bytes=16 * 1024 * 1024),
         cost_estimate=pl.CostEstimate(
             flops=8 * slots * owned * cols, bytes_accessed=8 * 1024 * 1024 // 4, transcendentals=0
         ),
-    )(*tables, x_own, z_own, z_came, *x_came)
+    )(*tables, own, near_came)
 
 
 def squared_table(weight_table):
@@ -511,37 +512,31 @@
     return jnp.einsum("czpmbr,pmbj->rczj", left, v, precision=exact)
 
 
-def by_rounds(images, class_index, pose_index, defocus_bin, defocus, rows_table, cols_table, plane_weight):
+def by_pairs(images, class_index, pose_index, defocus_bin, defocus, rows_table, cols_table, plane_weight):
     members = lax.axis_size("img")
-    rounds = members // 2
     rows = rows_table.shape[1]
     planes = plane_weight.shape[1]
     cols = cols_table.shape[2]
     owned = rows // members
-    outs = own_totals(
-        images, class_index, pose_index, defocus_bin, defocus, rows_table, cols_table, plane_weight, rounds
-    )
-    far_send, far_keep, near_send, near_keep, z_keep = outs[:5]
-    z_sends = outs[5:]
-    near = near_keep.shape[0]
-
-    def along_x(value):
-        return lax.ppermute(value, "img", [(i, i ^ 1) for i in range(members)])
-
-    def along_z(value, k):
-        return lax.ppermute(value, "img", [(i, i ^ (2 * k)) for i in range(members)])
-
-    far_ks, near_ks = range(near, rounds), range(1, near)
-    far_came = along_x(far_send)
-    z_came = [along_z(z_sends[k - 1], k) for k in (*far_ks, *near_ks)]
+
+    def exchange(value, flip):
+        return lax.ppermute(value, "img", [(i, i ^ flip) for i in range(members)])
+
+    far_send, far_keep, near_send, near_keep, z_send, z_keep = own_totals(
+        images, class_index, pose_index, defocus_bin, defocus, rows_table, cols_table, plane_weight, members
+    )
+    far_came = exchange(far_send, 1)
+    z_came = exchange(z_send, 4)
     tables = own_ridges(defocus, plane_weight, rows_table, cols_table, owned)
     far_keep, tables = lax.optimization_barrier((far_keep, tables))
-    z_own, x_send, *x_sends = fold_phase(far_keep, far_came, near_send, z_keep, z_came)
-    z_came = along_x(x_send)
-    x_came = [along_z(send, k) for send, k in zip(x_sends, far_ks)]
-    x_own, *x_sends = near_phase(near_keep, z_came)
-    x_came += [along_z(send, k) for send, k in zip(x_sends, near_ks)]
-    out = finish(tables, x_own, z_own, z_came, x_came)
+    far_a, far_b, x_send, z_kept = fold_phase(far_keep, far_came, near_send, z_keep, z_came)
+    far_a = exchange(far_a, 4)
+    x_came = exchange(x_send, 1)
+    far_b = exchange(far_b, 6)
+    own, near_send = near_phase(near_keep, z_kept, x_came)
+    near_came = exchange(near_send, 2)
+    own = far_phase(own, far_a, far_b)
+    out = finish(tables, own, near_came)
     return out.reshape(owned, CLASSES, planes, 2, cols)
 
 
@@ -552,7 +547,7 @@
     members = lax.axis_size("img")
     owned = rows // members
     (totals,) = own_totals(
-        images, class_index, pose_index, defocus_bin, defocus, rows_table, cols_table, plane_weight, 0
+        images, class_index, pose_index, defocus_bin, defocus, rows_table, cols_table, plane_weight, 1
     )
     slots = totals.shape[0]
     totals = totals.reshape(slots, members, owned, 2 * cols).transpose(1, 0, 2, 3)
@@ -569,8 +564,8 @@
     rows = arrays[5].shape[1]
     members = lax.axis_size("img")
     images = members * arrays[0].shape[0]
-    small = members >= 4 and members & (members - 1) == 0 and images <= 256 and rows % (16 * members) == 0
-    return (by_rounds if small else by_scatter)(*arrays)
+    paired = members == 8 and images <= 256 and rows % (16 * members) == 0
+    return (by_pairs if paired else by_scatter)(*arrays)
 
 
 def solution(mesh):

time: 31.8 us -> 32.2 us (1.013)
  starting transfers between devices: 10.9 us -> 12.2 us
  waiting for transfers between devices: 10.3 us -> 9.39 us
    ppermute x8 -> x6, starting transfers between devices: 10.9 us -> 12.2 us  [exchange(): return lax.ppermute(value, 'img', [(i, i ^ flip) for i in range(members)])]
    ppermute x8 -> x6, waiting for transfers between devices: 10.3 us -> 9.39 us  [exchange(): return lax.ppermute(value, 'img', [(i, i ^ flip) for i in range(members)])]
  transfers between devices with their start and end apart: 8 -> 6, of which waited for: 4 -> 4; matrix products, arithmetic and copies ran while one was open for 0% -> 0% of each run, Pallas kernels for 7% -> 7%
where the time goes in v12:
time: 32.2 us; the launch traced here: 32.1 us
  starting transfers between devices  12.2 us (38%)
  Pallas kernels  10.4 us (32%)
  waiting for transfers between devices  9.39 us (29%)
    ppermute x6, starting transfers between devices, exchange(): return lax.ppermute(value, 'img', [(i, i ^ flip) for i in range(members)])  12.2 us
    ppermute x6, waiting for transfers between devices, exchange(): return lax.ppermute(value, 'img', [(i, i ^ flip) for i in range(members)])  9.39 us
    pallas_call x1, Pallas kernels, own_totals(): pl.pallas_call(slices_kernel, out_shape=out_shape, in_specs=[any_place] *...  6.96 us
    pallas_call x1, Pallas kernels, own_ridges(): pl.pallas_call(ridge_kernel, out_shape=[table, table, jax.ShapeDtypeStruc...  2.09 us
    pallas_call x1, Pallas kernels, finish(): pl.pallas_call(finish_kernel, out_shape=jax.ShapeDtypeStruct((owned, 2 *...  1.23 us
  transfers between devices with their start and end apart: 6, of which 4 were waited for; matrix products, arithmetic and copies ran while one was open for 0% of the time, Pallas kernels for 7%

profile of v12, /device:TPU:0, one launch (start us, length us, event | category | flops | bytes accessed | tf_op | source)
XLA Modules:
  0.0 32.1 jit_solution(4596619246992336851)
XLA Ops:
  0.0 0.0 copy-start
  0.0 0.0 copy-start.1
  0.0 0.0 copy-start.2
  0.0 0.0 copy-start.3
  0.0 7.0 %shard_map.100 = (bf16[2,14,16,256]{3,2,1,0:T(8,128)(2,1)S(1)}, f32[2,14,16,256]{3,2,1,0:T(8,128)S(1)}, bf16[2,14,16,256]{3,2,1,0:T(8,128)(2,1)S(1)}, f32[2,14,1...) custom-call(s32[16]{0:T(128)} %bitcast.5, s32[16]{0:T(128)} %pose_hbm.1, ...), custom_call_target="tpu_custom_call" | custom-call | flops 2097152000 | bytes 6291456 | tf_op jit(solution)/shard_map/pallas_call | solution.py:264
  7.0 3.0 %collective-permute-start = (bf16[2,14,16,256]{3,2,1,0:T(8,128)(2,1)S(1)}, bf16[2,14,16,256]{3,2,1,0:T(8,128)(2,1)S(1)}, u32[]{:S(2)}, u32[]{:S(2)}) collective-permute-start(bf16[2,14,16,256]{3,2,1,0:T(8,128)(2,1)S(1)} %get-tuple-element.33), channel_id=1, source_target_pairs={{0,2},{2,0},{4,6},{6,4},{8,10},{10,8},{12,14},{14,12},{1,3},{3,1},... | collective-permute-start | bytes 688136 | tf_op jit(solution)/shard_map/ppermute | solution.py:523
  10.0 2.6 %collective-permute-start.1 = (bf16[4,3,16,256]{3,2,1,0:T(8,128)(2,1)S(1)}, bf16[4,3,16,256]{3,2,1,0:T(8,128)(2,1)S(1)}, u32[]{:S(2)}, u32[]{:S(2)}) collective-permute-start(bf16[4,3,16,256]{3,2,1,0:T(8,128)(2,1)S(1)} %get-tuple-element.36), channel_id=1, source_target_pairs={{0,8},{2,10},{4,12},{6,14},{8,0},{10,2},{12,4},{14,6},{1,9},{3,11}... | collective-permute-start | bytes 294920 | tf_op jit(solution)/shard_map/ppermute | solution.py:523
  12.6 0.0 copy-done
  12.6 0.0 copy-done.1
  12.6 0.0 copy-done.2
  12.6 0.0 copy-done.3
  12.6 2.1 %shard_map.101 = (bf16[128,2048]{1,0:T(8,128)(2,1)S(1)}, bf16[128,2048]{1,0:T(8,128)(2,1)S(1)}, f32[16,128]{1,0:T(8,128)S(1)}) custom-call(f32[16]{0:T(128)S(1)} %copy-done.3, f32[2,8]{1,0:T(2,128)S(1)} %bitcast.4, bf16[8,128,256]{2,1,0:T(8,128)(2,1)S(1)} %copy-done, bf16[8,256,128]{2,1,0:T(8,128)(2,1)S(1)} %copy-done.1), custom_call_target="tpu_custom_call" | custom-call | flops 1000 | bytes 1000 | tf_op jit(solution)/shard_map/pallas_call | solution.py:358
  14.7 2.6 %collective-permute-done.1.z_came = bf16[4,3,16,256]{3,2,1,0:T(8,128)(2,1)S(1)} collective-permute-done((bf16[4,3,16,256]{3,2,1,0:T(8,128)(2,1)S(1)}, bf16[4,3,16,256]{3,2,1,0:T(8,128)(2,1)S(1)}, u32[]{:S(2)}, u32[]{:S(2)}) %collective-permute-start.1) | collective-permute-done | bytes 98336 | tf_op jit(solution)/shard_map/ppermute | solution.py:523
  17.3 0.0 collective-permute-done.far_came
  17.3 0.1 shard_map.102
  17.3 0.6 %collective-permute-start.2 = (bf16[34,16,256]{2,1,0:T(8,128)(2,1)S(1)}, bf16[34,16,256]{2,1,0:T(8,128)(2,1)S(1)}, u32[]{:S(2)}, u32[]{:S(2)}) collective-permute-start(bf16[34,16,256]{2,1,0:T(8,128)(2,1)S(1)} %get-tuple-element.38), channel_id=1, source_target_pairs={{0,2},{2,0},{4,6},{6,4},{8,10},{10,8},{12,14},{14,12},{1,3},{3,1},... | collective-permute-start | bytes 835592 | tf_op jit(solution)/shard_map/ppermute | solution.py:523
  17.9 2.2 %collective-permute-start.3 = (bf16[14,16,256]{2,1,0:T(8,128)(2,1)S(1)}, bf16[14,16,256]{2,1,0:T(8,128)(2,1)S(1)}, u32[]{:S(2)}, u32[]{:S(2)}) collective-permute-start(bf16[14,16,256]{2,1,0:T(8,128)(2,1)S(1)} %get-tuple-element.40), channel_id=1, source_target_pairs={{0,8},{2,10},{4,12},{6,14},{8,0},{10,2},{12,4},{14,6},{1,9},{3,11}... | collective-permute-start | bytes 344072 | tf_op jit(solution)/shard_map/ppermute | solution.py:523
  20.1 1.3 %collective-permute-start.4 = (bf16[14,16,256]{2,1,0:T(8,128)(2,1)S(1)}, bf16[14,16,256]{2,1,0:T(8,128)(2,1)S(1)}, u32[]{:S(2)}, u32[]{:S(2)}) collective-permute-start(bf16[14,16,256]{2,1,0:T(8,128)(2,1)S(1)} %get-tuple-element.41), channel_id=1, source_target_pairs={{0,12},{2,14},{4,8},{6,10},{8,4},{10,6},{12,0},{14,2},{1,13},{3,15... | collective-permute-start | bytes 344072 | tf_op jit(solution)/shard_map/ppermute | solution.py:523
  21.4 2.5 %collective-permute-done.2.came = bf16[34,16,256]{2,1,0:T(8,128)(2,1)S(1)} collective-permute-done((bf16[34,16,256]{2,1,0:T(8,128)(2,1)S(1)}, bf16[34,16,256]{2,1,0:T(8,128)(2,1)S(1)}, u32[]{:S(2)}, u32[]{:S(2)}) %collective-permute-start.2) | collective-permute-done | bytes 278560 | tf_op jit(solution)/shard_map/ppermute | solution.py:523
  24.0 2.5 %collective-permute-start.5 = (bf16[17,16,256]{2,1,0:T(8,128)(2,1)S(1)}, bf16[17,16,256]{2,1,0:T(8,128)(2,1)S(1)}, u32[]{:S(2)}, u32[]{:S(2)}) collective-permute-start(bf16[17,16,256]{2,1,0:T(8,128)(2,1)S(1)} %get-tuple-element.42), channel_id=1, source_target_pairs={{0,4},{2,6},{4,0},{6,2},{8,12},{10,14},{12,8},{14,10},{1,5},{3,7},... | collective-permute-start | bytes 417800 | tf_op jit(solution)/shard_map/ppermute | solution.py:523
  26.5 2.5 %collective-permute-done.3.far_a = bf16[14,16,256]{2,1,0:T(8,128)(2,1)S(1)} collective-permute-done((bf16[14,16,256]{2,1,0:T(8,128)(2,1)S(1)}, bf16[14,16,256]{2,1,0:T(8,128)(2,1)S(1)}, u32[]{:S(2)}, u32[]{:S(2)}) %collective-permute-start.3) | collective-permute-done | bytes 114720 | tf_op jit(solution)/shard_map/ppermute | solution.py:523
  29.0 0.0 collective-permute-done.4.far_b
  29.0 1.8 %collective-permute-done.5.near_came = bf16[17,16,256]{2,1,0:T(8,128)(2,1)S(1)} collective-permute-done((bf16[17,16,256]{2,1,0:T(8,128)(2,1)S(1)}, bf16[17,16,256]{2,1,0:T(8,128)(2,1)S(1)}, u32[]{:S(2)}, u32[]{:S(2)}) %collective-permute-start.5) | collective-permute-done | bytes 139296 | tf_op jit(solution)/shard_map/ppermute | solution.py:523
  30.8 1.2 %shard_map.105 = f32[16,32,128]{2,1,0:T(8,128)} custom-call(bf16[128,2048]{1,0:T(8,128)(2,1)S(1)} %get-tuple-element.28.high_ref, bf16[128,2048]{1,0:T(8,128)(2,1)S(1)} %get-tuple-element.29.low_ref, f32[16,128]{1,0:T(8,128)S(1)} %get-tuple-element.30.share_ref, f32[17,16,256]{2,1,0:T(8,128)S(1)} %shard_map.104.own, ...), custom_call_target="tpu_custom_call" | custom-call | flops 262144 | bytes 2097152 | tf_op jit(solution)/shard_map/pallas_call | solution.py:472
  (2 shorter events, 0.1 us)
Async XLA Ops:
  0.0 12.6 %copy-start = (bf16[8,128,256]{2,1,0:T(8,128)(2,1)S(1)}, bf16[8,128,256]{2,1,0:T(8,128)(2,1)}, u32[]{:S(2)}) copy-start(bf16[8,128,256]{2,1,0:T(8,128)(2,1)} %rows_hbm.3) | copy-start | bytes 1572868
  0.0 12.6 %copy-start.1 = (bf16[8,256,128]{2,1,0:T(8,128)(2,1)S(1)}, bf16[8,256,128]{2,1,0:T(8,128)(2,1)}, u32[]{:S(2)}) copy-start(bf16[8,256,128]{2,1,0:T(8,128)(2,1)} %cols_hbm.3) | copy-start | bytes 1572868
  0.0 12.6 %copy-start.2 = (f32[8,2]{0,1:T(2,128)S(1)}, f32[8,2]{0,1:T(2,128)}, u32[]{:S(2)}) copy-start(f32[8,2]{0,1:T(2,128)} %param.17) | copy-start | bytes 196
  0.0 12.6 %copy-start.3 = (f32[16]{0:T(128)S(1)}, f32[16]{0:T(128)}, u32[]{:S(2)}) copy-start(f32[16]{0:T(128)} %defocus_hbm.3) | copy-start | bytes 196
  7.0 10.3 %collective-permute-start = (bf16[2,14,16,256]{3,2,1,0:T(8,128)(2,1)S(1)}, bf16[2,14,16,256]{3,2,1,0:T(8,128)(2,1)S(1)}, u32[]{:S(2)}, u32[]{:S(2)}) collective-permute-start(bf16[2,14,16,256]{3,2,1,0:T(8,128)(2,1)S(1)} %get-tuple-element.33), channel_id=1, source_target_pairs={{0,2},{2,0},{4,6},{6,4},{8,10},{10,8},{12,14},{14,12},{1,3},{3,1},... | collective-permute-start | bytes 688136 | tf_op jit(solution)/shard_map/ppermute | solution.py:523
  10.0 7.3 %collective-permute-start.1 = (bf16[4,3,16,256]{3,2,1,0:T(8,128)(2,1)S(1)}, bf16[4,3,16,256]{3,2,1,0:T(8,128)(2,1)S(1)}, u32[]{:S(2)}, u32[]{:S(2)}) collective-permute-start(bf16[4,3,16,256]{3,2,1,0:T(8,128)(2,1)S(1)} %get-tuple-element.36), channel_id=1, source_target_pairs={{0,8},{2,10},{4,12},{6,14},{8,0},{10,2},{12,4},{14,6},{1,9},{3,11}... | collective-permute-start | bytes 294920 | tf_op jit(solution)/shard_map/ppermute | solution.py:523
  17.3 6.6 %collective-permute-start.2 = (bf16[34,16,256]{2,1,0:T(8,128)(2,1)S(1)}, bf16[34,16,256]{2,1,0:T(8,128)(2,1)S(1)}, u32[]{:S(2)}, u32[]{:S(2)}) collective-permute-start(bf16[34,16,256]{2,1,0:T(8,128)(2,1)S(1)} %get-tuple-element.38), channel_id=1, source_target_pairs={{0,2},{2,0},{4,6},{6,4},{8,10},{10,8},{12,14},{14,12},{1,3},{3,1},... | collective-permute-start | bytes 835592 | tf_op jit(solution)/shard_map/ppermute | solution.py:523
  17.9 11.1 %collective-permute-start.3 = (bf16[14,16,256]{2,1,0:T(8,128)(2,1)S(1)}, bf16[14,16,256]{2,1,0:T(8,128)(2,1)S(1)}, u32[]{:S(2)}, u32[]{:S(2)}) collective-permute-start(bf16[14,16,256]{2,1,0:T(8,128)(2,1)S(1)} %get-tuple-element.40), channel_id=1, source_target_pairs={{0,8},{2,10},{4,12},{6,14},{8,0},{10,2},{12,4},{14,6},{1,9},{3,11}... | collective-permute-start | bytes 344072 | tf_op jit(solution)/shard_map/ppermute | solution.py:523
  20.1 8.9 %collective-permute-start.4 = (bf16[14,16,256]{2,1,0:T(8,128)(2,1)S(1)}, bf16[14,16,256]{2,1,0:T(8,128)(2,1)S(1)}, u32[]{:S(2)}, u32[]{:S(2)}) collective-permute-start(bf16[14,16,256]{2,1,0:T(8,128)(2,1)S(1)} %get-tuple-element.41), channel_id=1, source_target_pairs={{0,12},{2,14},{4,8},{6,10},{8,4},{10,6},{12,0},{14,2},{1,13},{3,15... | collective-permute-start | bytes 344072 | tf_op jit(solution)/shard_map/ppermute | solution.py:523
  24.0 6.8 %collective-permute-start.5 = (bf16[17,16,256]{2,1,0:T(8,128)(2,1)S(1)}, bf16[17,16,256]{2,1,0:T(8,128)(2,1)S(1)}, u32[]{:S(2)}, u32[]{:S(2)}) collective-permute-start(bf16[17,16,256]{2,1,0:T(8,128)(2,1)S(1)} %get-tuple-element.42), channel_id=1, source_target_pairs={{0,4},{2,6},{4,0},{6,2},{8,12},{10,14},{12,8},{14,10},{1,5},{3,7},... | collective-permute-start | bytes 417800 | tf_op jit(solution)/shard_map/ppermute | solution.py:523

commit v13 on v11

--- a/solution.py
+++ b/solution.py
@@ -107,6 +107,7 @@
     cos_x[...] = -turns_sine(turns + 0.25)
     sin_x[...] = -turns_sine(turns)
     totals[...] = jnp.zeros_like(totals)
+    leading = 1 if len(outs) > 1 else 0
     if len(outs) > 1:
         bins = defocus_ref.shape[0]
         count_row = iota((16, 2 * cols), 0)
@@ -115,7 +116,7 @@
         for i in range(count):
             hit = (count_row == class_ref[i]) & (count_lane == pose_ref[i] * bins + bin_ref[i])
             counts = counts + jnp.where(hit, 1.0, 0.0)
-        totals[planes * CLASSES] = jnp.tile(counts, (rows // 16, 1))
+        totals[0] = jnp.tile(counts, (rows // 16, 1))
 
     tile = 8
     tile_row = iota((tile, half), 0) == 0
@@ -130,10 +131,17 @@
     def along_rows(i):
         if i % GROUP == 0:
             copies[6 if i == 0 else 9 + i // GROUP].wait()
-        half_ref[i % SLOTS] = dot(dft_ref[...], images_ref[i]).astype(bf16)
+        two = jnp.concatenate([images_ref[i], images_ref[i + 1]], 1)
+        product = dot(dft_ref[...], two).astype(bf16)
+        for n in range(2):
+            half_ref[i // 2 % 2, n * box : (n + 1) * box] = product[:, n * box : (n + 1) * box]
 
     def along_columns(i):
-        y = dot(half_ref[i % SLOTS], dft_t_ref[...])
+        product = dot(half_ref[i // 2 % 2], dft_t_ref[...])
+        for n in range(2):
+            weigh(i + n, product[n * box : (n + 1) * box])
+
+    def weigh(i, y):
         sin_col = jnp.broadcast_to(wave_y[:, i : i + 1], (tall, half))
         cos_col = jnp.broadcast_to(wave_y[:, count + i : count + i + 1], (tall, half))
         near_ctf = sin_col * cos_x[i : i + 1, :half] + cos_col * sin_x[i : i + 1, :half]
@@ -182,7 +190,7 @@
         pose_rows = rows_fold[pl.ds(pl.multiple_of(pose * rows, rows), rows), :]
         piece = dot(pose_rows, mix_ref[i % SLOTS])
         for z in range(planes):
-            slot = z * CLASSES + class_ref[i]
+            slot = leading + z * CLASSES + class_ref[i]
             totals[slot] += plane_ref[z, pose] * piece
 
     copies[5].wait()
@@ -195,19 +203,21 @@
         far_two = dot(far, two).astype(bf16)
         cols_fold[p] = jnp.concatenate([near_two[:, :cols], far_two[:, :cols]], 1)
         cols_fold[p + 1] = jnp.concatenate([near_two[:, cols:], far_two[:, cols:]], 1)
-    along_rows(1)
+    along_rows(2)
     along_columns(0)
     copies[9].wait()
     rows_fold[...] = dot(
         rows_ref[...].reshape(poses * rows, box), near, ((1,), (1,))
     ).astype(bf16)
-    for step in range(2, count + 3):
-        if step >= 3:
-            insert(step - 3)
+    for step in range(4, count + 6, 2):
+        for n in range(2):
+            if step >= 6:
+                insert(step - 6 + n)
+        for n in range(2):
+            if step - 4 < count:
+                mix(step - 4 + n)
         if step - 2 < count:
-            mix(step - 2)
-        if step - 1 < count:
-            along_columns(step - 1)
+            along_columns(step - 2)
         if step < count:
             along_rows(step)
 
@@ -232,7 +242,7 @@
 
 
 SCRATCH = 20
-SLOTS = 3
+SLOTS = 4
 GROUP = 4
 Z_SLOTS = 3
 
@@ -276,7 +286,7 @@
             pltpu.VMEM((box // 2 + 8, lanes), f32),
             pltpu.VMEM((count, box), f32),
             pltpu.VMEM((count, box), f32),
-            pltpu.VMEM((SLOTS, box, box), bf16),
+            pltpu.VMEM((2, 2 * box, box), bf16),
             pltpu.VMEM((SLOTS, box + 16, box), bf16),
             pltpu.VMEM((SLOTS, box, 2 * cols), bf16),
             pltpu.VMEM((slots, rows, 2 * cols), f32),
@@ -431,23 +441,11 @@
     return call_in_vmem(near_kernel, (keep, came), out_shape)
 
 
-def finish_kernel(high_ref, low_ref, share_ref, x_own, z_own, z_came, *refs):
-    x_came, out_ref, ridge_ref = refs[:-2], refs[-2], refs[-1]
+def weight_kernel(high_ref, low_ref, share_ref, z_own, z_came, out_ref, ridge_ref):
     slots, pairs = share_ref.shape
     owned, _, cols = ridge_ref.shape
-    planes = slots // CLASSES
-    first = z_own.shape[0]
-
-    def summed(s):
-        if s < first:
-            return z_own[s] + z_came[z_came.shape[0] - first + s].astype(f32)
-        value = x_own[s - first]
-        for part in x_came:
-            value = value + part[s - first].astype(f32)
-        return value
-
-    counts = summed(slots)[:CLASSES, :pairs]
-    scaled = jnp.concatenate([counts] * planes, 0) * share_ref[...]
+    counts = z_own[0] + z_came[z_came.shape[0] - z_own.shape[0]].astype(f32)
+    scaled = jnp.concatenate([counts[:CLASSES, :pairs]] * (slots // CLASSES), 0) * share_ref[...]
     c_high, c_low = split_two(scaled)
     weight = (
         dot(c_high, high_ref[...]) + dot(c_low, high_ref[...]) + dot(c_high, low_ref[...])
@@ -456,29 +454,53 @@
     for r in range(owned):
         ridge_ref[r] = ridge[:, r * cols : (r + 1) * cols]
     for s in range(slots):
-        value = summed(s)
-        factor = ridge_ref[:, s, :]
+        out_ref[s] = ridge_ref[:, s, :]
+
+
+def own_weights(tables, z_own, z_came):
+    slots = tables[2].shape[0]
+    _, owned, wide = z_own.shape
+    cols = wide // 2
+    vmem = pl.BlockSpec(memory_space=pltpu.VMEM)
+    return pl.pallas_call(
+        weight_kernel,
+        out_shape=pltpu.VMEM((slots, owned, cols), f32),
+        in_specs=[vmem] * 5,
+        out_specs=vmem,
+        scratch_shapes=[pltpu.VMEM((owned, slots, cols), f32)],
+        compiler_params=pltpu.CompilerParams(vmem_limit_bytes=16 * 1024 * 1024),
+        cost_estimate=pl.CostEstimate(flops=1000, bytes_accessed=1000, transcendentals=0),
+    )(*tables, z_own, z_came)
+
+
+def finish_kernel(planes, ridge_ref, x_own, z_own, z_came, *refs):
+    x_came, out_ref = refs[:-1], refs[-1]
+    slots, owned, cols = ridge_ref.shape
+    first = z_own.shape[0]
+    for s in range(slots):
+        if s + 1 < first:
+            value = z_own[s + 1] + z_came[z_came.shape[0] - first + s + 1].astype(f32)
+        else:
+            value = x_own[s + 1 - first]
+            for part in x_came:
+                value = value + part[s + 1 - first].astype(f32)
+        factor = ridge_ref[s]
         place = (s % CLASSES) * planes + s // CLASSES
         out_ref[:, 2 * place, :] = value[:, :cols] * factor
         out_ref[:, 2 * place + 1, :] = value[:, cols:] * factor
 
 
-def finish(tables, x_own, z_own, z_came, x_came):
-    slots = tables[2].shape[0]
-    _, owned, wide = x_own.shape
-    cols = wide // 2
+def finish(planes, ridge, x_own, z_own, z_came, x_came):
+    slots, owned, cols = ridge.shape
     vmem = pl.BlockSpec(memory_space=pltpu.VMEM)
     return pl.pallas_call(
-        finish_kernel,
+        functools.partial(finish_kernel, planes),
         out_shape=jax.ShapeDtypeStruct((owned, 2 * slots, cols), f32),
-        in_specs=[vmem] * (6 + len(x_came)),
+        in_specs=[vmem] * (4 + len(x_came)),
         out_specs=vmem,
-        scratch_shapes=[pltpu.VMEM((owned, slots, cols), f32)],
         compiler_params=pltpu.CompilerParams(vmem_limit_bytes=16 * 1024 * 1024),
-        cost_estimate=pl.CostEstimate(
-            flops=8 * slots * owned * cols, bytes_accessed=8 * 1024 * 1024 // 4, transcendentals=0
-        ),
-    )(*tables, x_own, z_own, z_came, *x_came)
+        cost_estimate=pl.CostEstimate(flops=1000, bytes_accessed=1000, transcendentals=0),
+    )(ridge, x_own, z_own, z_came, *x_came)
 
 
 def squared_table(weight_table):
@@ -541,7 +563,8 @@
     x_came = [along_z(send, k) for send, k in zip(x_sends, far_ks)]
     x_own, *x_sends = near_phase(near_keep, z_came)
     x_came += [along_z(send, k) for send, k in zip(x_sends, near_ks)]
-    out = finish(tables, x_own, z_own, z_came, x_came)
+    ridge = own_weights(tables, z_own, z_came)
+    out = finish(planes, ridge, x_own, z_own, z_came, x_came)
     return out.reshape(owned, CLASSES, planes, 2, cols)
 
 

time: 31.8 us -> 30.5 us (0.959)
  Pallas kernels: 10.4 us -> 9.47 us
  waiting for transfers between devices: 10.3 us -> 9.89 us
    pallas_call x1, Pallas kernels: 6.97 us -> 5.96 us  [own_totals(): pl.pallas_call(slices_kernel, out_shape=out_shape, in_specs=[any_place] *...]
    ppermute x6, waiting for transfers between devices: 6.87 us -> 6.5 us  [along_z(): return lax.ppermute(value, 'img', [(i, i ^ 2 * k) for i in range(members)])]
    pallas_call x1 -> x2, Pallas kernels: 1.25 us -> 1.31 us  [the longest x1 0.94 us: finish(): pl.pallas_call(functools.partial(finish_kernel, planes), out_shape=jax.Sh...]
  transfers between devices with their start and end apart: 8 -> 8, of which waited for: 4 -> 4; matrix products, arithmetic and copies ran while one was open for 0% -> 0% of each run, Pallas kernels for 7% -> 8%
where the time goes in v13:
time: 30.5 us; the launch traced here: 30.4 us
  starting transfers between devices  10.9 us (36%)
  waiting for transfers between devices  9.89 us (32%)
  Pallas kernels  9.47 us (31%)
    ppermute x6, starting transfers between devices, along_z(): return lax.ppermute(value, 'img', [(i, i ^ 2 * k) for i in range(members)])  7.34 us
    ppermute x6, waiting for transfers between devices, along_z(): return lax.ppermute(value, 'img', [(i, i ^ 2 * k) for i in range(members)])  6.5 us
    pallas_call x1, Pallas kernels, own_totals(): pl.pallas_call(slices_kernel, out_shape=out_shape, in_specs=[any_place] *...  5.96 us
    ppermute x2, starting transfers between devices, along_x(): return lax.ppermute(value, 'img', [(i, i ^ 1) for i in range(members)])  3.61 us
    ppermute x2, waiting for transfers between devices, along_x(): return lax.ppermute(value, 'img', [(i, i ^ 1) for i in range(members)])  3.39 us
    pallas_call x1, Pallas kernels, own_ridges(): pl.pallas_call(ridge_kernel, out_shape=[table, table, jax.ShapeDtypeStruc...  2.09 us
    pallas_call x1, Pallas kernels, finish(): pl.pallas_call(functools.partial(finish_kernel, planes), out_shape=jax.Sh...  0.94 us
  transfers between devices with their start and end apart: 8, of which 4 were waited for; matrix products, arithmetic and copies ran while one was open for 0% of the time, Pallas kernels for 8%

profile of v13, /device:TPU:0, one launch (start us, length us, event | category | flops | bytes accessed | tf_op | source)
XLA Modules:
  0.0 30.4 jit_solution(4427191909367658134)
XLA Ops:
  0.0 0.0 copy-start
  0.0 0.0 copy-start.1
  0.0 0.0 copy-start.2
  0.0 0.0 copy-start.3
  0.0 6.0 %shard_map.100 = (bf16[2,14,16,256]{3,2,1,0:T(8,128)(2,1)S(1)}, f32[2,14,16,256]{3,2,1,0:T(8,128)S(1)}, bf16[2,14,16,256]{3,2,1,0:T(8,128)(2,1)S(1)}, f32[2,14,1...) custom-call(s32[16]{0:T(128)} %bitcast.5, ...), custom_call_target="tpu_custom_call" | custom-call | flops 2097152000 | bytes 6291456 | tf_op jit(solution)/shard_map/pallas_call | solution.py:275
  6.0 3.0 %collective-permute-start = (bf16[2,14,16,256]{3,2,1,0:T(8,128)(2,1)S(1)}, bf16[2,14,16,256]{3,2,1,0:T(8,128)(2,1)S(1)}, u32[]{:S(2)}, u32[]{:S(2)}) collective-permute-start(bf16[2,14,16,256]{3,2,1,0:T(8,128)(2,1)S(1)} %get-tuple-element.34), channel_id=1, source_target_pairs={{0,2},{2,0},{4,6},{6,4},{8,10},{10,8},{12,14},{14,12},{1,3},{3,1},... | collective-permute-start | bytes 688136 | tf_op jit(solution)/shard_map/ppermute | solution.py:551
  9.0 2.6 %collective-permute-start.1 = (bf16[2,3,16,256]{3,2,1,0:T(8,128)(2,1)S(1)}, bf16[2,3,16,256]{3,2,1,0:T(8,128)(2,1)S(1)}, u32[]{:S(2)}, u32[]{:S(2)}) collective-permute-start(bf16[2,3,16,256]{3,2,1,0:T(8,128)(2,1)S(1)} %get-tuple-element.37), channel_id=1, source_target_pairs={{0,8},{2,10},{4,12},{6,14},{8,0},{10,2},{12,4},{14,6},{1,9},{3,11}... | collective-permute-start | bytes 147464 | tf_op jit(solution)/shard_map/ppermute | solution.py:554
  11.6 1.3 %collective-permute-start.2 = (bf16[2,3,16,256]{3,2,1,0:T(8,128)(2,1)S(1)}, bf16[2,3,16,256]{3,2,1,0:T(8,128)(2,1)S(1)}, u32[]{:S(2)}, u32[]{:S(2)}) collective-permute-start(bf16[2,3,16,256]{3,2,1,0:T(8,128)(2,1)S(1)} %get-tuple-element.38), channel_id=1, source_target_pairs={{0,12},{2,14},{4,8},{6,10},{8,4},{10,6},{12,0},{14,2},{1,13},{3,15... | collective-permute-start | bytes 147464 | tf_op jit(solution)/shard_map/ppermute | solution.py:554
  12.9 0.2 collective-permute-start.3
  13.2 0.0 copy-done
  13.2 0.0 copy-done.1
  13.2 0.0 copy-done.2
  13.2 0.0 copy-done.3
  13.2 2.1 %shard_map.101 = (bf16[128,2048]{1,0:T(8,128)(2,1)S(1)}, bf16[128,2048]{1,0:T(8,128)(2,1)S(1)}, f32[16,128]{1,0:T(8,128)S(1)}) custom-call(f32[16]{0:T(128)S(1)} %copy-done.3, f32[2,8]{1,0:T(2,128)S(1)} %bitcast.4, bf16[8,128,256]{2,1,0:T(8,128)(2,1)S(1)} %copy-done, bf16[8,256,128]{2,1,0:T(8,128)(2,1)S(1)} %copy-done.1), custom_call_target="tpu_custom_call" | custom-call | flops 1000 | bytes 1000 | tf_op jit(solution)/shard_map/pallas_call | solution.py:369
  15.3 0.0 collective-permute-done.1.refs_0_
  15.3 2.3 %collective-permute-done.2.refs_1_ = bf16[2,3,16,256]{3,2,1,0:T(8,128)(2,1)S(1)} collective-permute-done((bf16[2,3,16,256]{3,2,1,0:T(8,128)(2,1)S(1)}, bf16[2,3,16,256]{3,2,1,0:T(8,128)(2,1)S(1)}, u32[]{:S(2)}, u32[]{:S(2)}) %collective-permute-start.2) | collective-permute-done | bytes 49184 | tf_op jit(solution)/shard_map/ppermute | solution.py:554
  17.5 0.0 collective-permute-done.3.refs_2_
  17.5 0.0 collective-permute-done.far_came
  17.5 0.1 shard_map.102
  17.6 0.6 %collective-permute-start.4 = (bf16[31,16,256]{2,1,0:T(8,128)(2,1)S(1)}, bf16[31,16,256]{2,1,0:T(8,128)(2,1)S(1)}, u32[]{:S(2)}, u32[]{:S(2)}) collective-permute-start(bf16[31,16,256]{2,1,0:T(8,128)(2,1)S(1)} %get-tuple-element.41), channel_id=1, source_target_pairs={{0,2},{2,0},{4,6},{6,4},{8,10},{10,8},{12,14},{14,12},{1,3},{3,1},... | collective-permute-start | bytes 761864 | tf_op jit(solution)/shard_map/ppermute | solution.py:551
  18.2 1.3 %collective-permute-start.5 = (bf16[14,16,256]{2,1,0:T(8,128)(2,1)S(1)}, bf16[14,16,256]{2,1,0:T(8,128)(2,1)S(1)}, u32[]{:S(2)}, u32[]{:S(2)}) collective-permute-start(bf16[14,16,256]{2,1,0:T(8,128)(2,1)S(1)} %get-tuple-element.44), channel_id=1, source_target_pairs={{0,8},{2,10},{4,12},{6,14},{8,0},{10,2},{12,4},{14,6},{1,9},{3,11}... | collective-permute-start | bytes 344072 | tf_op jit(solution)/shard_map/ppermute | solution.py:554
  19.5 1.1 %collective-permute-start.6 = (bf16[14,16,256]{2,1,0:T(8,128)(2,1)S(1)}, bf16[14,16,256]{2,1,0:T(8,128)(2,1)S(1)}, u32[]{:S(2)}, u32[]{:S(2)}) collective-permute-start(bf16[14,16,256]{2,1,0:T(8,128)(2,1)S(1)} %get-tuple-element.45), channel_id=1, source_target_pairs={{0,12},{2,14},{4,8},{6,10},{8,4},{10,6},{12,0},{14,2},{1,13},{3,15... | collective-permute-start | bytes 344072 | tf_op jit(solution)/shard_map/ppermute | solution.py:554
  20.6 3.4 %collective-permute-done.4.z_came.came = bf16[31,16,256]{2,1,0:T(8,128)(2,1)S(1)} collective-permute-done((bf16[31,16,256]{2,1,0:T(8,128)(2,1)S(1)}, bf16[31,16,256]{2,1,0:T(8,128)(2,1)S(1)}, u32[]{:S(2)}, u32[]{:S(2)}) %collective-permute-start.4) | collective-permute-done | bytes 253984 | tf_op jit(solution)/shard_map/ppermute | solution.py:551
  24.0 0.8 %collective-permute-start.7 = (bf16[14,16,256]{2,1,0:T(8,128)(2,1)S(1)}, bf16[14,16,256]{2,1,0:T(8,128)(2,1)S(1)}, u32[]{:S(2)}, u32[]{:S(2)}) collective-permute-start(bf16[14,16,256]{2,1,0:T(8,128)(2,1)S(1)} %get-tuple-element.46), channel_id=1, source_target_pairs={{0,4},{2,6},{4,0},{6,2},{8,12},{10,14},{12,8},{14,10},{1,5},{3,7},... | collective-permute-start | bytes 344072 | tf_op jit(solution)/shard_map/ppermute | solution.py:554
  24.8 0.4 %shard_map.103.ridge_ref = f32[16,16,128]{2,1,0:T(8,128)S(1)} custom-call(bf16[128,2048]{1,0:T(8,128)(2,1)S(1)} %get-tuple-element.30.high_ref, bf16[128,2048]{1,0:T(8,128)(2,1)S(1)} %get-tuple-element.31.low_ref, f32[16,128]{1,0:T(8,128)S(1)} %get-tuple-element.32.share_ref, f32[3,16,256]{2,1,0:T(8,128)S(1)} %get-tuple-element.40.z_own, ...), custom_call_target="tpu_custom_call" | custom-call | flops 1000 | bytes 1000 | tf_op jit(solution)/shard_map/pallas_call | solution.py:465
  25.2 3.0 %collective-permute-done.5.refs_0_ = bf16[14,16,256]{2,1,0:T(8,128)(2,1)S(1)} collective-permute-done((bf16[14,16,256]{2,1,0:T(8,128)(2,1)S(1)}, bf16[14,16,256]{2,1,0:T(8,128)(2,1)S(1)}, u32[]{:S(2)}, u32[]{:S(2)}) %collective-permute-start.5) | collective-permute-done | bytes 114720 | tf_op jit(solution)/shard_map/ppermute | solution.py:554
  28.2 0.0 collective-permute-done.6.refs_1_
  28.2 1.3 %collective-permute-done.7.refs_2_ = bf16[14,16,256]{2,1,0:T(8,128)(2,1)S(1)} collective-permute-done((bf16[14,16,256]{2,1,0:T(8,128)(2,1)S(1)}, bf16[14,16,256]{2,1,0:T(8,128)(2,1)S(1)}, u32[]{:S(2)}, u32[]{:S(2)}) %collective-permute-start.7) | collective-permute-done | bytes 114720 | tf_op jit(solution)/shard_map/ppermute | solution.py:554
  29.4 0.9 %shard_map.105 = f32[16,32,128]{2,1,0:T(8,128)} custom-call(f32[16,16,128]{2,1,0:T(8,128)S(1)} %shard_map.103.ridge_ref, f32[14,16,256]{2,1,0:T(8,128)S(1)} %get-tuple-element.43.x_own, f32[3,16,256]{2,1,0:T(8,128)S(1)} %get-tuple-element.40.z_own, bf16[31,16,256]{2,1,0:T(8,128)(2,1)S(1)} %collective-permute-done.4.z_came.came, ...), custom_call_target="tpu_custom_call" | custom-call | flops 1000 | bytes 1000 | tf_op jit(solution)/shard_map/pallas_call | solution.py:496
  (1 shorter events, 0.0 us)
Async XLA Ops:
  0.0 13.2 %copy-start = (bf16[8,128,256]{2,1,0:T(8,128)(2,1)S(1)}, bf16[8,128,256]{2,1,0:T(8,128)(2,1)}, u32[]{:S(2)}) copy-start(bf16[8,128,256]{2,1,0:T(8,128)(2,1)} %rows_hbm.3) | copy-start | bytes 1572868
  0.0 13.2 %copy-start.1 = (bf16[8,256,128]{2,1,0:T(8,128)(2,1)S(1)}, bf16[8,256,128]{2,1,0:T(8,128)(2,1)}, u32[]{:S(2)}) copy-start(bf16[8,256,128]{2,1,0:T(8,128)(2,1)} %cols_hbm.3) | copy-start | bytes 1572868
  0.0 13.2 %copy-start.2 = (f32[8,2]{0,1:T(2,128)S(1)}, f32[8,2]{0,1:T(2,128)}, u32[]{:S(2)}) copy-start(f32[8,2]{0,1:T(2,128)} %param.17) | copy-start | bytes 196
  0.0 13.2 %copy-start.3 = (f32[16]{0:T(128)S(1)}, f32[16]{0:T(128)}, u32[]{:S(2)}) copy-start(f32[16]{0:T(128)} %defocus_hbm.3) | copy-start | bytes 196
  6.0 11.6 %collective-permute-start = (bf16[2,14,16,256]{3,2,1,0:T(8,128)(2,1)S(1)}, bf16[2,14,16,256]{3,2,1,0:T(8,128)(2,1)S(1)}, u32[]{:S(2)}, u32[]{:S(2)}) collective-permute-start(bf16[2,14,16,256]{3,2,1,0:T(8,128)(2,1)S(1)} %get-tuple-element.34), channel_id=1, source_target_pairs={{0,2},{2,0},{4,6},{6,4},{8,10},{10,8},{12,14},{14,12},{1,3},{3,1},... | collective-permute-start | bytes 688136 | tf_op jit(solution)/shard_map/ppermute | solution.py:551
  9.0 6.3 %collective-permute-start.1 = (bf16[2,3,16,256]{3,2,1,0:T(8,128)(2,1)S(1)}, bf16[2,3,16,256]{3,2,1,0:T(8,128)(2,1)S(1)}, u32[]{:S(2)}, u32[]{:S(2)}) collective-permute-start(bf16[2,3,16,256]{3,2,1,0:T(8,128)(2,1)S(1)} %get-tuple-element.37), channel_id=1, source_target_pairs={{0,8},{2,10},{4,12},{6,14},{8,0},{10,2},{12,4},{14,6},{1,9},{3,11}... | collective-permute-start | bytes 147464 | tf_op jit(solution)/shard_map/ppermute | solution.py:554
  11.6 6.0 %collective-permute-start.2 = (bf16[2,3,16,256]{3,2,1,0:T(8,128)(2,1)S(1)}, bf16[2,3,16,256]{3,2,1,0:T(8,128)(2,1)S(1)}, u32[]{:S(2)}, u32[]{:S(2)}) collective-permute-start(bf16[2,3,16,256]{3,2,1,0:T(8,128)(2,1)S(1)} %get-tuple-element.38), channel_id=1, source_target_pairs={{0,12},{2,14},{4,8},{6,10},{8,4},{10,6},{12,0},{14,2},{1,13},{3,15... | collective-permute-start | bytes 147464 | tf_op jit(solution)/shard_map/ppermute | solution.py:554
  12.9 4.6 %collective-permute-start.3 = (bf16[2,3,16,256]{3,2,1,0:T(8,128)(2,1)S(1)}, bf16[2,3,16,256]{3,2,1,0:T(8,128)(2,1)S(1)}, u32[]{:S(2)}, u32[]{:S(2)}) collective-permute-start(bf16[2,3,16,256]{3,2,1,0:T(8,128)(2,1)S(1)} %get-tuple-element.39), channel_id=1, source_target_pairs={{0,4},{2,6},{4,0},{6,2},{8,12},{10,14},{12,8},{14,10},{1,5},{3,7},... | collective-permute-start | bytes 147464 | tf_op jit(solution)/shard_map/ppermute | solution.py:554
  17.6 6.3 %collective-permute-start.4 = (bf16[31,16,256]{2,1,0:T(8,128)(2,1)S(1)}, bf16[31,16,256]{2,1,0:T(8,128)(2,1)S(1)}, u32[]{:S(2)}, u32[]{:S(2)}) collective-permute-start(bf16[31,16,256]{2,1,0:T(8,128)(2,1)S(1)} %get-tuple-element.41), channel_id=1, source_target_pairs={{0,2},{2,0},{4,6},{6,4},{8,10},{10,8},{12,14},{14,12},{1,3},{3,1},... | collective-permute-start | bytes 761864 | tf_op jit(solution)/shard_map/ppermute | solution.py:551
  18.2 9.9 %collective-permute-start.5 = (bf16[14,16,256]{2,1,0:T(8,128)(2,1)S(1)}, bf16[14,16,256]{2,1,0:T(8,128)(2,1)S(1)}, u32[]{:S(2)}, u32[]{:S(2)}) collective-permute-start(bf16[14,16,256]{2,1,0:T(8,128)(2,1)S(1)} %get-tuple-element.44), channel_id=1, source_target_pairs={{0,8},{2,10},{4,12},{6,14},{8,0},{10,2},{12,4},{14,6},{1,9},{3,11}... | collective-permute-start | bytes 344072 | tf_op jit(solution)/shard_map/ppermute | solution.py:554
  19.5 8.7 %collective-permute-start.6 = (bf16[14,16,256]{2,1,0:T(8,128)(2,1)S(1)}, bf16[14,16,256]{2,1,0:T(8,128)(2,1)S(1)}, u32[]{:S(2)}, u32[]{:S(2)}) collective-permute-start(bf16[14,16,256]{2,1,0:T(8,128)(2,1)S(1)} %get-tuple-element.45), channel_id=1, source_target_pairs={{0,12},{2,14},{4,8},{6,10},{8,4},{10,6},{12,0},{14,2},{1,13},{3,15... | collective-permute-start | bytes 344072 | tf_op jit(solution)/shard_map/ppermute | solution.py:554
  24.0 5.4 %collective-permute-start.7 = (bf16[14,16,256]{2,1,0:T(8,128)(2,1)S(1)}, bf16[14,16,256]{2,1,0:T(8,128)(2,1)S(1)}, u32[]{:S(2)}, u32[]{:S(2)}) collective-permute-start(bf16[14,16,256]{2,1,0:T(8,128)(2,1)S(1)} %get-tuple-element.46), channel_id=1, source_target_pairs={{0,4},{2,6},{4,0},{6,2},{8,12},{10,14},{12,8},{14,10},{1,5},{3,7},... | collective-permute-start | bytes 344072 | tf_op jit(solution)/shard_map/ppermute | solution.py:554

commit v14 on v13

--- a/solution.py
+++ b/solution.py
@@ -129,16 +129,15 @@
         return jnp.concatenate([jnp.where(tile_row, 0.0, value[:tile]), value[tile:]], 0)
 
     def along_rows(i):
-        if i % GROUP == 0:
-            copies[6 if i == 0 else 9 + i // GROUP].wait()
-        two = jnp.concatenate([images_ref[i], images_ref[i + 1]], 1)
-        product = dot(dft_ref[...], two).astype(bf16)
-        for n in range(2):
-            half_ref[i // 2 % 2, n * box : (n + 1) * box] = product[:, n * box : (n + 1) * box]
+        copies[6 if i == 0 else 9 + i // GROUP].wait()
+        group = jnp.concatenate([images_ref[i + n] for n in range(GROUP)], 1)
+        product = dot(dft_ref[...], group).astype(bf16)
+        for n in range(GROUP):
+            half_ref[i // GROUP % 2, n * box : (n + 1) * box] = product[:, n * box : (n + 1) * box]
 
     def along_columns(i):
-        product = dot(half_ref[i // 2 % 2], dft_t_ref[...])
-        for n in range(2):
+        product = dot(half_ref[i // GROUP % 2], dft_t_ref[...])
+        for n in range(GROUP):
             weigh(i + n, product[n * box : (n + 1) * box])
 
     def weigh(i, y):
@@ -203,21 +202,20 @@
         far_two = dot(far, two).astype(bf16)
         cols_fold[p] = jnp.concatenate([near_two[:, :cols], far_two[:, :cols]], 1)
         cols_fold[p + 1] = jnp.concatenate([near_two[:, cols:], far_two[:, cols:]], 1)
-    along_rows(2)
+    along_rows(GROUP)
     along_columns(0)
     copies[9].wait()
     rows_fold[...] = dot(
         rows_ref[...].reshape(poses * rows, box), near, ((1,), (1,))
     ).astype(bf16)
-    for step in range(4, count + 6, 2):
-        for n in range(2):
-            if step >= 6:
-                insert(step - 6 + n)
-        for n in range(2):
-            if step - 4 < count:
-                mix(step - 4 + n)
-        if step - 2 < count:
-            along_columns(step - 2)
+    for step in range(2 * GROUP, count + 3 * GROUP, GROUP):
+        for n in range(GROUP):
+            if step >= 3 * GROUP:
+                insert(step - 3 * GROUP + n)
+            if step - 2 * GROUP < count:
+                mix(step - 2 * GROUP + n)
+        if step - GROUP < count:
+            along_columns(step - GROUP)
         if step < count:
             along_rows(step)
 
@@ -233,7 +231,7 @@
     for k in range(rounds):
         mine = pl.ds(pl.multiple_of((me ^ (2 * k)) * owned, owned), owned)
         theirs = pl.ds(pl.multiple_of((me ^ (2 * k + 1)) * owned, owned), owned)
-        keep, send, n = (near_keep, near_send, k) if k < near else (far_keep, far_send, k - near)
+        keep, send, n = (near_keep, near_send, k) if k < near else (far_keep, far_send, rounds - 1 - k)
         keep[n] = totals[-x_slots:, mine, :]
         send[n] = totals[-x_slots:, theirs, :].astype(bf16)
         z_out = z_keep if k == 0 else z_sends[k - 1]
@@ -242,7 +240,7 @@
 
 
 SCRATCH = 20
-SLOTS = 4
+SLOTS = 8
 GROUP = 4
 Z_SLOTS = 3
 
@@ -286,7 +284,7 @@
             pltpu.VMEM((box // 2 + 8, lanes), f32),
             pltpu.VMEM((count, box), f32),
             pltpu.VMEM((count, box), f32),
-            pltpu.VMEM((2, 2 * box, box), bf16),
+            pltpu.VMEM((2, GROUP * box, box), bf16),
             pltpu.VMEM((SLOTS, box + 16, box), bf16),
             pltpu.VMEM((SLOTS, box, 2 * cols), bf16),
             pltpu.VMEM((slots, rows, 2 * cols), f32),
@@ -553,7 +551,7 @@
     def along_z(value, k):
         return lax.ppermute(value, "img", [(i, i ^ (2 * k)) for i in range(members)])
 
-    far_ks, near_ks = range(near, rounds), range(1, near)
+    far_ks, near_ks = range(near, rounds)[::-1], range(1, near)
     far_came = along_x(far_send)
     z_came = [along_z(z_sends[k - 1], k) for k in (*far_ks, *near_ks)]
     tables = own_ridges(defocus, plane_weight, rows_table, cols_table, owned)

time: 30.5 us -> 31.3 us (1.026)
  waiting for transfers between devices: 9.89 us -> 10.9 us
    ppermute x6, waiting for transfers between devices: 6.5 us -> 7.12 us  [along_z(): return lax.ppermute(value, 'img', [(i, i ^ 2 * k) for i in range(members)])]
    ppermute x2, waiting for transfers between devices: 3.39 us -> 3.73 us  [along_x(): return lax.ppermute(value, 'img', [(i, i ^ 1) for i in range(members)])]
where the time goes in v14:
time: 31.3 us; the launch traced here: 31.1 us
  waiting for transfers between devices  10.9 us (35%)
  starting transfers between devices  10.8 us (35%)
  Pallas kernels  9.42 us (30%)
    ppermute x6, starting transfers between devices, along_z(): return lax.ppermute(value, 'img', [(i, i ^ 2 * k) for i in range(members)])  7.18 us
    ppermute x6, waiting for transfers between devices, along_z(): return lax.ppermute(value, 'img', [(i, i ^ 2 * k) for i in range(members)])  7.12 us
    pallas_call x1, Pallas kernels, own_totals(): pl.pallas_call(slices_kernel, out_shape=out_shape, in_specs=[any_place] *...  5.9 us
    ppermute x2, waiting for transfers between devices, along_x(): return lax.ppermute(value, 'img', [(i, i ^ 1) for i in range(members)])  3.73 us
    ppermute x2, starting transfers between devices, along_x(): return lax.ppermute(value, 'img', [(i, i ^ 1) for i in range(members)])  3.62 us
    pallas_call x1, Pallas kernels, own_ridges(): pl.pallas_call(ridge_kernel, out_shape=[table, table, jax.ShapeDtypeStruc...  2.09 us
    pallas_call x1, Pallas kernels, finish(): pl.pallas_call(functools.partial(finish_kernel, planes), out_shape=jax.Sh...  0.94 us
  transfers between devices with their start and end apart: 8, of which 4 were waited for; matrix products, arithmetic and copies ran while one was open for 0% of the time, Pallas kernels for 8%

profile of v14, /device:TPU:0, one launch (start us, length us, event | category | flops | bytes accessed | tf_op | source)
XLA Modules:
  0.0 31.1 jit_solution(2145175143408453035)
XLA Ops:
  0.0 0.0 copy-start
  0.0 0.0 copy-start.1
  0.0 0.0 copy-start.2
  0.0 0.0 copy-start.3
  0.0 5.9 %shard_map.100 = (bf16[2,14,16,256]{3,2,1,0:T(8,128)(2,1)S(1)}, f32[2,14,16,256]{3,2,1,0:T(8,128)S(1)}, bf16[2,14,16,256]{3,2,1,0:T(8,128)(2,1)S(1)}, f32[2,14,1...) custom-call(s32[16]{0:T(128)} %bitcast.5, ...), custom_call_target="tpu_custom_call" | custom-call | flops 2097152000 | bytes 6291456 | tf_op jit(solution)/shard_map/pallas_call | solution.py:273
  5.9 3.0 %collective-permute-start = (bf16[2,14,16,256]{3,2,1,0:T(8,128)(2,1)S(1)}, bf16[2,14,16,256]{3,2,1,0:T(8,128)(2,1)S(1)}, u32[]{:S(2)}, u32[]{:S(2)}) collective-permute-start(bf16[2,14,16,256]{3,2,1,0:T(8,128)(2,1)S(1)} %get-tuple-element.34), channel_id=1, source_target_pairs={{0,2},{2,0},{4,6},{6,4},{8,10},{10,8},{12,14},{14,12},{1,3},{3,1},... | collective-permute-start | bytes 688136 | tf_op jit(solution)/shard_map/ppermute | solution.py:549
  8.9 3.6 %collective-permute-start.1 = (bf16[2,3,16,256]{3,2,1,0:T(8,128)(2,1)S(1)}, bf16[2,3,16,256]{3,2,1,0:T(8,128)(2,1)S(1)}, u32[]{:S(2)}, u32[]{:S(2)}) collective-permute-start(bf16[2,3,16,256]{3,2,1,0:T(8,128)(2,1)S(1)} %get-tuple-element.37), channel_id=1, source_target_pairs={{0,12},{2,14},{4,8},{6,10},{8,4},{10,6},{12,0},{14,2},{1,13},{3,15... | collective-permute-start | bytes 147464 | tf_op jit(solution)/shard_map/ppermute | solution.py:552
  12.5 0.0 collective-permute-start.2
  12.5 0.8 %collective-permute-start.3 = (bf16[2,3,16,256]{3,2,1,0:T(8,128)(2,1)S(1)}, bf16[2,3,16,256]{3,2,1,0:T(8,128)(2,1)S(1)}, u32[]{:S(2)}, u32[]{:S(2)}) collective-permute-start(bf16[2,3,16,256]{3,2,1,0:T(8,128)(2,1)S(1)} %get-tuple-element.39), channel_id=1, source_target_pairs={{0,4},{2,6},{4,0},{6,2},{8,12},{10,14},{12,8},{14,10},{1,5},{3,7},... | collective-permute-start | bytes 147464 | tf_op jit(solution)/shard_map/ppermute | solution.py:552
  13.3 0.0 copy-done
  13.3 0.0 copy-done.1
  13.3 0.0 copy-done.2
  13.3 0.0 copy-done.3
  13.3 2.1 %shard_map.101 = (bf16[128,2048]{1,0:T(8,128)(2,1)S(1)}, bf16[128,2048]{1,0:T(8,128)(2,1)S(1)}, f32[16,128]{1,0:T(8,128)S(1)}) custom-call(f32[16]{0:T(128)S(1)} %copy-done.3, f32[2,8]{1,0:T(2,128)S(1)} %bitcast.4, bf16[8,128,256]{2,1,0:T(8,128)(2,1)S(1)} %copy-done, bf16[8,256,128]{2,1,0:T(8,128)(2,1)S(1)} %copy-done.1), custom_call_target="tpu_custom_call" | custom-call | flops 1000 | bytes 1000 | tf_op jit(solution)/shard_map/pallas_call | solution.py:367
  15.4 0.0 collective-permute-done.1.refs_0_
  15.4 2.1 %collective-permute-done.2.refs_1_ = bf16[2,3,16,256]{3,2,1,0:T(8,128)(2,1)S(1)} collective-permute-done((bf16[2,3,16,256]{3,2,1,0:T(8,128)(2,1)S(1)}, bf16[2,3,16,256]{3,2,1,0:T(8,128)(2,1)S(1)}, u32[]{:S(2)}, u32[]{:S(2)}) %collective-permute-start.2) | collective-permute-done | bytes 49184 | tf_op jit(solution)/shard_map/ppermute | solution.py:552
  17.5 0.0 collective-permute-done.3.refs_2_
  17.5 0.0 collective-permute-done.far_came
  17.5 0.1 shard_map.102
  17.6 0.6 %collective-permute-start.4 = (bf16[31,16,256]{2,1,0:T(8,128)(2,1)S(1)}, bf16[31,16,256]{2,1,0:T(8,128)(2,1)S(1)}, u32[]{:S(2)}, u32[]{:S(2)}) collective-permute-start(bf16[31,16,256]{2,1,0:T(8,128)(2,1)S(1)} %get-tuple-element.41), channel_id=1, source_target_pairs={{0,2},{2,0},{4,6},{6,4},{8,10},{10,8},{12,14},{14,12},{1,3},{3,1},... | collective-permute-start | bytes 761864 | tf_op jit(solution)/shard_map/ppermute | solution.py:549
  18.2 1.8 %collective-permute-start.5 = (bf16[14,16,256]{2,1,0:T(8,128)(2,1)S(1)}, bf16[14,16,256]{2,1,0:T(8,128)(2,1)S(1)}, u32[]{:S(2)}, u32[]{:S(2)}) collective-permute-start(bf16[14,16,256]{2,1,0:T(8,128)(2,1)S(1)} %get-tuple-element.44), channel_id=1, source_target_pairs={{0,12},{2,14},{4,8},{6,10},{8,4},{10,6},{12,0},{14,2},{1,13},{3,15... | collective-permute-start | bytes 344072 | tf_op jit(solution)/shard_map/ppermute | solution.py:552
  20.0 0.2 collective-permute-start.6
  20.2 3.7 %collective-permute-done.4.z_came.came = bf16[31,16,256]{2,1,0:T(8,128)(2,1)S(1)} collective-permute-done((bf16[31,16,256]{2,1,0:T(8,128)(2,1)S(1)}, bf16[31,16,256]{2,1,0:T(8,128)(2,1)S(1)}, u32[]{:S(2)}, u32[]{:S(2)}) %collective-permute-start.4) | collective-permute-done | bytes 253984 | tf_op jit(solution)/shard_map/ppermute | solution.py:549
  24.0 0.8 %collective-permute-start.7 = (bf16[14,16,256]{2,1,0:T(8,128)(2,1)S(1)}, bf16[14,16,256]{2,1,0:T(8,128)(2,1)S(1)}, u32[]{:S(2)}, u32[]{:S(2)}) collective-permute-start(bf16[14,16,256]{2,1,0:T(8,128)(2,1)S(1)} %get-tuple-element.46), channel_id=1, source_target_pairs={{0,4},{2,6},{4,0},{6,2},{8,12},{10,14},{12,8},{14,10},{1,5},{3,7},... | collective-permute-start | bytes 344072 | tf_op jit(solution)/shard_map/ppermute | solution.py:552
  24.8 0.4 %shard_map.103.ridge_ref = f32[16,16,128]{2,1,0:T(8,128)S(1)} custom-call(bf16[128,2048]{1,0:T(8,128)(2,1)S(1)} %get-tuple-element.30.high_ref, bf16[128,2048]{1,0:T(8,128)(2,1)S(1)} %get-tuple-element.31.low_ref, f32[16,128]{1,0:T(8,128)S(1)} %get-tuple-element.32.share_ref, f32[3,16,256]{2,1,0:T(8,128)S(1)} %get-tuple-element.40.z_own, ...), custom_call_target="tpu_custom_call" | custom-call | flops 1000 | bytes 1000 | tf_op jit(solution)/shard_map/pallas_call | solution.py:463
  25.1 0.0 collective-permute-done.5.refs_0_
  25.2 4.0 %collective-permute-done.6.refs_1_ = bf16[14,16,256]{2,1,0:T(8,128)(2,1)S(1)} collective-permute-done((bf16[14,16,256]{2,1,0:T(8,128)(2,1)S(1)}, bf16[14,16,256]{2,1,0:T(8,128)(2,1)S(1)}, u32[]{:S(2)}, u32[]{:S(2)}) %collective-permute-start.6) | collective-permute-done | bytes 114720 | tf_op jit(solution)/shard_map/ppermute | solution.py:552
  29.1 1.1 %collective-permute-done.7.refs_2_ = bf16[14,16,256]{2,1,0:T(8,128)(2,1)S(1)} collective-permute-done((bf16[14,16,256]{2,1,0:T(8,128)(2,1)S(1)}, bf16[14,16,256]{2,1,0:T(8,128)(2,1)S(1)}, u32[]{:S(2)}, u32[]{:S(2)}) %collective-permute-start.7) | collective-permute-done | bytes 114720 | tf_op jit(solution)/shard_map/ppermute | solution.py:552
  30.2 0.9 %shard_map.105 = f32[16,32,128]{2,1,0:T(8,128)} custom-call(f32[16,16,128]{2,1,0:T(8,128)S(1)} %shard_map.103.ridge_ref, f32[14,16,256]{2,1,0:T(8,128)S(1)} %get-tuple-element.43.x_own, f32[3,16,256]{2,1,0:T(8,128)S(1)} %get-tuple-element.40.z_own, bf16[31,16,256]{2,1,0:T(8,128)(2,1)S(1)} %collective-permute-done.4.z_came.came, ...), custom_call_target="tpu_custom_call" | custom-call | flops 1000 | bytes 1000 | tf_op jit(solution)/shard_map/pallas_call | solution.py:494
  (1 shorter events, 0.0 us)
Async XLA Ops:
  0.0 13.3 %copy-start = (bf16[8,128,256]{2,1,0:T(8,128)(2,1)S(1)}, bf16[8,128,256]{2,1,0:T(8,128)(2,1)}, u32[]{:S(2)}) copy-start(bf16[8,128,256]{2,1,0:T(8,128)(2,1)} %rows_hbm.3) | copy-start | bytes 1572868
  0.0 13.3 %copy-start.1 = (bf16[8,256,128]{2,1,0:T(8,128)(2,1)S(1)}, bf16[8,256,128]{2,1,0:T(8,128)(2,1)}, u32[]{:S(2)}) copy-start(bf16[8,256,128]{2,1,0:T(8,128)(2,1)} %cols_hbm.3) | copy-start | bytes 1572868
  0.0 13.3 %copy-start.2 = (f32[8,2]{0,1:T(2,128)S(1)}, f32[8,2]{0,1:T(2,128)}, u32[]{:S(2)}) copy-start(f32[8,2]{0,1:T(2,128)} %param.17) | copy-start | bytes 196
  0.0 13.3 %copy-start.3 = (f32[16]{0:T(128)S(1)}, f32[16]{0:T(128)}, u32[]{:S(2)}) copy-start(f32[16]{0:T(128)} %defocus_hbm.3) | copy-start | bytes 196
  5.9 11.6 %collective-permute-start = (bf16[2,14,16,256]{3,2,1,0:T(8,128)(2,1)S(1)}, bf16[2,14,16,256]{3,2,1,0:T(8,128)(2,1)S(1)}, u32[]{:S(2)}, u32[]{:S(2)}) collective-permute-start(bf16[2,14,16,256]{3,2,1,0:T(8,128)(2,1)S(1)} %get-tuple-element.34), channel_id=1, source_target_pairs={{0,2},{2,0},{4,6},{6,4},{8,10},{10,8},{12,14},{14,12},{1,3},{3,1},... | collective-permute-start | bytes 688136 | tf_op jit(solution)/shard_map/ppermute | solution.py:549
  8.9 6.5 %collective-permute-start.1 = (bf16[2,3,16,256]{3,2,1,0:T(8,128)(2,1)S(1)}, bf16[2,3,16,256]{3,2,1,0:T(8,128)(2,1)S(1)}, u32[]{:S(2)}, u32[]{:S(2)}) collective-permute-start(bf16[2,3,16,256]{3,2,1,0:T(8,128)(2,1)S(1)} %get-tuple-element.37), channel_id=1, source_target_pairs={{0,12},{2,14},{4,8},{6,10},{8,4},{10,6},{12,0},{14,2},{1,13},{3,15... | collective-permute-start | bytes 147464 | tf_op jit(solution)/shard_map/ppermute | solution.py:552
  12.5 5.0 %collective-permute-start.2 = (bf16[2,3,16,256]{3,2,1,0:T(8,128)(2,1)S(1)}, bf16[2,3,16,256]{3,2,1,0:T(8,128)(2,1)S(1)}, u32[]{:S(2)}, u32[]{:S(2)}) collective-permute-start(bf16[2,3,16,256]{3,2,1,0:T(8,128)(2,1)S(1)} %get-tuple-element.38), channel_id=1, source_target_pairs={{0,8},{2,10},{4,12},{6,14},{8,0},{10,2},{12,4},{14,6},{1,9},{3,11}... | collective-permute-start | bytes 147464 | tf_op jit(solution)/shard_map/ppermute | solution.py:552
  12.5 5.0 %collective-permute-start.3 = (bf16[2,3,16,256]{3,2,1,0:T(8,128)(2,1)S(1)}, bf16[2,3,16,256]{3,2,1,0:T(8,128)(2,1)S(1)}, u32[]{:S(2)}, u32[]{:S(2)}) collective-permute-start(bf16[2,3,16,256]{3,2,1,0:T(8,128)(2,1)S(1)} %get-tuple-element.39), channel_id=1, source_target_pairs={{0,4},{2,6},{4,0},{6,2},{8,12},{10,14},{12,8},{14,10},{1,5},{3,7},... | collective-permute-start | bytes 147464 | tf_op jit(solution)/shard_map/ppermute | solution.py:552
  17.6 6.3 %collective-permute-start.4 = (bf16[31,16,256]{2,1,0:T(8,128)(2,1)S(1)}, bf16[31,16,256]{2,1,0:T(8,128)(2,1)S(1)}, u32[]{:S(2)}, u32[]{:S(2)}) collective-permute-start(bf16[31,16,256]{2,1,0:T(8,128)(2,1)S(1)} %get-tuple-element.41), channel_id=1, source_target_pairs={{0,2},{2,0},{4,6},{6,4},{8,10},{10,8},{12,14},{14,12},{1,3},{3,1},... | collective-permute-start | bytes 761864 | tf_op jit(solution)/shard_map/ppermute | solution.py:549
  18.2 6.9 %collective-permute-start.5 = (bf16[14,16,256]{2,1,0:T(8,128)(2,1)S(1)}, bf16[14,16,256]{2,1,0:T(8,128)(2,1)S(1)}, u32[]{:S(2)}, u32[]{:S(2)}) collective-permute-start(bf16[14,16,256]{2,1,0:T(8,128)(2,1)S(1)} %get-tuple-element.44), channel_id=1, source_target_pairs={{0,12},{2,14},{4,8},{6,10},{8,4},{10,6},{12,0},{14,2},{1,13},{3,15... | collective-permute-start | bytes 344072 | tf_op jit(solution)/shard_map/ppermute | solution.py:552
  20.0 9.1 %collective-permute-start.6 = (bf16[14,16,256]{2,1,0:T(8,128)(2,1)S(1)}, bf16[14,16,256]{2,1,0:T(8,128)(2,1)S(1)}, u32[]{:S(2)}, u32[]{:S(2)}) collective-permute-start(bf16[14,16,256]{2,1,0:T(8,128)(2,1)S(1)} %get-tuple-element.45), channel_id=1, source_target_pairs={{0,8},{2,10},{4,12},{6,14},{8,0},{10,2},{12,4},{14,6},{1,9},{3,11}... | collective-permute-start | bytes 344072 | tf_op jit(solution)/shard_map/ppermute | solution.py:552
  24.0 6.2 %collective-permute-start.7 = (bf16[14,16,256]{2,1,0:T(8,128)(2,1)S(1)}, bf16[14,16,256]{2,1,0:T(8,128)(2,1)S(1)}, u32[]{:S(2)}, u32[]{:S(2)}) collective-permute-start(bf16[14,16,256]{2,1,0:T(8,128)(2,1)S(1)} %get-tuple-element.46), channel_id=1, source_target_pairs={{0,4},{2,6},{4,0},{6,2},{8,12},{10,14},{12,8},{14,10},{1,5},{3,7},... | collective-permute-start | bytes 344072 | tf_op jit(solution)/shard_map/ppermute | solution.py:552

commit v15 on v14

--- a/solution.py
+++ b/solution.py
@@ -222,30 +222,31 @@
     if len(outs) == 1:
         outs[0][...] = totals[...].astype(bf16)
         return
-    far_send, far_keep, near_send, near_keep, z_keep = outs[:5]
-    z_sends = outs[5:]
-    _, x_slots, owned, _ = near_keep.shape
-    rounds = len(z_sends) + 1
+    x_send, x_keep, own_send, own_keep, z_send, z_keep = outs
+    x_slots, owned, _ = own_keep.shape
     me = lax.axis_index("img")
-    near = near_keep.shape[0]
-    for k in range(rounds):
-        mine = pl.ds(pl.multiple_of((me ^ (2 * k)) * owned, owned), owned)
-        theirs = pl.ds(pl.multiple_of((me ^ (2 * k + 1)) * owned, owned), owned)
-        keep, send, n = (near_keep, near_send, k) if k < near else (far_keep, far_send, rounds - 1 - k)
-        keep[n] = totals[-x_slots:, mine, :]
-        send[n] = totals[-x_slots:, theirs, :].astype(bf16)
-        z_out = z_keep if k == 0 else z_sends[k - 1]
-        z_out[0] = totals[:-x_slots, mine, :].astype(z_out.dtype)
-        z_out[1] = totals[:-x_slots, theirs, :].astype(z_out.dtype)
+
+    def rows_of(flip):
+        return pl.ds(pl.multiple_of((me ^ flip) * owned, owned), owned)
+
+    for n, k in enumerate(LINE):
+        x_send[n] = totals[-x_slots:, rows_of(2 * k + 1), :].astype(bf16)
+        x_keep[n] = totals[-x_slots:, rows_of(2 * k), :]
+    own_send[...] = totals[-x_slots:, rows_of(1), :].astype(bf16)
+    own_keep[...] = totals[-x_slots:, rows_of(0), :]
+    for n in range(4):
+        z_send[n] = totals[:-x_slots, rows_of(n + 4), :].astype(bf16)
+        z_keep[n] = totals[:-x_slots, rows_of(n), :]
 
 
 SCRATCH = 20
+LINE = (2, 3, 1)
 SLOTS = 8
 GROUP = 4
-Z_SLOTS = 3
-
-
-def own_totals(images, class_index, pose_index, defocus_bin, defocus, rows_table, cols_table, plane_weight, turns_round):
+Z_SLOTS = 4
+
+
+def own_totals(images, class_index, pose_index, defocus_bin, defocus, rows_table, cols_table, plane_weight, members):
     count, box, _ = images.shape
     poses, rows, _ = rows_table.shape
     cols = cols_table.shape[2]
@@ -255,16 +256,15 @@
     any_place = pl.BlockSpec(memory_space=pl.ANY)
     vmem = pl.BlockSpec(memory_space=pltpu.VMEM)
     lanes = 128 * (-(-2 * count // 128))
-    if turns_round == 0:
+    if members == 1:
         out_shape = [jax.ShapeDtypeStruct((slots, rows, 2 * cols), bf16)]
     else:
         slots += 1
-        owned = rows // (2 * turns_round)
-        x_piece = (turns_round // 2, slots - Z_SLOTS, owned, 2 * cols)
-        z_piece = (2, Z_SLOTS, owned, 2 * cols)
-        out_shape = [pltpu.VMEM(x_piece, bf16), pltpu.VMEM(x_piece, f32)] * 2
-        out_shape += [pltpu.VMEM(z_piece, f32)]
-        out_shape += [pltpu.VMEM(z_piece, bf16)] * (turns_round - 1)
+        tail = (rows // members, 2 * cols)
+        x_slots = slots - Z_SLOTS
+        out_shape = []
+        for lead in ((len(LINE), x_slots), (x_slots,), (4, Z_SLOTS)):
+            out_shape += [pltpu.VMEM(lead + tail, bf16), pltpu.VMEM(lead + tail, f32)]
     operands = (
         class_index[:, 0], pose_index, defocus_bin, defocus, plane_weight.T,
         jnp.asarray(table_y, bf16), jnp.asarray(table_x.T.copy(), bf16),
@@ -395,54 +395,44 @@
     )(*arrays)
 
 
-def fold_kernel(far_keep, far_came, near_send, z_keep, *refs):
-    rounds = near_send.shape[0] + far_keep.shape[0]
-    z_came, refs = refs[: rounds - 1], refs[rounds - 1 :]
-    z_own, x_send, far_sends = refs[0], refs[1], refs[2:]
-    for k, send in enumerate(far_sends):
-        send[...] = (far_keep[k] + far_came[k].astype(f32)).astype(bf16)
-    near, x_slots = near_send.shape[:2]
-    for k in range(near):
-        x_send[k * x_slots : (k + 1) * x_slots] = near_send[k]
+def fold_kernel(x_keep, x_came, z_keep, z_came, own_send, far_a, far_b, near, z_kept, own_out):
+    own_out[...] = own_send[...]
+    x_slots, z_slots = x_keep.shape[1], z_keep.shape[1]
+    for n, send in enumerate((far_a, far_b, near)):
+        send[:x_slots] = (x_keep[n] + x_came[n].astype(f32)).astype(bf16)
     for side in range(2):
-        value = z_keep[side]
-        for came in z_came:
-            value = value + came[side].astype(f32)
-        if side == 0:
-            z_own[...] = value
-        else:
-            x_send[near * x_slots :] = value.astype(bf16)
-
-
-def fold_phase(far_keep, far_came, near_send, z_keep, z_came):
-    far, x_slots = far_keep.shape[:2]
-    z_slots = z_keep.shape[1]
-    tail = far_keep.shape[2:]
-    out_shape = [
-        pltpu.VMEM((z_slots,) + tail, f32),
-        pltpu.VMEM((near_send.shape[0] * x_slots + z_slots,) + tail, bf16),
-    ]
-    out_shape += [pltpu.VMEM((x_slots,) + tail, bf16)] * far
-    return call_in_vmem(fold_kernel, (far_keep, far_came, near_send, z_keep, *z_came), out_shape)
-
-
-def near_kernel(keep, came, own, *sends):
-    near, x_slots = keep.shape[:2]
-    for k, out in enumerate((own,) + sends):
-        part = came[k * x_slots : (k + 1) * x_slots].astype(f32)
-        out[...] = (keep[k] + part).astype(out.dtype)
-
-
-def near_phase(keep, came):
-    piece = keep.shape[1:]
-    out_shape = [pltpu.VMEM(piece, f32)] + [pltpu.VMEM(piece, bf16)] * (keep.shape[0] - 1)
-    return call_in_vmem(near_kernel, (keep, came), out_shape)
+        z_kept[side] = z_keep[side] + z_came[side].astype(f32)
+        first = x_slots + side * z_slots
+        near[first : first + z_slots] = (
+            z_keep[2 + side] + z_came[2 + side].astype(f32)
+        ).astype(bf16)
+
+
+def fold_phase(x_keep, x_came, z_keep, z_came, own_send):
+    x_slots, z_slots = x_keep.shape[1], z_keep.shape[1]
+    tail = x_keep.shape[2:]
+    out_shape = [pltpu.VMEM((x_slots,) + tail, bf16)] * 2
+    out_shape += [pltpu.VMEM((x_slots + 2 * z_slots,) + tail, bf16), pltpu.VMEM((2, z_slots) + tail, f32)]
+    out_shape += [pltpu.VMEM(own_send.shape, bf16)]
+    return call_in_vmem(fold_kernel, (x_keep, x_came, z_keep, z_came, own_send), out_shape)
+
+
+def side_kernel(z_kept, near_came, z_own, z_send):
+    z_slots = z_own.shape[0]
+    first = near_came.shape[0] - 2 * z_slots
+    z_own[...] = z_kept[0] + near_came[first : first + z_slots].astype(f32)
+    z_send[...] = (z_kept[1] + near_came[first + z_slots :].astype(f32)).astype(bf16)
+
+
+def side_phase(z_kept, near_came):
+    piece = z_kept.shape[1:]
+    return call_in_vmem(side_kernel, (z_kept, near_came), [pltpu.VMEM(piece, f32), pltpu.VMEM(piece, bf16)])
 
 
 def weight_kernel(high_ref, low_ref, share_ref, z_own, z_came, out_ref, ridge_ref):
     slots, pairs = share_ref.shape
     owned, _, cols = ridge_ref.shape
-    counts = z_own[0] + z_came[z_came.shape[0] - z_own.shape[0]].astype(f32)
+    counts = z_own[0] + z_came[0].astype(f32)
     scaled = jnp.concatenate([counts[:CLASSES, :pairs]] * (slots // CLASSES), 0) * share_ref[...]
     c_high, c_low = split_two(scaled)
     weight = (
@@ -477,7 +467,7 @@
     first = z_own.shape[0]
     for s in range(slots):
         if s + 1 < first:
-            value = z_own[s + 1] + z_came[z_came.shape[0] - first + s + 1].astype(f32)
+            value = z_own[s + 1] + z_came[s + 1].astype(f32)
         else:
             value = x_own[s + 1 - first]
             for part in x_came:
@@ -531,38 +521,31 @@
     return jnp.einsum("czpmbr,pmbj->rczj", left, v, precision=exact)
 
 
-def by_rounds(images, class_index, pose_index, defocus_bin, defocus, rows_table, cols_table, plane_weight):
+def by_pairs(images, class_index, pose_index, defocus_bin, defocus, rows_table, cols_table, plane_weight):
     members = lax.axis_size("img")
-    rounds = members // 2
     rows = rows_table.shape[1]
     planes = plane_weight.shape[1]
     cols = cols_table.shape[2]
     owned = rows // members
-    outs = own_totals(
-        images, class_index, pose_index, defocus_bin, defocus, rows_table, cols_table, plane_weight, rounds
-    )
-    far_send, far_keep, near_send, near_keep, z_keep = outs[:5]
-    z_sends = outs[5:]
-    near = near_keep.shape[0]
-
-    def along_x(value):
-        return lax.ppermute(value, "img", [(i, i ^ 1) for i in range(members)])
-
-    def along_z(value, k):
-        return lax.ppermute(value, "img", [(i, i ^ (2 * k)) for i in range(members)])
-
-    far_ks, near_ks = range(near, rounds)[::-1], range(1, near)
-    far_came = along_x(far_send)
-    z_came = [along_z(z_sends[k - 1], k) for k in (*far_ks, *near_ks)]
+
+    def exchange(value, flip):
+        return lax.ppermute(value, "img", [(i, i ^ flip) for i in range(members)])
+
+    x_send, x_keep, own_send, own_keep, z_send, z_keep = own_totals(
+        images, class_index, pose_index, defocus_bin, defocus, rows_table, cols_table, plane_weight, members
+    )
+    x_came = exchange(x_send, 1)
+    z_came = exchange(z_send, 4)
     tables = own_ridges(defocus, plane_weight, rows_table, cols_table, owned)
-    far_keep, tables = lax.optimization_barrier((far_keep, tables))
-    z_own, x_send, *x_sends = fold_phase(far_keep, far_came, near_send, z_keep, z_came)
-    z_came = along_x(x_send)
-    x_came = [along_z(send, k) for send, k in zip(x_sends, far_ks)]
-    x_own, *x_sends = near_phase(near_keep, z_came)
-    x_came += [along_z(send, k) for send, k in zip(x_sends, near_ks)]
+    x_keep, tables = lax.optimization_barrier((x_keep, tables))
+    far_a, far_b, near, z_kept, own_send = fold_phase(x_keep, x_came, z_keep, z_came, own_send)
+    near_came = exchange(near, 2)
+    far_a, far_b = exchange(far_a, 4), exchange(far_b, 6)
+    own_came = exchange(own_send, 1)
+    z_own, z_send = side_phase(z_kept, near_came)
+    z_came = exchange(z_send, 1)
     ridge = own_weights(tables, z_own, z_came)
-    out = finish(planes, ridge, x_own, z_own, z_came, x_came)
+    out = finish(planes, ridge, own_keep, z_own, z_came, (near_came, far_a, far_b, own_came))
     return out.reshape(owned, CLASSES, planes, 2, cols)
 
 
@@ -573,7 +556,7 @@
     members = lax.axis_size("img")
     owned = rows // members
     (totals,) = own_totals(
-        images, class_index, pose_index, defocus_bin, defocus, rows_table, cols_table, plane_weight, 0
+        images, class_index, pose_index, defocus_bin, defocus, rows_table, cols_table, plane_weight, 1
     )
     slots = totals.shape[0]
     totals = totals.reshape(slots, members, owned, 2 * cols).transpose(1, 0, 2, 3)
@@ -590,8 +573,8 @@
     rows = arrays[5].shape[1]
     members = lax.axis_size("img")
     images = members * arrays[0].shape[0]
-    small = members >= 4 and members & (members - 1) == 0 and images <= 256 and rows % (16 * members) == 0
-    return (by_rounds if small else by_scatter)(*arrays)
+    paired = members == 8 and images <= 256 and rows % (16 * members) == 0
+    return (by_pairs if paired else by_scatter)(*arrays)
 
 
 def solution(mesh):

time: 31.3 us -> 31.9 us (1.019)
    ppermute x8 -> x7, waiting for transfers between devices: 10.9 us -> 11.2 us  [exchange(): return lax.ppermute(value, 'img', [(i, i ^ flip) for i in range(members)])]
    ppermute x8 -> x7, starting transfers between devices: 10.8 us -> 10.8 us  [exchange(): return lax.ppermute(value, 'img', [(i, i ^ flip) for i in range(members)])]
  transfers between devices with their start and end apart: 8 -> 7, of which waited for: 4 -> 4; matrix products, arithmetic and copies ran while one was open for 0% -> 0% of each run, Pallas kernels for 8% -> 8%
where the time goes in v15:
time: 31.9 us; the launch traced here: 31.4 us
  waiting for transfers between devices  11.2 us (35%)
  starting transfers between devices  10.8 us (34%)
  Pallas kernels  9.4 us (29%)
    ppermute x7, waiting for transfers between devices, exchange(): return lax.ppermute(value, 'img', [(i, i ^ flip) for i in range(members)])  11.2 us
    ppermute x7, starting transfers between devices, exchange(): return lax.ppermute(value, 'img', [(i, i ^ flip) for i in range(members)])  10.8 us
    pallas_call x1, Pallas kernels, own_totals(): pl.pallas_call(slices_kernel, out_shape=out_shape, in_specs=[any_place] *...  5.9 us
    pallas_call x1, Pallas kernels, own_ridges(): pl.pallas_call(ridge_kernel, out_shape=[table, table, jax.ShapeDtypeStruc...  2.09 us
    pallas_call x1, Pallas kernels, finish(): pl.pallas_call(functools.partial(finish_kernel, planes), out_shape=jax.Sh...  0.94 us
  transfers between devices with their start and end apart: 7, of which 4 were waited for; matrix products, arithmetic and copies ran while one was open for 0% of the time, Pallas kernels for 8%

profile of v15, /device:TPU:0, one launch (start us, length us, event | category | flops | bytes accessed | tf_op | source)
XLA Modules:
  0.0 31.4 jit_solution(16172500006863957602)
XLA Ops:
  0.0 0.0 copy-start
  0.0 0.0 copy-start.1
  0.0 0.0 copy-start.2
  0.0 0.0 copy-start.3
  0.0 5.9 %shard_map.100 = (bf16[3,13,16,256]{3,2,1,0:T(8,128)(2,1)S(1)}, f32[3,13,16,256]{3,2,1,0:T(8,128)S(1)}, bf16[13,16,256]{2,1,0:T(8,128)(2,1)S(1)}, f32[13,16,256]...) custom-call(s32[16]{0:T(128)} %bitcast.5, s32[16]{0:T(128)} %pose_hbm.1, ...), custom_call_target="tpu_custom_call" | custom-call | flops 2097152000 | bytes 6291456 | tf_op jit(solution)/shard_map/pallas_call | solution.py:273
  5.9 3.0 %collective-permute-start = (bf16[3,13,16,256]{3,2,1,0:T(8,128)(2,1)S(1)}, bf16[3,13,16,256]{3,2,1,0:T(8,128)(2,1)S(1)}, u32[]{:S(2)}, u32[]{:S(2)}) collective-permute-start(bf16[3,13,16,256]{3,2,1,0:T(8,128)(2,1)S(1)} %get-tuple-element.33), channel_id=1, source_target_pairs={{0,2},{2,0},{4,6},{6,4},{8,10},{10,8},{12,14},{14,12},{1,3},{3,1},... | collective-permute-start | bytes 958472 | tf_op jit(solution)/shard_map/ppermute | solution.py:532
  8.9 2.6 %collective-permute-start.1 = (bf16[4,4,16,256]{3,2,1,0:T(8,128)(2,1)S(1)}, bf16[4,4,16,256]{3,2,1,0:T(8,128)(2,1)S(1)}, u32[]{:S(2)}, u32[]{:S(2)}) collective-permute-start(bf16[4,4,16,256]{3,2,1,0:T(8,128)(2,1)S(1)} %get-tuple-element.35), channel_id=1, source_target_pairs={{0,8},{2,10},{4,12},{6,14},{8,0},{10,2},{12,4},{14,6},{1,9},{3,11}... | collective-permute-start | bytes 393224 | tf_op jit(solution)/shard_map/ppermute | solution.py:532
  11.5 0.0 copy-done
  11.5 0.0 copy-done.1
  11.5 0.0 copy-done.2
  11.5 0.0 copy-done.3
  11.5 2.1 %shard_map.101 = (bf16[128,2048]{1,0:T(8,128)(2,1)S(1)}, bf16[128,2048]{1,0:T(8,128)(2,1)S(1)}, f32[16,128]{1,0:T(8,128)S(1)}) custom-call(f32[16]{0:T(128)S(1)} %copy-done.3, f32[2,8]{1,0:T(2,128)S(1)} %bitcast.4, bf16[8,128,256]{2,1,0:T(8,128)(2,1)S(1)} %copy-done, bf16[8,256,128]{2,1,0:T(8,128)(2,1)S(1)} %copy-done.1), custom_call_target="tpu_custom_call" | custom-call | flops 1000 | bytes 1000 | tf_op jit(solution)/shard_map/pallas_call | solution.py:367
  13.6 4.0 %collective-permute-done.1.z_came = bf16[4,4,16,256]{3,2,1,0:T(8,128)(2,1)S(1)} collective-permute-done((bf16[4,4,16,256]{3,2,1,0:T(8,128)(2,1)S(1)}, bf16[4,4,16,256]{3,2,1,0:T(8,128)(2,1)S(1)}, u32[]{:S(2)}, u32[]{:S(2)}) %collective-permute-start.1) | collective-permute-done | bytes 131104 | tf_op jit(solution)/shard_map/ppermute | solution.py:532
  17.6 0.0 collective-permute-done.x_came
  17.6 0.1 shard_map.102
  17.7 0.8 %collective-permute-start.2 = (bf16[21,16,256]{2,1,0:T(8,128)(2,1)S(1)}, bf16[21,16,256]{2,1,0:T(8,128)(2,1)S(1)}, u32[]{:S(2)}, u32[]{:S(2)}) collective-permute-start(bf16[21,16,256]{2,1,0:T(8,128)(2,1)S(1)} %get-tuple-element.38), channel_id=1, source_target_pairs={{0,4},{2,6},{4,0},{6,2},{8,12},{10,14},{12,8},{14,10},{1,5},{3,7},... | collective-permute-start | bytes 516104 | tf_op jit(solution)/shard_map/ppermute | solution.py:532
  18.4 3.4 %collective-permute-start.4 = (bf16[13,16,256]{2,1,0:T(8,128)(2,1)S(1)}, bf16[13,16,256]{2,1,0:T(8,128)(2,1)S(1)}, u32[]{:S(2)}, u32[]{:S(2)}) collective-permute-start(bf16[13,16,256]{2,1,0:T(8,128)(2,1)S(1)} %get-tuple-element.42), channel_id=1, source_target_pairs={{0,8},{2,10},{4,12},{6,14},{8,0},{10,2},{12,4},{14,6},{1,9},{3,11}... | collective-permute-start | bytes 319496 | tf_op jit(solution)/shard_map/ppermute | solution.py:532
  21.8 0.3 %collective-permute-start.5 = (bf16[13,16,256]{2,1,0:T(8,128)(2,1)S(1)}, bf16[13,16,256]{2,1,0:T(8,128)(2,1)S(1)}, u32[]{:S(2)}, u32[]{:S(2)}) collective-permute-start(bf16[13,16,256]{2,1,0:T(8,128)(2,1)S(1)} %get-tuple-element.43), channel_id=1, source_target_pairs={{0,12},{2,14},{4,8},{6,10},{8,4},{10,6},{12,0},{14,2},{1,13},{3,15... | collective-permute-start | bytes 319496 | tf_op jit(solution)/shard_map/ppermute | solution.py:532
  22.1 0.6 %collective-permute-start.6 = (bf16[13,16,256]{2,1,0:T(8,128)(2,1)S(1)}, bf16[13,16,256]{2,1,0:T(8,128)(2,1)S(1)}, u32[]{:S(2)}, u32[]{:S(2)}) collective-permute-start(bf16[13,16,256]{2,1,0:T(8,128)(2,1)S(1)} %get-tuple-element.44), channel_id=1, source_target_pairs={{0,2},{2,0},{4,6},{6,4},{8,10},{10,8},{12,14},{14,12},{1,3},{3,1},... | collective-permute-start | bytes 319496 | tf_op jit(solution)/shard_map/ppermute | solution.py:532
  22.8 2.5 %collective-permute-done.2.near_came.refs_0_ = bf16[21,16,256]{2,1,0:T(8,128)(2,1)S(1)} collective-permute-done((bf16[21,16,256]{2,1,0:T(8,128)(2,1)S(1)}, bf16[21,16,256]{2,1,0:T(8,128)(2,1)S(1)}, u32[]{:S(2)}, u32[]{:S(2)}) %collective-permute-start.2) | collective-permute-done | bytes 172064 | tf_op jit(solution)/shard_map/ppermute | solution.py:532
  25.2 0.1 collective-permute-start.3
  25.4 3.8 %collective-permute-done.3.z_came = bf16[4,16,256]{2,1,0:T(8,128)(2,1)S(1)} collective-permute-done((bf16[4,16,256]{2,1,0:T(8,128)(2,1)S(1)}, bf16[4,16,256]{2,1,0:T(8,128)(2,1)S(1)}, u32[]{:S(2)}, u32[]{:S(2)}) %collective-permute-start.3) | collective-permute-done | bytes 32800 | tf_op jit(solution)/shard_map/ppermute | solution.py:532
  29.2 0.4 %shard_map.104.ridge_ref = f32[16,16,128]{2,1,0:T(8,128)S(1)} custom-call(bf16[128,2048]{1,0:T(8,128)(2,1)S(1)} %get-tuple-element.29.high_ref, bf16[128,2048]{1,0:T(8,128)(2,1)S(1)} %get-tuple-element.30.low_ref, f32[16,128]{1,0:T(8,128)S(1)} %get-tuple-element.31.share_ref, f32[4,16,256]{2,1,0:T(8,128)S(1)} %get-tuple-element.39.z_own, ...), custom_call_target="tpu_custom_call" | custom-call | flops 1000 | bytes 1000 | tf_op jit(solution)/shard_map/pallas_call | solution.py:453
  29.6 0.0 collective-permute-done.4.refs_1_
  29.6 0.9 %collective-permute-done.5.refs_2_ = bf16[13,16,256]{2,1,0:T(8,128)(2,1)S(1)} collective-permute-done((bf16[13,16,256]{2,1,0:T(8,128)(2,1)S(1)}, bf16[13,16,256]{2,1,0:T(8,128)(2,1)S(1)}, u32[]{:S(2)}, u32[]{:S(2)}) %collective-permute-start.5) | collective-permute-done | bytes 106528 | tf_op jit(solution)/shard_map/ppermute | solution.py:532
  30.5 0.0 collective-permute-done.6.refs_3_
  30.5 0.9 %shard_map.105 = f32[16,32,128]{2,1,0:T(8,128)} custom-call(f32[16,16,128]{2,1,0:T(8,128)S(1)} %shard_map.104.ridge_ref, f32[13,16,256]{2,1,0:T(8,128)S(1)} %get-tuple-element.41.x_own, f32[4,16,256]{2,1,0:T(8,128)S(1)} %get-tuple-element.39.z_own, bf16[4,16,256]{2,1,0:T(8,128)(2,1)S(1)} %collective-permute-done.3.z_came, ...), custom_call_target="tpu_custom_call" | custom-call | flops 1000 | bytes 1000 | tf_op jit(solution)/shard_map/pallas_call | solution.py:484
  (1 shorter events, 0.0 us)
Async XLA Ops:
  0.0 11.5 %copy-start = (bf16[8,128,256]{2,1,0:T(8,128)(2,1)S(1)}, bf16[8,128,256]{2,1,0:T(8,128)(2,1)}, u32[]{:S(2)}) copy-start(bf16[8,128,256]{2,1,0:T(8,128)(2,1)} %rows_hbm.3) | copy-start | bytes 1572868
  0.0 11.5 %copy-start.1 = (bf16[8,256,128]{2,1,0:T(8,128)(2,1)S(1)}, bf16[8,256,128]{2,1,0:T(8,128)(2,1)}, u32[]{:S(2)}) copy-start(bf16[8,256,128]{2,1,0:T(8,128)(2,1)} %cols_hbm.3) | copy-start | bytes 1572868
  0.0 11.5 %copy-start.2 = (f32[8,2]{0,1:T(2,128)S(1)}, f32[8,2]{0,1:T(2,128)}, u32[]{:S(2)}) copy-start(f32[8,2]{0,1:T(2,128)} %param.17) | copy-start | bytes 196
  0.0 11.5 %copy-start.3 = (f32[16]{0:T(128)S(1)}, f32[16]{0:T(128)}, u32[]{:S(2)}) copy-start(f32[16]{0:T(128)} %defocus_hbm.3) | copy-start | bytes 196
  5.9 11.7 %collective-permute-start = (bf16[3,13,16,256]{3,2,1,0:T(8,128)(2,1)S(1)}, bf16[3,13,16,256]{3,2,1,0:T(8,128)(2,1)S(1)}, u32[]{:S(2)}, u32[]{:S(2)}) collective-permute-start(bf16[3,13,16,256]{3,2,1,0:T(8,128)(2,1)S(1)} %get-tuple-element.33), channel_id=1, source_target_pairs={{0,2},{2,0},{4,6},{6,4},{8,10},{10,8},{12,14},{14,12},{1,3},{3,1},... | collective-permute-start | bytes 958472 | tf_op jit(solution)/shard_map/ppermute | solution.py:532
  8.9 8.7 %collective-permute-start.1 = (bf16[4,4,16,256]{3,2,1,0:T(8,128)(2,1)S(1)}, bf16[4,4,16,256]{3,2,1,0:T(8,128)(2,1)S(1)}, u32[]{:S(2)}, u32[]{:S(2)}) collective-permute-start(bf16[4,4,16,256]{3,2,1,0:T(8,128)(2,1)S(1)} %get-tuple-element.35), channel_id=1, source_target_pairs={{0,8},{2,10},{4,12},{6,14},{8,0},{10,2},{12,4},{14,6},{1,9},{3,11}... | collective-permute-start | bytes 393224 | tf_op jit(solution)/shard_map/ppermute | solution.py:532
  17.7 7.5 %collective-permute-start.2 = (bf16[21,16,256]{2,1,0:T(8,128)(2,1)S(1)}, bf16[21,16,256]{2,1,0:T(8,128)(2,1)S(1)}, u32[]{:S(2)}, u32[]{:S(2)}) collective-permute-start(bf16[21,16,256]{2,1,0:T(8,128)(2,1)S(1)} %get-tuple-element.38), channel_id=1, source_target_pairs={{0,4},{2,6},{4,0},{6,2},{8,12},{10,14},{12,8},{14,10},{1,5},{3,7},... | collective-permute-start | bytes 516104 | tf_op jit(solution)/shard_map/ppermute | solution.py:532
  18.4 11.1 %collective-permute-start.4 = (bf16[13,16,256]{2,1,0:T(8,128)(2,1)S(1)}, bf16[13,16,256]{2,1,0:T(8,128)(2,1)S(1)}, u32[]{:S(2)}, u32[]{:S(2)}) collective-permute-start(bf16[13,16,256]{2,1,0:T(8,128)(2,1)S(1)} %get-tuple-element.42), channel_id=1, source_target_pairs={{0,8},{2,10},{4,12},{6,14},{8,0},{10,2},{12,4},{14,6},{1,9},{3,11}... | collective-permute-start | bytes 319496 | tf_op jit(solution)/shard_map/ppermute | solution.py:532
  21.8 8.7 %collective-permute-start.5 = (bf16[13,16,256]{2,1,0:T(8,128)(2,1)S(1)}, bf16[13,16,256]{2,1,0:T(8,128)(2,1)S(1)}, u32[]{:S(2)}, u32[]{:S(2)}) collective-permute-start(bf16[13,16,256]{2,1,0:T(8,128)(2,1)S(1)} %get-tuple-element.43), channel_id=1, source_target_pairs={{0,12},{2,14},{4,8},{6,10},{8,4},{10,6},{12,0},{14,2},{1,13},{3,15... | collective-permute-start | bytes 319496 | tf_op jit(solution)/shard_map/ppermute | solution.py:532
  22.1 8.3 %collective-permute-start.6 = (bf16[13,16,256]{2,1,0:T(8,128)(2,1)S(1)}, bf16[13,16,256]{2,1,0:T(8,128)(2,1)S(1)}, u32[]{:S(2)}, u32[]{:S(2)}) collective-permute-start(bf16[13,16,256]{2,1,0:T(8,128)(2,1)S(1)} %get-tuple-element.44), channel_id=1, source_target_pairs={{0,2},{2,0},{4,6},{6,4},{8,10},{10,8},{12,14},{14,12},{1,3},{3,1},... | collective-permute-start | bytes 319496 | tf_op jit(solution)/shard_map/ppermute | solution.py:532
  25.2 4.0 %collective-permute-start.3 = (bf16[4,16,256]{2,1,0:T(8,128)(2,1)S(1)}, bf16[4,16,256]{2,1,0:T(8,128)(2,1)S(1)}, u32[]{:S(2)}, u32[]{:S(2)}) collective-permute-start(bf16[4,16,256]{2,1,0:T(8,128)(2,1)S(1)} %get-tuple-element.40), channel_id=1, source_target_pairs={{0,2},{2,0},{4,6},{6,4},{8,10},{10,8},{12,14},{14,12},{1,3},{3,1},... | collective-permute-start | bytes 98312 | tf_op jit(solution)/shard_map/ppermute | solution.py:532

commit v16 on v15

--- a/solution.py
+++ b/solution.py
@@ -222,7 +222,8 @@
     if len(outs) == 1:
         outs[0][...] = totals[...].astype(bf16)
         return
-    x_send, x_keep, own_send, own_keep, z_send, z_keep = outs
+    x_send, x_keep, own_send, own_keep, z_keep = outs[:5]
+    z_sends = outs[5:]
     x_slots, owned, _ = own_keep.shape
     me = lax.axis_index("img")
 
@@ -234,16 +235,17 @@
         x_keep[n] = totals[-x_slots:, rows_of(2 * k), :]
     own_send[...] = totals[-x_slots:, rows_of(1), :].astype(bf16)
     own_keep[...] = totals[-x_slots:, rows_of(0), :]
-    for n in range(4):
-        z_send[n] = totals[:-x_slots, rows_of(n + 4), :].astype(bf16)
-        z_keep[n] = totals[:-x_slots, rows_of(n), :]
+    for side in range(2):
+        z_keep[side] = totals[:-x_slots, rows_of(side), :]
+        for n, k in enumerate(LINE):
+            z_sends[n][side] = totals[:-x_slots, rows_of(2 * k + side), :].astype(bf16)
 
 
 SCRATCH = 20
 LINE = (2, 3, 1)
 SLOTS = 8
 GROUP = 4
-Z_SLOTS = 4
+Z_SLOTS = 3
 
 
 def own_totals(images, class_index, pose_index, defocus_bin, defocus, rows_table, cols_table, plane_weight, members):
@@ -263,8 +265,10 @@
         tail = (rows // members, 2 * cols)
         x_slots = slots - Z_SLOTS
         out_shape = []
-        for lead in ((len(LINE), x_slots), (x_slots,), (4, Z_SLOTS)):
+        for lead in ((len(LINE), x_slots), (x_slots,)):
             out_shape += [pltpu.VMEM(lead + tail, bf16), pltpu.VMEM(lead + tail, f32)]
+        out_shape += [pltpu.VMEM((2, Z_SLOTS) + tail, f32)]
+        out_shape += [pltpu.VMEM((2, Z_SLOTS) + tail, bf16)] * len(LINE)
     operands = (
         class_index[:, 0], pose_index, defocus_bin, defocus, plane_weight.T,
         jnp.asarray(table_y, bf16), jnp.asarray(table_x.T.copy(), bf16),
@@ -395,38 +399,25 @@
     )(*arrays)
 
 
-def fold_kernel(x_keep, x_came, z_keep, z_came, own_send, far_a, far_b, near, z_kept, own_out):
+def fold_kernel(x_keep, x_came, own_send, z_keep, *refs):
+    z_came, refs = refs[: len(LINE)], refs[len(LINE) :]
+    x_sends, own_out, z_own, z_send = refs[: len(LINE)], *refs[len(LINE) :]
+    for n, send in enumerate(x_sends):
+        send[...] = (x_keep[n] + x_came[n].astype(f32)).astype(bf16)
     own_out[...] = own_send[...]
-    x_slots, z_slots = x_keep.shape[1], z_keep.shape[1]
-    for n, send in enumerate((far_a, far_b, near)):
-        send[:x_slots] = (x_keep[n] + x_came[n].astype(f32)).astype(bf16)
-    for side in range(2):
-        z_kept[side] = z_keep[side] + z_came[side].astype(f32)
-        first = x_slots + side * z_slots
-        near[first : first + z_slots] = (
-            z_keep[2 + side] + z_came[2 + side].astype(f32)
-        ).astype(bf16)
-
-
-def fold_phase(x_keep, x_came, z_keep, z_came, own_send):
-    x_slots, z_slots = x_keep.shape[1], z_keep.shape[1]
-    tail = x_keep.shape[2:]
-    out_shape = [pltpu.VMEM((x_slots,) + tail, bf16)] * 2
-    out_shape += [pltpu.VMEM((x_slots + 2 * z_slots,) + tail, bf16), pltpu.VMEM((2, z_slots) + tail, f32)]
-    out_shape += [pltpu.VMEM(own_send.shape, bf16)]
-    return call_in_vmem(fold_kernel, (x_keep, x_came, z_keep, z_came, own_send), out_shape)
-
-
-def side_kernel(z_kept, near_came, z_own, z_send):
-    z_slots = z_own.shape[0]
-    first = near_came.shape[0] - 2 * z_slots
-    z_own[...] = z_kept[0] + near_came[first : first + z_slots].astype(f32)
-    z_send[...] = (z_kept[1] + near_came[first + z_slots :].astype(f32)).astype(bf16)
-
-
-def side_phase(z_kept, near_came):
-    piece = z_kept.shape[1:]
-    return call_in_vmem(side_kernel, (z_kept, near_came), [pltpu.VMEM(piece, f32), pltpu.VMEM(piece, bf16)])
+    for side, out in enumerate((z_own, z_send)):
+        value = z_keep[side]
+        for came in z_came:
+            value = value + came[side].astype(f32)
+        out[...] = value.astype(out.dtype)
+
+
+def fold_phase(x_keep, x_came, own_send, z_keep, z_came):
+    piece = own_send.shape
+    z_piece = z_keep.shape[1:]
+    out_shape = [pltpu.VMEM(piece, bf16)] * (len(LINE) + 1)
+    out_shape += [pltpu.VMEM(z_piece, f32), pltpu.VMEM(z_piece, bf16)]
+    return call_in_vmem(fold_kernel, (x_keep, x_came, own_send, z_keep, *z_came), out_shape)
 
 
 def weight_kernel(high_ref, low_ref, share_ref, z_own, z_came, out_ref, ridge_ref):
@@ -531,21 +522,19 @@
     def exchange(value, flip):
         return lax.ppermute(value, "img", [(i, i ^ flip) for i in range(members)])
 
-    x_send, x_keep, own_send, own_keep, z_send, z_keep = own_totals(
+    x_send, x_keep, own_send, own_keep, z_keep, *z_sends = own_totals(
         images, class_index, pose_index, defocus_bin, defocus, rows_table, cols_table, plane_weight, members
     )
     x_came = exchange(x_send, 1)
-    z_came = exchange(z_send, 4)
+    z_came = [exchange(send, 2 * k) for send, k in zip(z_sends, LINE)]
     tables = own_ridges(defocus, plane_weight, rows_table, cols_table, owned)
     x_keep, tables = lax.optimization_barrier((x_keep, tables))
-    far_a, far_b, near, z_kept, own_send = fold_phase(x_keep, x_came, z_keep, z_came, own_send)
-    near_came = exchange(near, 2)
-    far_a, far_b = exchange(far_a, 4), exchange(far_b, 6)
+    *x_sends, own_send, z_own, z_send = fold_phase(x_keep, x_came, own_send, z_keep, z_came)
+    x_came = [exchange(send, 2 * k) for send, k in zip(x_sends, LINE)]
     own_came = exchange(own_send, 1)
-    z_own, z_send = side_phase(z_kept, near_came)
     z_came = exchange(z_send, 1)
     ridge = own_weights(tables, z_own, z_came)
-    out = finish(planes, ridge, own_keep, z_own, z_came, (near_came, far_a, far_b, own_came))
+    out = finish(planes, ridge, own_keep, z_own, z_came, (*x_came, own_came))
     return out.reshape(owned, CLASSES, planes, 2, cols)
 
 

time: 31.9 us -> 29.7 us (0.931)
  waiting for transfers between devices: 11.2 us -> 6.89 us
  starting transfers between devices: 10.8 us -> 13.2 us
    ppermute x7 -> x9, waiting for transfers between devices: 11.2 us -> 6.89 us  [exchange(): return lax.ppermute(value, 'img', [(i, i ^ flip) for i in range(members)])]
    ppermute x7 -> x9, starting transfers between devices: 10.8 us -> 13.2 us  [exchange(): return lax.ppermute(value, 'img', [(i, i ^ flip) for i in range(members)])]
  transfers between devices with their start and end apart: 7 -> 9, of which waited for: 4 -> 4; matrix products, arithmetic and copies ran while one was open for 0% -> 0% of each run, Pallas kernels for 8% -> 8%
where the time goes in v16:
time: 29.7 us; the launch traced here: 29.5 us
  starting transfers between devices  13.2 us (44%)
  Pallas kernels  9.39 us (32%)
  waiting for transfers between devices  6.89 us (23%)
    ppermute x9, starting transfers between devices, exchange(): return lax.ppermute(value, 'img', [(i, i ^ flip) for i in range(members)])  13.2 us
    ppermute x9, waiting for transfers between devices, exchange(): return lax.ppermute(value, 'img', [(i, i ^ flip) for i in range(members)])  6.89 us
    pallas_call x1, Pallas kernels, own_totals(): pl.pallas_call(slices_kernel, out_shape=out_shape, in_specs=[any_place] *...  5.9 us
    pallas_call x1, Pallas kernels, own_ridges(): pl.pallas_call(ridge_kernel, out_shape=[table, table, jax.ShapeDtypeStruc...  2.09 us
    pallas_call x1, Pallas kernels, finish(): pl.pallas_call(functools.partial(finish_kernel, planes), out_shape=jax.Sh...  0.95 us
  transfers between devices with their start and end apart: 9, of which 4 were waited for; matrix products, arithmetic and copies ran while one was open for 0% of the time, Pallas kernels for 8%

profile of v16, /device:TPU:0, one launch (start us, length us, event | category | flops | bytes accessed | tf_op | source)
XLA Modules:
  0.0 29.5 jit_solution(7638588136163183959)
XLA Ops:
  0.0 0.0 copy-start
  0.0 0.0 copy-start.1
  0.0 0.0 copy-start.2
  0.0 0.0 copy-start.3
  0.0 5.9 %shard_map.100 = (bf16[3,14,16,256]{3,2,1,0:T(8,128)(2,1)S(1)}, f32[3,14,16,256]{3,2,1,0:T(8,128)S(1)}, bf16[14,16,256]{2,1,0:T(8,128)(2,1)S(1)}, f32[14,16,256]...) custom-call(s32[16]{0:T(128)} %bitcast.5, ...), custom_call_target="tpu_custom_call" | custom-call | flops 2097152000 | bytes 6291456 | tf_op jit(solution)/shard_map/pallas_call | solution.py:277
  5.9 3.0 %collective-permute-start = (bf16[3,14,16,256]{3,2,1,0:T(8,128)(2,1)S(1)}, bf16[3,14,16,256]{3,2,1,0:T(8,128)(2,1)S(1)}, u32[]{:S(2)}, u32[]{:S(2)}) collective-permute-start(bf16[3,14,16,256]{3,2,1,0:T(8,128)(2,1)S(1)} %get-tuple-element.34), channel_id=1, source_target_pairs={{0,2},{2,0},{4,6},{6,4},{8,10},{10,8},{12,14},{14,12},{1,3},{3,1},... | collective-permute-start | bytes 1032200 | tf_op jit(solution)/shard_map/ppermute | solution.py:523
  8.9 2.6 %collective-permute-start.1 = (bf16[2,3,16,256]{3,2,1,0:T(8,128)(2,1)S(1)}, bf16[2,3,16,256]{3,2,1,0:T(8,128)(2,1)S(1)}, u32[]{:S(2)}, u32[]{:S(2)}) collective-permute-start(bf16[2,3,16,256]{3,2,1,0:T(8,128)(2,1)S(1)} %get-tuple-element.37), channel_id=1, source_target_pairs={{0,8},{2,10},{4,12},{6,14},{8,0},{10,2},{12,4},{14,6},{1,9},{3,11}... | collective-permute-start | bytes 147464 | tf_op jit(solution)/shard_map/ppermute | solution.py:523
  11.5 1.3 %collective-permute-start.2 = (bf16[2,3,16,256]{3,2,1,0:T(8,128)(2,1)S(1)}, bf16[2,3,16,256]{3,2,1,0:T(8,128)(2,1)S(1)}, u32[]{:S(2)}, u32[]{:S(2)}) collective-permute-start(bf16[2,3,16,256]{3,2,1,0:T(8,128)(2,1)S(1)} %get-tuple-element.38), channel_id=1, source_target_pairs={{0,12},{2,14},{4,8},{6,10},{8,4},{10,6},{12,0},{14,2},{1,13},{3,15... | collective-permute-start | bytes 147464 | tf_op jit(solution)/shard_map/ppermute | solution.py:523
  12.9 0.2 collective-permute-start.3
  13.1 0.0 copy-done
  13.1 0.0 copy-done.1
  13.1 0.0 copy-done.2
  13.1 0.0 copy-done.3
  13.1 2.1 %shard_map.101 = (bf16[128,2048]{1,0:T(8,128)(2,1)S(1)}, bf16[128,2048]{1,0:T(8,128)(2,1)S(1)}, f32[16,128]{1,0:T(8,128)S(1)}) custom-call(f32[16]{0:T(128)S(1)} %copy-done.3, f32[2,8]{1,0:T(2,128)S(1)} %bitcast.4, bf16[8,128,256]{2,1,0:T(8,128)(2,1)S(1)} %copy-done, bf16[8,256,128]{2,1,0:T(8,128)(2,1)S(1)} %copy-done.1), custom_call_target="tpu_custom_call" | custom-call | flops 1000 | bytes 1000 | tf_op jit(solution)/shard_map/pallas_call | solution.py:371
  15.2 0.0 collective-permute-done.1.refs_0_
  15.2 2.3 %collective-permute-done.2.refs_1_ = bf16[2,3,16,256]{3,2,1,0:T(8,128)(2,1)S(1)} collective-permute-done((bf16[2,3,16,256]{3,2,1,0:T(8,128)(2,1)S(1)}, bf16[2,3,16,256]{3,2,1,0:T(8,128)(2,1)S(1)}, u32[]{:S(2)}, u32[]{:S(2)}) %collective-permute-start.2) | collective-permute-done | bytes 49184 | tf_op jit(solution)/shard_map/ppermute | solution.py:523
  17.5 0.0 collective-permute-done.3.refs_2_
  17.5 0.0 collective-permute-done.x_came
  17.5 0.1 shard_map.102
  17.6 2.4 %collective-permute-start.5 = (bf16[14,16,256]{2,1,0:T(8,128)(2,1)S(1)}, bf16[14,16,256]{2,1,0:T(8,128)(2,1)S(1)}, u32[]{:S(2)}, u32[]{:S(2)}) collective-permute-start(bf16[14,16,256]{2,1,0:T(8,128)(2,1)S(1)} %get-tuple-element.43), channel_id=1, source_target_pairs={{0,8},{2,10},{4,12},{6,14},{8,0},{10,2},{12,4},{14,6},{1,9},{3,11}... | collective-permute-start | bytes 344072 | tf_op jit(solution)/shard_map/ppermute | solution.py:523
  20.0 1.3 %collective-permute-start.6 = (bf16[14,16,256]{2,1,0:T(8,128)(2,1)S(1)}, bf16[14,16,256]{2,1,0:T(8,128)(2,1)S(1)}, u32[]{:S(2)}, u32[]{:S(2)}) collective-permute-start(bf16[14,16,256]{2,1,0:T(8,128)(2,1)S(1)} %get-tuple-element.44), channel_id=1, source_target_pairs={{0,12},{2,14},{4,8},{6,10},{8,4},{10,6},{12,0},{14,2},{1,13},{3,15... | collective-permute-start | bytes 344072 | tf_op jit(solution)/shard_map/ppermute | solution.py:523
  21.3 0.2 collective-permute-start.7
  21.6 1.5 %collective-permute-start.8 = (bf16[14,16,256]{2,1,0:T(8,128)(2,1)S(1)}, bf16[14,16,256]{2,1,0:T(8,128)(2,1)S(1)}, u32[]{:S(2)}, u32[]{:S(2)}) collective-permute-start(bf16[14,16,256]{2,1,0:T(8,128)(2,1)S(1)} %get-tuple-element.46), channel_id=1, source_target_pairs={{0,2},{2,0},{4,6},{6,4},{8,10},{10,8},{12,14},{14,12},{1,3},{3,1},... | collective-permute-start | bytes 344072 | tf_op jit(solution)/shard_map/ppermute | solution.py:523
  23.1 0.5 %collective-permute-start.4 = (bf16[3,16,256]{2,1,0:T(8,128)(2,1)S(1)}, bf16[3,16,256]{2,1,0:T(8,128)(2,1)S(1)}, u32[]{:S(2)}, u32[]{:S(2)}) collective-permute-start(bf16[3,16,256]{2,1,0:T(8,128)(2,1)S(1)} %get-tuple-element.41), channel_id=1, source_target_pairs={{0,2},{2,0},{4,6},{6,4},{8,10},{10,8},{12,14},{14,12},{1,3},{3,1},... | collective-permute-start | bytes 73736 | tf_op jit(solution)/shard_map/ppermute | solution.py:523
  23.6 3.3 %collective-permute-done.4.z_came = bf16[3,16,256]{2,1,0:T(8,128)(2,1)S(1)} collective-permute-done((bf16[3,16,256]{2,1,0:T(8,128)(2,1)S(1)}, bf16[3,16,256]{2,1,0:T(8,128)(2,1)S(1)}, u32[]{:S(2)}, u32[]{:S(2)}) %collective-permute-start.4) | collective-permute-done | bytes 24608 | tf_op jit(solution)/shard_map/ppermute | solution.py:523
  26.9 0.4 %shard_map.103.ridge_ref = f32[16,16,128]{2,1,0:T(8,128)S(1)} custom-call(bf16[128,2048]{1,0:T(8,128)(2,1)S(1)} %get-tuple-element.30.high_ref, bf16[128,2048]{1,0:T(8,128)(2,1)S(1)} %get-tuple-element.31.low_ref, f32[16,128]{1,0:T(8,128)S(1)} %get-tuple-element.32.share_ref, f32[3,16,256]{2,1,0:T(8,128)S(1)} %get-tuple-element.40.z_own, ...), custom_call_target="tpu_custom_call" | custom-call | flops 1000 | bytes 1000 | tf_op jit(solution)/shard_map/pallas_call | solution.py:444
  27.3 1.1 %collective-permute-done.5.refs_0_ = bf16[14,16,256]{2,1,0:T(8,128)(2,1)S(1)} collective-permute-done((bf16[14,16,256]{2,1,0:T(8,128)(2,1)S(1)}, bf16[14,16,256]{2,1,0:T(8,128)(2,1)S(1)}, u32[]{:S(2)}, u32[]{:S(2)}) %collective-permute-start.5) | collective-permute-done | bytes 114720 | tf_op jit(solution)/shard_map/ppermute | solution.py:523
  28.4 0.0 collective-permute-done.6.refs_1_
  28.4 0.2 collective-permute-done.7.refs_2_
  28.6 0.0 collective-permute-done.8.refs_3_
  28.6 0.9 %shard_map.104 = f32[16,32,128]{2,1,0:T(8,128)} custom-call(f32[16,16,128]{2,1,0:T(8,128)S(1)} %shard_map.103.ridge_ref, f32[14,16,256]{2,1,0:T(8,128)S(1)} %get-tuple-element.42.x_own, f32[3,16,256]{2,1,0:T(8,128)S(1)} %get-tuple-element.40.z_own, bf16[3,16,256]{2,1,0:T(8,128)(2,1)S(1)} %collective-permute-done.4.z_came, ...), custom_call_target="tpu_custom_call" | custom-call | flops 1000 | bytes 1000 | tf_op jit(solution)/shard_map/pallas_call | solution.py:475
Async XLA Ops:
  0.0 13.1 %copy-start = (bf16[8,128,256]{2,1,0:T(8,128)(2,1)S(1)}, bf16[8,128,256]{2,1,0:T(8,128)(2,1)}, u32[]{:S(2)}) copy-start(bf16[8,128,256]{2,1,0:T(8,128)(2,1)} %rows_hbm.3) | copy-start | bytes 1572868
  0.0 13.1 %copy-start.1 = (bf16[8,256,128]{2,1,0:T(8,128)(2,1)S(1)}, bf16[8,256,128]{2,1,0:T(8,128)(2,1)}, u32[]{:S(2)}) copy-start(bf16[8,256,128]{2,1,0:T(8,128)(2,1)} %cols_hbm.3) | copy-start | bytes 1572868
  0.0 13.1 %copy-start.2 = (f32[8,2]{0,1:T(2,128)S(1)}, f32[8,2]{0,1:T(2,128)}, u32[]{:S(2)}) copy-start(f32[8,2]{0,1:T(2,128)} %param.17) | copy-start | bytes 196
  0.0 13.1 %copy-start.3 = (f32[16]{0:T(128)S(1)}, f32[16]{0:T(128)}, u32[]{:S(2)}) copy-start(f32[16]{0:T(128)} %defocus_hbm.3) | copy-start | bytes 196
  5.9 11.6 %collective-permute-start = (bf16[3,14,16,256]{3,2,1,0:T(8,128)(2,1)S(1)}, bf16[3,14,16,256]{3,2,1,0:T(8,128)(2,1)S(1)}, u32[]{:S(2)}, u32[]{:S(2)}) collective-permute-start(bf16[3,14,16,256]{3,2,1,0:T(8,128)(2,1)S(1)} %get-tuple-element.34), channel_id=1, source_target_pairs={{0,2},{2,0},{4,6},{6,4},{8,10},{10,8},{12,14},{14,12},{1,3},{3,1},... | collective-permute-start | bytes 1032200 | tf_op jit(solution)/shard_map/ppermute | solution.py:523
  8.9 6.3 %collective-permute-start.1 = (bf16[2,3,16,256]{3,2,1,0:T(8,128)(2,1)S(1)}, bf16[2,3,16,256]{3,2,1,0:T(8,128)(2,1)S(1)}, u32[]{:S(2)}, u32[]{:S(2)}) collective-permute-start(bf16[2,3,16,256]{3,2,1,0:T(8,128)(2,1)S(1)} %get-tuple-element.37), channel_id=1, source_target_pairs={{0,8},{2,10},{4,12},{6,14},{8,0},{10,2},{12,4},{14,6},{1,9},{3,11}... | collective-permute-start | bytes 147464 | tf_op jit(solution)/shard_map/ppermute | solution.py:523
  11.5 6.0 %collective-permute-start.2 = (bf16[2,3,16,256]{3,2,1,0:T(8,128)(2,1)S(1)}, bf16[2,3,16,256]{3,2,1,0:T(8,128)(2,1)S(1)}, u32[]{:S(2)}, u32[]{:S(2)}) collective-permute-start(bf16[2,3,16,256]{3,2,1,0:T(8,128)(2,1)S(1)} %get-tuple-element.38), channel_id=1, source_target_pairs={{0,12},{2,14},{4,8},{6,10},{8,4},{10,6},{12,0},{14,2},{1,13},{3,15... | collective-permute-start | bytes 147464 | tf_op jit(solution)/shard_map/ppermute | solution.py:523
  12.9 4.6 %collective-permute-start.3 = (bf16[2,3,16,256]{3,2,1,0:T(8,128)(2,1)S(1)}, bf16[2,3,16,256]{3,2,1,0:T(8,128)(2,1)S(1)}, u32[]{:S(2)}, u32[]{:S(2)}) collective-permute-start(bf16[2,3,16,256]{3,2,1,0:T(8,128)(2,1)S(1)} %get-tuple-element.39), channel_id=1, source_target_pairs={{0,4},{2,6},{4,0},{6,2},{8,12},{10,14},{12,8},{14,10},{1,5},{3,7},... | collective-permute-start | bytes 147464 | tf_op jit(solution)/shard_map/ppermute | solution.py:523
  17.6 10.8 %collective-permute-start.5 = (bf16[14,16,256]{2,1,0:T(8,128)(2,1)S(1)}, bf16[14,16,256]{2,1,0:T(8,128)(2,1)S(1)}, u32[]{:S(2)}, u32[]{:S(2)}) collective-permute-start(bf16[14,16,256]{2,1,0:T(8,128)(2,1)S(1)} %get-tuple-element.43), channel_id=1, source_target_pairs={{0,8},{2,10},{4,12},{6,14},{8,0},{10,2},{12,4},{14,6},{1,9},{3,11}... | collective-permute-start | bytes 344072 | tf_op jit(solution)/shard_map/ppermute | solution.py:523
  20.0 8.4 %collective-permute-start.6 = (bf16[14,16,256]{2,1,0:T(8,128)(2,1)S(1)}, bf16[14,16,256]{2,1,0:T(8,128)(2,1)S(1)}, u32[]{:S(2)}, u32[]{:S(2)}) collective-permute-start(bf16[14,16,256]{2,1,0:T(8,128)(2,1)S(1)} %get-tuple-element.44), channel_id=1, source_target_pairs={{0,12},{2,14},{4,8},{6,10},{8,4},{10,6},{12,0},{14,2},{1,13},{3,15... | collective-permute-start | bytes 344072 | tf_op jit(solution)/shard_map/ppermute | solution.py:523
  21.3 7.2 %collective-permute-start.7 = (bf16[14,16,256]{2,1,0:T(8,128)(2,1)S(1)}, bf16[14,16,256]{2,1,0:T(8,128)(2,1)S(1)}, u32[]{:S(2)}, u32[]{:S(2)}) collective-permute-start(bf16[14,16,256]{2,1,0:T(8,128)(2,1)S(1)} %get-tuple-element.45), channel_id=1, source_target_pairs={{0,4},{2,6},{4,0},{6,2},{8,12},{10,14},{12,8},{14,10},{1,5},{3,7},... | collective-permute-start | bytes 344072 | tf_op jit(solution)/shard_map/ppermute | solution.py:523
  21.6 7.0 %collective-permute-start.8 = (bf16[14,16,256]{2,1,0:T(8,128)(2,1)S(1)}, bf16[14,16,256]{2,1,0:T(8,128)(2,1)S(1)}, u32[]{:S(2)}, u32[]{:S(2)}) collective-permute-start(bf16[14,16,256]{2,1,0:T(8,128)(2,1)S(1)} %get-tuple-element.46), channel_id=1, source_target_pairs={{0,2},{2,0},{4,6},{6,4},{8,10},{10,8},{12,14},{14,12},{1,3},{3,1},... | collective-permute-start | bytes 344072 | tf_op jit(solution)/shard_map/ppermute | solution.py:523
  23.1 3.8 %collective-permute-start.4 = (bf16[3,16,256]{2,1,0:T(8,128)(2,1)S(1)}, bf16[3,16,256]{2,1,0:T(8,128)(2,1)S(1)}, u32[]{:S(2)}, u32[]{:S(2)}) collective-permute-start(bf16[3,16,256]{2,1,0:T(8,128)(2,1)S(1)} %get-tuple-element.41), channel_id=1, source_target_pairs={{0,2},{2,0},{4,6},{6,4},{8,10},{10,8},{12,14},{14,12},{1,3},{3,1},... | collective-permute-start | bytes 73736 | tf_op jit(solution)/shard_map/ppermute | solution.py:523

commit v17 on v16

--- a/solution.py
+++ b/solution.py
@@ -235,17 +235,16 @@
         x_keep[n] = totals[-x_slots:, rows_of(2 * k), :]
     own_send[...] = totals[-x_slots:, rows_of(1), :].astype(bf16)
     own_keep[...] = totals[-x_slots:, rows_of(0), :]
-    for side in range(2):
-        z_keep[side] = totals[:-x_slots, rows_of(side), :]
-        for n, k in enumerate(LINE):
-            z_sends[n][side] = totals[:-x_slots, rows_of(2 * k + side), :].astype(bf16)
+    for k, out in zip((0,) + LINE, (z_keep, *z_sends)):
+        out[:Z_SLOTS] = totals[:Z_SLOTS, rows_of(2 * k), :].astype(out.dtype)
+        out[Z_SLOTS:] = totals[1:Z_SLOTS, rows_of(2 * k + 1), :].astype(out.dtype)
 
 
 SCRATCH = 20
 LINE = (2, 3, 1)
 SLOTS = 8
 GROUP = 4
-Z_SLOTS = 3
+Z_SLOTS = 4
 
 
 def own_totals(images, class_index, pose_index, defocus_bin, defocus, rows_table, cols_table, plane_weight, members):
@@ -267,8 +266,8 @@
         out_shape = []
         for lead in ((len(LINE), x_slots), (x_slots,)):
             out_shape += [pltpu.VMEM(lead + tail, bf16), pltpu.VMEM(lead + tail, f32)]
-        out_shape += [pltpu.VMEM((2, Z_SLOTS) + tail, f32)]
-        out_shape += [pltpu.VMEM((2, Z_SLOTS) + tail, bf16)] * len(LINE)
+        out_shape += [pltpu.VMEM((2 * Z_SLOTS - 1,) + tail, f32)]
+        out_shape += [pltpu.VMEM((2 * Z_SLOTS - 1,) + tail, bf16)] * len(LINE)
     operands = (
         class_index[:, 0], pose_index, defocus_bin, defocus, plane_weight.T,
         jnp.asarray(table_y, bf16), jnp.asarray(table_x.T.copy(), bf16),
@@ -367,10 +366,10 @@
     any_place = pl.BlockSpec(memory_space=pl.ANY)
     vmem = pl.BlockSpec(memory_space=pltpu.VMEM)
     planes = plane_weight.T
-    table = jax.ShapeDtypeStruct((poses * bins, owned * cols), bf16)
+    table = pltpu.VMEM((poses * bins, owned * cols), bf16)
     return pl.pallas_call(
         ridge_kernel,
-        out_shape=[table, table, jax.ShapeDtypeStruct((planes.shape[0] * CLASSES, poses * bins), f32)],
+        out_shape=[table, table, pltpu.VMEM((planes.shape[0] * CLASSES, poses * bins), f32)],
         in_specs=[any_place] * 4,
         out_specs=[vmem] * 3,
         scratch_shapes=[
@@ -380,7 +379,7 @@
             pltpu.VMEM(cols_table.shape, bf16),
             pltpu.SemaphoreType.DMA((4,)),
         ],
-        compiler_params=pltpu.CompilerParams(vmem_limit_bytes=16 * 1024 * 1024),
+        compiler_params=pltpu.CompilerParams(vmem_limit_bytes=VMEM_LIMIT),
         cost_estimate=pl.CostEstimate(
             flops=1000, bytes_accessed=1000, transcendentals=0
         ),
@@ -405,16 +404,21 @@
     for n, send in enumerate(x_sends):
         send[...] = (x_keep[n] + x_came[n].astype(f32)).astype(bf16)
     own_out[...] = own_send[...]
-    for side, out in enumerate((z_own, z_send)):
-        value = z_keep[side]
+    for n in range(z_keep.shape[0]):
+        value = z_keep[n]
         for came in z_came:
-            value = value + came[side].astype(f32)
-        out[...] = value.astype(out.dtype)
+            value = value + came[n].astype(f32)
+        if n < Z_SLOTS:
+            z_own[n] = value
+        if n == 0:
+            z_send[n] = value.astype(bf16)
+        elif n >= Z_SLOTS:
+            z_send[n - Z_SLOTS + 1] = value.astype(bf16)
 
 
 def fold_phase(x_keep, x_came, own_send, z_keep, z_came):
     piece = own_send.shape
-    z_piece = z_keep.shape[1:]
+    z_piece = (Z_SLOTS,) + piece[1:]
     out_shape = [pltpu.VMEM(piece, bf16)] * (len(LINE) + 1)
     out_shape += [pltpu.VMEM(z_piece, f32), pltpu.VMEM(z_piece, bf16)]
     return call_in_vmem(fold_kernel, (x_keep, x_came, own_send, z_keep, *z_came), out_shape)

time: 29.7 us -> 29.1 us (0.980)
  waiting for transfers between devices: 6.89 us -> 6.32 us
  starting transfers between devices: 13.2 us -> 12.8 us
  Pallas kernels: 9.39 us -> 9.77 us
    ppermute x9, waiting for transfers between devices: 6.89 us -> 6.32 us  [exchange(): return lax.ppermute(value, 'img', [(i, i ^ flip) for i in range(members)])]
    pallas_call x1, Pallas kernels: 2.09 us -> 2.62 us  [own_ridges(): pl.pallas_call(ridge_kernel, out_shape=[table, table, pltpu.VMEM((planes....]
    ppermute x9, starting transfers between devices: 13.2 us -> 12.8 us  [exchange(): return lax.ppermute(value, 'img', [(i, i ^ flip) for i in range(members)])]
  transfers between devices with their start and end apart: 9 -> 9, of which waited for: 4 -> 4; matrix products, arithmetic and copies ran while one was open for 0% -> 0% of each run, Pallas kernels for 8% -> 10%
where the time goes in v17:
time: 29.1 us; the launch traced here: 28.9 us
  starting transfers between devices  12.8 us (44%)
  Pallas kernels  9.77 us (34%)
  waiting for transfers between devices  6.32 us (22%)
    ppermute x9, starting transfers between devices, exchange(): return lax.ppermute(value, 'img', [(i, i ^ flip) for i in range(members)])  12.8 us
    ppermute x9, waiting for transfers between devices, exchange(): return lax.ppermute(value, 'img', [(i, i ^ flip) for i in range(members)])  6.32 us
    pallas_call x1, Pallas kernels, own_totals(): pl.pallas_call(slices_kernel, out_shape=out_shape, in_specs=[any_place] *...  5.76 us
    pallas_call x1, Pallas kernels, own_ridges(): pl.pallas_call(ridge_kernel, out_shape=[table, table, pltpu.VMEM((planes....  2.62 us
    pallas_call x1, Pallas kernels, finish(): pl.pallas_call(functools.partial(finish_kernel, planes), out_shape=jax.Sh...  0.94 us
  transfers between devices with their start and end apart: 9, of which 4 were waited for; matrix products, arithmetic and copies ran while one was open for 0% of the time, Pallas kernels for 10%

profile of v17, /device:TPU:0, one launch (start us, length us, event | category | flops | bytes accessed | tf_op | source)
XLA Modules:
  0.0 28.9 jit_solution(11947896572284652501)
XLA Ops:
  0.0 5.8 %shard_map.100 = (bf16[3,13,16,256]{3,2,1,0:T(8,128)(2,1)S(1)}, f32[3,13,16,256]{3,2,1,0:T(8,128)S(1)}, bf16[13,16,256]{2,1,0:T(8,128)(2,1)S(1)}, f32[13,16,256]...) custom-call(s32[16]{0:T(128)} %bitcast.5, ...), custom_call_target="tpu_custom_call" | custom-call | flops 2097152000 | bytes 6291456 | tf_op jit(solution)/shard_map/pallas_call | solution.py:276
  5.8 3.0 %collective-permute-start = (bf16[3,13,16,256]{3,2,1,0:T(8,128)(2,1)S(1)}, bf16[3,13,16,256]{3,2,1,0:T(8,128)(2,1)S(1)}, u32[]{:S(2)}, u32[]{:S(2)}) collective-permute-start(bf16[3,13,16,256]{3,2,1,0:T(8,128)(2,1)S(1)} %get-tuple-element.34), channel_id=1, source_target_pairs={{0,2},{2,0},{4,6},{6,4},{8,10},{10,8},{12,14},{14,12},{1,3},{3,1},... | collective-permute-start | bytes 958472 | tf_op jit(solution)/shard_map/ppermute | solution.py:527
  8.8 2.6 %collective-permute-start.1 = (bf16[7,16,256]{2,1,0:T(8,128)(2,1)S(1)}, bf16[7,16,256]{2,1,0:T(8,128)(2,1)S(1)}, u32[]{:S(2)}, u32[]{:S(2)}) collective-permute-start(bf16[7,16,256]{2,1,0:T(8,128)(2,1)S(1)} %get-tuple-element.37), channel_id=1, source_target_pairs={{0,8},{2,10},{4,12},{6,14},{8,0},{10,2},{12,4},{14,6},{1,9},{3,11}... | collective-permute-start | bytes 172040 | tf_op jit(solution)/shard_map/ppermute | solution.py:527
  11.4 1.3 %collective-permute-start.2 = (bf16[7,16,256]{2,1,0:T(8,128)(2,1)S(1)}, bf16[7,16,256]{2,1,0:T(8,128)(2,1)S(1)}, u32[]{:S(2)}, u32[]{:S(2)}) collective-permute-start(bf16[7,16,256]{2,1,0:T(8,128)(2,1)S(1)} %get-tuple-element.38), channel_id=1, source_target_pairs={{0,12},{2,14},{4,8},{6,10},{8,4},{10,6},{12,0},{14,2},{1,13},{3,15... | collective-permute-start | bytes 172040 | tf_op jit(solution)/shard_map/ppermute | solution.py:527
  12.7 0.2 collective-permute-start.3
  12.9 2.6 %shard_map.101 = (bf16[128,2048]{1,0:T(8,128)(2,1)S(1)}, bf16[128,2048]{1,0:T(8,128)(2,1)S(1)}, f32[16,128]{1,0:T(8,128)S(1)}) custom-call(f32[16]{0:T(128)} %defocus_hbm.3, f32[2,8]{1,0:T(2,128)} %bitcast.4, bf16[8,128,256]{2,1,0:T(8,128)(2,1)} %rows_hbm.3, bf16[8,256,128]{2,1,0:T(8,128)(2,1)} %cols_hbm.3), custom_call_target="tpu_custom_call" | custom-call | flops 1000 | bytes 1000 | tf_op jit(solution)/shard_map/pallas_call | solution.py:370
  15.6 0.0 collective-permute-done.1.refs_0_
  15.6 1.9 %collective-permute-done.2.refs_1_ = bf16[7,16,256]{2,1,0:T(8,128)(2,1)S(1)} collective-permute-done((bf16[7,16,256]{2,1,0:T(8,128)(2,1)S(1)}, bf16[7,16,256]{2,1,0:T(8,128)(2,1)S(1)}, u32[]{:S(2)}, u32[]{:S(2)}) %collective-permute-start.2) | collective-permute-done | bytes 57376 | tf_op jit(solution)/shard_map/ppermute | solution.py:527
  17.4 0.1 collective-permute-done.3.refs_2_
  17.5 0.0 collective-permute-done.x_came
  17.5 0.1 shard_map.102
  17.6 1.9 %collective-permute-start.5 = (bf16[13,16,256]{2,1,0:T(8,128)(2,1)S(1)}, bf16[13,16,256]{2,1,0:T(8,128)(2,1)S(1)}, u32[]{:S(2)}, u32[]{:S(2)}) collective-permute-start(bf16[13,16,256]{2,1,0:T(8,128)(2,1)S(1)} %get-tuple-element.43), channel_id=1, source_target_pairs={{0,8},{2,10},{4,12},{6,14},{8,0},{10,2},{12,4},{14,6},{1,9},{3,11}... | collective-permute-start | bytes 319496 | tf_op jit(solution)/shard_map/ppermute | solution.py:527
  19.5 1.2 %collective-permute-start.6 = (bf16[13,16,256]{2,1,0:T(8,128)(2,1)S(1)}, bf16[13,16,256]{2,1,0:T(8,128)(2,1)S(1)}, u32[]{:S(2)}, u32[]{:S(2)}) collective-permute-start(bf16[13,16,256]{2,1,0:T(8,128)(2,1)S(1)} %get-tuple-element.44), channel_id=1, source_target_pairs={{0,12},{2,14},{4,8},{6,10},{8,4},{10,6},{12,0},{14,2},{1,13},{3,15... | collective-permute-start | bytes 319496 | tf_op jit(solution)/shard_map/ppermute | solution.py:527
  20.7 0.5 %collective-permute-start.7 = (bf16[13,16,256]{2,1,0:T(8,128)(2,1)S(1)}, bf16[13,16,256]{2,1,0:T(8,128)(2,1)S(1)}, u32[]{:S(2)}, u32[]{:S(2)}) collective-permute-start(bf16[13,16,256]{2,1,0:T(8,128)(2,1)S(1)} %get-tuple-element.45), channel_id=1, source_target_pairs={{0,4},{2,6},{4,0},{6,2},{8,12},{10,14},{12,8},{14,10},{1,5},{3,7},... | collective-permute-start | bytes 319496 | tf_op jit(solution)/shard_map/ppermute | solution.py:527
  21.2 1.2 %collective-permute-start.8 = (bf16[13,16,256]{2,1,0:T(8,128)(2,1)S(1)}, bf16[13,16,256]{2,1,0:T(8,128)(2,1)S(1)}, u32[]{:S(2)}, u32[]{:S(2)}) collective-permute-start(bf16[13,16,256]{2,1,0:T(8,128)(2,1)S(1)} %get-tuple-element.46), channel_id=1, source_target_pairs={{0,2},{2,0},{4,6},{6,4},{8,10},{10,8},{12,14},{14,12},{1,3},{3,1},... | collective-permute-start | bytes 319496 | tf_op jit(solution)/shard_map/ppermute | solution.py:527
  22.4 0.8 %collective-permute-start.4 = (bf16[4,16,256]{2,1,0:T(8,128)(2,1)S(1)}, bf16[4,16,256]{2,1,0:T(8,128)(2,1)S(1)}, u32[]{:S(2)}, u32[]{:S(2)}) collective-permute-start(bf16[4,16,256]{2,1,0:T(8,128)(2,1)S(1)} %get-tuple-element.41), channel_id=1, source_target_pairs={{0,2},{2,0},{4,6},{6,4},{8,10},{10,8},{12,14},{14,12},{1,3},{3,1},... | collective-permute-start | bytes 98312 | tf_op jit(solution)/shard_map/ppermute | solution.py:527
  23.2 3.1 %collective-permute-done.4.z_came = bf16[4,16,256]{2,1,0:T(8,128)(2,1)S(1)} collective-permute-done((bf16[4,16,256]{2,1,0:T(8,128)(2,1)S(1)}, bf16[4,16,256]{2,1,0:T(8,128)(2,1)S(1)}, u32[]{:S(2)}, u32[]{:S(2)}) %collective-permute-start.4) | collective-permute-done | bytes 32800 | tf_op jit(solution)/shard_map/ppermute | solution.py:527
  26.3 0.4 %shard_map.103.ridge_ref = f32[16,16,128]{2,1,0:T(8,128)S(1)} custom-call(bf16[128,2048]{1,0:T(8,128)(2,1)S(1)} %get-tuple-element.30.high_ref, bf16[128,2048]{1,0:T(8,128)(2,1)S(1)} %get-tuple-element.31.low_ref, f32[16,128]{1,0:T(8,128)S(1)} %get-tuple-element.32.share_ref, f32[4,16,256]{2,1,0:T(8,128)S(1)} %get-tuple-element.40.z_own, ...), custom_call_target="tpu_custom_call" | custom-call | flops 1000 | bytes 1000 | tf_op jit(solution)/shard_map/pallas_call | solution.py:448
  26.7 1.2 %collective-permute-done.5.refs_0_ = bf16[13,16,256]{2,1,0:T(8,128)(2,1)S(1)} collective-permute-done((bf16[13,16,256]{2,1,0:T(8,128)(2,1)S(1)}, bf16[13,16,256]{2,1,0:T(8,128)(2,1)S(1)}, u32[]{:S(2)}, u32[]{:S(2)}) %collective-permute-start.5) | collective-permute-done | bytes 106528 | tf_op jit(solution)/shard_map/ppermute | solution.py:527
  27.9 0.0 collective-permute-done.6.refs_1_
  27.9 0.0 collective-permute-done.7.refs_2_
  27.9 0.0 collective-permute-done.8.refs_3_
  27.9 0.9 %shard_map.104 = f32[16,32,128]{2,1,0:T(8,128)} custom-call(f32[16,16,128]{2,1,0:T(8,128)S(1)} %shard_map.103.ridge_ref, f32[13,16,256]{2,1,0:T(8,128)S(1)} %get-tuple-element.42.x_own, f32[4,16,256]{2,1,0:T(8,128)S(1)} %get-tuple-element.40.z_own, bf16[4,16,256]{2,1,0:T(8,128)(2,1)S(1)} %collective-permute-done.4.z_came, ...), custom_call_target="tpu_custom_call" | custom-call | flops 1000 | bytes 1000 | tf_op jit(solution)/shard_map/pallas_call | solution.py:479
Async XLA Ops:
  5.8 11.7 %collective-permute-start = (bf16[3,13,16,256]{3,2,1,0:T(8,128)(2,1)S(1)}, bf16[3,13,16,256]{3,2,1,0:T(8,128)(2,1)S(1)}, u32[]{:S(2)}, u32[]{:S(2)}) collective-permute-start(bf16[3,13,16,256]{3,2,1,0:T(8,128)(2,1)S(1)} %get-tuple-element.34), channel_id=1, source_target_pairs={{0,2},{2,0},{4,6},{6,4},{8,10},{10,8},{12,14},{14,12},{1,3},{3,1},... | collective-permute-start | bytes 958472 | tf_op jit(solution)/shard_map/ppermute | solution.py:527
  8.8 6.8 %collective-permute-start.1 = (bf16[7,16,256]{2,1,0:T(8,128)(2,1)S(1)}, bf16[7,16,256]{2,1,0:T(8,128)(2,1)S(1)}, u32[]{:S(2)}, u32[]{:S(2)}) collective-permute-start(bf16[7,16,256]{2,1,0:T(8,128)(2,1)S(1)} %get-tuple-element.37), channel_id=1, source_target_pairs={{0,8},{2,10},{4,12},{6,14},{8,0},{10,2},{12,4},{14,6},{1,9},{3,11}... | collective-permute-start | bytes 172040 | tf_op jit(solution)/shard_map/ppermute | solution.py:527
  11.4 6.1 %collective-permute-start.2 = (bf16[7,16,256]{2,1,0:T(8,128)(2,1)S(1)}, bf16[7,16,256]{2,1,0:T(8,128)(2,1)S(1)}, u32[]{:S(2)}, u32[]{:S(2)}) collective-permute-start(bf16[7,16,256]{2,1,0:T(8,128)(2,1)S(1)} %get-tuple-element.38), channel_id=1, source_target_pairs={{0,12},{2,14},{4,8},{6,10},{8,4},{10,6},{12,0},{14,2},{1,13},{3,15... | collective-permute-start | bytes 172040 | tf_op jit(solution)/shard_map/ppermute | solution.py:527
  12.7 4.8 %collective-permute-start.3 = (bf16[7,16,256]{2,1,0:T(8,128)(2,1)S(1)}, bf16[7,16,256]{2,1,0:T(8,128)(2,1)S(1)}, u32[]{:S(2)}, u32[]{:S(2)}) collective-permute-start(bf16[7,16,256]{2,1,0:T(8,128)(2,1)S(1)} %get-tuple-element.39), channel_id=1, source_target_pairs={{0,4},{2,6},{4,0},{6,2},{8,12},{10,14},{12,8},{14,10},{1,5},{3,7},... | collective-permute-start | bytes 172040 | tf_op jit(solution)/shard_map/ppermute | solution.py:527
  17.6 10.3 %collective-permute-start.5 = (bf16[13,16,256]{2,1,0:T(8,128)(2,1)S(1)}, bf16[13,16,256]{2,1,0:T(8,128)(2,1)S(1)}, u32[]{:S(2)}, u32[]{:S(2)}) collective-permute-start(bf16[13,16,256]{2,1,0:T(8,128)(2,1)S(1)} %get-tuple-element.43), channel_id=1, source_target_pairs={{0,8},{2,10},{4,12},{6,14},{8,0},{10,2},{12,4},{14,6},{1,9},{3,11}... | collective-permute-start | bytes 319496 | tf_op jit(solution)/shard_map/ppermute | solution.py:527
  19.5 8.4 %collective-permute-start.6 = (bf16[13,16,256]{2,1,0:T(8,128)(2,1)S(1)}, bf16[13,16,256]{2,1,0:T(8,128)(2,1)S(1)}, u32[]{:S(2)}, u32[]{:S(2)}) collective-permute-start(bf16[13,16,256]{2,1,0:T(8,128)(2,1)S(1)} %get-tuple-element.44), channel_id=1, source_target_pairs={{0,12},{2,14},{4,8},{6,10},{8,4},{10,6},{12,0},{14,2},{1,13},{3,15... | collective-permute-start | bytes 319496 | tf_op jit(solution)/shard_map/ppermute | solution.py:527
  20.7 7.3 %collective-permute-start.7 = (bf16[13,16,256]{2,1,0:T(8,128)(2,1)S(1)}, bf16[13,16,256]{2,1,0:T(8,128)(2,1)S(1)}, u32[]{:S(2)}, u32[]{:S(2)}) collective-permute-start(bf16[13,16,256]{2,1,0:T(8,128)(2,1)S(1)} %get-tuple-element.45), channel_id=1, source_target_pairs={{0,4},{2,6},{4,0},{6,2},{8,12},{10,14},{12,8},{14,10},{1,5},{3,7},... | collective-permute-start | bytes 319496 | tf_op jit(solution)/shard_map/ppermute | solution.py:527
  21.2 6.8 %collective-permute-start.8 = (bf16[13,16,256]{2,1,0:T(8,128)(2,1)S(1)}, bf16[13,16,256]{2,1,0:T(8,128)(2,1)S(1)}, u32[]{:S(2)}, u32[]{:S(2)}) collective-permute-start(bf16[13,16,256]{2,1,0:T(8,128)(2,1)S(1)} %get-tuple-element.46), channel_id=1, source_target_pairs={{0,2},{2,0},{4,6},{6,4},{8,10},{10,8},{12,14},{14,12},{1,3},{3,1},... | collective-permute-start | bytes 319496 | tf_op jit(solution)/shard_map/ppermute | solution.py:527
  22.4 3.9 %collective-permute-start.4 = (bf16[4,16,256]{2,1,0:T(8,128)(2,1)S(1)}, bf16[4,16,256]{2,1,0:T(8,128)(2,1)S(1)}, u32[]{:S(2)}, u32[]{:S(2)}) collective-permute-start(bf16[4,16,256]{2,1,0:T(8,128)(2,1)S(1)} %get-tuple-element.41), channel_id=1, source_target_pairs={{0,2},{2,0},{4,6},{6,4},{8,10},{10,8},{12,14},{14,12},{1,3},{3,1},... | collective-permute-start | bytes 98312 | tf_op jit(solution)/shard_map/ppermute | solution.py:527

commit v18 on v17

--- a/solution.py
+++ b/solution.py
@@ -136,9 +136,7 @@
             half_ref[i // GROUP % 2, n * box : (n + 1) * box] = product[:, n * box : (n + 1) * box]
 
     def along_columns(i):
-        product = dot(half_ref[i // GROUP % 2], dft_t_ref[...])
-        for n in range(GROUP):
-            weigh(i + n, product[n * box : (n + 1) * box])
+        return dot(half_ref[i // GROUP % 2], dft_t_ref[...])
 
     def weigh(i, y):
         sin_col = jnp.broadcast_to(wave_y[:, i : i + 1], (tall, half))
@@ -202,22 +200,23 @@
         far_two = dot(far, two).astype(bf16)
         cols_fold[p] = jnp.concatenate([near_two[:, :cols], far_two[:, :cols]], 1)
         cols_fold[p + 1] = jnp.concatenate([near_two[:, cols:], far_two[:, cols:]], 1)
-    along_rows(GROUP)
-    along_columns(0)
     copies[9].wait()
     rows_fold[...] = dot(
         rows_ref[...].reshape(poses * rows, box), near, ((1,), (1,))
     ).astype(bf16)
-    for step in range(2 * GROUP, count + 3 * GROUP, GROUP):
+    for first in range(0, count, GROUP):
+        if first + GROUP < count:
+            along_rows(first + GROUP)
+        product = along_columns(first)
         for n in range(GROUP):
-            if step >= 3 * GROUP:
-                insert(step - 3 * GROUP + n)
-            if step - 2 * GROUP < count:
-                mix(step - 2 * GROUP + n)
-        if step - GROUP < count:
-            along_columns(step - GROUP)
-        if step < count:
-            along_rows(step)
+            weigh(first + n, product[n * box : (n + 1) * box])
+            if first + n >= 1:
+                mix(first + n - 1)
+            if first + n >= 2:
+                insert(first + n - 2)
+    mix(count - 1)
+    insert(count - 2)
+    insert(count - 1)
 
     if len(outs) == 1:
         outs[0][...] = totals[...].astype(bf16)
@@ -457,20 +456,31 @@
 
 
 def finish_kernel(planes, ridge_ref, x_own, z_own, z_came, *refs):
-    x_came, out_ref = refs[:-1], refs[-1]
+    x_came, (out_hbm, out_ref, sent) = refs[:-3], refs[-3:]
     slots, owned, cols = ridge_ref.shape
     first = z_own.shape[0]
-    for s in range(slots):
-        if s + 1 < first:
-            value = z_own[s + 1] + z_came[s + 1].astype(f32)
-        else:
-            value = x_own[s + 1 - first]
-            for part in x_came:
-                value = value + part[s + 1 - first].astype(f32)
-        factor = ridge_ref[s]
-        place = (s % CLASSES) * planes + s // CLASSES
-        out_ref[:, 2 * place, :] = value[:, :cols] * factor
-        out_ref[:, 2 * place + 1, :] = value[:, cols:] * factor
+    copies = []
+    for n in range(OUT_PARTS):
+        places = range(n * slots // OUT_PARTS, (n + 1) * slots // OUT_PARTS)
+        for place in places:
+            s = place % planes * CLASSES + place // planes
+            if s + 1 < first:
+                value = z_own[s + 1] + z_came[s + 1].astype(f32)
+            else:
+                value = x_own[s + 1 - first]
+                for came in x_came:
+                    value = value + came[s + 1 - first].astype(f32)
+            factor = ridge_ref[s]
+            out_ref[:, 2 * place, :] = value[:, :cols] * factor
+            out_ref[:, 2 * place + 1, :] = value[:, cols:] * factor
+        part = pl.ds(2 * places[0], 2 * len(places))
+        copies.append(pltpu.make_async_copy(out_ref.at[:, part], out_hbm.at[:, part], sent.at[n]))
+        copies[-1].start()
+    for copy in copies:
+        copy.wait()
+
+
+OUT_PARTS = 2
 
 
 def finish(planes, ridge, x_own, z_own, z_came, x_came):
@@ -480,7 +490,11 @@
         functools.partial(finish_kernel, planes),
         out_shape=jax.ShapeDtypeStruct((owned, 2 * slots, cols), f32),
         in_specs=[vmem] * (4 + len(x_came)),
-        out_specs=vmem,
+        out_specs=pl.BlockSpec(memory_space=pl.ANY),
+        scratch_shapes=[
+            pltpu.VMEM((owned, 2 * slots, cols), f32),
+            pltpu.SemaphoreType.DMA((OUT_PARTS,)),
+        ],
         compiler_params=pltpu.CompilerParams(vmem_limit_bytes=16 * 1024 * 1024),
         cost_estimate=pl.CostEstimate(flops=1000, bytes_accessed=1000, transcendentals=0),
     )(ridge, x_own, z_own, z_came, *x_came)

time: 29.1 us -> 29.6 us (1.017)
  Pallas kernels: 9.77 us -> 10.3 us
    pallas_call x1, Pallas kernels: 5.76 us -> 6.28 us  [own_totals(): pl.pallas_call(slices_kernel, out_shape=out_shape, in_specs=[any_place] *...]
where the time goes in v18:
time: 29.6 us; the launch traced here: 29.4 us
  starting transfers between devices  12.7 us (43%)
  Pallas kernels  10.3 us (35%)
  waiting for transfers between devices  6.33 us (21%)
    ppermute x9, starting transfers between devices, exchange(): return lax.ppermute(value, 'img', [(i, i ^ flip) for i in range(members)])  12.7 us
    ppermute x9, waiting for transfers between devices, exchange(): return lax.ppermute(value, 'img', [(i, i ^ flip) for i in range(members)])  6.33 us
    pallas_call x1, Pallas kernels, own_totals(): pl.pallas_call(slices_kernel, out_shape=out_shape, in_specs=[any_place] *...  6.28 us
    pallas_call x1, Pallas kernels, own_ridges(): pl.pallas_call(ridge_kernel, out_shape=[table, table, pltpu.VMEM((planes....  2.62 us
    pallas_call x1, Pallas kernels, finish(): pl.pallas_call(functools.partial(finish_kernel, planes), out_shape=jax.Sh...  0.91 us
  transfers between devices with their start and end apart: 9, of which 4 were waited for; matrix products, arithmetic and copies ran while one was open for 0% of the time, Pallas kernels for 10%

profile of v18, /device:TPU:0, one launch (start us, length us, event | category | flops | bytes accessed | tf_op | source)
XLA Modules:
  0.0 29.4 jit_solution(2273307541703497881)
XLA Ops:
  0.0 6.3 %shard_map.100 = (bf16[3,13,16,256]{3,2,1,0:T(8,128)(2,1)S(1)}, f32[3,13,16,256]{3,2,1,0:T(8,128)S(1)}, bf16[13,16,256]{2,1,0:T(8,128)(2,1)S(1)}, f32[13,16,256]...) custom-call(s32[16]{0:T(128)} %bitcast.5, ...), custom_call_target="tpu_custom_call" | custom-call | flops 2097152000 | bytes 6291456 | tf_op jit(solution)/shard_map/pallas_call | solution.py:275
  6.3 3.0 %collective-permute-start = (bf16[3,13,16,256]{3,2,1,0:T(8,128)(2,1)S(1)}, bf16[3,13,16,256]{3,2,1,0:T(8,128)(2,1)S(1)}, u32[]{:S(2)}, u32[]{:S(2)}) collective-permute-start(bf16[3,13,16,256]{3,2,1,0:T(8,128)(2,1)S(1)} %get-tuple-element.34), channel_id=1, source_target_pairs={{0,2},{2,0},{4,6},{6,4},{8,10},{10,8},{12,14},{14,12},{1,3},{3,1},... | collective-permute-start | bytes 958472 | tf_op jit(solution)/shard_map/ppermute | solution.py:541
  9.3 2.6 %collective-permute-start.1 = (bf16[7,16,256]{2,1,0:T(8,128)(2,1)S(1)}, bf16[7,16,256]{2,1,0:T(8,128)(2,1)S(1)}, u32[]{:S(2)}, u32[]{:S(2)}) collective-permute-start(bf16[7,16,256]{2,1,0:T(8,128)(2,1)S(1)} %get-tuple-element.37), channel_id=1, source_target_pairs={{0,8},{2,10},{4,12},{6,14},{8,0},{10,2},{12,4},{14,6},{1,9},{3,11}... | collective-permute-start | bytes 172040 | tf_op jit(solution)/shard_map/ppermute | solution.py:541
  11.9 1.3 %collective-permute-start.2 = (bf16[7,16,256]{2,1,0:T(8,128)(2,1)S(1)}, bf16[7,16,256]{2,1,0:T(8,128)(2,1)S(1)}, u32[]{:S(2)}, u32[]{:S(2)}) collective-permute-start(bf16[7,16,256]{2,1,0:T(8,128)(2,1)S(1)} %get-tuple-element.38), channel_id=1, source_target_pairs={{0,12},{2,14},{4,8},{6,10},{8,4},{10,6},{12,0},{14,2},{1,13},{3,15... | collective-permute-start | bytes 172040 | tf_op jit(solution)/shard_map/ppermute | solution.py:541
  13.2 0.2 collective-permute-start.3
  13.5 2.6 %shard_map.101 = (bf16[128,2048]{1,0:T(8,128)(2,1)S(1)}, bf16[128,2048]{1,0:T(8,128)(2,1)S(1)}, f32[16,128]{1,0:T(8,128)S(1)}) custom-call(f32[16]{0:T(128)} %defocus_hbm.3, f32[2,8]{1,0:T(2,128)} %bitcast.4, bf16[8,128,256]{2,1,0:T(8,128)(2,1)} %rows_hbm.3, bf16[8,256,128]{2,1,0:T(8,128)(2,1)} %cols_hbm.3), custom_call_target="tpu_custom_call" | custom-call | flops 1000 | bytes 1000 | tf_op jit(solution)/shard_map/pallas_call | solution.py:369
  16.1 0.0 collective-permute-done.1.refs_0_
  16.1 1.9 %collective-permute-done.2.refs_1_ = bf16[7,16,256]{2,1,0:T(8,128)(2,1)S(1)} collective-permute-done((bf16[7,16,256]{2,1,0:T(8,128)(2,1)S(1)}, bf16[7,16,256]{2,1,0:T(8,128)(2,1)S(1)}, u32[]{:S(2)}, u32[]{:S(2)}) %collective-permute-start.2) | collective-permute-done | bytes 57376 | tf_op jit(solution)/shard_map/ppermute | solution.py:541
  18.0 0.1 collective-permute-done.3.refs_2_
  18.0 0.0 collective-permute-done.x_came
  18.0 0.1 shard_map.102
  18.1 1.9 %collective-permute-start.5 = (bf16[13,16,256]{2,1,0:T(8,128)(2,1)S(1)}, bf16[13,16,256]{2,1,0:T(8,128)(2,1)S(1)}, u32[]{:S(2)}, u32[]{:S(2)}) collective-permute-start(bf16[13,16,256]{2,1,0:T(8,128)(2,1)S(1)} %get-tuple-element.43), channel_id=1, source_target_pairs={{0,8},{2,10},{4,12},{6,14},{8,0},{10,2},{12,4},{14,6},{1,9},{3,11}... | collective-permute-start | bytes 319496 | tf_op jit(solution)/shard_map/ppermute | solution.py:541
  20.0 1.2 %collective-permute-start.6 = (bf16[13,16,256]{2,1,0:T(8,128)(2,1)S(1)}, bf16[13,16,256]{2,1,0:T(8,128)(2,1)S(1)}, u32[]{:S(2)}, u32[]{:S(2)}) collective-permute-start(bf16[13,16,256]{2,1,0:T(8,128)(2,1)S(1)} %get-tuple-element.44), channel_id=1, source_target_pairs={{0,12},{2,14},{4,8},{6,10},{8,4},{10,6},{12,0},{14,2},{1,13},{3,15... | collective-permute-start | bytes 319496 | tf_op jit(solution)/shard_map/ppermute | solution.py:541
  21.2 0.5 %collective-permute-start.7 = (bf16[13,16,256]{2,1,0:T(8,128)(2,1)S(1)}, bf16[13,16,256]{2,1,0:T(8,128)(2,1)S(1)}, u32[]{:S(2)}, u32[]{:S(2)}) collective-permute-start(bf16[13,16,256]{2,1,0:T(8,128)(2,1)S(1)} %get-tuple-element.45), channel_id=1, source_target_pairs={{0,4},{2,6},{4,0},{6,2},{8,12},{10,14},{12,8},{14,10},{1,5},{3,7},... | collective-permute-start | bytes 319496 | tf_op jit(solution)/shard_map/ppermute | solution.py:541
  21.7 1.2 %collective-permute-start.8 = (bf16[13,16,256]{2,1,0:T(8,128)(2,1)S(1)}, bf16[13,16,256]{2,1,0:T(8,128)(2,1)S(1)}, u32[]{:S(2)}, u32[]{:S(2)}) collective-permute-start(bf16[13,16,256]{2,1,0:T(8,128)(2,1)S(1)} %get-tuple-element.46), channel_id=1, source_target_pairs={{0,2},{2,0},{4,6},{6,4},{8,10},{10,8},{12,14},{14,12},{1,3},{3,1},... | collective-permute-start | bytes 319496 | tf_op jit(solution)/shard_map/ppermute | solution.py:541
  22.9 0.8 %collective-permute-start.4 = (bf16[4,16,256]{2,1,0:T(8,128)(2,1)S(1)}, bf16[4,16,256]{2,1,0:T(8,128)(2,1)S(1)}, u32[]{:S(2)}, u32[]{:S(2)}) collective-permute-start(bf16[4,16,256]{2,1,0:T(8,128)(2,1)S(1)} %get-tuple-element.41), channel_id=1, source_target_pairs={{0,2},{2,0},{4,6},{6,4},{8,10},{10,8},{12,14},{14,12},{1,3},{3,1},... | collective-permute-start | bytes 98312 | tf_op jit(solution)/shard_map/ppermute | solution.py:541
  23.7 3.1 %collective-permute-done.4.z_came = bf16[4,16,256]{2,1,0:T(8,128)(2,1)S(1)} collective-permute-done((bf16[4,16,256]{2,1,0:T(8,128)(2,1)S(1)}, bf16[4,16,256]{2,1,0:T(8,128)(2,1)S(1)}, u32[]{:S(2)}, u32[]{:S(2)}) %collective-permute-start.4) | collective-permute-done | bytes 32800 | tf_op jit(solution)/shard_map/ppermute | solution.py:541
  26.8 0.4 %shard_map.103.ridge_ref = f32[16,16,128]{2,1,0:T(8,128)S(1)} custom-call(bf16[128,2048]{1,0:T(8,128)(2,1)S(1)} %get-tuple-element.30.high_ref, bf16[128,2048]{1,0:T(8,128)(2,1)S(1)} %get-tuple-element.31.low_ref, f32[16,128]{1,0:T(8,128)S(1)} %get-tuple-element.32.share_ref, f32[4,16,256]{2,1,0:T(8,128)S(1)} %get-tuple-element.40.z_own, ...), custom_call_target="tpu_custom_call" | custom-call | flops 1000 | bytes 1000 | tf_op jit(solution)/shard_map/pallas_call | solution.py:447
  27.2 1.2 %collective-permute-done.5.refs_0_ = bf16[13,16,256]{2,1,0:T(8,128)(2,1)S(1)} collective-permute-done((bf16[13,16,256]{2,1,0:T(8,128)(2,1)S(1)}, bf16[13,16,256]{2,1,0:T(8,128)(2,1)S(1)}, u32[]{:S(2)}, u32[]{:S(2)}) %collective-permute-start.5) | collective-permute-done | bytes 106528 | tf_op jit(solution)/shard_map/ppermute | solution.py:541
  28.4 0.0 collective-permute-done.6.refs_1_
  28.4 0.0 collective-permute-done.7.refs_2_
  28.5 0.0 collective-permute-done.8.refs_3_
  28.5 0.9 %shard_map.104 = f32[16,32,128]{2,1,0:T(8,128)} custom-call(f32[16,16,128]{2,1,0:T(8,128)S(1)} %shard_map.103.ridge_ref, f32[13,16,256]{2,1,0:T(8,128)S(1)} %get-tuple-element.42.x_own, f32[4,16,256]{2,1,0:T(8,128)S(1)} %get-tuple-element.40.z_own, bf16[4,16,256]{2,1,0:T(8,128)(2,1)S(1)} %collective-permute-done.4.z_came, ...), custom_call_target="tpu_custom_call" | custom-call | flops 1000 | bytes 1000 | tf_op jit(solution)/shard_map/pallas_call | solution.py:489
Async XLA Ops:
  6.3 11.7 %collective-permute-start = (bf16[3,13,16,256]{3,2,1,0:T(8,128)(2,1)S(1)}, bf16[3,13,16,256]{3,2,1,0:T(8,128)(2,1)S(1)}, u32[]{:S(2)}, u32[]{:S(2)}) collective-permute-start(bf16[3,13,16,256]{3,2,1,0:T(8,128)(2,1)S(1)} %get-tuple-element.34), channel_id=1, source_target_pairs={{0,2},{2,0},{4,6},{6,4},{8,10},{10,8},{12,14},{14,12},{1,3},{3,1},... | collective-permute-start | bytes 958472 | tf_op jit(solution)/shard_map/ppermute | solution.py:541
  9.3 6.8 %collective-permute-start.1 = (bf16[7,16,256]{2,1,0:T(8,128)(2,1)S(1)}, bf16[7,16,256]{2,1,0:T(8,128)(2,1)S(1)}, u32[]{:S(2)}, u32[]{:S(2)}) collective-permute-start(bf16[7,16,256]{2,1,0:T(8,128)(2,1)S(1)} %get-tuple-element.37), channel_id=1, source_target_pairs={{0,8},{2,10},{4,12},{6,14},{8,0},{10,2},{12,4},{14,6},{1,9},{3,11}... | collective-permute-start | bytes 172040 | tf_op jit(solution)/shard_map/ppermute | solution.py:541
  11.9 6.1 %collective-permute-start.2 = (bf16[7,16,256]{2,1,0:T(8,128)(2,1)S(1)}, bf16[7,16,256]{2,1,0:T(8,128)(2,1)S(1)}, u32[]{:S(2)}, u32[]{:S(2)}) collective-permute-start(bf16[7,16,256]{2,1,0:T(8,128)(2,1)S(1)} %get-tuple-element.38), channel_id=1, source_target_pairs={{0,12},{2,14},{4,8},{6,10},{8,4},{10,6},{12,0},{14,2},{1,13},{3,15... | collective-permute-start | bytes 172040 | tf_op jit(solution)/shard_map/ppermute | solution.py:541
  13.2 4.8 %collective-permute-start.3 = (bf16[7,16,256]{2,1,0:T(8,128)(2,1)S(1)}, bf16[7,16,256]{2,1,0:T(8,128)(2,1)S(1)}, u32[]{:S(2)}, u32[]{:S(2)}) collective-permute-start(bf16[7,16,256]{2,1,0:T(8,128)(2,1)S(1)} %get-tuple-element.39), channel_id=1, source_target_pairs={{0,4},{2,6},{4,0},{6,2},{8,12},{10,14},{12,8},{14,10},{1,5},{3,7},... | collective-permute-start | bytes 172040 | tf_op jit(solution)/shard_map/ppermute | solution.py:541
  18.1 10.3 %collective-permute-start.5 = (bf16[13,16,256]{2,1,0:T(8,128)(2,1)S(1)}, bf16[13,16,256]{2,1,0:T(8,128)(2,1)S(1)}, u32[]{:S(2)}, u32[]{:S(2)}) collective-permute-start(bf16[13,16,256]{2,1,0:T(8,128)(2,1)S(1)} %get-tuple-element.43), channel_id=1, source_target_pairs={{0,8},{2,10},{4,12},{6,14},{8,0},{10,2},{12,4},{14,6},{1,9},{3,11}... | collective-permute-start | bytes 319496 | tf_op jit(solution)/shard_map/ppermute | solution.py:541
  20.0 8.4 %collective-permute-start.6 = (bf16[13,16,256]{2,1,0:T(8,128)(2,1)S(1)}, bf16[13,16,256]{2,1,0:T(8,128)(2,1)S(1)}, u32[]{:S(2)}, u32[]{:S(2)}) collective-permute-start(bf16[13,16,256]{2,1,0:T(8,128)(2,1)S(1)} %get-tuple-element.44), channel_id=1, source_target_pairs={{0,12},{2,14},{4,8},{6,10},{8,4},{10,6},{12,0},{14,2},{1,13},{3,15... | collective-permute-start | bytes 319496 | tf_op jit(solution)/shard_map/ppermute | solution.py:541
  21.2 7.3 %collective-permute-start.7 = (bf16[13,16,256]{2,1,0:T(8,128)(2,1)S(1)}, bf16[13,16,256]{2,1,0:T(8,128)(2,1)S(1)}, u32[]{:S(2)}, u32[]{:S(2)}) collective-permute-start(bf16[13,16,256]{2,1,0:T(8,128)(2,1)S(1)} %get-tuple-element.45), channel_id=1, source_target_pairs={{0,4},{2,6},{4,0},{6,2},{8,12},{10,14},{12,8},{14,10},{1,5},{3,7},... | collective-permute-start | bytes 319496 | tf_op jit(solution)/shard_map/ppermute | solution.py:541
  21.7 6.8 %collective-permute-start.8 = (bf16[13,16,256]{2,1,0:T(8,128)(2,1)S(1)}, bf16[13,16,256]{2,1,0:T(8,128)(2,1)S(1)}, u32[]{:S(2)}, u32[]{:S(2)}) collective-permute-start(bf16[13,16,256]{2,1,0:T(8,128)(2,1)S(1)} %get-tuple-element.46), channel_id=1, source_target_pairs={{0,2},{2,0},{4,6},{6,4},{8,10},{10,8},{12,14},{14,12},{1,3},{3,1},... | collective-permute-start | bytes 319496 | tf_op jit(solution)/shard_map/ppermute | solution.py:541
  22.9 3.9 %collective-permute-start.4 = (bf16[4,16,256]{2,1,0:T(8,128)(2,1)S(1)}, bf16[4,16,256]{2,1,0:T(8,128)(2,1)S(1)}, u32[]{:S(2)}, u32[]{:S(2)}) collective-permute-start(bf16[4,16,256]{2,1,0:T(8,128)(2,1)S(1)} %get-tuple-element.41), channel_id=1, source_target_pairs={{0,2},{2,0},{4,6},{6,4},{8,10},{10,8},{12,14},{14,12},{1,3},{3,1},... | collective-permute-start | bytes 98312 | tf_op jit(solution)/shard_map/ppermute | solution.py:541

commit v19 on v17

--- a/solution.py
+++ b/solution.py
@@ -136,9 +136,7 @@
             half_ref[i // GROUP % 2, n * box : (n + 1) * box] = product[:, n * box : (n + 1) * box]
 
     def along_columns(i):
-        product = dot(half_ref[i // GROUP % 2], dft_t_ref[...])
-        for n in range(GROUP):
-            weigh(i + n, product[n * box : (n + 1) * box])
+        return dot(half_ref[i // GROUP % 2], dft_t_ref[...])
 
     def weigh(i, y):
         sin_col = jnp.broadcast_to(wave_y[:, i : i + 1], (tall, half))
@@ -202,22 +200,22 @@
         far_two = dot(far, two).astype(bf16)
         cols_fold[p] = jnp.concatenate([near_two[:, :cols], far_two[:, :cols]], 1)
         cols_fold[p + 1] = jnp.concatenate([near_two[:, cols:], far_two[:, cols:]], 1)
-    along_rows(GROUP)
-    along_columns(0)
     copies[9].wait()
     rows_fold[...] = dot(
         rows_ref[...].reshape(poses * rows, box), near, ((1,), (1,))
     ).astype(bf16)
-    for step in range(2 * GROUP, count + 3 * GROUP, GROUP):
+    for step in range(GROUP, count + 3 * GROUP, GROUP):
+        if step < count:
+            along_rows(step)
+        if step - GROUP < count:
+            product = along_columns(step - GROUP)
         for n in range(GROUP):
+            if step - GROUP < count:
+                weigh(step - GROUP + n, product[n * box : (n + 1) * box])
+            if 0 <= step - 2 * GROUP < count:
+                mix(step - 2 * GROUP + n)
             if step >= 3 * GROUP:
                 insert(step - 3 * GROUP + n)
-            if step - 2 * GROUP < count:
-                mix(step - 2 * GROUP + n)
-        if step - GROUP < count:
-            along_columns(step - GROUP)
-        if step < count:
-            along_rows(step)
 
     if len(outs) == 1:
         outs[0][...] = totals[...].astype(bf16)

time: 29.1 us -> 28.9 us (level)
  no operation moved by 1% of the time
where the time goes in v19:
time: 28.9 us; the launch traced here: 28.8 us
  starting transfers between devices  12.7 us (44%)
  Pallas kernels  9.65 us (33%)
  waiting for transfers between devices  6.33 us (22%)
    ppermute x9, starting transfers between devices, exchange(): return lax.ppermute(value, 'img', [(i, i ^ flip) for i in range(members)])  12.7 us
    ppermute x9, waiting for transfers between devices, exchange(): return lax.ppermute(value, 'img', [(i, i ^ flip) for i in range(members)])  6.33 us
    pallas_call x1, Pallas kernels, own_totals(): pl.pallas_call(slices_kernel, out_shape=out_shape, in_specs=[any_place] *...  5.64 us
    pallas_call x1, Pallas kernels, own_ridges(): pl.pallas_call(ridge_kernel, out_shape=[table, table, pltpu.VMEM((planes....  2.62 us
    pallas_call x1, Pallas kernels, finish(): pl.pallas_call(functools.partial(finish_kernel, planes), out_shape=jax.Sh...  0.94 us
  transfers between devices with their start and end apart: 9, of which 4 were waited for; matrix products, arithmetic and copies ran while one was open for 0% of the time, Pallas kernels for 10%

profile of v19, /device:TPU:0, one launch (start us, length us, event | category | flops | bytes accessed | tf_op | source)
XLA Modules:
  0.0 28.8 jit_solution(1226486520352186150)
XLA Ops:
  0.0 5.6 %shard_map.100 = (bf16[3,13,16,256]{3,2,1,0:T(8,128)(2,1)S(1)}, f32[3,13,16,256]{3,2,1,0:T(8,128)S(1)}, bf16[13,16,256]{2,1,0:T(8,128)(2,1)S(1)}, f32[13,16,256]...) custom-call(s32[16]{0:T(128)} %bitcast.5, ...), custom_call_target="tpu_custom_call" | custom-call | flops 2097152000 | bytes 6291456 | tf_op jit(solution)/shard_map/pallas_call | solution.py:274
  5.6 3.0 %collective-permute-start = (bf16[3,13,16,256]{3,2,1,0:T(8,128)(2,1)S(1)}, bf16[3,13,16,256]{3,2,1,0:T(8,128)(2,1)S(1)}, u32[]{:S(2)}, u32[]{:S(2)}) collective-permute-start(bf16[3,13,16,256]{3,2,1,0:T(8,128)(2,1)S(1)} %get-tuple-element.34), channel_id=1, source_target_pairs={{0,2},{2,0},{4,6},{6,4},{8,10},{10,8},{12,14},{14,12},{1,3},{3,1},... | collective-permute-start | bytes 958472 | tf_op jit(solution)/shard_map/ppermute | solution.py:525
  8.7 2.6 %collective-permute-start.1 = (bf16[7,16,256]{2,1,0:T(8,128)(2,1)S(1)}, bf16[7,16,256]{2,1,0:T(8,128)(2,1)S(1)}, u32[]{:S(2)}, u32[]{:S(2)}) collective-permute-start(bf16[7,16,256]{2,1,0:T(8,128)(2,1)S(1)} %get-tuple-element.37), channel_id=1, source_target_pairs={{0,8},{2,10},{4,12},{6,14},{8,0},{10,2},{12,4},{14,6},{1,9},{3,11}... | collective-permute-start | bytes 172040 | tf_op jit(solution)/shard_map/ppermute | solution.py:525
  11.2 1.3 %collective-permute-start.2 = (bf16[7,16,256]{2,1,0:T(8,128)(2,1)S(1)}, bf16[7,16,256]{2,1,0:T(8,128)(2,1)S(1)}, u32[]{:S(2)}, u32[]{:S(2)}) collective-permute-start(bf16[7,16,256]{2,1,0:T(8,128)(2,1)S(1)} %get-tuple-element.38), channel_id=1, source_target_pairs={{0,12},{2,14},{4,8},{6,10},{8,4},{10,6},{12,0},{14,2},{1,13},{3,15... | collective-permute-start | bytes 172040 | tf_op jit(solution)/shard_map/ppermute | solution.py:525
  12.6 0.2 collective-permute-start.3
  12.8 2.6 %shard_map.101 = (bf16[128,2048]{1,0:T(8,128)(2,1)S(1)}, bf16[128,2048]{1,0:T(8,128)(2,1)S(1)}, f32[16,128]{1,0:T(8,128)S(1)}) custom-call(f32[16]{0:T(128)} %defocus_hbm.3, f32[2,8]{1,0:T(2,128)} %bitcast.4, bf16[8,128,256]{2,1,0:T(8,128)(2,1)} %rows_hbm.3, bf16[8,256,128]{2,1,0:T(8,128)(2,1)} %cols_hbm.3), custom_call_target="tpu_custom_call" | custom-call | flops 1000 | bytes 1000 | tf_op jit(solution)/shard_map/pallas_call | solution.py:368
  15.4 0.0 collective-permute-done.1.refs_0_
  15.4 1.9 %collective-permute-done.2.refs_1_ = bf16[7,16,256]{2,1,0:T(8,128)(2,1)S(1)} collective-permute-done((bf16[7,16,256]{2,1,0:T(8,128)(2,1)S(1)}, bf16[7,16,256]{2,1,0:T(8,128)(2,1)S(1)}, u32[]{:S(2)}, u32[]{:S(2)}) %collective-permute-start.2) | collective-permute-done | bytes 57376 | tf_op jit(solution)/shard_map/ppermute | solution.py:525
  17.3 0.1 collective-permute-done.3.refs_2_
  17.4 0.0 collective-permute-done.x_came
  17.4 0.1 shard_map.102
  17.5 1.9 %collective-permute-start.5 = (bf16[13,16,256]{2,1,0:T(8,128)(2,1)S(1)}, bf16[13,16,256]{2,1,0:T(8,128)(2,1)S(1)}, u32[]{:S(2)}, u32[]{:S(2)}) collective-permute-start(bf16[13,16,256]{2,1,0:T(8,128)(2,1)S(1)} %get-tuple-element.43), channel_id=1, source_target_pairs={{0,8},{2,10},{4,12},{6,14},{8,0},{10,2},{12,4},{14,6},{1,9},{3,11}... | collective-permute-start | bytes 319496 | tf_op jit(solution)/shard_map/ppermute | solution.py:525
  19.4 1.2 %collective-permute-start.6 = (bf16[13,16,256]{2,1,0:T(8,128)(2,1)S(1)}, bf16[13,16,256]{2,1,0:T(8,128)(2,1)S(1)}, u32[]{:S(2)}, u32[]{:S(2)}) collective-permute-start(bf16[13,16,256]{2,1,0:T(8,128)(2,1)S(1)} %get-tuple-element.44), channel_id=1, source_target_pairs={{0,12},{2,14},{4,8},{6,10},{8,4},{10,6},{12,0},{14,2},{1,13},{3,15... | collective-permute-start | bytes 319496 | tf_op jit(solution)/shard_map/ppermute | solution.py:525
  20.5 0.5 %collective-permute-start.7 = (bf16[13,16,256]{2,1,0:T(8,128)(2,1)S(1)}, bf16[13,16,256]{2,1,0:T(8,128)(2,1)S(1)}, u32[]{:S(2)}, u32[]{:S(2)}) collective-permute-start(bf16[13,16,256]{2,1,0:T(8,128)(2,1)S(1)} %get-tuple-element.45), channel_id=1, source_target_pairs={{0,4},{2,6},{4,0},{6,2},{8,12},{10,14},{12,8},{14,10},{1,5},{3,7},... | collective-permute-start | bytes 319496 | tf_op jit(solution)/shard_map/ppermute | solution.py:525
  21.0 1.2 %collective-permute-start.8 = (bf16[13,16,256]{2,1,0:T(8,128)(2,1)S(1)}, bf16[13,16,256]{2,1,0:T(8,128)(2,1)S(1)}, u32[]{:S(2)}, u32[]{:S(2)}) collective-permute-start(bf16[13,16,256]{2,1,0:T(8,128)(2,1)S(1)} %get-tuple-element.46), channel_id=1, source_target_pairs={{0,2},{2,0},{4,6},{6,4},{8,10},{10,8},{12,14},{14,12},{1,3},{3,1},... | collective-permute-start | bytes 319496 | tf_op jit(solution)/shard_map/ppermute | solution.py:525
  22.2 0.8 %collective-permute-start.4 = (bf16[4,16,256]{2,1,0:T(8,128)(2,1)S(1)}, bf16[4,16,256]{2,1,0:T(8,128)(2,1)S(1)}, u32[]{:S(2)}, u32[]{:S(2)}) collective-permute-start(bf16[4,16,256]{2,1,0:T(8,128)(2,1)S(1)} %get-tuple-element.41), channel_id=1, source_target_pairs={{0,2},{2,0},{4,6},{6,4},{8,10},{10,8},{12,14},{14,12},{1,3},{3,1},... | collective-permute-start | bytes 98312 | tf_op jit(solution)/shard_map/ppermute | solution.py:525
  23.1 3.1 %collective-permute-done.4.z_came = bf16[4,16,256]{2,1,0:T(8,128)(2,1)S(1)} collective-permute-done((bf16[4,16,256]{2,1,0:T(8,128)(2,1)S(1)}, bf16[4,16,256]{2,1,0:T(8,128)(2,1)S(1)}, u32[]{:S(2)}, u32[]{:S(2)}) %collective-permute-start.4) | collective-permute-done | bytes 32800 | tf_op jit(solution)/shard_map/ppermute | solution.py:525
  26.2 0.4 %shard_map.103.ridge_ref = f32[16,16,128]{2,1,0:T(8,128)S(1)} custom-call(bf16[128,2048]{1,0:T(8,128)(2,1)S(1)} %get-tuple-element.30.high_ref, bf16[128,2048]{1,0:T(8,128)(2,1)S(1)} %get-tuple-element.31.low_ref, f32[16,128]{1,0:T(8,128)S(1)} %get-tuple-element.32.share_ref, f32[4,16,256]{2,1,0:T(8,128)S(1)} %get-tuple-element.40.z_own, ...), custom_call_target="tpu_custom_call" | custom-call | flops 1000 | bytes 1000 | tf_op jit(solution)/shard_map/pallas_call | solution.py:446
  26.5 1.2 %collective-permute-done.5.refs_0_ = bf16[13,16,256]{2,1,0:T(8,128)(2,1)S(1)} collective-permute-done((bf16[13,16,256]{2,1,0:T(8,128)(2,1)S(1)}, bf16[13,16,256]{2,1,0:T(8,128)(2,1)S(1)}, u32[]{:S(2)}, u32[]{:S(2)}) %collective-permute-start.5) | collective-permute-done | bytes 106528 | tf_op jit(solution)/shard_map/ppermute | solution.py:525
  27.8 0.0 collective-permute-done.6.refs_1_
  27.8 0.0 collective-permute-done.7.refs_2_
  27.8 0.0 collective-permute-done.8.refs_3_
  27.8 0.9 %shard_map.104 = f32[16,32,128]{2,1,0:T(8,128)} custom-call(f32[16,16,128]{2,1,0:T(8,128)S(1)} %shard_map.103.ridge_ref, f32[13,16,256]{2,1,0:T(8,128)S(1)} %get-tuple-element.42.x_own, f32[4,16,256]{2,1,0:T(8,128)S(1)} %get-tuple-element.40.z_own, bf16[4,16,256]{2,1,0:T(8,128)(2,1)S(1)} %collective-permute-done.4.z_came, ...), custom_call_target="tpu_custom_call" | custom-call | flops 1000 | bytes 1000 | tf_op jit(solution)/shard_map/pallas_call | solution.py:477
Async XLA Ops:
  5.6 11.7 %collective-permute-start = (bf16[3,13,16,256]{3,2,1,0:T(8,128)(2,1)S(1)}, bf16[3,13,16,256]{3,2,1,0:T(8,128)(2,1)S(1)}, u32[]{:S(2)}, u32[]{:S(2)}) collective-permute-start(bf16[3,13,16,256]{3,2,1,0:T(8,128)(2,1)S(1)} %get-tuple-element.34), channel_id=1, source_target_pairs={{0,2},{2,0},{4,6},{6,4},{8,10},{10,8},{12,14},{14,12},{1,3},{3,1},... | collective-permute-start | bytes 958472 | tf_op jit(solution)/shard_map/ppermute | solution.py:525
  8.7 6.8 %collective-permute-start.1 = (bf16[7,16,256]{2,1,0:T(8,128)(2,1)S(1)}, bf16[7,16,256]{2,1,0:T(8,128)(2,1)S(1)}, u32[]{:S(2)}, u32[]{:S(2)}) collective-permute-start(bf16[7,16,256]{2,1,0:T(8,128)(2,1)S(1)} %get-tuple-element.37), channel_id=1, source_target_pairs={{0,8},{2,10},{4,12},{6,14},{8,0},{10,2},{12,4},{14,6},{1,9},{3,11}... | collective-permute-start | bytes 172040 | tf_op jit(solution)/shard_map/ppermute | solution.py:525
  11.2 6.1 %collective-permute-start.2 = (bf16[7,16,256]{2,1,0:T(8,128)(2,1)S(1)}, bf16[7,16,256]{2,1,0:T(8,128)(2,1)S(1)}, u32[]{:S(2)}, u32[]{:S(2)}) collective-permute-start(bf16[7,16,256]{2,1,0:T(8,128)(2,1)S(1)} %get-tuple-element.38), channel_id=1, source_target_pairs={{0,12},{2,14},{4,8},{6,10},{8,4},{10,6},{12,0},{14,2},{1,13},{3,15... | collective-permute-start | bytes 172040 | tf_op jit(solution)/shard_map/ppermute | solution.py:525
  12.6 4.8 %collective-permute-start.3 = (bf16[7,16,256]{2,1,0:T(8,128)(2,1)S(1)}, bf16[7,16,256]{2,1,0:T(8,128)(2,1)S(1)}, u32[]{:S(2)}, u32[]{:S(2)}) collective-permute-start(bf16[7,16,256]{2,1,0:T(8,128)(2,1)S(1)} %get-tuple-element.39), channel_id=1, source_target_pairs={{0,4},{2,6},{4,0},{6,2},{8,12},{10,14},{12,8},{14,10},{1,5},{3,7},... | collective-permute-start | bytes 172040 | tf_op jit(solution)/shard_map/ppermute | solution.py:525
  17.5 10.3 %collective-permute-start.5 = (bf16[13,16,256]{2,1,0:T(8,128)(2,1)S(1)}, bf16[13,16,256]{2,1,0:T(8,128)(2,1)S(1)}, u32[]{:S(2)}, u32[]{:S(2)}) collective-permute-start(bf16[13,16,256]{2,1,0:T(8,128)(2,1)S(1)} %get-tuple-element.43), channel_id=1, source_target_pairs={{0,8},{2,10},{4,12},{6,14},{8,0},{10,2},{12,4},{14,6},{1,9},{3,11}... | collective-permute-start | bytes 319496 | tf_op jit(solution)/shard_map/ppermute | solution.py:525
  19.4 8.4 %collective-permute-start.6 = (bf16[13,16,256]{2,1,0:T(8,128)(2,1)S(1)}, bf16[13,16,256]{2,1,0:T(8,128)(2,1)S(1)}, u32[]{:S(2)}, u32[]{:S(2)}) collective-permute-start(bf16[13,16,256]{2,1,0:T(8,128)(2,1)S(1)} %get-tuple-element.44), channel_id=1, source_target_pairs={{0,12},{2,14},{4,8},{6,10},{8,4},{10,6},{12,0},{14,2},{1,13},{3,15... | collective-permute-start | bytes 319496 | tf_op jit(solution)/shard_map/ppermute | solution.py:525
  20.5 7.3 %collective-permute-start.7 = (bf16[13,16,256]{2,1,0:T(8,128)(2,1)S(1)}, bf16[13,16,256]{2,1,0:T(8,128)(2,1)S(1)}, u32[]{:S(2)}, u32[]{:S(2)}) collective-permute-start(bf16[13,16,256]{2,1,0:T(8,128)(2,1)S(1)} %get-tuple-element.45), channel_id=1, source_target_pairs={{0,4},{2,6},{4,0},{6,2},{8,12},{10,14},{12,8},{14,10},{1,5},{3,7},... | collective-permute-start | bytes 319496 | tf_op jit(solution)/shard_map/ppermute | solution.py:525
  21.0 6.8 %collective-permute-start.8 = (bf16[13,16,256]{2,1,0:T(8,128)(2,1)S(1)}, bf16[13,16,256]{2,1,0:T(8,128)(2,1)S(1)}, u32[]{:S(2)}, u32[]{:S(2)}) collective-permute-start(bf16[13,16,256]{2,1,0:T(8,128)(2,1)S(1)} %get-tuple-element.46), channel_id=1, source_target_pairs={{0,2},{2,0},{4,6},{6,4},{8,10},{10,8},{12,14},{14,12},{1,3},{3,1},... | collective-permute-start | bytes 319496 | tf_op jit(solution)/shard_map/ppermute | solution.py:525
  22.2 3.9 %collective-permute-start.4 = (bf16[4,16,256]{2,1,0:T(8,128)(2,1)S(1)}, bf16[4,16,256]{2,1,0:T(8,128)(2,1)S(1)}, u32[]{:S(2)}, u32[]{:S(2)}) collective-permute-start(bf16[4,16,256]{2,1,0:T(8,128)(2,1)S(1)} %get-tuple-element.41), channel_id=1, source_target_pairs={{0,2},{2,0},{4,6},{6,4},{8,10},{10,8},{12,14},{14,12},{1,3},{3,1},... | collective-permute-start | bytes 98312 | tf_op jit(solution)/shard_map/ppermute | solution.py:525

commit v20 on v19

--- a/solution.py
+++ b/solution.py
@@ -241,7 +241,7 @@
 SCRATCH = 20
 LINE = (2, 3, 1)
 SLOTS = 8
-GROUP = 4
+GROUP = 2
 Z_SLOTS = 4
 
 

time: 28.9 us -> 29.7 us (1.028)
  Pallas kernels: 9.65 us -> 10.4 us
    pallas_call x1, Pallas kernels: 5.64 us -> 6.42 us  [own_totals(): pl.pallas_call(slices_kernel, out_shape=out_shape, in_specs=[any_place] *...]
  transfers between devices with their start and end apart: 9 -> 9, of which waited for: 4 -> 5; matrix products, arithmetic and copies ran while one was open for 0% -> 0% of each run, Pallas kernels for 10% -> 10%
where the time goes in v20:
time: 29.7 us; the launch traced here: 29.6 us
  starting transfers between devices  12.8 us (43%)
  Pallas kernels  10.4 us (35%)
  waiting for transfers between devices  6.32 us (21%)
    ppermute x9, starting transfers between devices, exchange(): return lax.ppermute(value, 'img', [(i, i ^ flip) for i in range(members)])  12.8 us
    pallas_call x1, Pallas kernels, own_totals(): pl.pallas_call(slices_kernel, out_shape=out_shape, in_specs=[any_place] *...  6.42 us
    ppermute x9, waiting for transfers between devices, exchange(): return lax.ppermute(value, 'img', [(i, i ^ flip) for i in range(members)])  6.32 us
    pallas_call x1, Pallas kernels, own_ridges(): pl.pallas_call(ridge_kernel, out_shape=[table, table, pltpu.VMEM((planes....  2.62 us
    pallas_call x1, Pallas kernels, finish(): pl.pallas_call(functools.partial(finish_kernel, planes), out_shape=jax.Sh...  0.94 us
  transfers between devices with their start and end apart: 9, of which 5 were waited for; matrix products, arithmetic and copies ran while one was open for 0% of the time, Pallas kernels for 10%

profile of v20, /device:TPU:0, one launch (start us, length us, event | category | flops | bytes accessed | tf_op | source)
XLA Modules:
  0.0 29.6 jit_solution(11329508855985819915)
XLA Ops:
  0.0 6.4 %shard_map.100 = (bf16[3,13,16,256]{3,2,1,0:T(8,128)(2,1)S(1)}, f32[3,13,16,256]{3,2,1,0:T(8,128)S(1)}, bf16[13,16,256]{2,1,0:T(8,128)(2,1)S(1)}, f32[13,16,256]...) custom-call(s32[16]{0:T(128)} %bitcast.5, ...), custom_call_target="tpu_custom_call" | custom-call | flops 2097152000 | bytes 6291456 | tf_op jit(solution)/shard_map/pallas_call | solution.py:274
  6.4 3.0 %collective-permute-start = (bf16[3,13,16,256]{3,2,1,0:T(8,128)(2,1)S(1)}, bf16[3,13,16,256]{3,2,1,0:T(8,128)(2,1)S(1)}, u32[]{:S(2)}, u32[]{:S(2)}) collective-permute-start(bf16[3,13,16,256]{3,2,1,0:T(8,128)(2,1)S(1)} %get-tuple-element.34), channel_id=1, source_target_pairs={{0,2},{2,0},{4,6},{6,4},{8,10},{10,8},{12,14},{14,12},{1,3},{3,1},... | collective-permute-start | bytes 958472 | tf_op jit(solution)/shard_map/ppermute | solution.py:525
  9.4 2.6 %collective-permute-start.1 = (bf16[7,16,256]{2,1,0:T(8,128)(2,1)S(1)}, bf16[7,16,256]{2,1,0:T(8,128)(2,1)S(1)}, u32[]{:S(2)}, u32[]{:S(2)}) collective-permute-start(bf16[7,16,256]{2,1,0:T(8,128)(2,1)S(1)} %get-tuple-element.37), channel_id=1, source_target_pairs={{0,8},{2,10},{4,12},{6,14},{8,0},{10,2},{12,4},{14,6},{1,9},{3,11}... | collective-permute-start | bytes 172040 | tf_op jit(solution)/shard_map/ppermute | solution.py:525
  12.0 1.3 %collective-permute-start.2 = (bf16[7,16,256]{2,1,0:T(8,128)(2,1)S(1)}, bf16[7,16,256]{2,1,0:T(8,128)(2,1)S(1)}, u32[]{:S(2)}, u32[]{:S(2)}) collective-permute-start(bf16[7,16,256]{2,1,0:T(8,128)(2,1)S(1)} %get-tuple-element.38), channel_id=1, source_target_pairs={{0,12},{2,14},{4,8},{6,10},{8,4},{10,6},{12,0},{14,2},{1,13},{3,15... | collective-permute-start | bytes 172040 | tf_op jit(solution)/shard_map/ppermute | solution.py:525
  13.4 0.2 collective-permute-start.3
  13.6 2.6 %shard_map.101 = (bf16[128,2048]{1,0:T(8,128)(2,1)S(1)}, bf16[128,2048]{1,0:T(8,128)(2,1)S(1)}, f32[16,128]{1,0:T(8,128)S(1)}) custom-call(f32[16]{0:T(128)} %defocus_hbm.3, f32[2,8]{1,0:T(2,128)} %bitcast.4, bf16[8,128,256]{2,1,0:T(8,128)(2,1)} %rows_hbm.3, bf16[8,256,128]{2,1,0:T(8,128)(2,1)} %cols_hbm.3), custom_call_target="tpu_custom_call" | custom-call | flops 1000 | bytes 1000 | tf_op jit(solution)/shard_map/pallas_call | solution.py:368
  16.2 0.0 collective-permute-done.1.refs_0_
  16.2 1.9 %collective-permute-done.2.refs_1_ = bf16[7,16,256]{2,1,0:T(8,128)(2,1)S(1)} collective-permute-done((bf16[7,16,256]{2,1,0:T(8,128)(2,1)S(1)}, bf16[7,16,256]{2,1,0:T(8,128)(2,1)S(1)}, u32[]{:S(2)}, u32[]{:S(2)}) %collective-permute-start.2) | collective-permute-done | bytes 57376 | tf_op jit(solution)/shard_map/ppermute | solution.py:525
  18.1 0.1 collective-permute-done.3.refs_2_
  18.2 0.0 collective-permute-done.x_came
  18.2 0.1 shard_map.102
  18.3 1.9 %collective-permute-start.5 = (bf16[13,16,256]{2,1,0:T(8,128)(2,1)S(1)}, bf16[13,16,256]{2,1,0:T(8,128)(2,1)S(1)}, u32[]{:S(2)}, u32[]{:S(2)}) collective-permute-start(bf16[13,16,256]{2,1,0:T(8,128)(2,1)S(1)} %get-tuple-element.43), channel_id=1, source_target_pairs={{0,8},{2,10},{4,12},{6,14},{8,0},{10,2},{12,4},{14,6},{1,9},{3,11}... | collective-permute-start | bytes 319496 | tf_op jit(solution)/shard_map/ppermute | solution.py:525
  20.1 1.2 %collective-permute-start.6 = (bf16[13,16,256]{2,1,0:T(8,128)(2,1)S(1)}, bf16[13,16,256]{2,1,0:T(8,128)(2,1)S(1)}, u32[]{:S(2)}, u32[]{:S(2)}) collective-permute-start(bf16[13,16,256]{2,1,0:T(8,128)(2,1)S(1)} %get-tuple-element.44), channel_id=1, source_target_pairs={{0,12},{2,14},{4,8},{6,10},{8,4},{10,6},{12,0},{14,2},{1,13},{3,15... | collective-permute-start | bytes 319496 | tf_op jit(solution)/shard_map/ppermute | solution.py:525
  21.3 0.5 %collective-permute-start.7 = (bf16[13,16,256]{2,1,0:T(8,128)(2,1)S(1)}, bf16[13,16,256]{2,1,0:T(8,128)(2,1)S(1)}, u32[]{:S(2)}, u32[]{:S(2)}) collective-permute-start(bf16[13,16,256]{2,1,0:T(8,128)(2,1)S(1)} %get-tuple-element.45), channel_id=1, source_target_pairs={{0,4},{2,6},{4,0},{6,2},{8,12},{10,14},{12,8},{14,10},{1,5},{3,7},... | collective-permute-start | bytes 319496 | tf_op jit(solution)/shard_map/ppermute | solution.py:525
  21.8 1.2 %collective-permute-start.8 = (bf16[13,16,256]{2,1,0:T(8,128)(2,1)S(1)}, bf16[13,16,256]{2,1,0:T(8,128)(2,1)S(1)}, u32[]{:S(2)}, u32[]{:S(2)}) collective-permute-start(bf16[13,16,256]{2,1,0:T(8,128)(2,1)S(1)} %get-tuple-element.46), channel_id=1, source_target_pairs={{0,2},{2,0},{4,6},{6,4},{8,10},{10,8},{12,14},{14,12},{1,3},{3,1},... | collective-permute-start | bytes 319496 | tf_op jit(solution)/shard_map/ppermute | solution.py:525
  23.0 0.8 %collective-permute-start.4 = (bf16[4,16,256]{2,1,0:T(8,128)(2,1)S(1)}, bf16[4,16,256]{2,1,0:T(8,128)(2,1)S(1)}, u32[]{:S(2)}, u32[]{:S(2)}) collective-permute-start(bf16[4,16,256]{2,1,0:T(8,128)(2,1)S(1)} %get-tuple-element.41), channel_id=1, source_target_pairs={{0,2},{2,0},{4,6},{6,4},{8,10},{10,8},{12,14},{14,12},{1,3},{3,1},... | collective-permute-start | bytes 98312 | tf_op jit(solution)/shard_map/ppermute | solution.py:525
  23.8 3.1 %collective-permute-done.4.z_came = bf16[4,16,256]{2,1,0:T(8,128)(2,1)S(1)} collective-permute-done((bf16[4,16,256]{2,1,0:T(8,128)(2,1)S(1)}, bf16[4,16,256]{2,1,0:T(8,128)(2,1)S(1)}, u32[]{:S(2)}, u32[]{:S(2)}) %collective-permute-start.4) | collective-permute-done | bytes 32800 | tf_op jit(solution)/shard_map/ppermute | solution.py:525
  26.9 0.4 %shard_map.103.ridge_ref = f32[16,16,128]{2,1,0:T(8,128)S(1)} custom-call(bf16[128,2048]{1,0:T(8,128)(2,1)S(1)} %get-tuple-element.30.high_ref, bf16[128,2048]{1,0:T(8,128)(2,1)S(1)} %get-tuple-element.31.low_ref, f32[16,128]{1,0:T(8,128)S(1)} %get-tuple-element.32.share_ref, f32[4,16,256]{2,1,0:T(8,128)S(1)} %get-tuple-element.40.z_own, ...), custom_call_target="tpu_custom_call" | custom-call | flops 1000 | bytes 1000 | tf_op jit(solution)/shard_map/pallas_call | solution.py:446
  27.3 1.2 %collective-permute-done.5.refs_0_ = bf16[13,16,256]{2,1,0:T(8,128)(2,1)S(1)} collective-permute-done((bf16[13,16,256]{2,1,0:T(8,128)(2,1)S(1)}, bf16[13,16,256]{2,1,0:T(8,128)(2,1)S(1)}, u32[]{:S(2)}, u32[]{:S(2)}) %collective-permute-start.5) | collective-permute-done | bytes 106528 | tf_op jit(solution)/shard_map/ppermute | solution.py:525
  28.6 0.0 collective-permute-done.6.refs_1_
  28.6 0.1 collective-permute-done.7.refs_2_
  28.6 0.0 collective-permute-done.8.refs_3_
  28.6 0.9 %shard_map.104 = f32[16,32,128]{2,1,0:T(8,128)} custom-call(f32[16,16,128]{2,1,0:T(8,128)S(1)} %shard_map.103.ridge_ref, f32[13,16,256]{2,1,0:T(8,128)S(1)} %get-tuple-element.42.x_own, f32[4,16,256]{2,1,0:T(8,128)S(1)} %get-tuple-element.40.z_own, bf16[4,16,256]{2,1,0:T(8,128)(2,1)S(1)} %collective-permute-done.4.z_came, ...), custom_call_target="tpu_custom_call" | custom-call | flops 1000 | bytes 1000 | tf_op jit(solution)/shard_map/pallas_call | solution.py:477
Async XLA Ops:
  6.4 11.7 %collective-permute-start = (bf16[3,13,16,256]{3,2,1,0:T(8,128)(2,1)S(1)}, bf16[3,13,16,256]{3,2,1,0:T(8,128)(2,1)S(1)}, u32[]{:S(2)}, u32[]{:S(2)}) collective-permute-start(bf16[3,13,16,256]{3,2,1,0:T(8,128)(2,1)S(1)} %get-tuple-element.34), channel_id=1, source_target_pairs={{0,2},{2,0},{4,6},{6,4},{8,10},{10,8},{12,14},{14,12},{1,3},{3,1},... | collective-permute-start | bytes 958472 | tf_op jit(solution)/shard_map/ppermute | solution.py:525
  9.4 6.8 %collective-permute-start.1 = (bf16[7,16,256]{2,1,0:T(8,128)(2,1)S(1)}, bf16[7,16,256]{2,1,0:T(8,128)(2,1)S(1)}, u32[]{:S(2)}, u32[]{:S(2)}) collective-permute-start(bf16[7,16,256]{2,1,0:T(8,128)(2,1)S(1)} %get-tuple-element.37), channel_id=1, source_target_pairs={{0,8},{2,10},{4,12},{6,14},{8,0},{10,2},{12,4},{14,6},{1,9},{3,11}... | collective-permute-start | bytes 172040 | tf_op jit(solution)/shard_map/ppermute | solution.py:525
  12.0 6.1 %collective-permute-start.2 = (bf16[7,16,256]{2,1,0:T(8,128)(2,1)S(1)}, bf16[7,16,256]{2,1,0:T(8,128)(2,1)S(1)}, u32[]{:S(2)}, u32[]{:S(2)}) collective-permute-start(bf16[7,16,256]{2,1,0:T(8,128)(2,1)S(1)} %get-tuple-element.38), channel_id=1, source_target_pairs={{0,12},{2,14},{4,8},{6,10},{8,4},{10,6},{12,0},{14,2},{1,13},{3,15... | collective-permute-start | bytes 172040 | tf_op jit(solution)/shard_map/ppermute | solution.py:525
  13.4 4.8 %collective-permute-start.3 = (bf16[7,16,256]{2,1,0:T(8,128)(2,1)S(1)}, bf16[7,16,256]{2,1,0:T(8,128)(2,1)S(1)}, u32[]{:S(2)}, u32[]{:S(2)}) collective-permute-start(bf16[7,16,256]{2,1,0:T(8,128)(2,1)S(1)} %get-tuple-element.39), channel_id=1, source_target_pairs={{0,4},{2,6},{4,0},{6,2},{8,12},{10,14},{12,8},{14,10},{1,5},{3,7},... | collective-permute-start | bytes 172040 | tf_op jit(solution)/shard_map/ppermute | solution.py:525
  18.3 10.3 %collective-permute-start.5 = (bf16[13,16,256]{2,1,0:T(8,128)(2,1)S(1)}, bf16[13,16,256]{2,1,0:T(8,128)(2,1)S(1)}, u32[]{:S(2)}, u32[]{:S(2)}) collective-permute-start(bf16[13,16,256]{2,1,0:T(8,128)(2,1)S(1)} %get-tuple-element.43), channel_id=1, source_target_pairs={{0,8},{2,10},{4,12},{6,14},{8,0},{10,2},{12,4},{14,6},{1,9},{3,11}... | collective-permute-start | bytes 319496 | tf_op jit(solution)/shard_map/ppermute | solution.py:525
  20.1 8.4 %collective-permute-start.6 = (bf16[13,16,256]{2,1,0:T(8,128)(2,1)S(1)}, bf16[13,16,256]{2,1,0:T(8,128)(2,1)S(1)}, u32[]{:S(2)}, u32[]{:S(2)}) collective-permute-start(bf16[13,16,256]{2,1,0:T(8,128)(2,1)S(1)} %get-tuple-element.44), channel_id=1, source_target_pairs={{0,12},{2,14},{4,8},{6,10},{8,4},{10,6},{12,0},{14,2},{1,13},{3,15... | collective-permute-start | bytes 319496 | tf_op jit(solution)/shard_map/ppermute | solution.py:525
  21.3 7.3 %collective-permute-start.7 = (bf16[13,16,256]{2,1,0:T(8,128)(2,1)S(1)}, bf16[13,16,256]{2,1,0:T(8,128)(2,1)S(1)}, u32[]{:S(2)}, u32[]{:S(2)}) collective-permute-start(bf16[13,16,256]{2,1,0:T(8,128)(2,1)S(1)} %get-tuple-element.45), channel_id=1, source_target_pairs={{0,4},{2,6},{4,0},{6,2},{8,12},{10,14},{12,8},{14,10},{1,5},{3,7},... | collective-permute-start | bytes 319496 | tf_op jit(solution)/shard_map/ppermute | solution.py:525
  21.8 6.8 %collective-permute-start.8 = (bf16[13,16,256]{2,1,0:T(8,128)(2,1)S(1)}, bf16[13,16,256]{2,1,0:T(8,128)(2,1)S(1)}, u32[]{:S(2)}, u32[]{:S(2)}) collective-permute-start(bf16[13,16,256]{2,1,0:T(8,128)(2,1)S(1)} %get-tuple-element.46), channel_id=1, source_target_pairs={{0,2},{2,0},{4,6},{6,4},{8,10},{10,8},{12,14},{14,12},{1,3},{3,1},... | collective-permute-start | bytes 319496 | tf_op jit(solution)/shard_map/ppermute | solution.py:525
  23.0 3.9 %collective-permute-start.4 = (bf16[4,16,256]{2,1,0:T(8,128)(2,1)S(1)}, bf16[4,16,256]{2,1,0:T(8,128)(2,1)S(1)}, u32[]{:S(2)}, u32[]{:S(2)}) collective-permute-start(bf16[4,16,256]{2,1,0:T(8,128)(2,1)S(1)} %get-tuple-element.41), channel_id=1, source_target_pairs={{0,2},{2,0},{4,6},{6,4},{8,10},{10,8},{12,14},{14,12},{1,3},{3,1},... | collective-permute-start | bytes 98312 | tf_op jit(solution)/shard_map/ppermute | solution.py:525

commit v21 on v19

--- a/solution.py
+++ b/solution.py
@@ -128,12 +128,14 @@
     def without_row(value):
         return jnp.concatenate([jnp.where(tile_row, 0.0, value[:tile]), value[tile:]], 0)
 
-    def along_rows(i):
-        copies[6 if i == 0 else 9 + i // GROUP].wait()
-        group = jnp.concatenate([images_ref[i + n] for n in range(GROUP)], 1)
+    def along_rows(i, wide):
+        if i % GROUP == 0:
+            copies[6 if i == 0 else 9 + i // GROUP].wait()
+        group = jnp.concatenate([images_ref[i + n] for n in range(wide)], 1)
         product = dot(dft_ref[...], group).astype(bf16)
-        for n in range(GROUP):
-            half_ref[i // GROUP % 2, n * box : (n + 1) * box] = product[:, n * box : (n + 1) * box]
+        for n in range(wide):
+            place = (i + n) % GROUP * box
+            half_ref[i // GROUP % 2, place : place + box] = product[:, n * box : (n + 1) * box]
 
     def along_columns(i):
         return dot(half_ref[i // GROUP % 2], dft_t_ref[...])
@@ -153,6 +155,7 @@
         spec = spec_ref.at[i % SLOTS]
         spec[0:half, 0:half] = (near_y * (cc + ss_in)).astype(bf16)
         spec[0:half, half:] = (far_y * jnp.where(col_zero, cs, cc - ss_in)).astype(bf16)
+        yield
         spec[half:box, 0:half] = (near_y * (sc_in - cs_in)).astype(bf16)
         spec[half:box, half:] = (far_y * jnp.where(col_zero, ss_row, sc_in + cs_in)).astype(bf16)
         sc_top = jnp.broadcast_to(sc[0:1], (16, half))
@@ -191,7 +194,7 @@
             totals[slot] += plane_ref[z, pose] * piece
 
     copies[5].wait()
-    along_rows(0)
+    along_rows(0, GROUP)
     copies[7].wait()
     copies[8].wait()
     for p in range(0, poses, 2):
@@ -205,17 +208,20 @@
         rows_ref[...].reshape(poses * rows, box), near, ((1,), (1,))
     ).astype(bf16)
     for step in range(GROUP, count + 3 * GROUP, GROUP):
-        if step < count:
-            along_rows(step)
         if step - GROUP < count:
             product = along_columns(step - GROUP)
         for n in range(GROUP):
+            parts = iter(())
             if step - GROUP < count:
-                weigh(step - GROUP + n, product[n * box : (n + 1) * box])
+                parts = weigh(step - GROUP + n, product[n * box : (n + 1) * box])
+            next(parts, None)
             if 0 <= step - 2 * GROUP < count:
                 mix(step - 2 * GROUP + n)
+            next(parts, None)
             if step >= 3 * GROUP:
                 insert(step - 3 * GROUP + n)
+            if step < count and n % 2 == 0:
+                along_rows(step + n, 2)
 
     if len(outs) == 1:
         outs[0][...] = totals[...].astype(bf16)

time: 28.9 us -> 28.9 us (level)
  no operation moved by 1% of the time
where the time goes in v21:
time: 28.9 us; the launch traced here: 28.8 us
  starting transfers between devices  12.8 us (44%)
  Pallas kernels  9.63 us (33%)
  waiting for transfers between devices  6.33 us (22%)
    ppermute x9, starting transfers between devices, exchange(): return lax.ppermute(value, 'img', [(i, i ^ flip) for i in range(members)])  12.8 us
    ppermute x9, waiting for transfers between devices, exchange(): return lax.ppermute(value, 'img', [(i, i ^ flip) for i in range(members)])  6.33 us
    pallas_call x1, Pallas kernels, own_totals(): pl.pallas_call(slices_kernel, out_shape=out_shape, in_specs=[any_place] *...  5.62 us
    pallas_call x1, Pallas kernels, own_ridges(): pl.pallas_call(ridge_kernel, out_shape=[table, table, pltpu.VMEM((planes....  2.62 us
    pallas_call x1, Pallas kernels, finish(): pl.pallas_call(functools.partial(finish_kernel, planes), out_shape=jax.Sh...  0.94 us
  transfers between devices with their start and end apart: 9, of which 4 were waited for; matrix products, arithmetic and copies ran while one was open for 0% of the time, Pallas kernels for 10%

profile of v21, /device:TPU:0, one launch (start us, length us, event | category | flops | bytes accessed | tf_op | source)
XLA Modules:
  0.0 28.8 jit_solution(5987141903389648335)
XLA Ops:
  0.0 5.6 %shard_map.100 = (bf16[3,13,16,256]{3,2,1,0:T(8,128)(2,1)S(1)}, f32[3,13,16,256]{3,2,1,0:T(8,128)S(1)}, bf16[13,16,256]{2,1,0:T(8,128)(2,1)S(1)}, f32[13,16,256]...) custom-call(s32[16]{0:T(128)} %bitcast.5, ...), custom_call_target="tpu_custom_call" | custom-call | flops 2097152000 | bytes 6291456 | tf_op jit(solution)/shard_map/pallas_call | solution.py:280
  5.6 3.0 %collective-permute-start = (bf16[3,13,16,256]{3,2,1,0:T(8,128)(2,1)S(1)}, bf16[3,13,16,256]{3,2,1,0:T(8,128)(2,1)S(1)}, u32[]{:S(2)}, u32[]{:S(2)}) collective-permute-start(bf16[3,13,16,256]{3,2,1,0:T(8,128)(2,1)S(1)} %get-tuple-element.34), channel_id=1, source_target_pairs={{0,2},{2,0},{4,6},{6,4},{8,10},{10,8},{12,14},{14,12},{1,3},{3,1},... | collective-permute-start | bytes 958472 | tf_op jit(solution)/shard_map/ppermute | solution.py:531
  8.6 2.6 %collective-permute-start.1 = (bf16[7,16,256]{2,1,0:T(8,128)(2,1)S(1)}, bf16[7,16,256]{2,1,0:T(8,128)(2,1)S(1)}, u32[]{:S(2)}, u32[]{:S(2)}) collective-permute-start(bf16[7,16,256]{2,1,0:T(8,128)(2,1)S(1)} %get-tuple-element.37), channel_id=1, source_target_pairs={{0,8},{2,10},{4,12},{6,14},{8,0},{10,2},{12,4},{14,6},{1,9},{3,11}... | collective-permute-start | bytes 172040 | tf_op jit(solution)/shard_map/ppermute | solution.py:531
  11.2 1.3 %collective-permute-start.2 = (bf16[7,16,256]{2,1,0:T(8,128)(2,1)S(1)}, bf16[7,16,256]{2,1,0:T(8,128)(2,1)S(1)}, u32[]{:S(2)}, u32[]{:S(2)}) collective-permute-start(bf16[7,16,256]{2,1,0:T(8,128)(2,1)S(1)} %get-tuple-element.38), channel_id=1, source_target_pairs={{0,12},{2,14},{4,8},{6,10},{8,4},{10,6},{12,0},{14,2},{1,13},{3,15... | collective-permute-start | bytes 172040 | tf_op jit(solution)/shard_map/ppermute | solution.py:531
  12.6 0.2 collective-permute-start.3
  12.8 2.6 %shard_map.101 = (bf16[128,2048]{1,0:T(8,128)(2,1)S(1)}, bf16[128,2048]{1,0:T(8,128)(2,1)S(1)}, f32[16,128]{1,0:T(8,128)S(1)}) custom-call(f32[16]{0:T(128)} %defocus_hbm.3, f32[2,8]{1,0:T(2,128)} %bitcast.4, bf16[8,128,256]{2,1,0:T(8,128)(2,1)} %rows_hbm.3, bf16[8,256,128]{2,1,0:T(8,128)(2,1)} %cols_hbm.3), custom_call_target="tpu_custom_call" | custom-call | flops 1000 | bytes 1000 | tf_op jit(solution)/shard_map/pallas_call | solution.py:374
  15.4 0.0 collective-permute-done.1.refs_0_
  15.4 1.9 %collective-permute-done.2.refs_1_ = bf16[7,16,256]{2,1,0:T(8,128)(2,1)S(1)} collective-permute-done((bf16[7,16,256]{2,1,0:T(8,128)(2,1)S(1)}, bf16[7,16,256]{2,1,0:T(8,128)(2,1)S(1)}, u32[]{:S(2)}, u32[]{:S(2)}) %collective-permute-start.2) | collective-permute-done | bytes 57376 | tf_op jit(solution)/shard_map/ppermute | solution.py:531
  17.3 0.1 collective-permute-done.3.refs_2_
  17.4 0.0 collective-permute-done.x_came
  17.4 0.1 shard_map.102
  17.5 1.9 %collective-permute-start.5 = (bf16[13,16,256]{2,1,0:T(8,128)(2,1)S(1)}, bf16[13,16,256]{2,1,0:T(8,128)(2,1)S(1)}, u32[]{:S(2)}, u32[]{:S(2)}) collective-permute-start(bf16[13,16,256]{2,1,0:T(8,128)(2,1)S(1)} %get-tuple-element.43), channel_id=1, source_target_pairs={{0,8},{2,10},{4,12},{6,14},{8,0},{10,2},{12,4},{14,6},{1,9},{3,11}... | collective-permute-start | bytes 319496 | tf_op jit(solution)/shard_map/ppermute | solution.py:531
  19.3 1.2 %collective-permute-start.6 = (bf16[13,16,256]{2,1,0:T(8,128)(2,1)S(1)}, bf16[13,16,256]{2,1,0:T(8,128)(2,1)S(1)}, u32[]{:S(2)}, u32[]{:S(2)}) collective-permute-start(bf16[13,16,256]{2,1,0:T(8,128)(2,1)S(1)} %get-tuple-element.44), channel_id=1, source_target_pairs={{0,12},{2,14},{4,8},{6,10},{8,4},{10,6},{12,0},{14,2},{1,13},{3,15... | collective-permute-start | bytes 319496 | tf_op jit(solution)/shard_map/ppermute | solution.py:531
  20.5 0.5 %collective-permute-start.7 = (bf16[13,16,256]{2,1,0:T(8,128)(2,1)S(1)}, bf16[13,16,256]{2,1,0:T(8,128)(2,1)S(1)}, u32[]{:S(2)}, u32[]{:S(2)}) collective-permute-start(bf16[13,16,256]{2,1,0:T(8,128)(2,1)S(1)} %get-tuple-element.45), channel_id=1, source_target_pairs={{0,4},{2,6},{4,0},{6,2},{8,12},{10,14},{12,8},{14,10},{1,5},{3,7},... | collective-permute-start | bytes 319496 | tf_op jit(solution)/shard_map/ppermute | solution.py:531
  21.0 1.2 %collective-permute-start.8 = (bf16[13,16,256]{2,1,0:T(8,128)(2,1)S(1)}, bf16[13,16,256]{2,1,0:T(8,128)(2,1)S(1)}, u32[]{:S(2)}, u32[]{:S(2)}) collective-permute-start(bf16[13,16,256]{2,1,0:T(8,128)(2,1)S(1)} %get-tuple-element.46), channel_id=1, source_target_pairs={{0,2},{2,0},{4,6},{6,4},{8,10},{10,8},{12,14},{14,12},{1,3},{3,1},... | collective-permute-start | bytes 319496 | tf_op jit(solution)/shard_map/ppermute | solution.py:531
  22.2 0.8 %collective-permute-start.4 = (bf16[4,16,256]{2,1,0:T(8,128)(2,1)S(1)}, bf16[4,16,256]{2,1,0:T(8,128)(2,1)S(1)}, u32[]{:S(2)}, u32[]{:S(2)}) collective-permute-start(bf16[4,16,256]{2,1,0:T(8,128)(2,1)S(1)} %get-tuple-element.41), channel_id=1, source_target_pairs={{0,2},{2,0},{4,6},{6,4},{8,10},{10,8},{12,14},{14,12},{1,3},{3,1},... | collective-permute-start | bytes 98312 | tf_op jit(solution)/shard_map/ppermute | solution.py:531
  23.0 3.1 %collective-permute-done.4.z_came = bf16[4,16,256]{2,1,0:T(8,128)(2,1)S(1)} collective-permute-done((bf16[4,16,256]{2,1,0:T(8,128)(2,1)S(1)}, bf16[4,16,256]{2,1,0:T(8,128)(2,1)S(1)}, u32[]{:S(2)}, u32[]{:S(2)}) %collective-permute-start.4) | collective-permute-done | bytes 32800 | tf_op jit(solution)/shard_map/ppermute | solution.py:531
  26.1 0.4 %shard_map.103.ridge_ref = f32[16,16,128]{2,1,0:T(8,128)S(1)} custom-call(bf16[128,2048]{1,0:T(8,128)(2,1)S(1)} %get-tuple-element.30.high_ref, bf16[128,2048]{1,0:T(8,128)(2,1)S(1)} %get-tuple-element.31.low_ref, f32[16,128]{1,0:T(8,128)S(1)} %get-tuple-element.32.share_ref, f32[4,16,256]{2,1,0:T(8,128)S(1)} %get-tuple-element.40.z_own, ...), custom_call_target="tpu_custom_call" | custom-call | flops 1000 | bytes 1000 | tf_op jit(solution)/shard_map/pallas_call | solution.py:452
  26.5 1.2 %collective-permute-done.5.refs_0_ = bf16[13,16,256]{2,1,0:T(8,128)(2,1)S(1)} collective-permute-done((bf16[13,16,256]{2,1,0:T(8,128)(2,1)S(1)}, bf16[13,16,256]{2,1,0:T(8,128)(2,1)S(1)}, u32[]{:S(2)}, u32[]{:S(2)}) %collective-permute-start.5) | collective-permute-done | bytes 106528 | tf_op jit(solution)/shard_map/ppermute | solution.py:531
  27.8 0.0 collective-permute-done.6.refs_1_
  27.8 0.0 collective-permute-done.7.refs_2_
  27.8 0.0 collective-permute-done.8.refs_3_
  27.8 0.9 %shard_map.104 = f32[16,32,128]{2,1,0:T(8,128)} custom-call(f32[16,16,128]{2,1,0:T(8,128)S(1)} %shard_map.103.ridge_ref, f32[13,16,256]{2,1,0:T(8,128)S(1)} %get-tuple-element.42.x_own, f32[4,16,256]{2,1,0:T(8,128)S(1)} %get-tuple-element.40.z_own, bf16[4,16,256]{2,1,0:T(8,128)(2,1)S(1)} %collective-permute-done.4.z_came, ...), custom_call_target="tpu_custom_call" | custom-call | flops 1000 | bytes 1000 | tf_op jit(solution)/shard_map/pallas_call | solution.py:483
Async XLA Ops:
  5.6 11.7 %collective-permute-start = (bf16[3,13,16,256]{3,2,1,0:T(8,128)(2,1)S(1)}, bf16[3,13,16,256]{3,2,1,0:T(8,128)(2,1)S(1)}, u32[]{:S(2)}, u32[]{:S(2)}) collective-permute-start(bf16[3,13,16,256]{3,2,1,0:T(8,128)(2,1)S(1)} %get-tuple-element.34), channel_id=1, source_target_pairs={{0,2},{2,0},{4,6},{6,4},{8,10},{10,8},{12,14},{14,12},{1,3},{3,1},... | collective-permute-start | bytes 958472 | tf_op jit(solution)/shard_map/ppermute | solution.py:531
  8.6 6.8 %collective-permute-start.1 = (bf16[7,16,256]{2,1,0:T(8,128)(2,1)S(1)}, bf16[7,16,256]{2,1,0:T(8,128)(2,1)S(1)}, u32[]{:S(2)}, u32[]{:S(2)}) collective-permute-start(bf16[7,16,256]{2,1,0:T(8,128)(2,1)S(1)} %get-tuple-element.37), channel_id=1, source_target_pairs={{0,8},{2,10},{4,12},{6,14},{8,0},{10,2},{12,4},{14,6},{1,9},{3,11}... | collective-permute-start | bytes 172040 | tf_op jit(solution)/shard_map/ppermute | solution.py:531
  11.2 6.1 %collective-permute-start.2 = (bf16[7,16,256]{2,1,0:T(8,128)(2,1)S(1)}, bf16[7,16,256]{2,1,0:T(8,128)(2,1)S(1)}, u32[]{:S(2)}, u32[]{:S(2)}) collective-permute-start(bf16[7,16,256]{2,1,0:T(8,128)(2,1)S(1)} %get-tuple-element.38), channel_id=1, source_target_pairs={{0,12},{2,14},{4,8},{6,10},{8,4},{10,6},{12,0},{14,2},{1,13},{3,15... | collective-permute-start | bytes 172040 | tf_op jit(solution)/shard_map/ppermute | solution.py:531
  12.6 4.8 %collective-permute-start.3 = (bf16[7,16,256]{2,1,0:T(8,128)(2,1)S(1)}, bf16[7,16,256]{2,1,0:T(8,128)(2,1)S(1)}, u32[]{:S(2)}, u32[]{:S(2)}) collective-permute-start(bf16[7,16,256]{2,1,0:T(8,128)(2,1)S(1)} %get-tuple-element.39), channel_id=1, source_target_pairs={{0,4},{2,6},{4,0},{6,2},{8,12},{10,14},{12,8},{14,10},{1,5},{3,7},... | collective-permute-start | bytes 172040 | tf_op jit(solution)/shard_map/ppermute | solution.py:531
  17.5 10.3 %collective-permute-start.5 = (bf16[13,16,256]{2,1,0:T(8,128)(2,1)S(1)}, bf16[13,16,256]{2,1,0:T(8,128)(2,1)S(1)}, u32[]{:S(2)}, u32[]{:S(2)}) collective-permute-start(bf16[13,16,256]{2,1,0:T(8,128)(2,1)S(1)} %get-tuple-element.43), channel_id=1, source_target_pairs={{0,8},{2,10},{4,12},{6,14},{8,0},{10,2},{12,4},{14,6},{1,9},{3,11}... | collective-permute-start | bytes 319496 | tf_op jit(solution)/shard_map/ppermute | solution.py:531
  19.3 8.4 %collective-permute-start.6 = (bf16[13,16,256]{2,1,0:T(8,128)(2,1)S(1)}, bf16[13,16,256]{2,1,0:T(8,128)(2,1)S(1)}, u32[]{:S(2)}, u32[]{:S(2)}) collective-permute-start(bf16[13,16,256]{2,1,0:T(8,128)(2,1)S(1)} %get-tuple-element.44), channel_id=1, source_target_pairs={{0,12},{2,14},{4,8},{6,10},{8,4},{10,6},{12,0},{14,2},{1,13},{3,15... | collective-permute-start | bytes 319496 | tf_op jit(solution)/shard_map/ppermute | solution.py:531
  20.5 7.3 %collective-permute-start.7 = (bf16[13,16,256]{2,1,0:T(8,128)(2,1)S(1)}, bf16[13,16,256]{2,1,0:T(8,128)(2,1)S(1)}, u32[]{:S(2)}, u32[]{:S(2)}) collective-permute-start(bf16[13,16,256]{2,1,0:T(8,128)(2,1)S(1)} %get-tuple-element.45), channel_id=1, source_target_pairs={{0,4},{2,6},{4,0},{6,2},{8,12},{10,14},{12,8},{14,10},{1,5},{3,7},... | collective-permute-start | bytes 319496 | tf_op jit(solution)/shard_map/ppermute | solution.py:531
  21.0 6.8 %collective-permute-start.8 = (bf16[13,16,256]{2,1,0:T(8,128)(2,1)S(1)}, bf16[13,16,256]{2,1,0:T(8,128)(2,1)S(1)}, u32[]{:S(2)}, u32[]{:S(2)}) collective-permute-start(bf16[13,16,256]{2,1,0:T(8,128)(2,1)S(1)} %get-tuple-element.46), channel_id=1, source_target_pairs={{0,2},{2,0},{4,6},{6,4},{8,10},{10,8},{12,14},{14,12},{1,3},{3,1},... | collective-permute-start | bytes 319496 | tf_op jit(solution)/shard_map/ppermute | solution.py:531
  22.2 3.9 %collective-permute-start.4 = (bf16[4,16,256]{2,1,0:T(8,128)(2,1)S(1)}, bf16[4,16,256]{2,1,0:T(8,128)(2,1)S(1)}, u32[]{:S(2)}, u32[]{:S(2)}) collective-permute-start(bf16[4,16,256]{2,1,0:T(8,128)(2,1)S(1)} %get-tuple-element.41), channel_id=1, source_target_pairs={{0,2},{2,0},{4,6},{6,4},{8,10},{10,8},{12,14},{14,12},{1,3},{3,1},... | collective-permute-start | bytes 98312 | tf_op jit(solution)/shard_map/ppermute | solution.py:531

commit v22 on v21

--- a/solution.py
+++ b/solution.py
@@ -246,8 +246,8 @@
 
 SCRATCH = 20
 LINE = (2, 3, 1)
-SLOTS = 8
-GROUP = 4
+SLOTS = 16
+GROUP = 8
 Z_SLOTS = 4
 
 

time: 28.9 us -> 28.6 us (0.990)
  Pallas kernels: 9.63 us -> 9.33 us
    pallas_call x1, Pallas kernels: 5.62 us -> 5.32 us  [own_totals(): pl.pallas_call(slices_kernel, out_shape=out_shape, in_specs=[any_place] *...]
where the time goes in v22:
time: 28.6 us; the launch traced here: 28.5 us
  starting transfers between devices  12.7 us (44%)
  Pallas kernels  9.33 us (33%)
  waiting for transfers between devices  6.33 us (22%)
    ppermute x9, starting transfers between devices, exchange(): return lax.ppermute(value, 'img', [(i, i ^ flip) for i in range(members)])  12.7 us
    ppermute x9, waiting for transfers between devices, exchange(): return lax.ppermute(value, 'img', [(i, i ^ flip) for i in range(members)])  6.33 us
    pallas_call x1, Pallas kernels, own_totals(): pl.pallas_call(slices_kernel, out_shape=out_shape, in_specs=[any_place] *...  5.32 us
    pallas_call x1, Pallas kernels, own_ridges(): pl.pallas_call(ridge_kernel, out_shape=[table, table, pltpu.VMEM((planes....  2.62 us
    pallas_call x1, Pallas kernels, finish(): pl.pallas_call(functools.partial(finish_kernel, planes), out_shape=jax.Sh...  0.94 us
  transfers between devices with their start and end apart: 9, of which 4 were waited for; matrix products, arithmetic and copies ran while one was open for 0% of the time, Pallas kernels for 10%

profile of v22, /device:TPU:0, one launch (start us, length us, event | category | flops | bytes accessed | tf_op | source)
XLA Modules:
  0.0 28.5 jit_solution(1173157082780599664)
XLA Ops:
  0.0 5.3 %shard_map.100 = (bf16[3,13,16,256]{3,2,1,0:T(8,128)(2,1)S(1)}, f32[3,13,16,256]{3,2,1,0:T(8,128)S(1)}, bf16[13,16,256]{2,1,0:T(8,128)(2,1)S(1)}, f32[13,16,256]...) custom-call(s32[16]{0:T(128)} %bitcast.5, ...), custom_call_target="tpu_custom_call" | custom-call | flops 2097152000 | bytes 6291456 | tf_op jit(solution)/shard_map/pallas_call | solution.py:280
  5.3 3.0 %collective-permute-start = (bf16[3,13,16,256]{3,2,1,0:T(8,128)(2,1)S(1)}, bf16[3,13,16,256]{3,2,1,0:T(8,128)(2,1)S(1)}, u32[]{:S(2)}, u32[]{:S(2)}) collective-permute-start(bf16[3,13,16,256]{3,2,1,0:T(8,128)(2,1)S(1)} %get-tuple-element.34), channel_id=1, source_target_pairs={{0,2},{2,0},{4,6},{6,4},{8,10},{10,8},{12,14},{14,12},{1,3},{3,1},... | collective-permute-start | bytes 958472 | tf_op jit(solution)/shard_map/ppermute | solution.py:531
  8.3 2.6 %collective-permute-start.1 = (bf16[7,16,256]{2,1,0:T(8,128)(2,1)S(1)}, bf16[7,16,256]{2,1,0:T(8,128)(2,1)S(1)}, u32[]{:S(2)}, u32[]{:S(2)}) collective-permute-start(bf16[7,16,256]{2,1,0:T(8,128)(2,1)S(1)} %get-tuple-element.37), channel_id=1, source_target_pairs={{0,8},{2,10},{4,12},{6,14},{8,0},{10,2},{12,4},{14,6},{1,9},{3,11}... | collective-permute-start | bytes 172040 | tf_op jit(solution)/shard_map/ppermute | solution.py:531
  10.9 1.4 %collective-permute-start.2 = (bf16[7,16,256]{2,1,0:T(8,128)(2,1)S(1)}, bf16[7,16,256]{2,1,0:T(8,128)(2,1)S(1)}, u32[]{:S(2)}, u32[]{:S(2)}) collective-permute-start(bf16[7,16,256]{2,1,0:T(8,128)(2,1)S(1)} %get-tuple-element.38), channel_id=1, source_target_pairs={{0,12},{2,14},{4,8},{6,10},{8,4},{10,6},{12,0},{14,2},{1,13},{3,15... | collective-permute-start | bytes 172040 | tf_op jit(solution)/shard_map/ppermute | solution.py:531
  12.3 0.2 collective-permute-start.3
  12.5 2.6 %shard_map.101 = (bf16[128,2048]{1,0:T(8,128)(2,1)S(1)}, bf16[128,2048]{1,0:T(8,128)(2,1)S(1)}, f32[16,128]{1,0:T(8,128)S(1)}) custom-call(f32[16]{0:T(128)} %defocus_hbm.3, f32[2,8]{1,0:T(2,128)} %bitcast.4, bf16[8,128,256]{2,1,0:T(8,128)(2,1)} %rows_hbm.3, bf16[8,256,128]{2,1,0:T(8,128)(2,1)} %cols_hbm.3), custom_call_target="tpu_custom_call" | custom-call | flops 1000 | bytes 1000 | tf_op jit(solution)/shard_map/pallas_call | solution.py:374
  15.1 0.0 collective-permute-done.1.refs_0_
  15.1 1.9 %collective-permute-done.2.refs_1_ = bf16[7,16,256]{2,1,0:T(8,128)(2,1)S(1)} collective-permute-done((bf16[7,16,256]{2,1,0:T(8,128)(2,1)S(1)}, bf16[7,16,256]{2,1,0:T(8,128)(2,1)S(1)}, u32[]{:S(2)}, u32[]{:S(2)}) %collective-permute-start.2) | collective-permute-done | bytes 57376 | tf_op jit(solution)/shard_map/ppermute | solution.py:531
  17.0 0.1 collective-permute-done.3.refs_2_
  17.1 0.0 collective-permute-done.x_came
  17.1 0.1 shard_map.102
  17.2 1.9 %collective-permute-start.5 = (bf16[13,16,256]{2,1,0:T(8,128)(2,1)S(1)}, bf16[13,16,256]{2,1,0:T(8,128)(2,1)S(1)}, u32[]{:S(2)}, u32[]{:S(2)}) collective-permute-start(bf16[13,16,256]{2,1,0:T(8,128)(2,1)S(1)} %get-tuple-element.43), channel_id=1, source_target_pairs={{0,8},{2,10},{4,12},{6,14},{8,0},{10,2},{12,4},{14,6},{1,9},{3,11}... | collective-permute-start | bytes 319496 | tf_op jit(solution)/shard_map/ppermute | solution.py:531
  19.1 1.2 %collective-permute-start.6 = (bf16[13,16,256]{2,1,0:T(8,128)(2,1)S(1)}, bf16[13,16,256]{2,1,0:T(8,128)(2,1)S(1)}, u32[]{:S(2)}, u32[]{:S(2)}) collective-permute-start(bf16[13,16,256]{2,1,0:T(8,128)(2,1)S(1)} %get-tuple-element.44), channel_id=1, source_target_pairs={{0,12},{2,14},{4,8},{6,10},{8,4},{10,6},{12,0},{14,2},{1,13},{3,15... | collective-permute-start | bytes 319496 | tf_op jit(solution)/shard_map/ppermute | solution.py:531
  20.2 0.5 %collective-permute-start.7 = (bf16[13,16,256]{2,1,0:T(8,128)(2,1)S(1)}, bf16[13,16,256]{2,1,0:T(8,128)(2,1)S(1)}, u32[]{:S(2)}, u32[]{:S(2)}) collective-permute-start(bf16[13,16,256]{2,1,0:T(8,128)(2,1)S(1)} %get-tuple-element.45), channel_id=1, source_target_pairs={{0,4},{2,6},{4,0},{6,2},{8,12},{10,14},{12,8},{14,10},{1,5},{3,7},... | collective-permute-start | bytes 319496 | tf_op jit(solution)/shard_map/ppermute | solution.py:531
  20.7 1.2 %collective-permute-start.8 = (bf16[13,16,256]{2,1,0:T(8,128)(2,1)S(1)}, bf16[13,16,256]{2,1,0:T(8,128)(2,1)S(1)}, u32[]{:S(2)}, u32[]{:S(2)}) collective-permute-start(bf16[13,16,256]{2,1,0:T(8,128)(2,1)S(1)} %get-tuple-element.46), channel_id=1, source_target_pairs={{0,2},{2,0},{4,6},{6,4},{8,10},{10,8},{12,14},{14,12},{1,3},{3,1},... | collective-permute-start | bytes 319496 | tf_op jit(solution)/shard_map/ppermute | solution.py:531
  21.9 0.8 %collective-permute-start.4 = (bf16[4,16,256]{2,1,0:T(8,128)(2,1)S(1)}, bf16[4,16,256]{2,1,0:T(8,128)(2,1)S(1)}, u32[]{:S(2)}, u32[]{:S(2)}) collective-permute-start(bf16[4,16,256]{2,1,0:T(8,128)(2,1)S(1)} %get-tuple-element.41), channel_id=1, source_target_pairs={{0,2},{2,0},{4,6},{6,4},{8,10},{10,8},{12,14},{14,12},{1,3},{3,1},... | collective-permute-start | bytes 98312 | tf_op jit(solution)/shard_map/ppermute | solution.py:531
  22.7 3.1 %collective-permute-done.4.z_came = bf16[4,16,256]{2,1,0:T(8,128)(2,1)S(1)} collective-permute-done((bf16[4,16,256]{2,1,0:T(8,128)(2,1)S(1)}, bf16[4,16,256]{2,1,0:T(8,128)(2,1)S(1)}, u32[]{:S(2)}, u32[]{:S(2)}) %collective-permute-start.4) | collective-permute-done | bytes 32800 | tf_op jit(solution)/shard_map/ppermute | solution.py:531
  25.8 0.4 %shard_map.103.ridge_ref = f32[16,16,128]{2,1,0:T(8,128)S(1)} custom-call(bf16[128,2048]{1,0:T(8,128)(2,1)S(1)} %get-tuple-element.30.high_ref, bf16[128,2048]{1,0:T(8,128)(2,1)S(1)} %get-tuple-element.31.low_ref, f32[16,128]{1,0:T(8,128)S(1)} %get-tuple-element.32.share_ref, f32[4,16,256]{2,1,0:T(8,128)S(1)} %get-tuple-element.40.z_own, ...), custom_call_target="tpu_custom_call" | custom-call | flops 1000 | bytes 1000 | tf_op jit(solution)/shard_map/pallas_call | solution.py:452
  26.2 1.2 %collective-permute-done.5.refs_0_ = bf16[13,16,256]{2,1,0:T(8,128)(2,1)S(1)} collective-permute-done((bf16[13,16,256]{2,1,0:T(8,128)(2,1)S(1)}, bf16[13,16,256]{2,1,0:T(8,128)(2,1)S(1)}, u32[]{:S(2)}, u32[]{:S(2)}) %collective-permute-start.5) | collective-permute-done | bytes 106528 | tf_op jit(solution)/shard_map/ppermute | solution.py:531
  27.5 0.0 collective-permute-done.6.refs_1_
  27.5 0.0 collective-permute-done.7.refs_2_
  27.5 0.0 collective-permute-done.8.refs_3_
  27.5 0.9 %shard_map.104 = f32[16,32,128]{2,1,0:T(8,128)} custom-call(f32[16,16,128]{2,1,0:T(8,128)S(1)} %shard_map.103.ridge_ref, f32[13,16,256]{2,1,0:T(8,128)S(1)} %get-tuple-element.42.x_own, f32[4,16,256]{2,1,0:T(8,128)S(1)} %get-tuple-element.40.z_own, bf16[4,16,256]{2,1,0:T(8,128)(2,1)S(1)} %collective-permute-done.4.z_came, ...), custom_call_target="tpu_custom_call" | custom-call | flops 1000 | bytes 1000 | tf_op jit(solution)/shard_map/pallas_call | solution.py:483
Async XLA Ops:
  5.3 11.7 %collective-permute-start = (bf16[3,13,16,256]{3,2,1,0:T(8,128)(2,1)S(1)}, bf16[3,13,16,256]{3,2,1,0:T(8,128)(2,1)S(1)}, u32[]{:S(2)}, u32[]{:S(2)}) collective-permute-start(bf16[3,13,16,256]{3,2,1,0:T(8,128)(2,1)S(1)} %get-tuple-element.34), channel_id=1, source_target_pairs={{0,2},{2,0},{4,6},{6,4},{8,10},{10,8},{12,14},{14,12},{1,3},{3,1},... | collective-permute-start | bytes 958472 | tf_op jit(solution)/shard_map/ppermute | solution.py:531
  8.3 6.8 %collective-permute-start.1 = (bf16[7,16,256]{2,1,0:T(8,128)(2,1)S(1)}, bf16[7,16,256]{2,1,0:T(8,128)(2,1)S(1)}, u32[]{:S(2)}, u32[]{:S(2)}) collective-permute-start(bf16[7,16,256]{2,1,0:T(8,128)(2,1)S(1)} %get-tuple-element.37), channel_id=1, source_target_pairs={{0,8},{2,10},{4,12},{6,14},{8,0},{10,2},{12,4},{14,6},{1,9},{3,11}... | collective-permute-start | bytes 172040 | tf_op jit(solution)/shard_map/ppermute | solution.py:531
  10.9 6.1 %collective-permute-start.2 = (bf16[7,16,256]{2,1,0:T(8,128)(2,1)S(1)}, bf16[7,16,256]{2,1,0:T(8,128)(2,1)S(1)}, u32[]{:S(2)}, u32[]{:S(2)}) collective-permute-start(bf16[7,16,256]{2,1,0:T(8,128)(2,1)S(1)} %get-tuple-element.38), channel_id=1, source_target_pairs={{0,12},{2,14},{4,8},{6,10},{8,4},{10,6},{12,0},{14,2},{1,13},{3,15... | collective-permute-start | bytes 172040 | tf_op jit(solution)/shard_map/ppermute | solution.py:531
  12.3 4.8 %collective-permute-start.3 = (bf16[7,16,256]{2,1,0:T(8,128)(2,1)S(1)}, bf16[7,16,256]{2,1,0:T(8,128)(2,1)S(1)}, u32[]{:S(2)}, u32[]{:S(2)}) collective-permute-start(bf16[7,16,256]{2,1,0:T(8,128)(2,1)S(1)} %get-tuple-element.39), channel_id=1, source_target_pairs={{0,4},{2,6},{4,0},{6,2},{8,12},{10,14},{12,8},{14,10},{1,5},{3,7},... | collective-permute-start | bytes 172040 | tf_op jit(solution)/shard_map/ppermute | solution.py:531
  17.2 10.3 %collective-permute-start.5 = (bf16[13,16,256]{2,1,0:T(8,128)(2,1)S(1)}, bf16[13,16,256]{2,1,0:T(8,128)(2,1)S(1)}, u32[]{:S(2)}, u32[]{:S(2)}) collective-permute-start(bf16[13,16,256]{2,1,0:T(8,128)(2,1)S(1)} %get-tuple-element.43), channel_id=1, source_target_pairs={{0,8},{2,10},{4,12},{6,14},{8,0},{10,2},{12,4},{14,6},{1,9},{3,11}... | collective-permute-start | bytes 319496 | tf_op jit(solution)/shard_map/ppermute | solution.py:531
  19.1 8.4 %collective-permute-start.6 = (bf16[13,16,256]{2,1,0:T(8,128)(2,1)S(1)}, bf16[13,16,256]{2,1,0:T(8,128)(2,1)S(1)}, u32[]{:S(2)}, u32[]{:S(2)}) collective-permute-start(bf16[13,16,256]{2,1,0:T(8,128)(2,1)S(1)} %get-tuple-element.44), channel_id=1, source_target_pairs={{0,12},{2,14},{4,8},{6,10},{8,4},{10,6},{12,0},{14,2},{1,13},{3,15... | collective-permute-start | bytes 319496 | tf_op jit(solution)/shard_map/ppermute | solution.py:531
  20.2 7.3 %collective-permute-start.7 = (bf16[13,16,256]{2,1,0:T(8,128)(2,1)S(1)}, bf16[13,16,256]{2,1,0:T(8,128)(2,1)S(1)}, u32[]{:S(2)}, u32[]{:S(2)}) collective-permute-start(bf16[13,16,256]{2,1,0:T(8,128)(2,1)S(1)} %get-tuple-element.45), channel_id=1, source_target_pairs={{0,4},{2,6},{4,0},{6,2},{8,12},{10,14},{12,8},{14,10},{1,5},{3,7},... | collective-permute-start | bytes 319496 | tf_op jit(solution)/shard_map/ppermute | solution.py:531
  20.7 6.8 %collective-permute-start.8 = (bf16[13,16,256]{2,1,0:T(8,128)(2,1)S(1)}, bf16[13,16,256]{2,1,0:T(8,128)(2,1)S(1)}, u32[]{:S(2)}, u32[]{:S(2)}) collective-permute-start(bf16[13,16,256]{2,1,0:T(8,128)(2,1)S(1)} %get-tuple-element.46), channel_id=1, source_target_pairs={{0,2},{2,0},{4,6},{6,4},{8,10},{10,8},{12,14},{14,12},{1,3},{3,1},... | collective-permute-start | bytes 319496 | tf_op jit(solution)/shard_map/ppermute | solution.py:531
  21.9 3.9 %collective-permute-start.4 = (bf16[4,16,256]{2,1,0:T(8,128)(2,1)S(1)}, bf16[4,16,256]{2,1,0:T(8,128)(2,1)S(1)}, u32[]{:S(2)}, u32[]{:S(2)}) collective-permute-start(bf16[4,16,256]{2,1,0:T(8,128)(2,1)S(1)} %get-tuple-element.41), channel_id=1, source_target_pairs={{0,2},{2,0},{4,6},{6,4},{8,10},{10,8},{12,14},{14,12},{1,3},{3,1},... | collective-permute-start | bytes 98312 | tf_op jit(solution)/shard_map/ppermute | solution.py:531

commit v23 on v22

--- a/solution.py
+++ b/solution.py
@@ -67,11 +67,11 @@
     pairs = (
         (class_hbm, class_ref), (pose_hbm, pose_ref), (bin_hbm, bin_ref),
         (defocus_hbm, defocus_ref), (plane_hbm, plane_ref),
-        (dft_hbm, dft_ref), (images_hbm.at[0:GROUP], images_ref.at[0:GROUP]),
+        (dft_hbm, dft_ref), (images_hbm.at[0:LOAD], images_ref.at[0:LOAD]),
         (dft_t_hbm, dft_t_ref), (cols_hbm, cols_ref), (rows_hbm, rows_ref),
     ) + tuple(
-        (images_hbm.at[i : i + GROUP], images_ref.at[i : i + GROUP])
-        for i in range(GROUP, count, GROUP)
+        (images_hbm.at[i : i + LOAD], images_ref.at[i : i + LOAD])
+        for i in range(LOAD, count, LOAD)
     )
     copies = [
         pltpu.make_async_copy(source, target, arrived.at[n])
@@ -129,8 +129,8 @@
         return jnp.concatenate([jnp.where(tile_row, 0.0, value[:tile]), value[tile:]], 0)
 
     def along_rows(i, wide):
-        if i % GROUP == 0:
-            copies[6 if i == 0 else 9 + i // GROUP].wait()
+        if i % LOAD == 0:
+            copies[6 if i == 0 else 9 + i // LOAD].wait()
         group = jnp.concatenate([images_ref[i + n] for n in range(wide)], 1)
         product = dot(dft_ref[...], group).astype(bf16)
         for n in range(wide):
@@ -194,7 +194,7 @@
             totals[slot] += plane_ref[z, pose] * piece
 
     copies[5].wait()
-    along_rows(0, GROUP)
+    along_rows(0, LOAD)
     copies[7].wait()
     copies[8].wait()
     for p in range(0, poses, 2):
@@ -203,25 +203,27 @@
         far_two = dot(far, two).astype(bf16)
         cols_fold[p] = jnp.concatenate([near_two[:, :cols], far_two[:, :cols]], 1)
         cols_fold[p + 1] = jnp.concatenate([near_two[:, cols:], far_two[:, cols:]], 1)
+    for i in range(LOAD, GROUP, LOAD):
+        along_rows(i, LOAD)
     copies[9].wait()
     rows_fold[...] = dot(
         rows_ref[...].reshape(poses * rows, box), near, ((1,), (1,))
     ).astype(bf16)
-    for step in range(GROUP, count + 3 * GROUP, GROUP):
-        if step - GROUP < count:
-            product = along_columns(step - GROUP)
-        for n in range(GROUP):
-            parts = iter(())
-            if step - GROUP < count:
-                parts = weigh(step - GROUP + n, product[n * box : (n + 1) * box])
-            next(parts, None)
-            if 0 <= step - 2 * GROUP < count:
-                mix(step - 2 * GROUP + n)
-            next(parts, None)
-            if step >= 3 * GROUP:
-                insert(step - 3 * GROUP + n)
-            if step < count and n % 2 == 0:
-                along_rows(step + n, 2)
+    for i in range(count + 2 * LAG):
+        parts = iter(())
+        if i < count:
+            if i % GROUP == 0:
+                product = along_columns(i)
+            n = i % GROUP
+            parts = weigh(i, product[n * box : (n + 1) * box])
+        next(parts, None)
+        if 0 <= i - LAG < count:
+            mix(i - LAG)
+        next(parts, None)
+        if i >= 2 * LAG:
+            insert(i - 2 * LAG)
+        if i + GROUP < count and i % 2 == 0:
+            along_rows(i + GROUP, 2)
 
     if len(outs) == 1:
         outs[0][...] = totals[...].astype(bf16)
@@ -248,6 +250,8 @@
 LINE = (2, 3, 1)
 SLOTS = 16
 GROUP = 8
+LOAD = 4
+LAG = 6
 Z_SLOTS = 4
 
 
@@ -285,7 +289,7 @@
         scratch_shapes=[pltpu.SMEM(x.shape, x.dtype) for x in operands[:5]]
         + [pltpu.VMEM(x.shape, x.dtype) for x in operands[5:]]
         + [
-            pltpu.SemaphoreType.DMA((9 + count // GROUP,)),
+            pltpu.SemaphoreType.DMA((9 + count // LOAD,)),
             pltpu.VMEM((poses * rows, box), bf16),
             pltpu.VMEM((poses, box, 2 * cols), bf16),
             pltpu.VMEM((box // 2 + 8, lanes), f32),

time: 28.6 us -> 28.9 us (1.010)
  Pallas kernels: 9.33 us -> 9.67 us
    pallas_call x1, Pallas kernels: 5.32 us -> 5.65 us  [own_totals(): pl.pallas_call(slices_kernel, out_shape=out_shape, in_specs=[any_place] *...]
where the time goes in v23:
time: 28.9 us; the launch traced here: 28.8 us
  starting transfers between devices  12.7 us (44%)
  Pallas kernels  9.67 us (33%)
  waiting for transfers between devices  6.33 us (22%)
    ppermute x9, starting transfers between devices, exchange(): return lax.ppermute(value, 'img', [(i, i ^ flip) for i in range(members)])  12.7 us
    ppermute x9, waiting for transfers between devices, exchange(): return lax.ppermute(value, 'img', [(i, i ^ flip) for i in range(members)])  6.33 us
    pallas_call x1, Pallas kernels, own_totals(): pl.pallas_call(slices_kernel, out_shape=out_shape, in_specs=[any_place] *...  5.65 us
    pallas_call x1, Pallas kernels, own_ridges(): pl.pallas_call(ridge_kernel, out_shape=[table, table, pltpu.VMEM((planes....  2.62 us
    pallas_call x1, Pallas kernels, finish(): pl.pallas_call(functools.partial(finish_kernel, planes), out_shape=jax.Sh...  0.94 us
  transfers between devices with their start and end apart: 9, of which 4 were waited for; matrix products, arithmetic and copies ran while one was open for 0% of the time, Pallas kernels for 10%

profile of v23, /device:TPU:0, one launch (start us, length us, event | category | flops | bytes accessed | tf_op | source)
XLA Modules:
  0.0 28.8 jit_solution(8824525809254698657)
XLA Ops:
  0.0 5.7 %shard_map.100 = (bf16[3,13,16,256]{3,2,1,0:T(8,128)(2,1)S(1)}, f32[3,13,16,256]{3,2,1,0:T(8,128)S(1)}, bf16[13,16,256]{2,1,0:T(8,128)(2,1)S(1)}, f32[13,16,256]...) custom-call(s32[16]{0:T(128)} %bitcast.5, ...), custom_call_target="tpu_custom_call" | custom-call | flops 2097152000 | bytes 6291456 | tf_op jit(solution)/shard_map/pallas_call | solution.py:284
  5.7 3.0 %collective-permute-start = (bf16[3,13,16,256]{3,2,1,0:T(8,128)(2,1)S(1)}, bf16[3,13,16,256]{3,2,1,0:T(8,128)(2,1)S(1)}, u32[]{:S(2)}, u32[]{:S(2)}) collective-permute-start(bf16[3,13,16,256]{3,2,1,0:T(8,128)(2,1)S(1)} %get-tuple-element.34), channel_id=1, source_target_pairs={{0,2},{2,0},{4,6},{6,4},{8,10},{10,8},{12,14},{14,12},{1,3},{3,1},... | collective-permute-start | bytes 958472 | tf_op jit(solution)/shard_map/ppermute | solution.py:535
  8.7 2.6 %collective-permute-start.1 = (bf16[7,16,256]{2,1,0:T(8,128)(2,1)S(1)}, bf16[7,16,256]{2,1,0:T(8,128)(2,1)S(1)}, u32[]{:S(2)}, u32[]{:S(2)}) collective-permute-start(bf16[7,16,256]{2,1,0:T(8,128)(2,1)S(1)} %get-tuple-element.37), channel_id=1, source_target_pairs={{0,8},{2,10},{4,12},{6,14},{8,0},{10,2},{12,4},{14,6},{1,9},{3,11}... | collective-permute-start | bytes 172040 | tf_op jit(solution)/shard_map/ppermute | solution.py:535
  11.3 1.4 %collective-permute-start.2 = (bf16[7,16,256]{2,1,0:T(8,128)(2,1)S(1)}, bf16[7,16,256]{2,1,0:T(8,128)(2,1)S(1)}, u32[]{:S(2)}, u32[]{:S(2)}) collective-permute-start(bf16[7,16,256]{2,1,0:T(8,128)(2,1)S(1)} %get-tuple-element.38), channel_id=1, source_target_pairs={{0,12},{2,14},{4,8},{6,10},{8,4},{10,6},{12,0},{14,2},{1,13},{3,15... | collective-permute-start | bytes 172040 | tf_op jit(solution)/shard_map/ppermute | solution.py:535
  12.6 0.2 collective-permute-start.3
  12.8 2.6 %shard_map.101 = (bf16[128,2048]{1,0:T(8,128)(2,1)S(1)}, bf16[128,2048]{1,0:T(8,128)(2,1)S(1)}, f32[16,128]{1,0:T(8,128)S(1)}) custom-call(f32[16]{0:T(128)} %defocus_hbm.3, f32[2,8]{1,0:T(2,128)} %bitcast.4, bf16[8,128,256]{2,1,0:T(8,128)(2,1)} %rows_hbm.3, bf16[8,256,128]{2,1,0:T(8,128)(2,1)} %cols_hbm.3), custom_call_target="tpu_custom_call" | custom-call | flops 1000 | bytes 1000 | tf_op jit(solution)/shard_map/pallas_call | solution.py:378
  15.5 0.0 collective-permute-done.1.refs_0_
  15.5 1.9 %collective-permute-done.2.refs_1_ = bf16[7,16,256]{2,1,0:T(8,128)(2,1)S(1)} collective-permute-done((bf16[7,16,256]{2,1,0:T(8,128)(2,1)S(1)}, bf16[7,16,256]{2,1,0:T(8,128)(2,1)S(1)}, u32[]{:S(2)}, u32[]{:S(2)}) %collective-permute-start.2) | collective-permute-done | bytes 57376 | tf_op jit(solution)/shard_map/ppermute | solution.py:535
  17.3 0.1 collective-permute-done.3.refs_2_
  17.4 0.0 collective-permute-done.x_came
  17.4 0.1 shard_map.102
  17.5 1.9 %collective-permute-start.5 = (bf16[13,16,256]{2,1,0:T(8,128)(2,1)S(1)}, bf16[13,16,256]{2,1,0:T(8,128)(2,1)S(1)}, u32[]{:S(2)}, u32[]{:S(2)}) collective-permute-start(bf16[13,16,256]{2,1,0:T(8,128)(2,1)S(1)} %get-tuple-element.43), channel_id=1, source_target_pairs={{0,8},{2,10},{4,12},{6,14},{8,0},{10,2},{12,4},{14,6},{1,9},{3,11}... | collective-permute-start | bytes 319496 | tf_op jit(solution)/shard_map/ppermute | solution.py:535
  19.4 1.2 %collective-permute-start.6 = (bf16[13,16,256]{2,1,0:T(8,128)(2,1)S(1)}, bf16[13,16,256]{2,1,0:T(8,128)(2,1)S(1)}, u32[]{:S(2)}, u32[]{:S(2)}) collective-permute-start(bf16[13,16,256]{2,1,0:T(8,128)(2,1)S(1)} %get-tuple-element.44), channel_id=1, source_target_pairs={{0,12},{2,14},{4,8},{6,10},{8,4},{10,6},{12,0},{14,2},{1,13},{3,15... | collective-permute-start | bytes 319496 | tf_op jit(solution)/shard_map/ppermute | solution.py:535
  20.5 0.5 %collective-permute-start.7 = (bf16[13,16,256]{2,1,0:T(8,128)(2,1)S(1)}, bf16[13,16,256]{2,1,0:T(8,128)(2,1)S(1)}, u32[]{:S(2)}, u32[]{:S(2)}) collective-permute-start(bf16[13,16,256]{2,1,0:T(8,128)(2,1)S(1)} %get-tuple-element.45), channel_id=1, source_target_pairs={{0,4},{2,6},{4,0},{6,2},{8,12},{10,14},{12,8},{14,10},{1,5},{3,7},... | collective-permute-start | bytes 319496 | tf_op jit(solution)/shard_map/ppermute | solution.py:535
  21.0 1.2 %collective-permute-start.8 = (bf16[13,16,256]{2,1,0:T(8,128)(2,1)S(1)}, bf16[13,16,256]{2,1,0:T(8,128)(2,1)S(1)}, u32[]{:S(2)}, u32[]{:S(2)}) collective-permute-start(bf16[13,16,256]{2,1,0:T(8,128)(2,1)S(1)} %get-tuple-element.46), channel_id=1, source_target_pairs={{0,2},{2,0},{4,6},{6,4},{8,10},{10,8},{12,14},{14,12},{1,3},{3,1},... | collective-permute-start | bytes 319496 | tf_op jit(solution)/shard_map/ppermute | solution.py:535
  22.3 0.8 %collective-permute-start.4 = (bf16[4,16,256]{2,1,0:T(8,128)(2,1)S(1)}, bf16[4,16,256]{2,1,0:T(8,128)(2,1)S(1)}, u32[]{:S(2)}, u32[]{:S(2)}) collective-permute-start(bf16[4,16,256]{2,1,0:T(8,128)(2,1)S(1)} %get-tuple-element.41), channel_id=1, source_target_pairs={{0,2},{2,0},{4,6},{6,4},{8,10},{10,8},{12,14},{14,12},{1,3},{3,1},... | collective-permute-start | bytes 98312 | tf_op jit(solution)/shard_map/ppermute | solution.py:535
  23.1 3.1 %collective-permute-done.4.z_came = bf16[4,16,256]{2,1,0:T(8,128)(2,1)S(1)} collective-permute-done((bf16[4,16,256]{2,1,0:T(8,128)(2,1)S(1)}, bf16[4,16,256]{2,1,0:T(8,128)(2,1)S(1)}, u32[]{:S(2)}, u32[]{:S(2)}) %collective-permute-start.4) | collective-permute-done | bytes 32800 | tf_op jit(solution)/shard_map/ppermute | solution.py:535
  26.2 0.4 %shard_map.103.ridge_ref = f32[16,16,128]{2,1,0:T(8,128)S(1)} custom-call(bf16[128,2048]{1,0:T(8,128)(2,1)S(1)} %get-tuple-element.30.high_ref, bf16[128,2048]{1,0:T(8,128)(2,1)S(1)} %get-tuple-element.31.low_ref, f32[16,128]{1,0:T(8,128)S(1)} %get-tuple-element.32.share_ref, f32[4,16,256]{2,1,0:T(8,128)S(1)} %get-tuple-element.40.z_own, ...), custom_call_target="tpu_custom_call" | custom-call | flops 1000 | bytes 1000 | tf_op jit(solution)/shard_map/pallas_call | solution.py:456
  26.6 1.2 %collective-permute-done.5.refs_0_ = bf16[13,16,256]{2,1,0:T(8,128)(2,1)S(1)} collective-permute-done((bf16[13,16,256]{2,1,0:T(8,128)(2,1)S(1)}, bf16[13,16,256]{2,1,0:T(8,128)(2,1)S(1)}, u32[]{:S(2)}, u32[]{:S(2)}) %collective-permute-start.5) | collective-permute-done | bytes 106528 | tf_op jit(solution)/shard_map/ppermute | solution.py:535
  27.8 0.0 collective-permute-done.6.refs_1_
  27.8 0.0 collective-permute-done.7.refs_2_
  27.8 0.0 collective-permute-done.8.refs_3_
  27.8 0.9 %shard_map.104 = f32[16,32,128]{2,1,0:T(8,128)} custom-call(f32[16,16,128]{2,1,0:T(8,128)S(1)} %shard_map.103.ridge_ref, f32[13,16,256]{2,1,0:T(8,128)S(1)} %get-tuple-element.42.x_own, f32[4,16,256]{2,1,0:T(8,128)S(1)} %get-tuple-element.40.z_own, bf16[4,16,256]{2,1,0:T(8,128)(2,1)S(1)} %collective-permute-done.4.z_came, ...), custom_call_target="tpu_custom_call" | custom-call | flops 1000 | bytes 1000 | tf_op jit(solution)/shard_map/pallas_call | solution.py:487
Async XLA Ops:
  5.7 11.7 %collective-permute-start = (bf16[3,13,16,256]{3,2,1,0:T(8,128)(2,1)S(1)}, bf16[3,13,16,256]{3,2,1,0:T(8,128)(2,1)S(1)}, u32[]{:S(2)}, u32[]{:S(2)}) collective-permute-start(bf16[3,13,16,256]{3,2,1,0:T(8,128)(2,1)S(1)} %get-tuple-element.34), channel_id=1, source_target_pairs={{0,2},{2,0},{4,6},{6,4},{8,10},{10,8},{12,14},{14,12},{1,3},{3,1},... | collective-permute-start | bytes 958472 | tf_op jit(solution)/shard_map/ppermute | solution.py:535
  8.7 6.8 %collective-permute-start.1 = (bf16[7,16,256]{2,1,0:T(8,128)(2,1)S(1)}, bf16[7,16,256]{2,1,0:T(8,128)(2,1)S(1)}, u32[]{:S(2)}, u32[]{:S(2)}) collective-permute-start(bf16[7,16,256]{2,1,0:T(8,128)(2,1)S(1)} %get-tuple-element.37), channel_id=1, source_target_pairs={{0,8},{2,10},{4,12},{6,14},{8,0},{10,2},{12,4},{14,6},{1,9},{3,11}... | collective-permute-start | bytes 172040 | tf_op jit(solution)/shard_map/ppermute | solution.py:535
  11.3 6.1 %collective-permute-start.2 = (bf16[7,16,256]{2,1,0:T(8,128)(2,1)S(1)}, bf16[7,16,256]{2,1,0:T(8,128)(2,1)S(1)}, u32[]{:S(2)}, u32[]{:S(2)}) collective-permute-start(bf16[7,16,256]{2,1,0:T(8,128)(2,1)S(1)} %get-tuple-element.38), channel_id=1, source_target_pairs={{0,12},{2,14},{4,8},{6,10},{8,4},{10,6},{12,0},{14,2},{1,13},{3,15... | collective-permute-start | bytes 172040 | tf_op jit(solution)/shard_map/ppermute | solution.py:535
  12.6 4.8 %collective-permute-start.3 = (bf16[7,16,256]{2,1,0:T(8,128)(2,1)S(1)}, bf16[7,16,256]{2,1,0:T(8,128)(2,1)S(1)}, u32[]{:S(2)}, u32[]{:S(2)}) collective-permute-start(bf16[7,16,256]{2,1,0:T(8,128)(2,1)S(1)} %get-tuple-element.39), channel_id=1, source_target_pairs={{0,4},{2,6},{4,0},{6,2},{8,12},{10,14},{12,8},{14,10},{1,5},{3,7},... | collective-permute-start | bytes 172040 | tf_op jit(solution)/shard_map/ppermute | solution.py:535
  17.5 10.3 %collective-permute-start.5 = (bf16[13,16,256]{2,1,0:T(8,128)(2,1)S(1)}, bf16[13,16,256]{2,1,0:T(8,128)(2,1)S(1)}, u32[]{:S(2)}, u32[]{:S(2)}) collective-permute-start(bf16[13,16,256]{2,1,0:T(8,128)(2,1)S(1)} %get-tuple-element.43), channel_id=1, source_target_pairs={{0,8},{2,10},{4,12},{6,14},{8,0},{10,2},{12,4},{14,6},{1,9},{3,11}... | collective-permute-start | bytes 319496 | tf_op jit(solution)/shard_map/ppermute | solution.py:535
  19.4 8.4 %collective-permute-start.6 = (bf16[13,16,256]{2,1,0:T(8,128)(2,1)S(1)}, bf16[13,16,256]{2,1,0:T(8,128)(2,1)S(1)}, u32[]{:S(2)}, u32[]{:S(2)}) collective-permute-start(bf16[13,16,256]{2,1,0:T(8,128)(2,1)S(1)} %get-tuple-element.44), channel_id=1, source_target_pairs={{0,12},{2,14},{4,8},{6,10},{8,4},{10,6},{12,0},{14,2},{1,13},{3,15... | collective-permute-start | bytes 319496 | tf_op jit(solution)/shard_map/ppermute | solution.py:535
  20.5 7.3 %collective-permute-start.7 = (bf16[13,16,256]{2,1,0:T(8,128)(2,1)S(1)}, bf16[13,16,256]{2,1,0:T(8,128)(2,1)S(1)}, u32[]{:S(2)}, u32[]{:S(2)}) collective-permute-start(bf16[13,16,256]{2,1,0:T(8,128)(2,1)S(1)} %get-tuple-element.45), channel_id=1, source_target_pairs={{0,4},{2,6},{4,0},{6,2},{8,12},{10,14},{12,8},{14,10},{1,5},{3,7},... | collective-permute-start | bytes 319496 | tf_op jit(solution)/shard_map/ppermute | solution.py:535
  21.0 6.8 %collective-permute-start.8 = (bf16[13,16,256]{2,1,0:T(8,128)(2,1)S(1)}, bf16[13,16,256]{2,1,0:T(8,128)(2,1)S(1)}, u32[]{:S(2)}, u32[]{:S(2)}) collective-permute-start(bf16[13,16,256]{2,1,0:T(8,128)(2,1)S(1)} %get-tuple-element.46), channel_id=1, source_target_pairs={{0,2},{2,0},{4,6},{6,4},{8,10},{10,8},{12,14},{14,12},{1,3},{3,1},... | collective-permute-start | bytes 319496 | tf_op jit(solution)/shard_map/ppermute | solution.py:535
  22.3 3.9 %collective-permute-start.4 = (bf16[4,16,256]{2,1,0:T(8,128)(2,1)S(1)}, bf16[4,16,256]{2,1,0:T(8,128)(2,1)S(1)}, u32[]{:S(2)}, u32[]{:S(2)}) collective-permute-start(bf16[4,16,256]{2,1,0:T(8,128)(2,1)S(1)} %get-tuple-element.41), channel_id=1, source_target_pairs={{0,2},{2,0},{4,6},{6,4},{8,10},{10,8},{12,14},{14,12},{1,3},{3,1},... | collective-permute-start | bytes 98312 | tf_op jit(solution)/shard_map/ppermute | solution.py:535

commit v24 on v23

--- a/solution.py
+++ b/solution.py
@@ -251,7 +251,7 @@
 SLOTS = 16
 GROUP = 8
 LOAD = 4
-LAG = 6
+LAG = 8
 Z_SLOTS = 4
 
 

time: 28.9 us -> 28.7 us (level)
  no operation moved by 1% of the time
where the time goes in v24:
time: 28.7 us; the launch traced here: 28.6 us
  starting transfers between devices  12.7 us (44%)
  Pallas kernels  9.46 us (33%)
  waiting for transfers between devices  6.33 us (22%)
    ppermute x9, starting transfers between devices, exchange(): return lax.ppermute(value, 'img', [(i, i ^ flip) for i in range(members)])  12.7 us
    ppermute x9, waiting for transfers between devices, exchange(): return lax.ppermute(value, 'img', [(i, i ^ flip) for i in range(members)])  6.33 us
    pallas_call x1, Pallas kernels, own_totals(): pl.pallas_call(slices_kernel, out_shape=out_shape, in_specs=[any_place] *...  5.45 us
    pallas_call x1, Pallas kernels, own_ridges(): pl.pallas_call(ridge_kernel, out_shape=[table, table, pltpu.VMEM((planes....  2.62 us
    pallas_call x1, Pallas kernels, finish(): pl.pallas_call(functools.partial(finish_kernel, planes), out_shape=jax.Sh...  0.94 us
  transfers between devices with their start and end apart: 9, of which 4 were waited for; matrix products, arithmetic and copies ran while one was open for 0% of the time, Pallas kernels for 10%

profile of v24, /device:TPU:0, one launch (start us, length us, event | category | flops | bytes accessed | tf_op | source)
XLA Modules:
  0.0 28.6 jit_solution(5289646092402906389)
XLA Ops:
  0.0 5.5 %shard_map.100 = (bf16[3,13,16,256]{3,2,1,0:T(8,128)(2,1)S(1)}, f32[3,13,16,256]{3,2,1,0:T(8,128)S(1)}, bf16[13,16,256]{2,1,0:T(8,128)(2,1)S(1)}, f32[13,16,256]...) custom-call(s32[16]{0:T(128)} %bitcast.5, ...), custom_call_target="tpu_custom_call" | custom-call | flops 2097152000 | bytes 6291456 | tf_op jit(solution)/shard_map/pallas_call | solution.py:284
  5.5 3.0 %collective-permute-start = (bf16[3,13,16,256]{3,2,1,0:T(8,128)(2,1)S(1)}, bf16[3,13,16,256]{3,2,1,0:T(8,128)(2,1)S(1)}, u32[]{:S(2)}, u32[]{:S(2)}) collective-permute-start(bf16[3,13,16,256]{3,2,1,0:T(8,128)(2,1)S(1)} %get-tuple-element.34), channel_id=1, source_target_pairs={{0,2},{2,0},{4,6},{6,4},{8,10},{10,8},{12,14},{14,12},{1,3},{3,1},... | collective-permute-start | bytes 958472 | tf_op jit(solution)/shard_map/ppermute | solution.py:535
  8.5 2.6 %collective-permute-start.1 = (bf16[7,16,256]{2,1,0:T(8,128)(2,1)S(1)}, bf16[7,16,256]{2,1,0:T(8,128)(2,1)S(1)}, u32[]{:S(2)}, u32[]{:S(2)}) collective-permute-start(bf16[7,16,256]{2,1,0:T(8,128)(2,1)S(1)} %get-tuple-element.37), channel_id=1, source_target_pairs={{0,8},{2,10},{4,12},{6,14},{8,0},{10,2},{12,4},{14,6},{1,9},{3,11}... | collective-permute-start | bytes 172040 | tf_op jit(solution)/shard_map/ppermute | solution.py:535
  11.1 1.3 %collective-permute-start.2 = (bf16[7,16,256]{2,1,0:T(8,128)(2,1)S(1)}, bf16[7,16,256]{2,1,0:T(8,128)(2,1)S(1)}, u32[]{:S(2)}, u32[]{:S(2)}) collective-permute-start(bf16[7,16,256]{2,1,0:T(8,128)(2,1)S(1)} %get-tuple-element.38), channel_id=1, source_target_pairs={{0,12},{2,14},{4,8},{6,10},{8,4},{10,6},{12,0},{14,2},{1,13},{3,15... | collective-permute-start | bytes 172040 | tf_op jit(solution)/shard_map/ppermute | solution.py:535
  12.4 0.2 collective-permute-start.3
  12.6 2.6 %shard_map.101 = (bf16[128,2048]{1,0:T(8,128)(2,1)S(1)}, bf16[128,2048]{1,0:T(8,128)(2,1)S(1)}, f32[16,128]{1,0:T(8,128)S(1)}) custom-call(f32[16]{0:T(128)} %defocus_hbm.3, f32[2,8]{1,0:T(2,128)} %bitcast.4, bf16[8,128,256]{2,1,0:T(8,128)(2,1)} %rows_hbm.3, bf16[8,256,128]{2,1,0:T(8,128)(2,1)} %cols_hbm.3), custom_call_target="tpu_custom_call" | custom-call | flops 1000 | bytes 1000 | tf_op jit(solution)/shard_map/pallas_call | solution.py:378
  15.3 0.0 collective-permute-done.1.refs_0_
  15.3 1.9 %collective-permute-done.2.refs_1_ = bf16[7,16,256]{2,1,0:T(8,128)(2,1)S(1)} collective-permute-done((bf16[7,16,256]{2,1,0:T(8,128)(2,1)S(1)}, bf16[7,16,256]{2,1,0:T(8,128)(2,1)S(1)}, u32[]{:S(2)}, u32[]{:S(2)}) %collective-permute-start.2) | collective-permute-done | bytes 57376 | tf_op jit(solution)/shard_map/ppermute | solution.py:535
  17.1 0.1 collective-permute-done.3.refs_2_
  17.2 0.0 collective-permute-done.x_came
  17.2 0.1 shard_map.102
  17.3 1.9 %collective-permute-start.5 = (bf16[13,16,256]{2,1,0:T(8,128)(2,1)S(1)}, bf16[13,16,256]{2,1,0:T(8,128)(2,1)S(1)}, u32[]{:S(2)}, u32[]{:S(2)}) collective-permute-start(bf16[13,16,256]{2,1,0:T(8,128)(2,1)S(1)} %get-tuple-element.43), channel_id=1, source_target_pairs={{0,8},{2,10},{4,12},{6,14},{8,0},{10,2},{12,4},{14,6},{1,9},{3,11}... | collective-permute-start | bytes 319496 | tf_op jit(solution)/shard_map/ppermute | solution.py:535
  19.2 1.2 %collective-permute-start.6 = (bf16[13,16,256]{2,1,0:T(8,128)(2,1)S(1)}, bf16[13,16,256]{2,1,0:T(8,128)(2,1)S(1)}, u32[]{:S(2)}, u32[]{:S(2)}) collective-permute-start(bf16[13,16,256]{2,1,0:T(8,128)(2,1)S(1)} %get-tuple-element.44), channel_id=1, source_target_pairs={{0,12},{2,14},{4,8},{6,10},{8,4},{10,6},{12,0},{14,2},{1,13},{3,15... | collective-permute-start | bytes 319496 | tf_op jit(solution)/shard_map/ppermute | solution.py:535
  20.3 0.5 %collective-permute-start.7 = (bf16[13,16,256]{2,1,0:T(8,128)(2,1)S(1)}, bf16[13,16,256]{2,1,0:T(8,128)(2,1)S(1)}, u32[]{:S(2)}, u32[]{:S(2)}) collective-permute-start(bf16[13,16,256]{2,1,0:T(8,128)(2,1)S(1)} %get-tuple-element.45), channel_id=1, source_target_pairs={{0,4},{2,6},{4,0},{6,2},{8,12},{10,14},{12,8},{14,10},{1,5},{3,7},... | collective-permute-start | bytes 319496 | tf_op jit(solution)/shard_map/ppermute | solution.py:535
  20.8 1.2 %collective-permute-start.8 = (bf16[13,16,256]{2,1,0:T(8,128)(2,1)S(1)}, bf16[13,16,256]{2,1,0:T(8,128)(2,1)S(1)}, u32[]{:S(2)}, u32[]{:S(2)}) collective-permute-start(bf16[13,16,256]{2,1,0:T(8,128)(2,1)S(1)} %get-tuple-element.46), channel_id=1, source_target_pairs={{0,2},{2,0},{4,6},{6,4},{8,10},{10,8},{12,14},{14,12},{1,3},{3,1},... | collective-permute-start | bytes 319496 | tf_op jit(solution)/shard_map/ppermute | solution.py:535
  22.1 0.8 %collective-permute-start.4 = (bf16[4,16,256]{2,1,0:T(8,128)(2,1)S(1)}, bf16[4,16,256]{2,1,0:T(8,128)(2,1)S(1)}, u32[]{:S(2)}, u32[]{:S(2)}) collective-permute-start(bf16[4,16,256]{2,1,0:T(8,128)(2,1)S(1)} %get-tuple-element.41), channel_id=1, source_target_pairs={{0,2},{2,0},{4,6},{6,4},{8,10},{10,8},{12,14},{14,12},{1,3},{3,1},... | collective-permute-start | bytes 98312 | tf_op jit(solution)/shard_map/ppermute | solution.py:535
  22.9 3.1 %collective-permute-done.4.z_came = bf16[4,16,256]{2,1,0:T(8,128)(2,1)S(1)} collective-permute-done((bf16[4,16,256]{2,1,0:T(8,128)(2,1)S(1)}, bf16[4,16,256]{2,1,0:T(8,128)(2,1)S(1)}, u32[]{:S(2)}, u32[]{:S(2)}) %collective-permute-start.4) | collective-permute-done | bytes 32800 | tf_op jit(solution)/shard_map/ppermute | solution.py:535
  26.0 0.4 %shard_map.103.ridge_ref = f32[16,16,128]{2,1,0:T(8,128)S(1)} custom-call(bf16[128,2048]{1,0:T(8,128)(2,1)S(1)} %get-tuple-element.30.high_ref, bf16[128,2048]{1,0:T(8,128)(2,1)S(1)} %get-tuple-element.31.low_ref, f32[16,128]{1,0:T(8,128)S(1)} %get-tuple-element.32.share_ref, f32[4,16,256]{2,1,0:T(8,128)S(1)} %get-tuple-element.40.z_own, ...), custom_call_target="tpu_custom_call" | custom-call | flops 1000 | bytes 1000 | tf_op jit(solution)/shard_map/pallas_call | solution.py:456
  26.4 1.2 %collective-permute-done.5.refs_0_ = bf16[13,16,256]{2,1,0:T(8,128)(2,1)S(1)} collective-permute-done((bf16[13,16,256]{2,1,0:T(8,128)(2,1)S(1)}, bf16[13,16,256]{2,1,0:T(8,128)(2,1)S(1)}, u32[]{:S(2)}, u32[]{:S(2)}) %collective-permute-start.5) | collective-permute-done | bytes 106528 | tf_op jit(solution)/shard_map/ppermute | solution.py:535
  27.6 0.0 collective-permute-done.6.refs_1_
  27.6 0.0 collective-permute-done.7.refs_2_
  27.6 0.0 collective-permute-done.8.refs_3_
  27.6 0.9 %shard_map.104 = f32[16,32,128]{2,1,0:T(8,128)} custom-call(f32[16,16,128]{2,1,0:T(8,128)S(1)} %shard_map.103.ridge_ref, f32[13,16,256]{2,1,0:T(8,128)S(1)} %get-tuple-element.42.x_own, f32[4,16,256]{2,1,0:T(8,128)S(1)} %get-tuple-element.40.z_own, bf16[4,16,256]{2,1,0:T(8,128)(2,1)S(1)} %collective-permute-done.4.z_came, ...), custom_call_target="tpu_custom_call" | custom-call | flops 1000 | bytes 1000 | tf_op jit(solution)/shard_map/pallas_call | solution.py:487
Async XLA Ops:
  5.5 11.7 %collective-permute-start = (bf16[3,13,16,256]{3,2,1,0:T(8,128)(2,1)S(1)}, bf16[3,13,16,256]{3,2,1,0:T(8,128)(2,1)S(1)}, u32[]{:S(2)}, u32[]{:S(2)}) collective-permute-start(bf16[3,13,16,256]{3,2,1,0:T(8,128)(2,1)S(1)} %get-tuple-element.34), channel_id=1, source_target_pairs={{0,2},{2,0},{4,6},{6,4},{8,10},{10,8},{12,14},{14,12},{1,3},{3,1},... | collective-permute-start | bytes 958472 | tf_op jit(solution)/shard_map/ppermute | solution.py:535
  8.5 6.8 %collective-permute-start.1 = (bf16[7,16,256]{2,1,0:T(8,128)(2,1)S(1)}, bf16[7,16,256]{2,1,0:T(8,128)(2,1)S(1)}, u32[]{:S(2)}, u32[]{:S(2)}) collective-permute-start(bf16[7,16,256]{2,1,0:T(8,128)(2,1)S(1)} %get-tuple-element.37), channel_id=1, source_target_pairs={{0,8},{2,10},{4,12},{6,14},{8,0},{10,2},{12,4},{14,6},{1,9},{3,11}... | collective-permute-start | bytes 172040 | tf_op jit(solution)/shard_map/ppermute | solution.py:535
  11.1 6.1 %collective-permute-start.2 = (bf16[7,16,256]{2,1,0:T(8,128)(2,1)S(1)}, bf16[7,16,256]{2,1,0:T(8,128)(2,1)S(1)}, u32[]{:S(2)}, u32[]{:S(2)}) collective-permute-start(bf16[7,16,256]{2,1,0:T(8,128)(2,1)S(1)} %get-tuple-element.38), channel_id=1, source_target_pairs={{0,12},{2,14},{4,8},{6,10},{8,4},{10,6},{12,0},{14,2},{1,13},{3,15... | collective-permute-start | bytes 172040 | tf_op jit(solution)/shard_map/ppermute | solution.py:535
  12.4 4.8 %collective-permute-start.3 = (bf16[7,16,256]{2,1,0:T(8,128)(2,1)S(1)}, bf16[7,16,256]{2,1,0:T(8,128)(2,1)S(1)}, u32[]{:S(2)}, u32[]{:S(2)}) collective-permute-start(bf16[7,16,256]{2,1,0:T(8,128)(2,1)S(1)} %get-tuple-element.39), channel_id=1, source_target_pairs={{0,4},{2,6},{4,0},{6,2},{8,12},{10,14},{12,8},{14,10},{1,5},{3,7},... | collective-permute-start | bytes 172040 | tf_op jit(solution)/shard_map/ppermute | solution.py:535
  17.3 10.3 %collective-permute-start.5 = (bf16[13,16,256]{2,1,0:T(8,128)(2,1)S(1)}, bf16[13,16,256]{2,1,0:T(8,128)(2,1)S(1)}, u32[]{:S(2)}, u32[]{:S(2)}) collective-permute-start(bf16[13,16,256]{2,1,0:T(8,128)(2,1)S(1)} %get-tuple-element.43), channel_id=1, source_target_pairs={{0,8},{2,10},{4,12},{6,14},{8,0},{10,2},{12,4},{14,6},{1,9},{3,11}... | collective-permute-start | bytes 319496 | tf_op jit(solution)/shard_map/ppermute | solution.py:535
  19.2 8.4 %collective-permute-start.6 = (bf16[13,16,256]{2,1,0:T(8,128)(2,1)S(1)}, bf16[13,16,256]{2,1,0:T(8,128)(2,1)S(1)}, u32[]{:S(2)}, u32[]{:S(2)}) collective-permute-start(bf16[13,16,256]{2,1,0:T(8,128)(2,1)S(1)} %get-tuple-element.44), channel_id=1, source_target_pairs={{0,12},{2,14},{4,8},{6,10},{8,4},{10,6},{12,0},{14,2},{1,13},{3,15... | collective-permute-start | bytes 319496 | tf_op jit(solution)/shard_map/ppermute | solution.py:535
  20.3 7.3 %collective-permute-start.7 = (bf16[13,16,256]{2,1,0:T(8,128)(2,1)S(1)}, bf16[13,16,256]{2,1,0:T(8,128)(2,1)S(1)}, u32[]{:S(2)}, u32[]{:S(2)}) collective-permute-start(bf16[13,16,256]{2,1,0:T(8,128)(2,1)S(1)} %get-tuple-element.45), channel_id=1, source_target_pairs={{0,4},{2,6},{4,0},{6,2},{8,12},{10,14},{12,8},{14,10},{1,5},{3,7},... | collective-permute-start | bytes 319496 | tf_op jit(solution)/shard_map/ppermute | solution.py:535
  20.8 6.8 %collective-permute-start.8 = (bf16[13,16,256]{2,1,0:T(8,128)(2,1)S(1)}, bf16[13,16,256]{2,1,0:T(8,128)(2,1)S(1)}, u32[]{:S(2)}, u32[]{:S(2)}) collective-permute-start(bf16[13,16,256]{2,1,0:T(8,128)(2,1)S(1)} %get-tuple-element.46), channel_id=1, source_target_pairs={{0,2},{2,0},{4,6},{6,4},{8,10},{10,8},{12,14},{14,12},{1,3},{3,1},... | collective-permute-start | bytes 319496 | tf_op jit(solution)/shard_map/ppermute | solution.py:535
  22.1 3.9 %collective-permute-start.4 = (bf16[4,16,256]{2,1,0:T(8,128)(2,1)S(1)}, bf16[4,16,256]{2,1,0:T(8,128)(2,1)S(1)}, u32[]{:S(2)}, u32[]{:S(2)}) collective-permute-start(bf16[4,16,256]{2,1,0:T(8,128)(2,1)S(1)} %get-tuple-element.41), channel_id=1, source_target_pairs={{0,2},{2,0},{4,6},{6,4},{8,10},{10,8},{12,14},{14,12},{1,3},{3,1},... | collective-permute-start | bytes 98312 | tf_op jit(solution)/shard_map/ppermute | solution.py:535

commit v25 on v22

--- a/solution.py
+++ b/solution.py
@@ -247,7 +247,7 @@
 SCRATCH = 20
 LINE = (2, 3, 1)
 SLOTS = 16
-GROUP = 8
+GROUP = 16
 Z_SLOTS = 4
 
 

time: 28.6 us -> 28.5 us (level)
  transfers between devices with their start and end apart: 9 -> 9, of which waited for: 4 -> 5; matrix products, arithmetic and copies ran while one was open for 0% -> 0% of each run, Pallas kernels for 10% -> 11%
where the time goes in v25:
time: 28.5 us; the launch traced here: 28.4 us
  starting transfers between devices  12.8 us (45%)
  Pallas kernels  9.23 us (32%)
  waiting for transfers between devices  6.32 us (22%)
    ppermute x9, starting transfers between devices, exchange(): return lax.ppermute(value, 'img', [(i, i ^ flip) for i in range(members)])  12.8 us
    ppermute x9, waiting for transfers between devices, exchange(): return lax.ppermute(value, 'img', [(i, i ^ flip) for i in range(members)])  6.32 us
    pallas_call x1, Pallas kernels, own_totals(): pl.pallas_call(slices_kernel, out_shape=out_shape, in_specs=[any_place] *...  5.22 us
    pallas_call x1, Pallas kernels, own_ridges(): pl.pallas_call(ridge_kernel, out_shape=[table, table, pltpu.VMEM((planes....  2.62 us
    pallas_call x1, Pallas kernels, finish(): pl.pallas_call(functools.partial(finish_kernel, planes), out_shape=jax.Sh...  0.94 us
  transfers between devices with their start and end apart: 9, of which 5 were waited for; matrix products, arithmetic and copies ran while one was open for 0% of the time, Pallas kernels for 11%

profile of v25, /device:TPU:0, one launch (start us, length us, event | category | flops | bytes accessed | tf_op | source)
XLA Modules:
  0.0 28.4 jit_solution(4523238304421187975)
XLA Ops:
  0.0 5.2 %shard_map.100 = (bf16[3,13,16,256]{3,2,1,0:T(8,128)(2,1)S(1)}, f32[3,13,16,256]{3,2,1,0:T(8,128)S(1)}, bf16[13,16,256]{2,1,0:T(8,128)(2,1)S(1)}, f32[13,16,256]...) custom-call(s32[16]{0:T(128)} %bitcast.5, ...), custom_call_target="tpu_custom_call" | custom-call | flops 2097152000 | bytes 6291456 | tf_op jit(solution)/shard_map/pallas_call | solution.py:280
  5.2 3.0 %collective-permute-start = (bf16[3,13,16,256]{3,2,1,0:T(8,128)(2,1)S(1)}, bf16[3,13,16,256]{3,2,1,0:T(8,128)(2,1)S(1)}, u32[]{:S(2)}, u32[]{:S(2)}) collective-permute-start(bf16[3,13,16,256]{3,2,1,0:T(8,128)(2,1)S(1)} %get-tuple-element.34), channel_id=1, source_target_pairs={{0,2},{2,0},{4,6},{6,4},{8,10},{10,8},{12,14},{14,12},{1,3},{3,1},... | collective-permute-start | bytes 958472 | tf_op jit(solution)/shard_map/ppermute | solution.py:531
  8.2 2.6 %collective-permute-start.1 = (bf16[7,16,256]{2,1,0:T(8,128)(2,1)S(1)}, bf16[7,16,256]{2,1,0:T(8,128)(2,1)S(1)}, u32[]{:S(2)}, u32[]{:S(2)}) collective-permute-start(bf16[7,16,256]{2,1,0:T(8,128)(2,1)S(1)} %get-tuple-element.37), channel_id=1, source_target_pairs={{0,8},{2,10},{4,12},{6,14},{8,0},{10,2},{12,4},{14,6},{1,9},{3,11}... | collective-permute-start | bytes 172040 | tf_op jit(solution)/shard_map/ppermute | solution.py:531
  10.8 1.3 %collective-permute-start.2 = (bf16[7,16,256]{2,1,0:T(8,128)(2,1)S(1)}, bf16[7,16,256]{2,1,0:T(8,128)(2,1)S(1)}, u32[]{:S(2)}, u32[]{:S(2)}) collective-permute-start(bf16[7,16,256]{2,1,0:T(8,128)(2,1)S(1)} %get-tuple-element.38), channel_id=1, source_target_pairs={{0,12},{2,14},{4,8},{6,10},{8,4},{10,6},{12,0},{14,2},{1,13},{3,15... | collective-permute-start | bytes 172040 | tf_op jit(solution)/shard_map/ppermute | solution.py:531
  12.2 0.2 collective-permute-start.3
  12.4 2.6 %shard_map.101 = (bf16[128,2048]{1,0:T(8,128)(2,1)S(1)}, bf16[128,2048]{1,0:T(8,128)(2,1)S(1)}, f32[16,128]{1,0:T(8,128)S(1)}) custom-call(f32[16]{0:T(128)} %defocus_hbm.3, f32[2,8]{1,0:T(2,128)} %bitcast.4, bf16[8,128,256]{2,1,0:T(8,128)(2,1)} %rows_hbm.3, bf16[8,256,128]{2,1,0:T(8,128)(2,1)} %cols_hbm.3), custom_call_target="tpu_custom_call" | custom-call | flops 1000 | bytes 1000 | tf_op jit(solution)/shard_map/pallas_call | solution.py:374
  15.0 0.0 collective-permute-done.1.refs_0_
  15.0 1.9 %collective-permute-done.2.refs_1_ = bf16[7,16,256]{2,1,0:T(8,128)(2,1)S(1)} collective-permute-done((bf16[7,16,256]{2,1,0:T(8,128)(2,1)S(1)}, bf16[7,16,256]{2,1,0:T(8,128)(2,1)S(1)}, u32[]{:S(2)}, u32[]{:S(2)}) %collective-permute-start.2) | collective-permute-done | bytes 57376 | tf_op jit(solution)/shard_map/ppermute | solution.py:531
  16.9 0.1 collective-permute-done.3.refs_2_
  17.0 0.0 collective-permute-done.x_came
  17.0 0.1 shard_map.102
  17.1 1.9 %collective-permute-start.5 = (bf16[13,16,256]{2,1,0:T(8,128)(2,1)S(1)}, bf16[13,16,256]{2,1,0:T(8,128)(2,1)S(1)}, u32[]{:S(2)}, u32[]{:S(2)}) collective-permute-start(bf16[13,16,256]{2,1,0:T(8,128)(2,1)S(1)} %get-tuple-element.43), channel_id=1, source_target_pairs={{0,8},{2,10},{4,12},{6,14},{8,0},{10,2},{12,4},{14,6},{1,9},{3,11}... | collective-permute-start | bytes 319496 | tf_op jit(solution)/shard_map/ppermute | solution.py:531
  19.0 1.2 %collective-permute-start.6 = (bf16[13,16,256]{2,1,0:T(8,128)(2,1)S(1)}, bf16[13,16,256]{2,1,0:T(8,128)(2,1)S(1)}, u32[]{:S(2)}, u32[]{:S(2)}) collective-permute-start(bf16[13,16,256]{2,1,0:T(8,128)(2,1)S(1)} %get-tuple-element.44), channel_id=1, source_target_pairs={{0,12},{2,14},{4,8},{6,10},{8,4},{10,6},{12,0},{14,2},{1,13},{3,15... | collective-permute-start | bytes 319496 | tf_op jit(solution)/shard_map/ppermute | solution.py:531
  20.1 0.5 %collective-permute-start.7 = (bf16[13,16,256]{2,1,0:T(8,128)(2,1)S(1)}, bf16[13,16,256]{2,1,0:T(8,128)(2,1)S(1)}, u32[]{:S(2)}, u32[]{:S(2)}) collective-permute-start(bf16[13,16,256]{2,1,0:T(8,128)(2,1)S(1)} %get-tuple-element.45), channel_id=1, source_target_pairs={{0,4},{2,6},{4,0},{6,2},{8,12},{10,14},{12,8},{14,10},{1,5},{3,7},... | collective-permute-start | bytes 319496 | tf_op jit(solution)/shard_map/ppermute | solution.py:531
  20.6 1.2 %collective-permute-start.8 = (bf16[13,16,256]{2,1,0:T(8,128)(2,1)S(1)}, bf16[13,16,256]{2,1,0:T(8,128)(2,1)S(1)}, u32[]{:S(2)}, u32[]{:S(2)}) collective-permute-start(bf16[13,16,256]{2,1,0:T(8,128)(2,1)S(1)} %get-tuple-element.46), channel_id=1, source_target_pairs={{0,2},{2,0},{4,6},{6,4},{8,10},{10,8},{12,14},{14,12},{1,3},{3,1},... | collective-permute-start | bytes 319496 | tf_op jit(solution)/shard_map/ppermute | solution.py:531
  21.8 0.8 %collective-permute-start.4 = (bf16[4,16,256]{2,1,0:T(8,128)(2,1)S(1)}, bf16[4,16,256]{2,1,0:T(8,128)(2,1)S(1)}, u32[]{:S(2)}, u32[]{:S(2)}) collective-permute-start(bf16[4,16,256]{2,1,0:T(8,128)(2,1)S(1)} %get-tuple-element.41), channel_id=1, source_target_pairs={{0,2},{2,0},{4,6},{6,4},{8,10},{10,8},{12,14},{14,12},{1,3},{3,1},... | collective-permute-start | bytes 98312 | tf_op jit(solution)/shard_map/ppermute | solution.py:531
  22.6 3.1 %collective-permute-done.4.z_came = bf16[4,16,256]{2,1,0:T(8,128)(2,1)S(1)} collective-permute-done((bf16[4,16,256]{2,1,0:T(8,128)(2,1)S(1)}, bf16[4,16,256]{2,1,0:T(8,128)(2,1)S(1)}, u32[]{:S(2)}, u32[]{:S(2)}) %collective-permute-start.4) | collective-permute-done | bytes 32800 | tf_op jit(solution)/shard_map/ppermute | solution.py:531
  25.8 0.4 %shard_map.103.ridge_ref = f32[16,16,128]{2,1,0:T(8,128)S(1)} custom-call(bf16[128,2048]{1,0:T(8,128)(2,1)S(1)} %get-tuple-element.30.high_ref, bf16[128,2048]{1,0:T(8,128)(2,1)S(1)} %get-tuple-element.31.low_ref, f32[16,128]{1,0:T(8,128)S(1)} %get-tuple-element.32.share_ref, f32[4,16,256]{2,1,0:T(8,128)S(1)} %get-tuple-element.40.z_own, ...), custom_call_target="tpu_custom_call" | custom-call | flops 1000 | bytes 1000 | tf_op jit(solution)/shard_map/pallas_call | solution.py:452
  26.1 1.2 %collective-permute-done.5.refs_0_ = bf16[13,16,256]{2,1,0:T(8,128)(2,1)S(1)} collective-permute-done((bf16[13,16,256]{2,1,0:T(8,128)(2,1)S(1)}, bf16[13,16,256]{2,1,0:T(8,128)(2,1)S(1)}, u32[]{:S(2)}, u32[]{:S(2)}) %collective-permute-start.5) | collective-permute-done | bytes 106528 | tf_op jit(solution)/shard_map/ppermute | solution.py:531
  27.4 0.0 collective-permute-done.6.refs_1_
  27.4 0.1 collective-permute-done.7.refs_2_
  27.4 0.0 collective-permute-done.8.refs_3_
  27.4 0.9 %shard_map.104 = f32[16,32,128]{2,1,0:T(8,128)} custom-call(f32[16,16,128]{2,1,0:T(8,128)S(1)} %shard_map.103.ridge_ref, f32[13,16,256]{2,1,0:T(8,128)S(1)} %get-tuple-element.42.x_own, f32[4,16,256]{2,1,0:T(8,128)S(1)} %get-tuple-element.40.z_own, bf16[4,16,256]{2,1,0:T(8,128)(2,1)S(1)} %collective-permute-done.4.z_came, ...), custom_call_target="tpu_custom_call" | custom-call | flops 1000 | bytes 1000 | tf_op jit(solution)/shard_map/pallas_call | solution.py:483
Async XLA Ops:
  5.2 11.7 %collective-permute-start = (bf16[3,13,16,256]{3,2,1,0:T(8,128)(2,1)S(1)}, bf16[3,13,16,256]{3,2,1,0:T(8,128)(2,1)S(1)}, u32[]{:S(2)}, u32[]{:S(2)}) collective-permute-start(bf16[3,13,16,256]{3,2,1,0:T(8,128)(2,1)S(1)} %get-tuple-element.34), channel_id=1, source_target_pairs={{0,2},{2,0},{4,6},{6,4},{8,10},{10,8},{12,14},{14,12},{1,3},{3,1},... | collective-permute-start | bytes 958472 | tf_op jit(solution)/shard_map/ppermute | solution.py:531
  8.2 6.8 %collective-permute-start.1 = (bf16[7,16,256]{2,1,0:T(8,128)(2,1)S(1)}, bf16[7,16,256]{2,1,0:T(8,128)(2,1)S(1)}, u32[]{:S(2)}, u32[]{:S(2)}) collective-permute-start(bf16[7,16,256]{2,1,0:T(8,128)(2,1)S(1)} %get-tuple-element.37), channel_id=1, source_target_pairs={{0,8},{2,10},{4,12},{6,14},{8,0},{10,2},{12,4},{14,6},{1,9},{3,11}... | collective-permute-start | bytes 172040 | tf_op jit(solution)/shard_map/ppermute | solution.py:531
  10.8 6.1 %collective-permute-start.2 = (bf16[7,16,256]{2,1,0:T(8,128)(2,1)S(1)}, bf16[7,16,256]{2,1,0:T(8,128)(2,1)S(1)}, u32[]{:S(2)}, u32[]{:S(2)}) collective-permute-start(bf16[7,16,256]{2,1,0:T(8,128)(2,1)S(1)} %get-tuple-element.38), channel_id=1, source_target_pairs={{0,12},{2,14},{4,8},{6,10},{8,4},{10,6},{12,0},{14,2},{1,13},{3,15... | collective-permute-start | bytes 172040 | tf_op jit(solution)/shard_map/ppermute | solution.py:531
  12.2 4.8 %collective-permute-start.3 = (bf16[7,16,256]{2,1,0:T(8,128)(2,1)S(1)}, bf16[7,16,256]{2,1,0:T(8,128)(2,1)S(1)}, u32[]{:S(2)}, u32[]{:S(2)}) collective-permute-start(bf16[7,16,256]{2,1,0:T(8,128)(2,1)S(1)} %get-tuple-element.39), channel_id=1, source_target_pairs={{0,4},{2,6},{4,0},{6,2},{8,12},{10,14},{12,8},{14,10},{1,5},{3,7},... | collective-permute-start | bytes 172040 | tf_op jit(solution)/shard_map/ppermute | solution.py:531
  17.1 10.3 %collective-permute-start.5 = (bf16[13,16,256]{2,1,0:T(8,128)(2,1)S(1)}, bf16[13,16,256]{2,1,0:T(8,128)(2,1)S(1)}, u32[]{:S(2)}, u32[]{:S(2)}) collective-permute-start(bf16[13,16,256]{2,1,0:T(8,128)(2,1)S(1)} %get-tuple-element.43), channel_id=1, source_target_pairs={{0,8},{2,10},{4,12},{6,14},{8,0},{10,2},{12,4},{14,6},{1,9},{3,11}... | collective-permute-start | bytes 319496 | tf_op jit(solution)/shard_map/ppermute | solution.py:531
  19.0 8.4 %collective-permute-start.6 = (bf16[13,16,256]{2,1,0:T(8,128)(2,1)S(1)}, bf16[13,16,256]{2,1,0:T(8,128)(2,1)S(1)}, u32[]{:S(2)}, u32[]{:S(2)}) collective-permute-start(bf16[13,16,256]{2,1,0:T(8,128)(2,1)S(1)} %get-tuple-element.44), channel_id=1, source_target_pairs={{0,12},{2,14},{4,8},{6,10},{8,4},{10,6},{12,0},{14,2},{1,13},{3,15... | collective-permute-start | bytes 319496 | tf_op jit(solution)/shard_map/ppermute | solution.py:531
  20.1 7.3 %collective-permute-start.7 = (bf16[13,16,256]{2,1,0:T(8,128)(2,1)S(1)}, bf16[13,16,256]{2,1,0:T(8,128)(2,1)S(1)}, u32[]{:S(2)}, u32[]{:S(2)}) collective-permute-start(bf16[13,16,256]{2,1,0:T(8,128)(2,1)S(1)} %get-tuple-element.45), channel_id=1, source_target_pairs={{0,4},{2,6},{4,0},{6,2},{8,12},{10,14},{12,8},{14,10},{1,5},{3,7},... | collective-permute-start | bytes 319496 | tf_op jit(solution)/shard_map/ppermute | solution.py:531
  20.6 6.8 %collective-permute-start.8 = (bf16[13,16,256]{2,1,0:T(8,128)(2,1)S(1)}, bf16[13,16,256]{2,1,0:T(8,128)(2,1)S(1)}, u32[]{:S(2)}, u32[]{:S(2)}) collective-permute-start(bf16[13,16,256]{2,1,0:T(8,128)(2,1)S(1)} %get-tuple-element.46), channel_id=1, source_target_pairs={{0,2},{2,0},{4,6},{6,4},{8,10},{10,8},{12,14},{14,12},{1,3},{3,1},... | collective-permute-start | bytes 319496 | tf_op jit(solution)/shard_map/ppermute | solution.py:531
  21.8 3.9 %collective-permute-start.4 = (bf16[4,16,256]{2,1,0:T(8,128)(2,1)S(1)}, bf16[4,16,256]{2,1,0:T(8,128)(2,1)S(1)}, u32[]{:S(2)}, u32[]{:S(2)}) collective-permute-start(bf16[4,16,256]{2,1,0:T(8,128)(2,1)S(1)} %get-tuple-element.41), channel_id=1, source_target_pairs={{0,2},{2,0},{4,6},{6,4},{8,10},{10,8},{12,14},{14,12},{1,3},{3,1},... | collective-permute-start | bytes 98312 | tf_op jit(solution)/shard_map/ppermute | solution.py:531

commit v26 on v25

--- a/solution.py
+++ b/solution.py
@@ -218,8 +218,9 @@
             if 0 <= step - 2 * GROUP < count:
                 mix(step - 2 * GROUP + n)
             next(parts, None)
-            if step >= 3 * GROUP:
-                insert(step - 3 * GROUP + n)
+            late = step - 2 * GROUP + n - GROUP // 2
+            if step >= 2 * GROUP and 0 <= late < count:
+                insert(late)
             if step < count and n % 2 == 0:
                 along_rows(step + n, 2)
 

time: 28.5 us -> 28.6 us (level)
  transfers between devices with their start and end apart: 9 -> 9, of which waited for: 5 -> 5; matrix products, arithmetic and copies ran while one was open for 0% -> 0% of each run, Pallas kernels for 11% -> 10%
where the time goes in v26:
time: 28.6 us; the launch traced here: 28.4 us
  starting transfers between devices  12.8 us (45%)
  Pallas kernels  9.29 us (32%)
  waiting for transfers between devices  6.32 us (22%)
    ppermute x9, starting transfers between devices, exchange(): return lax.ppermute(value, 'img', [(i, i ^ flip) for i in range(members)])  12.8 us
    ppermute x9, waiting for transfers between devices, exchange(): return lax.ppermute(value, 'img', [(i, i ^ flip) for i in range(members)])  6.32 us
    pallas_call x1, Pallas kernels, own_totals(): pl.pallas_call(slices_kernel, out_shape=out_shape, in_specs=[any_place] *...  5.27 us
    pallas_call x1, Pallas kernels, own_ridges(): pl.pallas_call(ridge_kernel, out_shape=[table, table, pltpu.VMEM((planes....  2.62 us
    pallas_call x1, Pallas kernels, finish(): pl.pallas_call(functools.partial(finish_kernel, planes), out_shape=jax.Sh...  0.94 us
  transfers between devices with their start and end apart: 9, of which 5 were waited for; matrix products, arithmetic and copies ran while one was open for 0% of the time, Pallas kernels for 10%

profile of v26, /device:TPU:0, one launch (start us, length us, event | category | flops | bytes accessed | tf_op | source)
XLA Modules:
  0.0 28.4 jit_solution(11813655902224124157)
XLA Ops:
  0.0 5.3 %shard_map.100 = (bf16[3,13,16,256]{3,2,1,0:T(8,128)(2,1)S(1)}, f32[3,13,16,256]{3,2,1,0:T(8,128)S(1)}, bf16[13,16,256]{2,1,0:T(8,128)(2,1)S(1)}, f32[13,16,256]...) custom-call(s32[16]{0:T(128)} %bitcast.5, ...), custom_call_target="tpu_custom_call" | custom-call | flops 2097152000 | bytes 6291456 | tf_op jit(solution)/shard_map/pallas_call | solution.py:281
  5.3 3.0 %collective-permute-start = (bf16[3,13,16,256]{3,2,1,0:T(8,128)(2,1)S(1)}, bf16[3,13,16,256]{3,2,1,0:T(8,128)(2,1)S(1)}, u32[]{:S(2)}, u32[]{:S(2)}) collective-permute-start(bf16[3,13,16,256]{3,2,1,0:T(8,128)(2,1)S(1)} %get-tuple-element.34), channel_id=1, source_target_pairs={{0,2},{2,0},{4,6},{6,4},{8,10},{10,8},{12,14},{14,12},{1,3},{3,1},... | collective-permute-start | bytes 958472 | tf_op jit(solution)/shard_map/ppermute | solution.py:532
  8.3 2.6 %collective-permute-start.1 = (bf16[7,16,256]{2,1,0:T(8,128)(2,1)S(1)}, bf16[7,16,256]{2,1,0:T(8,128)(2,1)S(1)}, u32[]{:S(2)}, u32[]{:S(2)}) collective-permute-start(bf16[7,16,256]{2,1,0:T(8,128)(2,1)S(1)} %get-tuple-element.37), channel_id=1, source_target_pairs={{0,8},{2,10},{4,12},{6,14},{8,0},{10,2},{12,4},{14,6},{1,9},{3,11}... | collective-permute-start | bytes 172040 | tf_op jit(solution)/shard_map/ppermute | solution.py:532
  10.9 1.3 %collective-permute-start.2 = (bf16[7,16,256]{2,1,0:T(8,128)(2,1)S(1)}, bf16[7,16,256]{2,1,0:T(8,128)(2,1)S(1)}, u32[]{:S(2)}, u32[]{:S(2)}) collective-permute-start(bf16[7,16,256]{2,1,0:T(8,128)(2,1)S(1)} %get-tuple-element.38), channel_id=1, source_target_pairs={{0,12},{2,14},{4,8},{6,10},{8,4},{10,6},{12,0},{14,2},{1,13},{3,15... | collective-permute-start | bytes 172040 | tf_op jit(solution)/shard_map/ppermute | solution.py:532
  12.2 0.2 collective-permute-start.3
  12.5 2.6 %shard_map.101 = (bf16[128,2048]{1,0:T(8,128)(2,1)S(1)}, bf16[128,2048]{1,0:T(8,128)(2,1)S(1)}, f32[16,128]{1,0:T(8,128)S(1)}) custom-call(f32[16]{0:T(128)} %defocus_hbm.3, f32[2,8]{1,0:T(2,128)} %bitcast.4, bf16[8,128,256]{2,1,0:T(8,128)(2,1)} %rows_hbm.3, bf16[8,256,128]{2,1,0:T(8,128)(2,1)} %cols_hbm.3), custom_call_target="tpu_custom_call" | custom-call | flops 1000 | bytes 1000 | tf_op jit(solution)/shard_map/pallas_call | solution.py:375
  15.1 0.0 collective-permute-done.1.refs_0_
  15.1 1.9 %collective-permute-done.2.refs_1_ = bf16[7,16,256]{2,1,0:T(8,128)(2,1)S(1)} collective-permute-done((bf16[7,16,256]{2,1,0:T(8,128)(2,1)S(1)}, bf16[7,16,256]{2,1,0:T(8,128)(2,1)S(1)}, u32[]{:S(2)}, u32[]{:S(2)}) %collective-permute-start.2) | collective-permute-done | bytes 57376 | tf_op jit(solution)/shard_map/ppermute | solution.py:532
  17.0 0.1 collective-permute-done.3.refs_2_
  17.0 0.0 collective-permute-done.x_came
  17.0 0.1 shard_map.102
  17.1 1.9 %collective-permute-start.5 = (bf16[13,16,256]{2,1,0:T(8,128)(2,1)S(1)}, bf16[13,16,256]{2,1,0:T(8,128)(2,1)S(1)}, u32[]{:S(2)}, u32[]{:S(2)}) collective-permute-start(bf16[13,16,256]{2,1,0:T(8,128)(2,1)S(1)} %get-tuple-element.43), channel_id=1, source_target_pairs={{0,8},{2,10},{4,12},{6,14},{8,0},{10,2},{12,4},{14,6},{1,9},{3,11}... | collective-permute-start | bytes 319496 | tf_op jit(solution)/shard_map/ppermute | solution.py:532
  19.0 1.2 %collective-permute-start.6 = (bf16[13,16,256]{2,1,0:T(8,128)(2,1)S(1)}, bf16[13,16,256]{2,1,0:T(8,128)(2,1)S(1)}, u32[]{:S(2)}, u32[]{:S(2)}) collective-permute-start(bf16[13,16,256]{2,1,0:T(8,128)(2,1)S(1)} %get-tuple-element.44), channel_id=1, source_target_pairs={{0,12},{2,14},{4,8},{6,10},{8,4},{10,6},{12,0},{14,2},{1,13},{3,15... | collective-permute-start | bytes 319496 | tf_op jit(solution)/shard_map/ppermute | solution.py:532
  20.2 0.5 %collective-permute-start.7 = (bf16[13,16,256]{2,1,0:T(8,128)(2,1)S(1)}, bf16[13,16,256]{2,1,0:T(8,128)(2,1)S(1)}, u32[]{:S(2)}, u32[]{:S(2)}) collective-permute-start(bf16[13,16,256]{2,1,0:T(8,128)(2,1)S(1)} %get-tuple-element.45), channel_id=1, source_target_pairs={{0,4},{2,6},{4,0},{6,2},{8,12},{10,14},{12,8},{14,10},{1,5},{3,7},... | collective-permute-start | bytes 319496 | tf_op jit(solution)/shard_map/ppermute | solution.py:532
  20.7 1.2 %collective-permute-start.8 = (bf16[13,16,256]{2,1,0:T(8,128)(2,1)S(1)}, bf16[13,16,256]{2,1,0:T(8,128)(2,1)S(1)}, u32[]{:S(2)}, u32[]{:S(2)}) collective-permute-start(bf16[13,16,256]{2,1,0:T(8,128)(2,1)S(1)} %get-tuple-element.46), channel_id=1, source_target_pairs={{0,2},{2,0},{4,6},{6,4},{8,10},{10,8},{12,14},{14,12},{1,3},{3,1},... | collective-permute-start | bytes 319496 | tf_op jit(solution)/shard_map/ppermute | solution.py:532
  21.9 0.8 %collective-permute-start.4 = (bf16[4,16,256]{2,1,0:T(8,128)(2,1)S(1)}, bf16[4,16,256]{2,1,0:T(8,128)(2,1)S(1)}, u32[]{:S(2)}, u32[]{:S(2)}) collective-permute-start(bf16[4,16,256]{2,1,0:T(8,128)(2,1)S(1)} %get-tuple-element.41), channel_id=1, source_target_pairs={{0,2},{2,0},{4,6},{6,4},{8,10},{10,8},{12,14},{14,12},{1,3},{3,1},... | collective-permute-start | bytes 98312 | tf_op jit(solution)/shard_map/ppermute | solution.py:532
  22.7 3.1 %collective-permute-done.4.z_came = bf16[4,16,256]{2,1,0:T(8,128)(2,1)S(1)} collective-permute-done((bf16[4,16,256]{2,1,0:T(8,128)(2,1)S(1)}, bf16[4,16,256]{2,1,0:T(8,128)(2,1)S(1)}, u32[]{:S(2)}, u32[]{:S(2)}) %collective-permute-start.4) | collective-permute-done | bytes 32800 | tf_op jit(solution)/shard_map/ppermute | solution.py:532
  25.8 0.4 %shard_map.103.ridge_ref = f32[16,16,128]{2,1,0:T(8,128)S(1)} custom-call(bf16[128,2048]{1,0:T(8,128)(2,1)S(1)} %get-tuple-element.30.high_ref, bf16[128,2048]{1,0:T(8,128)(2,1)S(1)} %get-tuple-element.31.low_ref, f32[16,128]{1,0:T(8,128)S(1)} %get-tuple-element.32.share_ref, f32[4,16,256]{2,1,0:T(8,128)S(1)} %get-tuple-element.40.z_own, ...), custom_call_target="tpu_custom_call" | custom-call | flops 1000 | bytes 1000 | tf_op jit(solution)/shard_map/pallas_call | solution.py:453
  26.2 1.2 %collective-permute-done.5.refs_0_ = bf16[13,16,256]{2,1,0:T(8,128)(2,1)S(1)} collective-permute-done((bf16[13,16,256]{2,1,0:T(8,128)(2,1)S(1)}, bf16[13,16,256]{2,1,0:T(8,128)(2,1)S(1)}, u32[]{:S(2)}, u32[]{:S(2)}) %collective-permute-start.5) | collective-permute-done | bytes 106528 | tf_op jit(solution)/shard_map/ppermute | solution.py:532
  27.4 0.0 collective-permute-done.6.refs_1_
  27.4 0.1 collective-permute-done.7.refs_2_
  27.5 0.0 collective-permute-done.8.refs_3_
  27.5 0.9 %shard_map.104 = f32[16,32,128]{2,1,0:T(8,128)} custom-call(f32[16,16,128]{2,1,0:T(8,128)S(1)} %shard_map.103.ridge_ref, f32[13,16,256]{2,1,0:T(8,128)S(1)} %get-tuple-element.42.x_own, f32[4,16,256]{2,1,0:T(8,128)S(1)} %get-tuple-element.40.z_own, bf16[4,16,256]{2,1,0:T(8,128)(2,1)S(1)} %collective-permute-done.4.z_came, ...), custom_call_target="tpu_custom_call" | custom-call | flops 1000 | bytes 1000 | tf_op jit(solution)/shard_map/pallas_call | solution.py:484
Async XLA Ops:
  5.3 11.7 %collective-permute-start = (bf16[3,13,16,256]{3,2,1,0:T(8,128)(2,1)S(1)}, bf16[3,13,16,256]{3,2,1,0:T(8,128)(2,1)S(1)}, u32[]{:S(2)}, u32[]{:S(2)}) collective-permute-start(bf16[3,13,16,256]{3,2,1,0:T(8,128)(2,1)S(1)} %get-tuple-element.34), channel_id=1, source_target_pairs={{0,2},{2,0},{4,6},{6,4},{8,10},{10,8},{12,14},{14,12},{1,3},{3,1},... | collective-permute-start | bytes 958472 | tf_op jit(solution)/shard_map/ppermute | solution.py:532
  8.3 6.8 %collective-permute-start.1 = (bf16[7,16,256]{2,1,0:T(8,128)(2,1)S(1)}, bf16[7,16,256]{2,1,0:T(8,128)(2,1)S(1)}, u32[]{:S(2)}, u32[]{:S(2)}) collective-permute-start(bf16[7,16,256]{2,1,0:T(8,128)(2,1)S(1)} %get-tuple-element.37), channel_id=1, source_target_pairs={{0,8},{2,10},{4,12},{6,14},{8,0},{10,2},{12,4},{14,6},{1,9},{3,11}... | collective-permute-start | bytes 172040 | tf_op jit(solution)/shard_map/ppermute | solution.py:532
  10.9 6.1 %collective-permute-start.2 = (bf16[7,16,256]{2,1,0:T(8,128)(2,1)S(1)}, bf16[7,16,256]{2,1,0:T(8,128)(2,1)S(1)}, u32[]{:S(2)}, u32[]{:S(2)}) collective-permute-start(bf16[7,16,256]{2,1,0:T(8,128)(2,1)S(1)} %get-tuple-element.38), channel_id=1, source_target_pairs={{0,12},{2,14},{4,8},{6,10},{8,4},{10,6},{12,0},{14,2},{1,13},{3,15... | collective-permute-start | bytes 172040 | tf_op jit(solution)/shard_map/ppermute | solution.py:532
  12.2 4.8 %collective-permute-start.3 = (bf16[7,16,256]{2,1,0:T(8,128)(2,1)S(1)}, bf16[7,16,256]{2,1,0:T(8,128)(2,1)S(1)}, u32[]{:S(2)}, u32[]{:S(2)}) collective-permute-start(bf16[7,16,256]{2,1,0:T(8,128)(2,1)S(1)} %get-tuple-element.39), channel_id=1, source_target_pairs={{0,4},{2,6},{4,0},{6,2},{8,12},{10,14},{12,8},{14,10},{1,5},{3,7},... | collective-permute-start | bytes 172040 | tf_op jit(solution)/shard_map/ppermute | solution.py:532
  17.1 10.3 %collective-permute-start.5 = (bf16[13,16,256]{2,1,0:T(8,128)(2,1)S(1)}, bf16[13,16,256]{2,1,0:T(8,128)(2,1)S(1)}, u32[]{:S(2)}, u32[]{:S(2)}) collective-permute-start(bf16[13,16,256]{2,1,0:T(8,128)(2,1)S(1)} %get-tuple-element.43), channel_id=1, source_target_pairs={{0,8},{2,10},{4,12},{6,14},{8,0},{10,2},{12,4},{14,6},{1,9},{3,11}... | collective-permute-start | bytes 319496 | tf_op jit(solution)/shard_map/ppermute | solution.py:532
  19.0 8.4 %collective-permute-start.6 = (bf16[13,16,256]{2,1,0:T(8,128)(2,1)S(1)}, bf16[13,16,256]{2,1,0:T(8,128)(2,1)S(1)}, u32[]{:S(2)}, u32[]{:S(2)}) collective-permute-start(bf16[13,16,256]{2,1,0:T(8,128)(2,1)S(1)} %get-tuple-element.44), channel_id=1, source_target_pairs={{0,12},{2,14},{4,8},{6,10},{8,4},{10,6},{12,0},{14,2},{1,13},{3,15... | collective-permute-start | bytes 319496 | tf_op jit(solution)/shard_map/ppermute | solution.py:532
  20.2 7.3 %collective-permute-start.7 = (bf16[13,16,256]{2,1,0:T(8,128)(2,1)S(1)}, bf16[13,16,256]{2,1,0:T(8,128)(2,1)S(1)}, u32[]{:S(2)}, u32[]{:S(2)}) collective-permute-start(bf16[13,16,256]{2,1,0:T(8,128)(2,1)S(1)} %get-tuple-element.45), channel_id=1, source_target_pairs={{0,4},{2,6},{4,0},{6,2},{8,12},{10,14},{12,8},{14,10},{1,5},{3,7},... | collective-permute-start | bytes 319496 | tf_op jit(solution)/shard_map/ppermute | solution.py:532
  20.7 6.8 %collective-permute-start.8 = (bf16[13,16,256]{2,1,0:T(8,128)(2,1)S(1)}, bf16[13,16,256]{2,1,0:T(8,128)(2,1)S(1)}, u32[]{:S(2)}, u32[]{:S(2)}) collective-permute-start(bf16[13,16,256]{2,1,0:T(8,128)(2,1)S(1)} %get-tuple-element.46), channel_id=1, source_target_pairs={{0,2},{2,0},{4,6},{6,4},{8,10},{10,8},{12,14},{14,12},{1,3},{3,1},... | collective-permute-start | bytes 319496 | tf_op jit(solution)/shard_map/ppermute | solution.py:532
  21.9 3.9 %collective-permute-start.4 = (bf16[4,16,256]{2,1,0:T(8,128)(2,1)S(1)}, bf16[4,16,256]{2,1,0:T(8,128)(2,1)S(1)}, u32[]{:S(2)}, u32[]{:S(2)}) collective-permute-start(bf16[4,16,256]{2,1,0:T(8,128)(2,1)S(1)} %get-tuple-element.41), channel_id=1, source_target_pairs={{0,2},{2,0},{4,6},{6,4},{8,10},{10,8},{12,14},{14,12},{1,3},{3,1},... | collective-permute-start | bytes 98312 | tf_op jit(solution)/shard_map/ppermute | solution.py:532
